TPU v7x, 32 devices: a whole 2x2x4 slice. The times are simulated.
32 devices in a mesh: dp: 4 (over y, x), tensor: 8 (over z, core).
Axes of the slice: x: 2, y: 2, z: 4, core: 2. Of those that a mesh axis runs over, the one named last changes fastest.
Arguments:
- inputs: bfloat16 [4096, 8192], P(('dp', 'tensor')), may hold values from -6 to 6
- queries: bfloat16 [4096, 6144], P('dp', 'tensor'), may hold values from -6 to 6
- keys_values: bfloat16 [4096, 1024], P('dp', 'tensor'), may hold values from -6 to 6
- out_grad: bfloat16 [4096, 6144], P('dp', 'tensor'), may hold values from -6 to 6
- weight_mask: int32 [8192, 1024], P('dp', 'tensor'), may hold values 0 or 1
- clip_mask: int32 [4096, 8], P('dp', 'tensor'), may hold values 0 or 1
Outputs:
- query_grad: bfloat16 [4096, 6144], P('dp', 'tensor')
- weight_grad: float32 [8192, 1024], P('dp', 'tensor')
All inputs are finite; a program needn't handle non-finite values. No bound on the sum of `weight_mask` or of `clip_mask` on one device may be relied on, other than what follows from the above.
Results may differ from a plain program's by a relative error of at most 0.0056.
Values may be sent and summed in bfloat16 or wider, within the bound.
No kernel may reach another device: no remote copies, remote signals or barrier semaphores. Data moves between devices by JAX's collectives and lax.ppermute only.
A program may use at most 192 MiB of HBM per device.

v0:
```python
import jax
import jax.numpy as jnp
from jax import lax
from jax.sharding import PartitionSpec as P


def partner_2(value, axis, distance):
    mask = 2**distance
    pairs = [(source, source ^ mask) for source in range(lax.axis_size(axis))]
    return lax.ppermute(value, axis, pairs)


def head_backward(query, keys, values, upstream):
    length = query.shape[0]
    height = min(512, length)
    factor = query.shape[1] ** (-0.5)
    query_pieces = []
    key_grad = jnp.zeros(keys.shape, jnp.float32)
    value_grad = jnp.zeros(values.shape, jnp.float32)
    for block in range(length // height):
        first = block * height
        finish = first + height
        query_block = query[first:finish]
        upstream_block = upstream[first:finish]
        key_block = keys[:finish]
        value_block = values[:finish]
        scores = jnp.dot(query_block, key_block.T, preferred_element_type=jnp.float32) * factor
        row_place = first + lax.broadcasted_iota(jnp.int32, scores.shape, 0)
        col_place = lax.broadcasted_iota(jnp.int32, scores.shape, 1)
        scores = jnp.where(col_place <= row_place, scores, -jnp.inf)
        biggest = jnp.max(scores, axis=1, keepdims=True)
        weights = jnp.exp(scores - biggest)
        weights = weights / jnp.sum(weights, axis=1, keepdims=True)
        weights_half = weights.astype(jnp.bfloat16)
        value_grad = value_grad.at[:finish].add(
            jnp.dot(weights_half.T, upstream_block, preferred_element_type=jnp.float32)
        )
        product = jnp.dot(upstream_block, value_block.T, preferred_element_type=jnp.float32)
        center = jnp.sum(weights * product, axis=1, keepdims=True)
        score_grad = (weights * (product - center) * factor).astype(jnp.bfloat16)
        query_pieces.append(jnp.dot(score_grad, key_block, preferred_element_type=jnp.float32))
        key_grad = key_grad.at[:finish].add(
            jnp.dot(score_grad.T, query_block, preferred_element_type=jnp.float32)
        )
    return (jnp.concatenate(query_pieces, 0).astype(jnp.bfloat16), key_grad, value_grad)


def contract_rows(left, right):
    return lax.dot_general(
        left, right, (((0,), (0,)), ((), ())), preferred_element_type=jnp.float32
    )


def per_device(inputs, queries, keys_values, out_grad, weight_mask, clip_mask):
    length, width = queries.shape
    depth = keys_values.shape[1]
    heads = width // depth
    is_even = lax.axis_index("tensor") % 2 == 0
    partner = partner_2(keys_values, "tensor", 0)
    keys = jnp.where(is_even, keys_values, partner)
    values = jnp.where(is_even, partner, keys_values)
    query_heads = queries.reshape(length, heads, depth).transpose(1, 0, 2)
    upstream_heads = out_grad.reshape(length, heads, depth).transpose(1, 0, 2)

    def per_head(carry, items):
        query_part, key_part, value_part = head_backward(items[0], keys, values, items[1])
        return ((carry[0] + key_part, carry[1] + value_part), query_part)

    zeros = jnp.zeros((length, depth), jnp.float32)
    sums, query_stack = lax.scan(per_head, (zeros, zeros), (query_heads, upstream_heads))
    key_sum, value_sum = sums
    query_out = query_stack.transpose(1, 0, 2).reshape(length, width)
    own_mask = clip_mask.astype(jnp.float32)
    mine = jnp.where(is_even, key_sum, value_sum)
    theirs = jnp.where(is_even, value_sum, key_sum)
    arrived = partner_2(theirs, "tensor", 0)
    needed = ((mine + arrived) * own_mask).astype(jnp.bfloat16)
    term = contract_rows(lax.all_gather(inputs, "tensor", axis=0, tiled=True), needed)
    summed = lax.psum_scatter(term, "dp", scatter_dimension=0, tiled=True)
    weight_grad = jnp.where(weight_mask == 1, summed, jnp.zeros_like(summed))
    return (query_out, weight_grad)


def solution(mesh):
    in_specs = (
        P(("dp", "tensor"), None),
        P("dp", "tensor"),
        P("dp", "tensor"),
        P("dp", "tensor"),
        P("dp", "tensor"),
        P("dp", "tensor"),
    )
    out_specs = (P("dp", "tensor"), P("dp", "tensor"))
    return jax.shard_map(
        per_device, mesh=mesh, in_specs=in_specs, out_specs=out_specs, check_vma=False
    )
```

profile of v0, /device:TPU:0, one launch (start us, length us, event | category | flops | bytes accessed | tf_op | source)
XLA Modules:
  0.0 234.5 jit_solution(3168473237139887049)
XLA Ops:
  8.7 1.6 copy.11
  10.3 1.6 copy.12
  11.9 1.7 broadcast_select_fusion.1
  13.6 103.2 %while.24 = (s32[]{:T(128)}, f32[1024,128]{1,0:T(8,128)}, f32[1024,128]{1,0:T(8,128)}, bf16[6,1024,128]{1,2,0:T(8,128)(2,1)}, bf16[6,1024,128]{1,2,0:T(8,128)(2,...) while((s32[]{:T(128)}, f32[1024,128]{1,0:T(8,128)}, ...), condition=%wide.region_7.8_spmd.clone, body=%wide.region_0.7_spmd.clone.sunk | while | flops 1023014400 | bytes 52871580 | solution.py:70
  13.6 1.7 fusion.70
  15.8 1.8 multiply_reduce_fusion.4
  19.7 1.6 multiply_reduce_fusion.5
  23.6 2.3 fusion.75
  25.9 1.3 fusion.76
  27.3 1.8 fusion.77
  30.8 1.7 fusion.70
  32.9 1.8 multiply_reduce_fusion.4
  36.9 1.5 multiply_reduce_fusion.5
  40.7 2.5 %fusion.75 = f32[1024,128]{1,0:T(8,128)} fusion(bf16[512,1024]{1,0:T(8,128)(2,1)S(1)} %multiply_convert_fusion.6, f32[1024,128]{1,0:T(8,128)} %get-tuple-element.348, f32[512,128]{1,0:T(8,128)S(1)} %fusion.74, pred[]{:T(512)S(6)} %compare.51, bf16[6,1024,128]{1,2,0:T(8,128)(2,1)} %get-tuple-element.362, s32[]{:T(128)S(6)} %copy.34, s32[]{:T(128)S(6)} %add.114), kind=kOutput, calls=%fused_computation.11.clone.1 | convolution fusion | flops 134610944 | bytes 2490377 | tf_op jit(solution)/shard_map/while/body/eval_jaxpr/dot_general | solution.py:43
  43.1 1.3 fusion.76
  44.5 1.8 fusion.77
  48.0 1.7 fusion.70
  50.1 1.8 multiply_reduce_fusion.4
  54.1 1.5 multiply_reduce_fusion.5
  57.9 2.5 %fusion.75 = f32[1024,128]{1,0:T(8,128)} fusion(bf16[512,1024]{1,0:T(8,128)(2,1)S(1)} %multiply_convert_fusion.6, f32[1024,128]{1,0:T(8,128)} %get-tuple-element.348, f32[512,128]{1,0:T(8,128)S(1)} %fusion.74, pred[]{:T(512)S(6)} %compare.51, bf16[6,1024,128]{1,2,0:T(8,128)(2,1)} %get-tuple-element.362, s32[]{:T(128)S(6)} %copy.34, s32[]{:T(128)S(6)} %add.114), kind=kOutput, calls=%fused_computation.11.clone.1 | convolution fusion | flops 134610944 | bytes 2490377 | tf_op jit(solution)/shard_map/while/body/eval_jaxpr/dot_general | solution.py:43
  60.3 1.3 fusion.76
  61.7 1.8 fusion.77
  65.2 1.7 fusion.70
  67.3 1.8 multiply_reduce_fusion.4
  71.3 1.5 multiply_reduce_fusion.5
  75.0 2.5 %fusion.75 = f32[1024,128]{1,0:T(8,128)} fusion(bf16[512,1024]{1,0:T(8,128)(2,1)S(1)} %multiply_convert_fusion.6, f32[1024,128]{1,0:T(8,128)} %get-tuple-element.348, f32[512,128]{1,0:T(8,128)S(1)} %fusion.74, pred[]{:T(512)S(6)} %compare.51, bf16[6,1024,128]{1,2,0:T(8,128)(2,1)} %get-tuple-element.362, s32[]{:T(128)S(6)} %copy.34, s32[]{:T(128)S(6)} %add.114), kind=kOutput, calls=%fused_computation.11.clone.1 | convolution fusion | flops 134610944 | bytes 2490377 | tf_op jit(solution)/shard_map/while/body/eval_jaxpr/dot_general | solution.py:43
  77.5 1.3 fusion.76
  78.8 1.8 fusion.77
  82.4 1.7 fusion.70
  84.5 1.8 multiply_reduce_fusion.4
  88.5 1.5 multiply_reduce_fusion.5
  92.2 2.5 %fusion.75 = f32[1024,128]{1,0:T(8,128)} fusion(bf16[512,1024]{1,0:T(8,128)(2,1)S(1)} %multiply_convert_fusion.6, f32[1024,128]{1,0:T(8,128)} %get-tuple-element.348, f32[512,128]{1,0:T(8,128)S(1)} %fusion.74, pred[]{:T(512)S(6)} %compare.51, bf16[6,1024,128]{1,2,0:T(8,128)(2,1)} %get-tuple-element.362, s32[]{:T(128)S(6)} %copy.34, s32[]{:T(128)S(6)} %add.114), kind=kOutput, calls=%fused_computation.11.clone.1 | convolution fusion | flops 134610944 | bytes 2490377 | tf_op jit(solution)/shard_map/while/body/eval_jaxpr/dot_general | solution.py:43
  94.7 1.3 fusion.76
  96.1 1.8 fusion.77
  99.6 1.7 fusion.70
  101.7 1.8 multiply_reduce_fusion.4
  105.7 1.5 multiply_reduce_fusion.5
  109.5 2.5 %fusion.75 = f32[1024,128]{1,0:T(8,128)} fusion(bf16[512,1024]{1,0:T(8,128)(2,1)S(1)} %multiply_convert_fusion.6, f32[1024,128]{1,0:T(8,128)} %get-tuple-element.348, f32[512,128]{1,0:T(8,128)S(1)} %fusion.74, pred[]{:T(512)S(6)} %compare.51, bf16[6,1024,128]{1,2,0:T(8,128)(2,1)} %get-tuple-element.362, s32[]{:T(128)S(6)} %copy.34, s32[]{:T(128)S(6)} %add.114), kind=kOutput, calls=%fused_computation.11.clone.1 | convolution fusion | flops 134610944 | bytes 2490377 | tf_op jit(solution)/shard_map/while/body/eval_jaxpr/dot_general | solution.py:43
  112.0 1.3 fusion.76
  113.3 1.8 fusion.77
  118.5 1.5 collective-permute-done.1
  120.0 43.5 %all-gather.2.cloned.1.call-done = bf16[1024,8192]{1,0:T(8,128)(2,1)} async-done(((bf16[128,8192]{1,0:T(8,128)(2,1)}), bf16[1024,8192]{1,0:T(8,128)(2,1)}) %all-gather.2.cloned.1.call-update) | async-done | bytes 16777232 | tf_op jit(solution)/shard_map/all_gather | solution.py:78
  163.5 10.5 %convolution_bitcast_fusion = f32[8192,128]{0,1:T(8,128)} fusion(bf16[1024,8192]{1,0:T(8,128)(2,1)} %all-gather.2.cloned.1.call-done, f32[1024,128]{1,0:T(8,128)S(1)} %collective-permute-done.1, f32[1024,128]{1,0:T(8,128)} %get-tuple-element.204, f32[1024,128]{1,0:T(8,128)} %get-tuple-element.205, f32[1024]{0:T(1024)S(1)} %bitcast.93, pred[]{:T(512)S(6)} %eq.11), kind=kOutput, calls=%fused_computation.47 | convolution fusion | flops 2148007936 | bytes 22548480 | tf_op jit(solution)/shard_map/dot_general | solution.py:49
  174.0 1.7 copy.16
  175.7 1.6 copy.17
  177.2 47.8 %reduce-scatter.2.cloned.1.call-done = f32[2048,128]{0,1:T(8,128)} async-done(((f32[8192,128]{0,1:T(8,128)}), f32[2048,128]{0,1:T(8,128)}) %reduce-scatter.2.cloned.1.call-update) | async-done | bytes 1048592 | tf_op jit(solution)/shard_map/reduce_scatter | solution.py:79
  225.0 1.3 compare_select_fusion
  226.4 1.3 copy.18
  (190 shorter events, 42.3 us)
Async XLA Ops:
  7.2 1.0 copy-start.11
  7.2 1.5 copy-start.8
  7.2 156.3 %all-gather.2.cloned.1.call-start = ((), (), s32[]{:S(2)}) async-start(), calls=%async_computation.1 | async-start | bytes 18874368 | tf_op jit(solution)/shard_map/all_gather | solution.py:78
  7.9 2.4 %copy-start.9 = (bf16[1024,768]{1,0:T(8,128)(2,1)S(1)}, bf16[1024,768]{1,0:T(8,128)(2,1)}, u32[]{:S(2)}) copy-start(bf16[1024,768]{1,0:T(8,128)(2,1)} %param.23) | copy-start | bytes 4718596
  7.9 217.1 %reduce-scatter.2.cloned.1.call-start = ((), (), s32[]{:S(2)}) async-start(), calls=%async_computation.2 | async-start | bytes 5242880 | tf_op jit(solution)/shard_map/reduce_scatter | solution.py:79
  8.1 3.8 %collective-permute-start = (bf16[1024,128]{1,0:T(8,128)(2,1)S(1)}, bf16[1024,128]{1,0:T(8,128)(2,1)}, u32[]{:S(2)}, u32[]{:S(2)}) collective-permute-start(bf16[1024,128]{1,0:T(8,128)(2,1)S(1)} %copy-done.11), channel_id=1, source_target_pairs={{0,1},{1,0},{2,3},{3,2},{4,5},{5,4},{6,7},{7,6},{8,9},{9,8},{10,11... | collective-permute-start | bytes 786440 | tf_op jit(solution)/shard_map/ppermute | solution.py:10
  13.6 104.9 %copy-start.12 = (s32[1024,1]{0,1:T(1,128)S(1)}, s32[1024,1]{0,1:T(1,128)}, u32[]{:S(2)}) copy-start(s32[1024,1]{0,1:T(1,128)} %param.25) | copy-start | bytes 12292
  13.6 4.7 %copy-start.4 = (bf16[1024,128]{1,0:T(8,128)(2,1)}, bf16[1024,128]{1,0:T(8,128)(2,1)S(1)}, u32[]{:S(2)}) copy-start(bf16[1024,128]{1,0:T(8,128)(2,1)S(1)} %get-tuple-element.363) | copy-start | bytes 786436 | tf_op jit(solution)/shard_map/while
  19.5 1.8 copy-start.2
  23.6 2.3 copy-start.3
  25.9 1.3 copy-start.6
  27.2 1.8 copy-start.5
  27.3 2.3 copy-start.1
  29.1 0.8 copy-start.7
  30.8 4.7 %copy-start.4 = (bf16[1024,128]{1,0:T(8,128)(2,1)}, bf16[1024,128]{1,0:T(8,128)(2,1)S(1)}, u32[]{:S(2)}) copy-start(bf16[1024,128]{1,0:T(8,128)(2,1)S(1)} %get-tuple-element.363) | copy-start | bytes 786436 | tf_op jit(solution)/shard_map/while
  36.7 1.7 copy-start.2
  40.7 2.5 %copy-start.3 = (f32[512,512]{0,1:T(8,128)S(1)}, f32[512,512]{0,1:T(8,128)}, u32[]{:S(2)}) copy-start(f32[512,512]{0,1:T(8,128)} %copy-done.2) | copy-start | bytes 3145732 | tf_op jit(solution)/shard_map/while
  43.1 1.3 copy-start.6
  44.4 1.8 copy-start.5
  44.5 2.3 copy-start.1
  46.3 0.8 copy-start.7
  48.0 4.6 %copy-start.4 = (bf16[1024,128]{1,0:T(8,128)(2,1)}, bf16[1024,128]{1,0:T(8,128)(2,1)S(1)}, u32[]{:S(2)}) copy-start(bf16[1024,128]{1,0:T(8,128)(2,1)S(1)} %get-tuple-element.363) | copy-start | bytes 786436 | tf_op jit(solution)/shard_map/while
  53.9 1.7 copy-start.2
  57.9 2.5 %copy-start.3 = (f32[512,512]{0,1:T(8,128)S(1)}, f32[512,512]{0,1:T(8,128)}, u32[]{:S(2)}) copy-start(f32[512,512]{0,1:T(8,128)} %copy-done.2) | copy-start | bytes 3145732 | tf_op jit(solution)/shard_map/while
  60.3 1.3 copy-start.6
  61.6 1.8 copy-start.5
  61.6 2.3 copy-start.1
  65.2 4.6 %copy-start.4 = (bf16[1024,128]{1,0:T(8,128)(2,1)}, bf16[1024,128]{1,0:T(8,128)(2,1)S(1)}, u32[]{:S(2)}) copy-start(bf16[1024,128]{1,0:T(8,128)(2,1)S(1)} %get-tuple-element.363) | copy-start | bytes 786436 | tf_op jit(solution)/shard_map/while
  71.1 1.7 copy-start.2
  75.0 2.5 %copy-start.3 = (f32[512,512]{0,1:T(8,128)S(1)}, f32[512,512]{0,1:T(8,128)}, u32[]{:S(2)}) copy-start(f32[512,512]{0,1:T(8,128)} %copy-done.2) | copy-start | bytes 3145732 | tf_op jit(solution)/shard_map/while
  77.5 1.3 copy-start.6
  78.8 1.8 copy-start.5
  78.8 2.3 copy-start.1
  82.4 4.6 %copy-start.4 = (bf16[1024,128]{1,0:T(8,128)(2,1)}, bf16[1024,128]{1,0:T(8,128)(2,1)S(1)}, u32[]{:S(2)}) copy-start(bf16[1024,128]{1,0:T(8,128)(2,1)S(1)} %get-tuple-element.363) | copy-start | bytes 786436 | tf_op jit(solution)/shard_map/while
  88.3 1.7 copy-start.2
  92.2 2.5 %copy-start.3 = (f32[512,512]{0,1:T(8,128)S(1)}, f32[512,512]{0,1:T(8,128)}, u32[]{:S(2)}) copy-start(f32[512,512]{0,1:T(8,128)} %copy-done.2) | copy-start | bytes 3145732 | tf_op jit(solution)/shard_map/while
  94.7 1.3 copy-start.6
  96.0 1.8 copy-start.5
  96.1 2.3 copy-start.1
  99.6 4.6 %copy-start.4 = (bf16[1024,128]{1,0:T(8,128)(2,1)}, bf16[1024,128]{1,0:T(8,128)(2,1)S(1)}, u32[]{:S(2)}) copy-start(bf16[1024,128]{1,0:T(8,128)(2,1)S(1)} %get-tuple-element.363) | copy-start | bytes 786436 | tf_op jit(solution)/shard_map/while
  105.5 1.7 copy-start.2
  109.4 2.6 %copy-start.3 = (f32[512,512]{0,1:T(8,128)S(1)}, f32[512,512]{0,1:T(8,128)}, u32[]{:S(2)}) copy-start(f32[512,512]{0,1:T(8,128)} %copy-done.2) | copy-start | bytes 3145732 | tf_op jit(solution)/shard_map/while
  112.0 1.3 copy-start.6
  113.3 1.8 copy-start.5
  113.3 2.3 copy-start.1
  115.1 0.8 copy-start.7
  118.0 2.0 collective-permute-start.1
  173.9 1.7 copy-start.10
  (9 other events, 7.2 us)
Sparse Core Ops, SparseCore 0:
  9.6 153.7 all-gather.1
  174.1 50.9 reduce-scatter.1
where the time goes:
time: 236 us; the launch traced here: 235 us
  waiting for transfers between devices  93.5 us (40%)
  matrix products  92.7 us (39%)
  local copies, waits for them, and re-layouts  18.2 us (8%)
  between operations  14.1 us (6%)
  other arithmetic  14 us (6%)
    reduce_scatter x1, waiting for transfers between devices, per_device(): summed = lax.psum_scatter(term, 'dp', scatter_dimension=0, tiled=True)  47.8 us
    all_gather x1, waiting for transfers between devices, per_device(): lax.all_gather(inputs, 'tensor', axis=0, tiled=True)  43.5 us
    dot_general x12, matrix products, head_backward(): jnp.dot(score_grad.T, query_block, preferred_element_type=jnp.float32)  21.9 us
    dot_general x12, matrix products, head_backward(): jnp.dot(upstream_block, value_block.T, preferred_element_type=jnp.float32)  20 us
    dot_general x12, matrix products, head_backward(): jnp.dot(weights_half.T, upstream_block, preferred_element_type=jnp.float32)  18.4 us
    dot_general x12, matrix products, head_backward(): jnp.dot(query_block, key_block.T, preferred_element_type=jnp.float32)  17.2 us
    dot_general x1, matrix products, contract_rows(): lax.dot_general(left, right, (((0,), (0,)), ((), ())), preferred_element_...  10.5 us
    unnamed x15, local copies, waits for them, and re-layouts  8.08 us
  transfers between devices with their start and end apart: 4, of which 3 were waited for; matrix products, arithmetic and copies ran while one was open for 45% of the time, Pallas kernels for 0%

commit v1 on v0

v1 whole, which is shorter than its diff:
```python
import functools
import math

import jax
import jax.numpy as jnp
from jax import lax
from jax.experimental import pallas as pl
from jax.experimental.pallas import tpu as pltpu
from jax.sharding import PartitionSpec as P

F32 = jnp.float32
BF16 = jnp.bfloat16
VMEM_LIMIT = 56 * 2**20


def swap(value, axis, mask):
    pairs = [(source, source ^ mask) for source in range(lax.axis_size(axis))]
    return lax.ppermute(value, axis, pairs)


def dot(left, right, left_dim, right_dim):
    dims = (((left_dim,), (right_dim,)), ((), ()))
    return lax.dot_general(left, right, dims, preferred_element_type=F32)


def attention_kernel(height, own_ref, other_ref, q_ref, up_ref, dq_ref, mine_ref, theirs_ref, k_ref, v_ref, dk_ref, dv_ref):
    length, depth = q_ref.shape
    factor = depth**-0.5
    power = factor * math.log2(math.e)
    head = pl.program_id(0)
    is_even = lax.axis_index("tensor") % 2 == 0

    @pl.when(head == 0)
    def _():
        k_ref[...] = jnp.where(is_even, own_ref[...], other_ref[...])
        v_ref[...] = jnp.where(is_even, other_ref[...], own_ref[...])
        dk_ref[...] = jnp.zeros_like(dk_ref)
        dv_ref[...] = jnp.zeros_like(dv_ref)

    for block in reversed(range(length // height)):
        first = block * height
        finish = first + height
        query = q_ref[first:finish]
        upstream = up_ref[first:finish]
        keys = k_ref[:finish]
        values = v_ref[:finish]
        scores = dot(keys, query, 1, 1)
        key_place = lax.broadcasted_iota(jnp.int32, (height, height), 0)
        query_place = lax.broadcasted_iota(jnp.int32, (height, height), 1)
        corner = jnp.where(key_place <= query_place, scores[first:], -jnp.inf)
        scores = corner if block == 0 else jnp.concatenate([scores[:first], corner], 0)
        biggest = jnp.max(scores, axis=0, keepdims=True)
        weights = jnp.exp2((scores - biggest) * power)
        weights = weights * (1.0 / jnp.sum(weights, axis=0, keepdims=True))
        product = dot(values, upstream, 1, 1)
        center = jnp.sum(weights * product, axis=0, keepdims=True)
        score_grad = (weights * (product - center) * factor).astype(BF16)
        dv_ref[:finish] += dot(weights.astype(BF16), upstream, 1, 0)
        dk_ref[:finish] += dot(score_grad, query, 1, 0)
        dq_ref[first:finish] = dot(score_grad, keys, 0, 0).astype(BF16)

    @pl.when(head == pl.num_programs(0) - 1)
    def _():
        mine_ref[...] = jnp.where(is_even, dk_ref[...], dv_ref[...])
        theirs_ref[...] = jnp.where(is_even, dv_ref[...], dk_ref[...])


def attention(own, other, queries, out_grad):
    length, width = queries.shape
    depth = own.shape[1]
    height = min(512, length)
    column = pl.BlockSpec((length, depth), lambda h: (0, h))
    whole = pl.BlockSpec((length, depth), lambda h: (0, 0))
    sums = jax.ShapeDtypeStruct((length, depth), F32)
    return pl.pallas_call(
        functools.partial(attention_kernel, height),
        grid=(width // depth,),
        in_specs=[whole, whole, column, column],
        out_specs=[column, whole, whole],
        out_shape=[jax.ShapeDtypeStruct((length, width), BF16), sums, sums],
        scratch_shapes=[
            pltpu.VMEM((length, depth), BF16),
            pltpu.VMEM((length, depth), BF16),
            pltpu.VMEM((length, depth), F32),
            pltpu.VMEM((length, depth), F32),
        ],
        compiler_params=pltpu.CompilerParams(
            vmem_limit_bytes=VMEM_LIMIT, dimension_semantics=("arbitrary",)
        ),
        name="attention",
    )(own, other, queries, out_grad)


def kv_kernel(rows, mine_ref, arrived_ref, mask_ref, out_ref):
    place = lax.axis_index("tensor")
    chip, core = place // 2, place % 2
    for step in range(out_ref.shape[0]):
        for half in range(2):
            start = ((chip ^ step) * 2 + (core ^ half)) * rows
            span = pl.ds(pl.multiple_of(start, rows), rows)
            total = (mine_ref[span, :] + arrived_ref[span, :]).T
            keep = mask_ref[:, span].astype(F32)
            out_ref[step, :, half * rows : (half + 1) * rows] = (total * keep).astype(BF16)


def kv_blocks(mine, arrived, mask, rows):
    length, depth = mine.shape
    return pl.pallas_call(
        functools.partial(kv_kernel, rows),
        out_shape=jax.ShapeDtypeStruct((length // (2 * rows), depth, 2 * rows), BF16),
        compiler_params=pltpu.CompilerParams(vmem_limit_bytes=VMEM_LIMIT),
        name="kv_blocks",
    )(mine, arrived, mask)


def project_kernel(parts, *refs):
    out_ref = refs[-1]
    total = None
    for part in range(parts):
        grads = refs[2 * parts + part]
        rows = refs[0].shape[0]
        for half in range(2):
            term = dot(grads[:, half * rows : (half + 1) * rows], refs[2 * part + half][...], 1, 0)
            total = term if total is None else total + term
    out_ref[...] = total.astype(out_ref.dtype)


def project(pairs, grads, first, wide, dtype, tile):
    rows = pairs[0][0].shape[0]
    height, tokens = grads[0].shape
    skip = first // tile
    in_specs = [pl.BlockSpec((rows, tile), lambda j: (0, j + skip)) for _ in range(2 * len(pairs))]
    in_specs += [pl.BlockSpec((height, tokens), lambda j: (0, 0)) for _ in grads]
    return pl.pallas_call(
        functools.partial(project_kernel, len(pairs)),
        grid=(wide // tile,),
        in_specs=in_specs,
        out_specs=pl.BlockSpec((height, tile), lambda j: (0, j)),
        out_shape=jax.ShapeDtypeStruct((height, wide), dtype),
        compiler_params=pltpu.CompilerParams(
            vmem_limit_bytes=VMEM_LIMIT, dimension_semantics=("arbitrary",)
        ),
        name="project",
    )(*[x for pair in pairs for x in pair], *grads)


def finish_kernel(parts, *refs):
    total = refs[0][...]
    for part in range(1, parts):
        total = total + refs[part][...].astype(F32)
    refs[-1][...] = jnp.where(refs[parts][...] == 1, total.T, 0.0)


def finish(terms, weight_mask, tile):
    depth = terms[0].shape[0]
    height = weight_mask.shape[0]
    across = pl.BlockSpec((depth, tile), lambda j: (0, j))
    down = pl.BlockSpec((tile, depth), lambda j: (j, 0))
    return pl.pallas_call(
        functools.partial(finish_kernel, len(terms)),
        grid=(height // tile,),
        in_specs=[across] * len(terms) + [down],
        out_specs=down,
        out_shape=jax.ShapeDtypeStruct((height, depth), F32),
        compiler_params=pltpu.CompilerParams(
            vmem_limit_bytes=VMEM_LIMIT, dimension_semantics=("arbitrary",)
        ),
        name="finish",
    )(*terms, weight_mask)


def per_device(inputs, queries, keys_values, out_grad, weight_mask, clip_mask):
    depth = keys_values.shape[1]
    rows = inputs.shape[0]
    groups = lax.axis_size("dp")
    chips = lax.axis_size("tensor") // 2
    block = weight_mask.shape[0]
    row_place = lax.axis_index("dp")

    other = swap(keys_values, "tensor", 1)
    mine_rows = []
    for step in range(groups):
        start = (row_place ^ step) * block
        part = lax.dynamic_slice(inputs, (0, start), (rows, block))
        mine_rows.append(part if step == 0 else swap(part, "dp", step))
    pairs = [(part, swap(part, "tensor", 1)) for part in mine_rows]

    query_grad, mine, theirs = attention(keys_values, other, queries, out_grad)
    arrived = swap(theirs, "tensor", 1)
    blocks = kv_blocks(mine, arrived, clip_mask.reshape(1, -1), rows)

    def column(step):
        return blocks[step] if step == 0 else swap(blocks[step], "tensor", 2 * step)

    order = sorted(range(chips), key=lambda s: [(s >> b) & 1 for b in range(8)])
    stacked = jnp.concatenate([column(step) for step in order], 0)
    grads = [stacked if step == 0 else swap(stacked, "dp", step) for step in range(groups)]

    cuts = 2 if block % 1024 == 0 else 1
    wide = block // cuts
    tile = min(512, wide)
    half = chips // 2 * depth
    pieces = []
    for cut in range(cuts):
        away = project(pairs, [g[half:] for g in grads], cut * wide, wide, BF16, tile)
        pieces.append(swap(away, "tensor", 2))
    kept = project(pairs, [g[:half] for g in grads], 0, block, F32, tile)
    finals = []
    for cut in range(cuts):
        own = kept[:, cut * wide : (cut + 1) * wide]
        terms = [own, pieces[cut]]
        size, bit = half, 2
        while size > depth:
            size, bit = size // 2, bit * 2
            away = sum(t[size:].astype(F32) for t in terms).astype(BF16)
            terms = [t[:size] for t in terms] + [swap(away, "tensor", bit)]
        finals.append(terms)
    merged = [jnp.concatenate([f[k] for f in finals], 1) for k in range(len(finals[0]))]
    weight_grad = finish(merged, weight_mask, min(512, block))
    return (query_grad, weight_grad)


def solution(mesh):
    spec = P("dp", "tensor")
    in_specs = (P(("dp", "tensor"), None), spec, spec, spec, spec, spec)
    return jax.shard_map(
        per_device, mesh=mesh, in_specs=in_specs, out_specs=(spec, spec), check_vma=False
    )
```

time: 236 us -> 132 us (0.56)
  matrix products: 92.7 us -> 0 us
  Pallas kernels: 0 us -> 39.3 us
  waiting for transfers between devices: 93.5 us -> 57.1 us
  starting transfers between devices: 1.02 us -> 23.1 us
  between operations: 14.1 us -> 0.84 us
  local copies, waits for them, and re-layouts: 18.2 us -> 7.12 us
  other arithmetic: 14 us -> 3.69 us
    dot_general x61 -> x0, matrix products: 92.7 us -> none  [the longest x12 21.9 us: head_backward(): jnp.dot(score_grad.T, query_block, preferred_element_type=jnp.float32)]
    ppermute x2 -> x19, waiting for transfers between devices: 1.53 us -> 57.1 us  [swap(): return lax.ppermute(value, axis, pairs)]
    reduce_scatter x1 -> x0, waiting for transfers between devices: 47.8 us -> none  [per_device(): summed = lax.psum_scatter(term, 'dp', scatter_dimension=0, tiled=True)]
    all_gather x1 -> x0, waiting for transfers between devices: 43.5 us -> none  [per_device(): lax.all_gather(inputs, 'tensor', axis=0, tiled=True)]
    pallas_call x0 -> x6, Pallas kernels: none -> 39.3 us  [the longest x1 19.7 us: attention(): pl.pallas_call(functools.partial(attention_kernel, height), grid=(width /...]
    ppermute x2 -> x19, starting transfers between devices: 0.95 us -> 23.1 us  [swap(): return lax.ppermute(value, axis, pairs)]
    unnamed x15 -> x27, local copies, waits for them, and re-layouts: 8.08 us -> 2.77 us
    dynamic_update_slice x12 -> x0, local copies, waits for them, and re-layouts: 5.22 us -> none  [per_device(): lax.scan(per_head, (zeros, zeros), (query_heads, upstream_heads))]
  transfers between devices with their start and end apart: 4 -> 19, of which waited for: 3 -> 11; matrix products, arithmetic and copies ran while one was open for 45% -> 4% of each run, Pallas kernels for 0% -> 9%
where the time goes in v1:
time: 132 us; the launch traced here: 131 us
  waiting for transfers between devices  57.1 us (43%)
  Pallas kernels  39.3 us (30%)
  starting transfers between devices  23.1 us (18%)
  local copies, waits for them, and re-layouts  7.12 us (5%)
  other arithmetic  3.69 us (3%)
    ppermute x19, waiting for transfers between devices, swap(): return lax.ppermute(value, axis, pairs)  57.1 us
    ppermute x19, starting transfers between devices, swap(): return lax.ppermute(value, axis, pairs)  23.1 us
    pallas_call x1, Pallas kernels, attention(): pl.pallas_call(functools.partial(attention_kernel, height), grid=(width /...  19.7 us
    pallas_call x3, Pallas kernels, project(): pl.pallas_call(functools.partial(project_kernel, len(pairs)), grid=(wide...  13.5 us
    pallas_call x1, Pallas kernels, finish(): pl.pallas_call(functools.partial(finish_kernel, len(terms)), grid=(height...  4.02 us
    unnamed x27, local copies, waits for them, and re-layouts  2.77 us
  transfers between devices with their start and end apart: 19, of which 11 were waited for; matrix products, arithmetic and copies ran while one was open for 4% of the time, Pallas kernels for 9%

profile of v1, /device:TPU:0, one launch (start us, length us, event | category | flops | bytes accessed | tf_op | source)
XLA Modules:
  0.0 131.2 jit_solution(2461619229388179869)
XLA Ops:
  0.6 0.5 collective-permute-start
  1.2 1.4 %collective-permute-done.other_ref = bf16[1024,128]{1,0:T(8,128)(2,1)S(1)} collective-permute-done((bf16[1024,128]{1,0:T(8,128)(2,1)}, bf16[1024,128]{1,0:T(8,128)(2,1)S(1)}, u32[]{:S(2)}, u32[]{:S(2)}) %collective-permute-start) | collective-permute-done | bytes 262176 | tf_op jit(solution)/shard_map/ppermute | solution.py:18
  2.5 0.7 copy-done.12
  3.2 19.7 %attention.1 = (bf16[1024,768]{1,0:T(8,128)(2,1)}, f32[1024,128]{1,0:T(8,128)}, f32[1024,128]{1,0:T(8,128)}) custom-call(bf16[1024,128]{1,0:T(8,128)(2,1)} %own_ref.1, bf16[1024,128]{1,0:T(8,128)(2,1)} %copy-done.12, bf16[1024,768]{1,0:T(8,128)(2,1)} %q_ref.1, bf16[1024,768]{1,0:T(8,128)(2,1)} %up_ref.1), custom_call_target="tpu_custom_call" | custom-call | tf_op jit(solution)/shard_map/attention/pallas_call | solution.py:75
  22.9 0.4 collective-permute-start.8
  23.3 0.1 constant_dynamic-slice_fusion
  23.5 3.7 %collective-permute-start.6 = (bf16[128,2048]{1,0:T(8,128)(2,1)S(1)}, bf16[128,2048]{1,0:T(8,128)(2,1)S(1)}, u32[]{:S(2)}, u32[]{:S(2)}) collective-permute-start(bf16[128,2048]{1,0:T(8,128)(2,1)S(1)} %get-tuple-element.10), channel_id=1, source_target_pairs={{0,24},{8,16},{16,8},{24,0},{1,25},{9,17},{17,9},{25,1},{2,26},{10... | collective-permute-start | bytes 1572872 | tf_op jit(solution)/shard_map/ppermute | solution.py:18
  27.1 0.5 collective-permute-start.2
  27.8 0.8 copy-done.11
  28.6 2.1 %kv_blocks.1 = bf16[4,128,256]{2,1,0:T(8,128)(2,1)} custom-call(f32[1024,128]{1,0:T(8,128)} %get-tuple-element.6.mine_ref, f32[1024,128]{1,0:T(8,128)} %copy-done.11, s32[1,1024]{1,0:T(1,128)} %bitcast.9), custom_call_target="tpu_custom_call" | custom-call | tf_op jit(solution)/shard_map/kv_blocks/pallas_call | solution.py:108
  30.7 1.0 slice_bitcast_fusion.1
  31.6 2.1 %collective-permute-start.10 = (bf16[128,256]{1,0:T(8,128)(2,1)S(1)}, bf16[128,256]{1,0:T(8,128)(2,1)S(1)}, u32[]{:S(2)}, u32[]{:S(2)}) collective-permute-start(bf16[128,256]{1,0:T(8,128)(2,1)S(1)} %get-tuple-element.20), channel_id=1, source_target_pairs={{0,2},{1,3},{2,0},{3,1},{4,6},{5,7},{6,4},{7,5},{8,10},{9,11},{10,... | collective-permute-start | bytes 196616 | tf_op jit(solution)/shard_map/ppermute | solution.py:18
  33.7 2.5 %collective-permute-start.11 = (bf16[128,256]{1,0:T(8,128)(2,1)S(1)}, bf16[128,256]{1,0:T(8,128)(2,1)S(1)}, u32[]{:S(2)}, u32[]{:S(2)}) collective-permute-start(bf16[128,256]{1,0:T(8,128)(2,1)S(1)} %get-tuple-element.21), channel_id=1, source_target_pairs={{0,6},{1,7},{2,4},{3,5},{4,2},{5,3},{6,0},{7,1},{8,14},{9,15},{10,... | collective-permute-start | bytes 196616 | tf_op jit(solution)/shard_map/ppermute | solution.py:18
  36.1 3.1 %collective-permute-start.9 = (bf16[128,256]{1,0:T(8,128)(2,1)S(1)}, bf16[128,256]{1,0:T(8,128)(2,1)S(1)}, u32[]{:S(2)}, u32[]{:S(2)}) collective-permute-start(bf16[128,256]{1,0:T(8,128)(2,1)S(1)} %get-tuple-element.22), channel_id=1, source_target_pairs={{0,4},{1,5},{2,6},{3,7},{4,0},{5,1},{6,2},{7,3},{8,12},{9,13},{10,... | collective-permute-start | bytes 196616 | tf_op jit(solution)/shard_map/ppermute | solution.py:18
  39.3 0.8 collective-permute-done.11
  40.1 1.5 %collective-permute-done.9 = bf16[128,256]{1,0:T(8,128)(2,1)S(1)} collective-permute-done((bf16[128,256]{1,0:T(8,128)(2,1)S(1)}, bf16[128,256]{1,0:T(8,128)(2,1)S(1)}, u32[]{:S(2)}, u32[]{:S(2)}) %collective-permute-start.9) | collective-permute-done | bytes 65568 | tf_op jit(solution)/shard_map/ppermute | solution.py:18
  41.6 2.5 %collective-permute-start.14 = (bf16[512,256]{1,0:T(8,128)(2,1)S(1)}, bf16[512,256]{1,0:T(8,128)(2,1)S(1)}, u32[]{:S(2)}, u32[]{:S(2)}) collective-permute-start(bf16[512,256]{1,0:T(8,128)(2,1)S(1)} %pad_maximum_fusion.2), channel_id=1, source_target_pairs={{0,24},{8,16},{16,8},{24,0},{1,25},{9,17},{17,9},{25,1},{2,26},{10... | collective-permute-start | bytes 786440 | tf_op jit(solution)/shard_map/ppermute | solution.py:18
  44.1 0.5 collective-permute-start.13
  44.8 6.9 %collective-permute-done.2.refs_2_ = bf16[128,2048]{1,0:T(8,128)(2,1)S(1)} collective-permute-done((bf16[128,2048]{1,0:T(8,128)(2,1)S(1)}, bf16[128,2048]{1,0:T(8,128)(2,1)S(1)}, u32[]{:S(2)}, u32[]{:S(2)}) %collective-permute-start.2) | collective-permute-done | bytes 524320 | tf_op jit(solution)/shard_map/ppermute | solution.py:18
  51.7 0.5 collective-permute-start.3
  52.2 4.4 %collective-permute-done.14 = bf16[512,256]{1,0:T(8,128)(2,1)S(1)} collective-permute-done((bf16[512,256]{1,0:T(8,128)(2,1)S(1)}, bf16[512,256]{1,0:T(8,128)(2,1)S(1)}, u32[]{:S(2)}, u32[]{:S(2)}) %collective-permute-start.14) | collective-permute-done | bytes 262176 | tf_op jit(solution)/shard_map/ppermute | solution.py:18
  56.6 5.5 %collective-permute-done.13 = bf16[512,256]{1,0:T(8,128)(2,1)S(1)} collective-permute-done((bf16[512,256]{1,0:T(8,128)(2,1)S(1)}, bf16[512,256]{1,0:T(8,128)(2,1)S(1)}, u32[]{:S(2)}, u32[]{:S(2)}) %collective-permute-start.13) | collective-permute-done | bytes 262176 | tf_op jit(solution)/shard_map/ppermute | solution.py:18
  62.0 1.7 %collective-permute-start.12 = (bf16[512,256]{1,0:T(8,128)(2,1)S(1)}, bf16[512,256]{1,0:T(8,128)(2,1)S(1)}, u32[]{:S(2)}, u32[]{:S(2)}) collective-permute-start(bf16[512,256]{1,0:T(8,128)(2,1)S(1)} %pad_maximum_fusion.2), channel_id=1, source_target_pairs={{0,8},{8,0},{16,24},{24,16},{1,9},{9,1},{17,25},{25,17},{2,10},{10... | collective-permute-start | bytes 786440 | tf_op jit(solution)/shard_map/ppermute | solution.py:18
  63.7 0.7 fusion.2
  64.4 0.7 fusion.3
  65.2 5.1 %collective-permute-done.12 = bf16[512,256]{1,0:T(8,128)(2,1)S(1)} collective-permute-done((bf16[512,256]{1,0:T(8,128)(2,1)S(1)}, bf16[512,256]{1,0:T(8,128)(2,1)S(1)}, u32[]{:S(2)}, u32[]{:S(2)}) %collective-permute-start.12) | collective-permute-done | bytes 262176 | tf_op jit(solution)/shard_map/ppermute | solution.py:18
  70.3 0.7 fusion.4
  71.1 0.7 copy-done.5
  71.8 0.2 copy-done.6
  72.0 0.2 copy-done.7
  72.1 0.2 copy-done.8
  72.3 3.8 %project.4 = bf16[256,1024]{1,0:T(8,128)(2,1)} custom-call(bf16[128,2048]{1,0:T(8,128)(2,1)} %copy-done.1, bf16[128,2048]{1,0:T(8,128)(2,1)} %copy-done.5, bf16[128,2048]{1,0:T(8,128)(2,1)} %copy-done.3, bf16[128,2048]{1,0:T(8,128)(2,1)} %copy-done.7, bf16[128,2048]{1,0:T(8,128)(2,1)} %copy-done.4, bf16[128,2048]{1,0:T(8,128)(2,1)} %copy-done.8, ...), custom_call_target="tpu_custom_call" | custom-call | tf_op jit(solution)/shard_map/project/pallas_call | solution.py:134
  76.1 1.8 %collective-permute-start.15 = (bf16[256,1024]{1,0:T(8,128)(2,1)}, bf16[256,1024]{1,0:T(8,128)(2,1)S(1)}, u32[]{:S(2)}, u32[]{:S(2)}) collective-permute-start(bf16[256,1024]{1,0:T(8,128)(2,1)} %project.4), channel_id=1, source_target_pairs={{0,2},{1,3},{2,0},{3,1},{4,6},{5,7},{6,4},{7,5},{8,10},{9,11},{10,... | collective-permute-start | bytes 1572872 | tf_op jit(solution)/shard_map/ppermute | solution.py:18
  77.8 3.7 %project.5 = bf16[256,1024]{1,0:T(8,128)(2,1)} custom-call(bf16[128,2048]{1,0:T(8,128)(2,1)} %copy-done.1, bf16[128,2048]{1,0:T(8,128)(2,1)} %copy-done.5, bf16[128,2048]{1,0:T(8,128)(2,1)} %copy-done.3, bf16[128,2048]{1,0:T(8,128)(2,1)} %copy-done.7, bf16[128,2048]{1,0:T(8,128)(2,1)} %copy-done.4, bf16[128,2048]{1,0:T(8,128)(2,1)} %copy-done.8, ...), custom_call_target="tpu_custom_call" | custom-call | tf_op jit(solution)/shard_map/project/pallas_call | solution.py:134
  81.6 0.3 collective-permute-start.16
  81.8 0.6 pad_maximum_fusion.3.refs_8_
  82.5 6.0 %project.3 = f32[256,2048]{1,0:T(8,128)} custom-call(bf16[128,2048]{1,0:T(8,128)(2,1)} %copy-done.1, bf16[128,2048]{1,0:T(8,128)(2,1)} %copy-done.5, bf16[128,2048]{1,0:T(8,128)(2,1)} %copy-done.3, bf16[128,2048]{1,0:T(8,128)(2,1)} %copy-done.7, bf16[128,2048]{1,0:T(8,128)(2,1)} %copy-done.4, bf16[128,2048]{1,0:T(8,128)(2,1)} %copy-done.8, ...), custom_call_target="tpu_custom_call" | custom-call | tf_op jit(solution)/shard_map/project/pallas_call | solution.py:134
  88.5 2.6 %collective-permute-done.15 = bf16[256,1024]{1,0:T(8,128)(2,1)S(1)} collective-permute-done((bf16[256,1024]{1,0:T(8,128)(2,1)}, bf16[256,1024]{1,0:T(8,128)(2,1)S(1)}, u32[]{:S(2)}, u32[]{:S(2)}) %collective-permute-start.15) | collective-permute-done | bytes 524320 | tf_op jit(solution)/shard_map/ppermute | solution.py:18
  91.1 9.4 %collective-permute-done.16 = bf16[256,1024]{1,0:T(8,128)(2,1)S(1)} collective-permute-done((bf16[256,1024]{1,0:T(8,128)(2,1)}, bf16[256,1024]{1,0:T(8,128)(2,1)S(1)}, u32[]{:S(2)}, u32[]{:S(2)}) %collective-permute-start.16) | collective-permute-done | bytes 524320 | tf_op jit(solution)/shard_map/ppermute | solution.py:18
  100.5 1.3 %fusion.1 = (bf16[128,1024]{1,0:T(8,128)(2,1)S(1)}, bf16[128,1024]{1,0:T(8,128)(2,1)S(1)}) fusion(f32[256,2048]{1,0:T(8,128)} %project.3, bf16[256,1024]{1,0:T(8,128)(2,1)S(1)} %collective-permute-done.15, bf16[256,1024]{1,0:T(8,128)(2,1)S(1)} %collective-permute-done.16), kind=kLoop, calls=%fused_computation.3 | loop fusion | flops 786432 | bytes 2097152 | tf_op jit(solution)/shard_map/convert_element_type | solution.py:215
  101.9 2.8 %collective-permute-start.17 = (bf16[128,1024]{1,0:T(8,128)(2,1)S(1)}, bf16[128,1024]{1,0:T(8,128)(2,1)S(1)}, u32[]{:S(2)}, u32[]{:S(2)}) collective-permute-start(bf16[128,1024]{1,0:T(8,128)(2,1)S(1)} %get-tuple-element.8), channel_id=1, source_target_pairs={{0,4},{1,5},{2,6},{3,7},{4,0},{5,1},{6,2},{7,3},{8,12},{9,13},{10,... | collective-permute-start | bytes 786440 | tf_op jit(solution)/shard_map/ppermute | solution.py:18
  104.7 0.2 collective-permute-start.18
  104.9 1.1 concatenate.24.refs_0_
  106.0 0.8 pad_maximum_fusion.refs_1_
  106.8 15.1 %collective-permute-done.17 = bf16[128,1024]{1,0:T(8,128)(2,1)S(1)} collective-permute-done((bf16[128,1024]{1,0:T(8,128)(2,1)S(1)}, bf16[128,1024]{1,0:T(8,128)(2,1)S(1)}, u32[]{:S(2)}, u32[]{:S(2)}) %collective-permute-start.17) | collective-permute-done | bytes 262176 | tf_op jit(solution)/shard_map/ppermute | solution.py:18
  121.9 4.4 %collective-permute-done.18 = bf16[128,1024]{1,0:T(8,128)(2,1)S(1)} collective-permute-done((bf16[128,1024]{1,0:T(8,128)(2,1)S(1)}, bf16[128,1024]{1,0:T(8,128)(2,1)S(1)}, u32[]{:S(2)}, u32[]{:S(2)}) %collective-permute-start.18) | collective-permute-done | bytes 262176 | tf_op jit(solution)/shard_map/ppermute | solution.py:18
  126.3 0.8 pad_maximum_fusion.1.refs_2_
  127.1 4.0 %finish.1 = f32[2048,128]{1,0:T(8,128)} custom-call(f32[128,2048]{1,0:T(8,128)} %concatenate.24.refs_0_, bf16[128,2048]{1,0:T(8,128)(2,1)} %pad_maximum_fusion.refs_1_, bf16[128,2048]{1,0:T(8,128)(2,1)} %pad_maximum_fusion.1.refs_2_, s32[2048,128]{1,0:T(8,128)} %refs_3_.1), custom_call_target="tpu_custom_call" | custom-call | tf_op jit(solution)/shard_map/finish/pallas_call | solution.py:159
  (37 shorter events, 0.3 us)
Async XLA Ops:
  0.6 22.7 %copy-start.9 = (bf16[128,8192]{1,0:T(8,128)(2,1)S(1)}, bf16[128,8192]{1,0:T(8,128)(2,1)}, u32[]{:S(2)}) copy-start(bf16[128,8192]{1,0:T(8,128)(2,1)} %param.6) | copy-start | bytes 6291460
  0.6 1.9 %collective-permute-start = (bf16[1024,128]{1,0:T(8,128)(2,1)}, bf16[1024,128]{1,0:T(8,128)(2,1)S(1)}, u32[]{:S(2)}, u32[]{:S(2)}) collective-permute-start(bf16[1024,128]{1,0:T(8,128)(2,1)} %own_ref.1), channel_id=1, source_target_pairs={{0,1},{1,0},{2,3},{3,2},{4,5},{5,4},{6,7},{7,6},{8,9},{9,8},{10,11... | collective-permute-start | bytes 786440 | tf_op jit(solution)/shard_map/ppermute | solution.py:18
  2.5 0.7 copy-start.12
  22.9 4.8 %collective-permute-start.8 = (f32[1024,128]{1,0:T(8,128)}, f32[1024,128]{1,0:T(8,128)S(1)}, u32[]{:S(2)}, u32[]{:S(2)}) collective-permute-start(f32[1024,128]{1,0:T(8,128)} %get-tuple-element.7), channel_id=1, source_target_pairs={{0,1},{1,0},{2,3},{3,2},{4,5},{5,4},{6,7},{7,6},{8,9},{9,8},{10,11... | collective-permute-start | bytes 1572872 | tf_op jit(solution)/shard_map/ppermute | solution.py:18
  23.4 47.5 %copy-start.1 = (bf16[128,2048]{1,0:T(8,128)(2,1)}, bf16[128,2048]{1,0:T(8,128)(2,1)S(1)}, u32[]{:S(2)}) copy-start(bf16[128,2048]{1,0:T(8,128)(2,1)S(1)} %get-tuple-element.12.refs_0_) | copy-start | bytes 1572868
  23.5 21.2 %collective-permute-start.6 = (bf16[128,2048]{1,0:T(8,128)(2,1)S(1)}, bf16[128,2048]{1,0:T(8,128)(2,1)S(1)}, u32[]{:S(2)}, u32[]{:S(2)}) collective-permute-start(bf16[128,2048]{1,0:T(8,128)(2,1)S(1)} %get-tuple-element.10), channel_id=1, source_target_pairs={{0,24},{8,16},{16,8},{24,0},{1,25},{9,17},{17,9},{25,1},{2,26},{10... | collective-permute-start | bytes 1572872 | tf_op jit(solution)/shard_map/ppermute | solution.py:18
  27.1 24.5 %collective-permute-start.2 = (bf16[128,2048]{1,0:T(8,128)(2,1)S(1)}, bf16[128,2048]{1,0:T(8,128)(2,1)S(1)}, u32[]{:S(2)}, u32[]{:S(2)}) collective-permute-start(bf16[128,2048]{1,0:T(8,128)(2,1)S(1)} %get-tuple-element.11), channel_id=1, source_target_pairs={{0,8},{8,0},{16,24},{24,16},{1,9},{9,1},{17,25},{25,17},{2,10},{10... | collective-permute-start | bytes 1572872 | tf_op jit(solution)/shard_map/ppermute | solution.py:18
  27.7 24.0 %collective-permute-start.4 = (bf16[128,2048]{1,0:T(8,128)(2,1)S(1)}, bf16[128,2048]{1,0:T(8,128)(2,1)S(1)}, u32[]{:S(2)}, u32[]{:S(2)}) collective-permute-start(bf16[128,2048]{1,0:T(8,128)(2,1)S(1)} %get-tuple-element.13), channel_id=1, source_target_pairs={{0,16},{8,24},{16,0},{24,8},{1,17},{9,25},{17,1},{25,9},{2,18},{10... | collective-permute-start | bytes 1572872 | tf_op jit(solution)/shard_map/ppermute | solution.py:18
  27.8 0.8 copy-start.11
  31.6 4.5 %collective-permute-start.10 = (bf16[128,256]{1,0:T(8,128)(2,1)S(1)}, bf16[128,256]{1,0:T(8,128)(2,1)S(1)}, u32[]{:S(2)}, u32[]{:S(2)}) collective-permute-start(bf16[128,256]{1,0:T(8,128)(2,1)S(1)} %get-tuple-element.20), channel_id=1, source_target_pairs={{0,2},{1,3},{2,0},{3,1},{4,6},{5,7},{6,4},{7,5},{8,10},{9,11},{10,... | collective-permute-start | bytes 196616 | tf_op jit(solution)/shard_map/ppermute | solution.py:18
  33.7 6.4 %collective-permute-start.11 = (bf16[128,256]{1,0:T(8,128)(2,1)S(1)}, bf16[128,256]{1,0:T(8,128)(2,1)S(1)}, u32[]{:S(2)}, u32[]{:S(2)}) collective-permute-start(bf16[128,256]{1,0:T(8,128)(2,1)S(1)} %get-tuple-element.21), channel_id=1, source_target_pairs={{0,6},{1,7},{2,4},{3,5},{4,2},{5,3},{6,0},{7,1},{8,14},{9,15},{10,... | collective-permute-start | bytes 196616 | tf_op jit(solution)/shard_map/ppermute | solution.py:18
  36.1 5.5 %collective-permute-start.9 = (bf16[128,256]{1,0:T(8,128)(2,1)S(1)}, bf16[128,256]{1,0:T(8,128)(2,1)S(1)}, u32[]{:S(2)}, u32[]{:S(2)}) collective-permute-start(bf16[128,256]{1,0:T(8,128)(2,1)S(1)} %get-tuple-element.22), channel_id=1, source_target_pairs={{0,4},{1,5},{2,6},{3,7},{4,0},{5,1},{6,2},{7,3},{8,12},{9,13},{10,... | collective-permute-start | bytes 196616 | tf_op jit(solution)/shard_map/ppermute | solution.py:18
  41.6 14.9 %collective-permute-start.14 = (bf16[512,256]{1,0:T(8,128)(2,1)S(1)}, bf16[512,256]{1,0:T(8,128)(2,1)S(1)}, u32[]{:S(2)}, u32[]{:S(2)}) collective-permute-start(bf16[512,256]{1,0:T(8,128)(2,1)S(1)} %pad_maximum_fusion.2), channel_id=1, source_target_pairs={{0,24},{8,16},{16,8},{24,0},{1,25},{9,17},{17,9},{25,1},{2,26},{10... | collective-permute-start | bytes 786440 | tf_op jit(solution)/shard_map/ppermute | solution.py:18
  44.1 17.9 %collective-permute-start.13 = (bf16[512,256]{1,0:T(8,128)(2,1)S(1)}, bf16[512,256]{1,0:T(8,128)(2,1)S(1)}, u32[]{:S(2)}, u32[]{:S(2)}) collective-permute-start(bf16[512,256]{1,0:T(8,128)(2,1)S(1)} %pad_maximum_fusion.2), channel_id=1, source_target_pairs={{0,16},{8,24},{16,0},{24,8},{1,17},{9,25},{17,1},{25,9},{2,18},{10... | collective-permute-start | bytes 786440 | tf_op jit(solution)/shard_map/ppermute | solution.py:18
  44.7 26.4 %copy-start.10 = (bf16[256,256]{1,0:T(8,128)(2,1)}, bf16[256,256]{1,0:T(8,128)(2,1)S(1)}, u32[]{:S(2)}) copy-start(bf16[256,256]{1,0:T(8,128)(2,1)S(1)} %constant_dynamic-update-slice_fusion.refs_8_) | copy-start | bytes 393220
  44.7 26.4 %copy-start.2 = (bf16[128,2048]{1,0:T(8,128)(2,1)}, bf16[128,2048]{1,0:T(8,128)(2,1)S(1)}, u32[]{:S(2)}) copy-start(bf16[128,2048]{1,0:T(8,128)(2,1)S(1)} %collective-permute-done.6.refs_6_) | copy-start | bytes 1572868
  44.7 26.3 %collective-permute-start.1 = (bf16[128,2048]{1,0:T(8,128)(2,1)S(1)}, bf16[128,2048]{1,0:T(8,128)(2,1)S(1)}, u32[]{:S(2)}, u32[]{:S(2)}) collective-permute-start(bf16[128,2048]{1,0:T(8,128)(2,1)S(1)} %get-tuple-element.12.refs_0_), channel_id=1, source_target_pairs={{0,1},{1,0},{2,3},{3,2},{4,5},{5,4},{6,7},{7,6},{8,9},{9,8},{10,11... | collective-permute-start | bytes 1572872 | tf_op jit(solution)/shard_map/ppermute | solution.py:18
  51.6 19.4 %copy-start.3 = (bf16[128,2048]{1,0:T(8,128)(2,1)}, bf16[128,2048]{1,0:T(8,128)(2,1)S(1)}, u32[]{:S(2)}) copy-start(bf16[128,2048]{1,0:T(8,128)(2,1)S(1)} %collective-permute-done.2.refs_2_) | copy-start | bytes 1572868
  51.6 19.3 %collective-permute-start.7 = (bf16[128,2048]{1,0:T(8,128)(2,1)S(1)}, bf16[128,2048]{1,0:T(8,128)(2,1)S(1)}, u32[]{:S(2)}, u32[]{:S(2)}) collective-permute-start(bf16[128,2048]{1,0:T(8,128)(2,1)S(1)} %collective-permute-done.6.refs_6_), channel_id=1, source_target_pairs={{0,1},{1,0},{2,3},{3,2},{4,5},{5,4},{6,7},{7,6},{8,9},{9,8},{10,11... | collective-permute-start | bytes 1572872 | tf_op jit(solution)/shard_map/ppermute | solution.py:18
  51.7 19.4 %copy-start.4 = (bf16[128,2048]{1,0:T(8,128)(2,1)}, bf16[128,2048]{1,0:T(8,128)(2,1)S(1)}, u32[]{:S(2)}) copy-start(bf16[128,2048]{1,0:T(8,128)(2,1)S(1)} %collective-permute-done.4.refs_4_) | copy-start | bytes 1572868
  51.7 19.3 %collective-permute-start.3 = (bf16[128,2048]{1,0:T(8,128)(2,1)S(1)}, bf16[128,2048]{1,0:T(8,128)(2,1)S(1)}, u32[]{:S(2)}, u32[]{:S(2)}) collective-permute-start(bf16[128,2048]{1,0:T(8,128)(2,1)S(1)} %collective-permute-done.2.refs_2_), channel_id=1, source_target_pairs={{0,1},{1,0},{2,3},{3,2},{4,5},{5,4},{6,7},{7,6},{8,9},{9,8},{10,11... | collective-permute-start | bytes 1572872 | tf_op jit(solution)/shard_map/ppermute | solution.py:18
  56.6 14.5 %collective-permute-start.5 = (bf16[128,2048]{1,0:T(8,128)(2,1)S(1)}, bf16[128,2048]{1,0:T(8,128)(2,1)S(1)}, u32[]{:S(2)}, u32[]{:S(2)}) collective-permute-start(bf16[128,2048]{1,0:T(8,128)(2,1)S(1)} %collective-permute-done.4.refs_4_), channel_id=1, source_target_pairs={{0,1},{1,0},{2,3},{3,2},{4,5},{5,4},{6,7},{7,6},{8,9},{9,8},{10,11... | collective-permute-start | bytes 1572872 | tf_op jit(solution)/shard_map/ppermute | solution.py:18
  62.0 8.2 %collective-permute-start.12 = (bf16[512,256]{1,0:T(8,128)(2,1)S(1)}, bf16[512,256]{1,0:T(8,128)(2,1)S(1)}, u32[]{:S(2)}, u32[]{:S(2)}) collective-permute-start(bf16[512,256]{1,0:T(8,128)(2,1)S(1)} %pad_maximum_fusion.2), channel_id=1, source_target_pairs={{0,8},{8,0},{16,24},{24,16},{1,9},{9,1},{17,25},{25,17},{2,10},{10... | collective-permute-start | bytes 786440 | tf_op jit(solution)/shard_map/ppermute | solution.py:18
  71.0 0.8 copy-start.5
  71.0 1.0 copy-start.6
  71.0 1.1 copy-start.7
  71.0 1.3 copy-start.8
  76.1 15.1 %collective-permute-start.15 = (bf16[256,1024]{1,0:T(8,128)(2,1)}, bf16[256,1024]{1,0:T(8,128)(2,1)S(1)}, u32[]{:S(2)}, u32[]{:S(2)}) collective-permute-start(bf16[256,1024]{1,0:T(8,128)(2,1)} %project.4), channel_id=1, source_target_pairs={{0,2},{1,3},{2,0},{3,1},{4,6},{5,7},{6,4},{7,5},{8,10},{9,11},{10,... | collective-permute-start | bytes 1572872 | tf_op jit(solution)/shard_map/ppermute | solution.py:18
  81.6 19.0 %collective-permute-start.16 = (bf16[256,1024]{1,0:T(8,128)(2,1)}, bf16[256,1024]{1,0:T(8,128)(2,1)S(1)}, u32[]{:S(2)}, u32[]{:S(2)}) collective-permute-start(bf16[256,1024]{1,0:T(8,128)(2,1)} %project.5), channel_id=1, source_target_pairs={{0,2},{1,3},{2,0},{3,1},{4,6},{5,7},{6,4},{7,5},{8,10},{9,11},{10,... | collective-permute-start | bytes 1572872 | tf_op jit(solution)/shard_map/ppermute | solution.py:18
  88.5 16.4 %copy-start = (f32[256,2048]{1,0:T(8,128)S(1)}, f32[256,2048]{1,0:T(8,128)}, u32[]{:S(2)}) copy-start(f32[256,2048]{1,0:T(8,128)} %project.3) | copy-start | bytes 6291460
  101.9 20.0 %collective-permute-start.17 = (bf16[128,1024]{1,0:T(8,128)(2,1)S(1)}, bf16[128,1024]{1,0:T(8,128)(2,1)S(1)}, u32[]{:S(2)}, u32[]{:S(2)}) collective-permute-start(bf16[128,1024]{1,0:T(8,128)(2,1)S(1)} %get-tuple-element.8), channel_id=1, source_target_pairs={{0,4},{1,5},{2,6},{3,7},{4,0},{5,1},{6,2},{7,3},{8,12},{9,13},{10,... | collective-permute-start | bytes 786440 | tf_op jit(solution)/shard_map/ppermute | solution.py:18
  104.7 21.6 %collective-permute-start.18 = (bf16[128,1024]{1,0:T(8,128)(2,1)S(1)}, bf16[128,1024]{1,0:T(8,128)(2,1)S(1)}, u32[]{:S(2)}, u32[]{:S(2)}) collective-permute-start(bf16[128,1024]{1,0:T(8,128)(2,1)S(1)} %get-tuple-element.9), channel_id=1, source_target_pairs={{0,4},{1,5},{2,6},{3,7},{4,0},{5,1},{6,2},{7,3},{8,12},{9,13},{10,... | collective-permute-start | bytes 786440 | tf_op jit(solution)/shard_map/ppermute | solution.py:18

commit v2 on v1

v2 whole, which is shorter than its diff:
```python
import functools
import math

import jax
import jax.numpy as jnp
from jax import lax
from jax.experimental import pallas as pl
from jax.experimental.pallas import tpu as pltpu
from jax.sharding import PartitionSpec as P

F32 = jnp.float32
BF16 = jnp.bfloat16
VMEM_LIMIT = 56 * 2**20
IN_ORDER = pltpu.CompilerParams(
    vmem_limit_bytes=VMEM_LIMIT, dimension_semantics=("arbitrary",)
)


def cost(flops, moved, exponents=0):
    return pl.CostEstimate(flops=flops, bytes_accessed=moved, transcendentals=exponents)


def swap(value, axis, mask):
    pairs = [(source, source ^ mask) for source in range(lax.axis_size(axis))]
    return lax.ppermute(value, axis, pairs)


def dot(left, right, left_dim, right_dim):
    dims = (((left_dim,), (right_dim,)), ((), ()))
    return lax.dot_general(left, right, dims, preferred_element_type=F32)


def attention_kernel(height, own_ref, other_ref, q_ref, up_ref, dq_ref, mine_ref, theirs_ref, k_ref, v_ref, dk_ref, dv_ref):
    length, depth = q_ref.shape
    factor = depth**-0.5
    power = factor * math.log2(math.e)
    head = pl.program_id(0)
    is_even = lax.axis_index("tensor") % 2 == 0

    @pl.when(head == 0)
    def _():
        k_ref[...] = jnp.where(is_even, own_ref[...], other_ref[...])
        v_ref[...] = jnp.where(is_even, other_ref[...], own_ref[...])
        dk_ref[...] = jnp.zeros_like(dk_ref)
        dv_ref[...] = jnp.zeros_like(dv_ref)

    for block in reversed(range(length // height)):
        first = block * height
        finish = first + height
        query = q_ref[first:finish]
        upstream = up_ref[first:finish]
        keys = k_ref[:finish]
        values = v_ref[:finish]
        scores = dot(keys, query, 1, 1)
        key_place = lax.broadcasted_iota(jnp.int32, (height, height), 0)
        query_place = lax.broadcasted_iota(jnp.int32, (height, height), 1)
        corner = jnp.where(key_place <= query_place, scores[first:], -jnp.inf)
        scores = corner if block == 0 else jnp.concatenate([scores[:first], corner], 0)
        biggest = jnp.max(scores, axis=0, keepdims=True)
        weights = jnp.exp2((scores - biggest) * power)
        weights = weights * (1.0 / jnp.sum(weights, axis=0, keepdims=True))
        product = dot(values, upstream, 1, 1)
        center = jnp.sum(weights * product, axis=0, keepdims=True)
        score_grad = (weights * (product - center) * factor).astype(BF16)
        dv_ref[:finish] += dot(weights.astype(BF16), upstream, 1, 0)
        dk_ref[:finish] += dot(score_grad, query, 1, 0)
        dq_ref[first:finish] = dot(score_grad, keys, 0, 0).astype(BF16)

    @pl.when(head == pl.num_programs(0) - 1)
    def _():
        mine_ref[...] = jnp.where(is_even, dk_ref[...], dv_ref[...])
        theirs_ref[...] = jnp.where(is_even, dv_ref[...], dk_ref[...])


def attention(own, other, queries, out_grad):
    length, width = queries.shape
    depth = own.shape[1]
    height = min(512, length)
    column = pl.BlockSpec((length, depth), lambda h: (0, h))
    whole = pl.BlockSpec((length, depth), lambda h: (0, 0))
    sums = jax.ShapeDtypeStruct((length, depth), F32)
    return pl.pallas_call(
        functools.partial(attention_kernel, height),
        grid=(width // depth,),
        in_specs=[whole, whole, column, column],
        out_specs=[column, whole, whole],
        out_shape=[jax.ShapeDtypeStruct((length, width), BF16), sums, sums],
        scratch_shapes=[
            pltpu.VMEM((length, depth), BF16),
            pltpu.VMEM((length, depth), BF16),
            pltpu.VMEM((length, depth), F32),
            pltpu.VMEM((length, depth), F32),
        ],
        compiler_params=IN_ORDER,
        cost_estimate=cost(
            20 * length * length * width,
            6 * queries.nbytes,
            length * length * width // depth,
        ),
        name="attention",
    )(own, other, queries, out_grad)


def kv_kernel(rows, mine_ref, arrived_ref, mask_ref, *out_refs):
    place = lax.axis_index("tensor")
    chip, core = place // 2, place % 2
    for step, out_ref in enumerate(out_refs):
        for half in range(2):
            start = ((chip ^ step) * 2 + (core ^ half)) * rows
            span = pl.ds(pl.multiple_of(start, rows), rows)
            total = mine_ref[span, :] + arrived_ref[span, :].astype(F32)
            keep = mask_ref[span, :].astype(F32)
            out_ref[half * rows : (half + 1) * rows, :] = (total * keep).astype(BF16)


def kv_blocks(mine, arrived, mask, rows):
    length, depth = mine.shape
    count = length // (2 * rows)
    return pl.pallas_call(
        functools.partial(kv_kernel, rows),
        out_shape=[jax.ShapeDtypeStruct((2 * rows, depth), BF16)] * count,
        compiler_params=pltpu.CompilerParams(vmem_limit_bytes=VMEM_LIMIT),
        cost_estimate=cost(0, 2 * mine.nbytes),
        name="kv_blocks",
    )(mine, arrived, mask)


def turn_kernel(first_ref, second_ref, out_ref):
    rows = first_ref.shape[0]
    out_ref[:, :rows] = first_ref[...].T
    out_ref[:, rows:] = second_ref[...].T


def turn(first, second):
    rows, wide = first.shape
    tile = min(512, wide)
    return pl.pallas_call(
        turn_kernel,
        grid=(wide // tile,),
        in_specs=[pl.BlockSpec((rows, tile), lambda j: (0, j))] * 2,
        out_specs=pl.BlockSpec((tile, 2 * rows), lambda j: (j, 0)),
        out_shape=jax.ShapeDtypeStruct((wide, 2 * rows), first.dtype),
        compiler_params=IN_ORDER,
        cost_estimate=cost(0, 4 * first.nbytes),
        name="turn",
    )(first, second)


def project_kernel(parts, *refs):
    total = dot(refs[0][...], refs[parts][...], 1, 0)
    for part in range(1, parts):
        total += dot(refs[part][...], refs[parts + part][...], 1, 0)
    refs[-1][...] = total.astype(refs[-1].dtype)


def project(turned, grads, first, wide, dtype):
    tokens, columns = grads[0].shape
    tile = min(512, wide)
    skip = first // tile
    return pl.pallas_call(
        functools.partial(project_kernel, len(grads)),
        grid=(wide // tile,),
        in_specs=[pl.BlockSpec((tile, tokens), lambda j: (j + skip, 0))] * len(grads)
        + [pl.BlockSpec((tokens, columns), lambda j: (0, 0))] * len(grads),
        out_specs=pl.BlockSpec((tile, columns), lambda j: (j, 0)),
        out_shape=jax.ShapeDtypeStruct((wide, columns), dtype),
        compiler_params=IN_ORDER,
        cost_estimate=cost(
            2 * len(grads) * wide * tokens * columns,
            len(grads) * (wide * tokens + tokens * columns) * 2,
        ),
        name="project",
    )(*turned, *grads)


def add_kernel(*refs):
    total = refs[0][...].astype(F32)
    for ref in refs[1:-1]:
        total += ref[...].astype(F32)
    refs[-1][...] = total.astype(refs[-1].dtype)


def add_columns(terms, columns):
    wide = terms[0].shape[0]
    tile = min(512, wide)
    return pl.pallas_call(
        add_kernel,
        grid=(wide // tile,),
        in_specs=[pl.BlockSpec((tile, columns), lambda j: (j, 1))] * len(terms),
        out_specs=pl.BlockSpec((tile, columns), lambda j: (j, 0)),
        out_shape=jax.ShapeDtypeStruct((wide, columns), BF16),
        compiler_params=IN_ORDER,
        cost_estimate=cost(0, 8 * len(terms) * wide * columns),
        name="add_columns",
    )(*terms)


def finish_kernel(parts, *refs):
    total = refs[1][...].astype(F32)
    for part in range(1, parts):
        total += refs[1 + part][...].astype(F32)
    refs[-1][...] = jnp.where(refs[0][...] == 1, total, 0.0)


def finish(terms, weight_mask, result, first):
    height, depth = weight_mask.shape
    wide = terms[0].shape[0]
    tile = min(512, wide)
    skip = first // tile
    place = pl.BlockSpec((tile, depth), lambda j: (j + skip, 0))
    in_specs = [place] + [pl.BlockSpec((tile, depth), lambda j: (j, 0))] * len(terms)
    args = [weight_mask, *terms]
    aliases = {}
    if result is not None:
        aliases = {len(args): 0}
        in_specs.append(pl.BlockSpec(memory_space=pl.ANY))
        args.append(result)
    return pl.pallas_call(
        functools.partial(finish_kernel, len(terms)),
        grid=(wide // tile,),
        in_specs=in_specs,
        out_specs=place,
        out_shape=jax.ShapeDtypeStruct((height, depth), F32),
        input_output_aliases=aliases,
        compiler_params=IN_ORDER,
        cost_estimate=cost(0, 16 * wide * depth),
        name="finish",
    )(*args)


def per_device(inputs, queries, keys_values, out_grad, weight_mask, clip_mask):
    depth = keys_values.shape[1]
    rows = inputs.shape[0]
    groups = lax.axis_size("dp")
    chips = lax.axis_size("tensor") // 2
    block = weight_mask.shape[0]
    row_place = lax.axis_index("dp")

    other = swap(keys_values, "tensor", 1)
    mine_rows = []
    for step in range(groups):
        start = (row_place ^ step) * block
        part = lax.dynamic_slice(inputs, (0, start), (rows, block))
        mine_rows.append(part if step == 0 else swap(part, "dp", step))
    turned = [turn(part, swap(part, "tensor", 1)) for part in mine_rows]

    query_grad, mine, theirs = attention(keys_values, other, queries, out_grad)
    arrived = swap(theirs, "tensor", 1)
    blocks = kv_blocks(mine, arrived, clip_mask, rows)

    def gather(steps):
        parts = [blocks[s] if s == 0 else swap(blocks[s], "tensor", 2 * s) for s in steps]
        stacked = jnp.concatenate(parts, 1)
        return [stacked if s == 0 else swap(stacked, "dp", s) for s in range(groups)]

    order = sorted(range(chips), key=lambda s: [(s >> b) & 1 for b in range(8)])
    half = chips // 2
    odd = gather(order[half:])
    even = gather(order[:half])

    cuts = 2 if block % 1024 == 0 else 1
    wide = block // cuts
    sent = [
        swap(project(turned, odd, cut * wide, wide, BF16), "tensor", 2) for cut in range(cuts)
    ]
    weight_grad = None
    for cut in range(cuts):
        terms = [project(turned, even, cut * wide, wide, F32), sent[cut]]
        columns, bit = half * depth, 2
        while columns > depth:
            columns, bit = columns // 2, bit * 2
            terms.append(swap(add_columns(terms, columns), "tensor", bit))
        weight_grad = finish(terms, weight_mask, weight_grad, cut * wide)
    return (query_grad, weight_grad)


def solution(mesh):
    spec = P("dp", "tensor")
    in_specs = (P(("dp", "tensor"), None), spec, spec, spec, spec, spec)
    return jax.shard_map(
        per_device, mesh=mesh, in_specs=in_specs, out_specs=(spec, spec), check_vma=False
    )
```

time: 132 us -> 135 us (1.023)
  Pallas kernels: 39.3 us -> 56.8 us
  waiting for transfers between devices: 57.1 us -> 41 us
  other arithmetic: 3.69 us -> 0 us
  local copies, waits for them, and re-layouts: 7.12 us -> 9.99 us
  starting transfers between devices: 23.1 us -> 25.8 us
    pallas_call x5 -> x13, Pallas kernels: 19.6 us -> 37 us  [the longest x4 14.5 us: turn(): pl.pallas_call(turn_kernel, grid=(wide // tile,), in_specs=[pl.BlockSpec(...]
    ppermute x19 -> x22, waiting for transfers between devices: 57.1 us -> 41 us  [swap(): return lax.ppermute(value, axis, pairs)]
    unnamed x27 -> x47, local copies, waits for them, and re-layouts: 2.77 us -> 8.23 us
    ppermute x19 -> x22, starting transfers between devices: 23.1 us -> 25.8 us  [swap(): return lax.ppermute(value, axis, pairs)]
    concatenate x4 -> x0, other arithmetic: 2.34 us -> none  [the longest x2 1.68 us: per_device(): jnp.concatenate([f[k] for f in finals], 1)]
    slice x5 -> x0, local copies, waits for them, and re-layouts: 2.19 us -> none  [the longest x3 2.15 us: per_device(): g[half:]]
    dynamic_slice x1, local copies, waits for them, and re-layouts: 0.14 us -> 1.73 us  [per_device(): part = lax.dynamic_slice(inputs, (0, start), (rows, block))]
  transfers between devices with their start and end apart: 19 -> 22, of which waited for: 11 -> 8; matrix products, arithmetic and copies ran while one was open for 4% -> 2% of each run, Pallas kernels for 9% -> 38%
where the time goes in v2:
time: 135 us; the launch traced here: 134 us
  Pallas kernels  56.8 us (42%)
  waiting for transfers between devices  41 us (30%)
  starting transfers between devices  25.8 us (19%)
  local copies, waits for them, and re-layouts  9.99 us (7%)
    ppermute x22, waiting for transfers between devices, swap(): return lax.ppermute(value, axis, pairs)  41 us
    ppermute x22, starting transfers between devices, swap(): return lax.ppermute(value, axis, pairs)  25.8 us
    pallas_call x1, Pallas kernels, attention(): pl.pallas_call(functools.partial(attention_kernel, height), grid=(width /...  19.7 us
    pallas_call x4, Pallas kernels, turn(): pl.pallas_call(turn_kernel, grid=(wide // tile,), in_specs=[pl.BlockSpec(...  14.5 us
    pallas_call x4, Pallas kernels, project(): pl.pallas_call(functools.partial(project_kernel, len(grads)), grid=(wide...  12.5 us
    unnamed x47, local copies, waits for them, and re-layouts  8.23 us
    pallas_call x2, Pallas kernels, finish(): pl.pallas_call(functools.partial(finish_kernel, len(terms)), grid=(wide /...  4.19 us
    pallas_call x2, Pallas kernels, add_columns(): pl.pallas_call(add_kernel, grid=(wide // tile,), in_specs=[pl.BlockSpec((...  3.63 us
  transfers between devices with their start and end apart: 22, of which 8 were waited for; matrix products, arithmetic and copies ran while one was open for 2% of the time, Pallas kernels for 38%

profile of v2, /device:TPU:0, one launch (start us, length us, event | category | flops | bytes accessed | tf_op | source)
XLA Modules:
  0.0 134.4 jit_solution(11480780329696964584)
XLA Ops:
  0.6 0.5 collective-permute-start
  1.1 1.7 %constant_dynamic-slice_fusion = (bf16[128,2048]{1,0:T(8,128)(2,1)S(1)}, bf16[128,2048]{1,0:T(8,128)(2,1)S(1)}, bf16[128,2048]{1,0:T(8,128)(2,1)S(1)}, bf16[128,2048]{1,0:T(8,128)(2,1)S(1)}) fusion(bf16[128,8192]{1,0:T(8,128)(2,1)} %param.6, s32[]{:T(128)S(6)} %select_n.15, s32[]{:T(128)S(6)} %select_n.13, s32[]{:T(128)S(6)} %select_n.12, s32[]{:T(128)S(6)} %select_n.14), kind=kLoop, calls=%fused_computation.4 | loop fusion | bytes 4194320 | tf_op jit(solution)/shard_map/dynamic_slice | solution.py:243
  2.9 3.6 %collective-permute-start.6 = (bf16[128,2048]{1,0:T(8,128)(2,1)S(1)}, bf16[128,2048]{1,0:T(8,128)(2,1)S(1)}, u32[]{:S(2)}, u32[]{:S(2)}) collective-permute-start(bf16[128,2048]{1,0:T(8,128)(2,1)S(1)} %get-tuple-element.16), channel_id=1, source_target_pairs={{0,24},{8,16},{16,8},{24,0},{1,25},{9,17},{17,9},{25,1},{2,26},{10... | collective-permute-start | bytes 1572872 | tf_op jit(solution)/shard_map/ppermute | solution.py:25
  6.4 0.5 collective-permute-start.2
  7.1 0.7 copy-done.20
  7.8 19.7 %attention.1 = (bf16[1024,768]{1,0:T(8,128)(2,1)}, f32[1024,128]{1,0:T(8,128)}, f32[1024,128]{1,0:T(8,128)}) custom-call(bf16[1024,128]{1,0:T(8,128)(2,1)} %own_ref.1, bf16[1024,128]{1,0:T(8,128)(2,1)} %copy-done.20, bf16[1024,768]{1,0:T(8,128)(2,1)} %q_ref.1, bf16[1024,768]{1,0:T(8,128)(2,1)} %up_ref.1), custom_call_target="tpu_custom_call" | custom-call | flops 16106127360 | bytes 9437184 | tf_op jit(solution)/shard_map/attention/pallas_call | solution.py:82
  27.6 0.5 collective-permute-start.1
  28.1 2.4 %collective-permute-done.2.first_ref = bf16[128,2048]{1,0:T(8,128)(2,1)S(1)} collective-permute-done((bf16[128,2048]{1,0:T(8,128)(2,1)S(1)}, bf16[128,2048]{1,0:T(8,128)(2,1)S(1)}, u32[]{:S(2)}, u32[]{:S(2)}) %collective-permute-start.2) | collective-permute-done | bytes 524320 | tf_op jit(solution)/shard_map/ppermute | solution.py:25
  30.5 0.5 collective-permute-start.5
  31.0 1.0 copy.9.mask_ref
  32.1 0.8 copy-done.5
  32.9 2.2 %kv_blocks.1 = (bf16[256,128]{1,0:T(8,128)(2,1)}, bf16[256,128]{1,0:T(8,128)(2,1)}, bf16[256,128]{1,0:T(8,128)(2,1)}, bf16[256,128]{1,0:T(8,128)(2,1)}) custom-call(f32[1024,128]{1,0:T(8,128)} %get-tuple-element.10.mine_ref, f32[1024,128]{1,0:T(8,128)} %copy-done.5, s32[1024,1]{1,0:T(8,128)} %copy.9.mask_ref), custom_call_target="tpu_custom_call" | custom-call | bytes 1048576 | tf_op jit(solution)/shard_map/kv_blocks/pallas_call | solution.py:119
  35.1 1.6 %collective-permute-start.13 = (bf16[256,128]{1,0:T(8,128)(2,1)}, bf16[256,128]{1,0:T(8,128)(2,1)S(1)}, u32[]{:S(2)}, u32[]{:S(2)}) collective-permute-start(bf16[256,128]{1,0:T(8,128)(2,1)} %get-tuple-element.14), channel_id=1, source_target_pairs={{0,2},{1,3},{2,0},{3,1},{4,6},{5,7},{6,4},{7,5},{8,10},{9,11},{10,... | collective-permute-start | bytes 196616 | tf_op jit(solution)/shard_map/ppermute | solution.py:25
  36.7 2.9 %collective-permute-done.13 = bf16[256,128]{1,0:T(8,128)(2,1)S(1)} collective-permute-done((bf16[256,128]{1,0:T(8,128)(2,1)}, bf16[256,128]{1,0:T(8,128)(2,1)S(1)}, u32[]{:S(2)}, u32[]{:S(2)}) %collective-permute-start.13) | collective-permute-done | bytes 65568 | tf_op jit(solution)/shard_map/ppermute | solution.py:25
  39.6 3.6 %collective-permute-start.14 = (bf16[256,128]{1,0:T(8,128)(2,1)}, bf16[256,128]{1,0:T(8,128)(2,1)S(1)}, u32[]{:S(2)}, u32[]{:S(2)}) collective-permute-start(bf16[256,128]{1,0:T(8,128)(2,1)} %get-tuple-element.15), channel_id=1, source_target_pairs={{0,6},{1,7},{2,4},{3,5},{4,2},{5,3},{6,0},{7,1},{8,14},{9,15},{10,... | collective-permute-start | bytes 196616 | tf_op jit(solution)/shard_map/ppermute | solution.py:25
  43.2 2.7 %collective-permute-done.14 = bf16[256,128]{1,0:T(8,128)(2,1)S(1)} collective-permute-done((bf16[256,128]{1,0:T(8,128)(2,1)}, bf16[256,128]{1,0:T(8,128)(2,1)S(1)}, u32[]{:S(2)}, u32[]{:S(2)}) %collective-permute-start.14) | collective-permute-done | bytes 65568 | tf_op jit(solution)/shard_map/ppermute | solution.py:25
  45.9 2.2 %collective-permute-start.17 = (bf16[256,256]{1,0:T(8,128)(2,1)S(1)}, bf16[256,256]{1,0:T(8,128)(2,1)S(1)}, u32[]{:S(2)}, u32[]{:S(2)}) collective-permute-start(bf16[256,256]{1,0:T(8,128)(2,1)S(1)} %constant_dynamic-update-slice_fusion.2.refs_4_), channel_id=1, source_target_pairs={{0,24},{8,16},{16,8},{24,0},{1,25},{9,17},{17,9},{25,1},{2,26},{10... | collective-permute-start | bytes 393224 | tf_op jit(solution)/shard_map/ppermute | solution.py:25
  48.2 0.8 collective-permute-start.16
  48.9 0.5 collective-permute-start.15
  49.5 3.6 %turn.4.refs_0_ = bf16[2048,256]{1,0:T(8,128)(2,1)} custom-call(bf16[128,2048]{1,0:T(8,128)(2,1)} %copy-done.2, bf16[128,2048]{1,0:T(8,128)(2,1)} %copy-done.15), custom_call_target="tpu_custom_call" | custom-call | bytes 2097152 | tf_op jit(solution)/shard_map/turn/pallas_call | solution.py:137
  53.1 3.6 %turn.7.refs_3_ = bf16[2048,256]{1,0:T(8,128)(2,1)} custom-call(bf16[128,2048]{1,0:T(8,128)(2,1)} %copy-done.14, bf16[128,2048]{1,0:T(8,128)(2,1)} %collective-permute-done.7.second_ref), custom_call_target="tpu_custom_call" | custom-call | bytes 2097152 | tf_op jit(solution)/shard_map/turn/pallas_call | solution.py:137
  56.8 3.6 %turn.5.refs_1_ = bf16[2048,256]{1,0:T(8,128)(2,1)} custom-call(bf16[128,2048]{1,0:T(8,128)(2,1)} %copy-done.13, bf16[128,2048]{1,0:T(8,128)(2,1)} %collective-permute-done.3.second_ref), custom_call_target="tpu_custom_call" | custom-call | bytes 2097152 | tf_op jit(solution)/shard_map/turn/pallas_call | solution.py:137
  60.4 3.6 %turn.6.refs_2_ = bf16[2048,256]{1,0:T(8,128)(2,1)} custom-call(bf16[128,2048]{1,0:T(8,128)(2,1)} %copy-done.12, bf16[128,2048]{1,0:T(8,128)(2,1)} %collective-permute-done.5.second_ref), custom_call_target="tpu_custom_call" | custom-call | bytes 2097152 | tf_op jit(solution)/shard_map/turn/pallas_call | solution.py:137
  64.1 0.6 copy-done.6
  64.8 0.7 copy-done.8
  65.4 3.1 %project.7 = bf16[1024,256]{1,0:T(8,128)(2,1)} custom-call(bf16[2048,256]{1,0:T(8,128)(2,1)} %turn.4.refs_0_, bf16[2048,256]{1,0:T(8,128)(2,1)} %turn.5.refs_1_, bf16[2048,256]{1,0:T(8,128)(2,1)} %turn.6.refs_2_, bf16[2048,256]{1,0:T(8,128)(2,1)} %turn.7.refs_3_, bf16[256,256]{1,0:T(8,128)(2,1)} %copy-done.3, bf16[256,256]{1,0:T(8,128)(2,1)} %copy-done.8, ...), custom_call_target="tpu_custom_call" | custom-call | flops 536870912 | bytes 2621440 | tf_op jit(solution)/shard_map/project/pallas_call | solution.py:160
  68.7 3.1 %project.5 = bf16[1024,256]{1,0:T(8,128)(2,1)} custom-call(bf16[2048,256]{1,0:T(8,128)(2,1)} %turn.4.refs_0_, bf16[2048,256]{1,0:T(8,128)(2,1)} %turn.5.refs_1_, bf16[2048,256]{1,0:T(8,128)(2,1)} %turn.6.refs_2_, bf16[2048,256]{1,0:T(8,128)(2,1)} %turn.7.refs_3_, bf16[256,256]{1,0:T(8,128)(2,1)} %copy-done.3, bf16[256,256]{1,0:T(8,128)(2,1)} %copy-done.8, ...), custom_call_target="tpu_custom_call" | custom-call | flops 536870912 | bytes 2621440 | tf_op jit(solution)/shard_map/project/pallas_call | solution.py:160
  71.8 1.8 %collective-permute-start.18 = (bf16[1024,256]{1,0:T(8,128)(2,1)}, bf16[1024,256]{1,0:T(8,128)(2,1)S(1)}, u32[]{:S(2)}, u32[]{:S(2)}) collective-permute-start(bf16[1024,256]{1,0:T(8,128)(2,1)} %project.5), channel_id=1, source_target_pairs={{0,2},{1,3},{2,0},{3,1},{4,6},{5,7},{6,4},{7,5},{8,10},{9,11},{10,... | collective-permute-start | bytes 1572872 | tf_op jit(solution)/shard_map/ppermute | solution.py:25
  73.6 2.2 %collective-permute-start.9 = (bf16[256,128]{1,0:T(8,128)(2,1)S(1)}, bf16[256,128]{1,0:T(8,128)(2,1)S(1)}, u32[]{:S(2)}, u32[]{:S(2)}) collective-permute-start(bf16[256,128]{1,0:T(8,128)(2,1)S(1)} %copy-done.21), channel_id=1, source_target_pairs={{0,4},{1,5},{2,6},{3,7},{4,0},{5,1},{6,2},{7,3},{8,12},{9,13},{10,... | collective-permute-start | bytes 196616 | tf_op jit(solution)/shard_map/ppermute | solution.py:25
  75.9 14.9 %collective-permute-done.9 = bf16[256,128]{1,0:T(8,128)(2,1)S(1)} collective-permute-done((bf16[256,128]{1,0:T(8,128)(2,1)S(1)}, bf16[256,128]{1,0:T(8,128)(2,1)S(1)}, u32[]{:S(2)}, u32[]{:S(2)}) %collective-permute-start.9) | collective-permute-done | bytes 65568 | tf_op jit(solution)/shard_map/ppermute | solution.py:25
  90.8 2.2 %collective-permute-start.12 = (bf16[256,256]{1,0:T(8,128)(2,1)S(1)}, bf16[256,256]{1,0:T(8,128)(2,1)S(1)}, u32[]{:S(2)}, u32[]{:S(2)}) collective-permute-start(bf16[256,256]{1,0:T(8,128)(2,1)S(1)} %constant_dynamic-update-slice_fusion.refs_4_), channel_id=1, source_target_pairs={{0,24},{8,16},{16,8},{24,0},{1,25},{9,17},{17,9},{25,1},{2,26},{10... | collective-permute-start | bytes 393224 | tf_op jit(solution)/shard_map/ppermute | solution.py:25
  93.4 1.0 collective-permute-start.10
  94.4 2.4 %collective-permute-done.12.refs_7_ = bf16[256,256]{1,0:T(8,128)(2,1)S(1)} collective-permute-done((bf16[256,256]{1,0:T(8,128)(2,1)S(1)}, bf16[256,256]{1,0:T(8,128)(2,1)S(1)}, u32[]{:S(2)}, u32[]{:S(2)}) %collective-permute-start.12) | collective-permute-done | bytes 131104 | tf_op jit(solution)/shard_map/ppermute | solution.py:25
  96.8 1.4 %collective-permute-done.11.refs_6_ = bf16[256,256]{1,0:T(8,128)(2,1)S(1)} collective-permute-done((bf16[256,256]{1,0:T(8,128)(2,1)S(1)}, bf16[256,256]{1,0:T(8,128)(2,1)S(1)}, u32[]{:S(2)}, u32[]{:S(2)}) %collective-permute-start.11) | collective-permute-done | bytes 131104 | tf_op jit(solution)/shard_map/ppermute | solution.py:25
  98.3 0.5 copy-done.10
  98.8 0.7 copy-done.11
  99.5 3.2 %project.6.refs_0_.refs_1_ = f32[1024,256]{1,0:T(8,128)} custom-call(bf16[2048,256]{1,0:T(8,128)(2,1)} %turn.4.refs_0_, bf16[2048,256]{1,0:T(8,128)(2,1)} %turn.5.refs_1_, bf16[2048,256]{1,0:T(8,128)(2,1)} %turn.6.refs_2_, bf16[2048,256]{1,0:T(8,128)(2,1)} %turn.7.refs_3_, bf16[256,256]{1,0:T(8,128)(2,1)} %copy-done.4, bf16[256,256]{1,0:T(8,128)(2,1)} %copy-done.11, ...), custom_call_target="tpu_custom_call" | custom-call | flops 536870912 | bytes 2621440 | tf_op jit(solution)/shard_map/project/pallas_call | solution.py:160
  102.7 3.2 %project.4.refs_0_.refs_1_ = f32[1024,256]{1,0:T(8,128)} custom-call(bf16[2048,256]{1,0:T(8,128)(2,1)} %turn.4.refs_0_, bf16[2048,256]{1,0:T(8,128)(2,1)} %turn.5.refs_1_, bf16[2048,256]{1,0:T(8,128)(2,1)} %turn.6.refs_2_, bf16[2048,256]{1,0:T(8,128)(2,1)} %turn.7.refs_3_, bf16[256,256]{1,0:T(8,128)(2,1)} %copy-done.4, bf16[256,256]{1,0:T(8,128)(2,1)} %copy-done.11, ...), custom_call_target="tpu_custom_call" | custom-call | flops 536870912 | bytes 2621440 | tf_op jit(solution)/shard_map/project/pallas_call | solution.py:160
  105.9 0.8 copy-done
  106.7 1.8 %add_columns.3 = bf16[1024,128]{1,0:T(8,128)(2,1)} custom-call(f32[1024,256]{1,0:T(8,128)} %project.6.refs_0_.refs_1_, bf16[1024,256]{1,0:T(8,128)(2,1)} %copy-done), custom_call_target="tpu_custom_call" | custom-call | bytes 2097152 | tf_op jit(solution)/shard_map/add_columns/pallas_call | solution.py:186
  108.5 3.4 %collective-permute-start.21 = (bf16[1024,128]{1,0:T(8,128)(2,1)}, bf16[1024,128]{1,0:T(8,128)(2,1)S(1)}, u32[]{:S(2)}, u32[]{:S(2)}) collective-permute-start(bf16[1024,128]{1,0:T(8,128)(2,1)} %add_columns.3), channel_id=1, source_target_pairs={{0,4},{1,5},{2,6},{3,7},{4,0},{5,1},{6,2},{7,3},{8,12},{9,13},{10,... | collective-permute-start | bytes 786440 | tf_op jit(solution)/shard_map/ppermute | solution.py:25
  111.9 0.8 copy-done.1
  112.7 1.8 %add_columns.2 = bf16[1024,128]{1,0:T(8,128)(2,1)} custom-call(f32[1024,256]{1,0:T(8,128)} %project.4.refs_0_.refs_1_, bf16[1024,256]{1,0:T(8,128)(2,1)} %copy-done.1), custom_call_target="tpu_custom_call" | custom-call | bytes 2097152 | tf_op jit(solution)/shard_map/add_columns/pallas_call | solution.py:186
  114.5 14.2 %collective-permute-done.21.refs_3_ = bf16[1024,128]{1,0:T(8,128)(2,1)S(1)} collective-permute-done((bf16[1024,128]{1,0:T(8,128)(2,1)}, bf16[1024,128]{1,0:T(8,128)(2,1)S(1)}, u32[]{:S(2)}, u32[]{:S(2)}) %collective-permute-start.21) | collective-permute-done | bytes 262176 | tf_op jit(solution)/shard_map/ppermute | solution.py:25
  128.7 0.7 copy-done.17
  129.4 2.1 %finish.2.refs_4_ = f32[2048,128]{1,0:T(8,128)} custom-call(s32[2048,128]{1,0:T(8,128)} %refs_0_.3, f32[1024,256]{1,0:T(8,128)} %project.6.refs_0_.refs_1_, bf16[1024,256]{1,0:T(8,128)(2,1)} %copy-done, bf16[1024,128]{1,0:T(8,128)(2,1)} %copy-done.17), custom_call_target="tpu_custom_call" | custom-call | bytes 2097152 | tf_op jit(solution)/shard_map/finish/pallas_call | solution.py:218
  131.5 0.7 copy-done.16
  132.3 2.1 %finish.3 = f32[2048,128]{1,0:T(8,128)} custom-call(s32[2048,128]{1,0:T(8,128)} %refs_0_.3, f32[1024,256]{1,0:T(8,128)} %project.4.refs_0_.refs_1_, bf16[1024,256]{1,0:T(8,128)(2,1)} %copy-done.1, bf16[1024,128]{1,0:T(8,128)(2,1)} %copy-done.16, f32[2048,128]{1,0:T(8,128)} %finish.2.refs_4_), custom_call_target="tpu_custom_call", output_to_operand_aliasing={{}: (4, {})} | custom-call | bytes 2097152 | tf_op jit(solution)/shard_map/finish/pallas_call | solution.py:218
  (60 shorter events, 1.2 us)
Async XLA Ops:
  0.6 6.5 %collective-permute-start = (bf16[1024,128]{1,0:T(8,128)(2,1)}, bf16[1024,128]{1,0:T(8,128)(2,1)S(1)}, u32[]{:S(2)}, u32[]{:S(2)}) collective-permute-start(bf16[1024,128]{1,0:T(8,128)(2,1)} %own_ref.1), channel_id=1, source_target_pairs={{0,1},{1,0},{2,3},{3,2},{4,5},{5,4},{6,7},{7,6},{8,9},{9,8},{10,11... | collective-permute-start | bytes 786440 | tf_op jit(solution)/shard_map/ppermute | solution.py:25
  2.9 24.7 %copy-start.2 = (bf16[128,2048]{1,0:T(8,128)(2,1)}, bf16[128,2048]{1,0:T(8,128)(2,1)S(1)}, u32[]{:S(2)}) copy-start(bf16[128,2048]{1,0:T(8,128)(2,1)S(1)} %get-tuple-element.18.first_ref) | copy-start | bytes 1572868
  2.9 25.2 %collective-permute-start.6 = (bf16[128,2048]{1,0:T(8,128)(2,1)S(1)}, bf16[128,2048]{1,0:T(8,128)(2,1)S(1)}, u32[]{:S(2)}, u32[]{:S(2)}) collective-permute-start(bf16[128,2048]{1,0:T(8,128)(2,1)S(1)} %get-tuple-element.16), channel_id=1, source_target_pairs={{0,24},{8,16},{16,8},{24,0},{1,25},{9,17},{17,9},{25,1},{2,26},{10... | collective-permute-start | bytes 1572872 | tf_op jit(solution)/shard_map/ppermute | solution.py:25
  6.4 24.1 %collective-permute-start.2 = (bf16[128,2048]{1,0:T(8,128)(2,1)S(1)}, bf16[128,2048]{1,0:T(8,128)(2,1)S(1)}, u32[]{:S(2)}, u32[]{:S(2)}) collective-permute-start(bf16[128,2048]{1,0:T(8,128)(2,1)S(1)} %get-tuple-element.17), channel_id=1, source_target_pairs={{0,8},{8,0},{16,24},{24,16},{1,9},{9,1},{17,25},{25,17},{2,10},{10... | collective-permute-start | bytes 1572872 | tf_op jit(solution)/shard_map/ppermute | solution.py:25
  7.0 24.1 %copy-start.19 = (s32[1024,1]{0,1:T(1,128)S(1)}, s32[1024,1]{0,1:T(1,128)}, u32[]{:S(2)}) copy-start(s32[1024,1]{0,1:T(1,128)} %param.11) | copy-start | bytes 12292
  7.0 23.5 %collective-permute-start.4 = (bf16[128,2048]{1,0:T(8,128)(2,1)S(1)}, bf16[128,2048]{1,0:T(8,128)(2,1)S(1)}, u32[]{:S(2)}, u32[]{:S(2)}) collective-permute-start(bf16[128,2048]{1,0:T(8,128)(2,1)S(1)} %get-tuple-element.19), channel_id=1, source_target_pairs={{0,16},{8,24},{16,0},{24,8},{1,17},{9,25},{17,1},{25,9},{2,18},{10... | collective-permute-start | bytes 1572872 | tf_op jit(solution)/shard_map/ppermute | solution.py:25
  7.1 0.7 copy-start.20
  27.5 4.5 %collective-permute-start.8 = (f32[1024,128]{1,0:T(8,128)}, f32[1024,128]{1,0:T(8,128)S(1)}, u32[]{:S(2)}, u32[]{:S(2)}) collective-permute-start(f32[1024,128]{1,0:T(8,128)} %get-tuple-element.11), channel_id=1, source_target_pairs={{0,1},{1,0},{2,3},{3,2},{4,5},{5,4},{6,7},{7,6},{8,9},{9,8},{10,11... | collective-permute-start | bytes 1572872 | tf_op jit(solution)/shard_map/ppermute | solution.py:25
  27.6 20.6 %collective-permute-start.1 = (bf16[128,2048]{1,0:T(8,128)(2,1)S(1)}, bf16[128,2048]{1,0:T(8,128)(2,1)S(1)}, u32[]{:S(2)}, u32[]{:S(2)}) collective-permute-start(bf16[128,2048]{1,0:T(8,128)(2,1)S(1)} %get-tuple-element.18.first_ref), channel_id=1, source_target_pairs={{0,1},{1,0},{2,3},{3,2},{4,5},{5,4},{6,7},{7,6},{8,9},{9,8},{10,11... | collective-permute-start | bytes 1572872 | tf_op jit(solution)/shard_map/ppermute | solution.py:25
  28.1 25.0 %copy-start.14 = (bf16[128,2048]{1,0:T(8,128)(2,1)}, bf16[128,2048]{1,0:T(8,128)(2,1)S(1)}, u32[]{:S(2)}) copy-start(bf16[128,2048]{1,0:T(8,128)(2,1)S(1)} %collective-permute-done.6.first_ref) | copy-start | bytes 1572868
  28.1 20.9 %collective-permute-start.7 = (bf16[128,2048]{1,0:T(8,128)(2,1)S(1)}, bf16[128,2048]{1,0:T(8,128)(2,1)}, u32[]{:S(2)}, u32[]{:S(2)}) collective-permute-start(bf16[128,2048]{1,0:T(8,128)(2,1)S(1)} %collective-permute-done.6.first_ref), channel_id=1, source_target_pairs={{0,1},{1,0},{2,3},{3,2},{4,5},{5,4},{6,7},{7,6},{8,9},{9,8},{10,11... | collective-permute-start | bytes 1572872 | tf_op jit(solution)/shard_map/ppermute | solution.py:25
  30.5 26.2 %copy-start.13 = (bf16[128,2048]{1,0:T(8,128)(2,1)}, bf16[128,2048]{1,0:T(8,128)(2,1)S(1)}, u32[]{:S(2)}) copy-start(bf16[128,2048]{1,0:T(8,128)(2,1)S(1)} %collective-permute-done.2.first_ref) | copy-start | bytes 1572868
  30.5 26.2 %collective-permute-start.3 = (bf16[128,2048]{1,0:T(8,128)(2,1)S(1)}, bf16[128,2048]{1,0:T(8,128)(2,1)}, u32[]{:S(2)}, u32[]{:S(2)}) collective-permute-start(bf16[128,2048]{1,0:T(8,128)(2,1)S(1)} %collective-permute-done.2.first_ref), channel_id=1, source_target_pairs={{0,1},{1,0},{2,3},{3,2},{4,5},{5,4},{6,7},{7,6},{8,9},{9,8},{10,11... | collective-permute-start | bytes 1572872 | tf_op jit(solution)/shard_map/ppermute | solution.py:25
  30.5 22.6 %copy-start.12 = (bf16[128,2048]{1,0:T(8,128)(2,1)}, bf16[128,2048]{1,0:T(8,128)(2,1)S(1)}, u32[]{:S(2)}) copy-start(bf16[128,2048]{1,0:T(8,128)(2,1)S(1)} %collective-permute-done.4.first_ref) | copy-start | bytes 1572868
  30.5 29.9 %collective-permute-start.5 = (bf16[128,2048]{1,0:T(8,128)(2,1)S(1)}, bf16[128,2048]{1,0:T(8,128)(2,1)}, u32[]{:S(2)}, u32[]{:S(2)}) collective-permute-start(bf16[128,2048]{1,0:T(8,128)(2,1)S(1)} %collective-permute-done.4.first_ref), channel_id=1, source_target_pairs={{0,1},{1,0},{2,3},{3,2},{4,5},{5,4},{6,7},{7,6},{8,9},{9,8},{10,11... | collective-permute-start | bytes 1572872 | tf_op jit(solution)/shard_map/ppermute | solution.py:25
  32.1 0.8 copy-start.5
  35.1 4.5 %collective-permute-start.13 = (bf16[256,128]{1,0:T(8,128)(2,1)}, bf16[256,128]{1,0:T(8,128)(2,1)S(1)}, u32[]{:S(2)}, u32[]{:S(2)}) collective-permute-start(bf16[256,128]{1,0:T(8,128)(2,1)} %get-tuple-element.14), channel_id=1, source_target_pairs={{0,2},{1,3},{2,0},{3,1},{4,6},{5,7},{6,4},{7,5},{8,10},{9,11},{10,... | collective-permute-start | bytes 196616 | tf_op jit(solution)/shard_map/ppermute | solution.py:25
  39.6 6.3 %collective-permute-start.14 = (bf16[256,128]{1,0:T(8,128)(2,1)}, bf16[256,128]{1,0:T(8,128)(2,1)S(1)}, u32[]{:S(2)}, u32[]{:S(2)}) collective-permute-start(bf16[256,128]{1,0:T(8,128)(2,1)} %get-tuple-element.15), channel_id=1, source_target_pairs={{0,6},{1,7},{2,4},{3,5},{4,2},{5,3},{6,0},{7,1},{8,14},{9,15},{10,... | collective-permute-start | bytes 196616 | tf_op jit(solution)/shard_map/ppermute | solution.py:25
  45.9 10.8 %copy-start.3 = (bf16[256,256]{1,0:T(8,128)(2,1)}, bf16[256,256]{1,0:T(8,128)(2,1)S(1)}, u32[]{:S(2)}) copy-start(bf16[256,256]{1,0:T(8,128)(2,1)S(1)} %constant_dynamic-update-slice_fusion.2.refs_4_) | copy-start | bytes 393220
  45.9 18.1 %collective-permute-start.17 = (bf16[256,256]{1,0:T(8,128)(2,1)S(1)}, bf16[256,256]{1,0:T(8,128)(2,1)S(1)}, u32[]{:S(2)}, u32[]{:S(2)}) collective-permute-start(bf16[256,256]{1,0:T(8,128)(2,1)S(1)} %constant_dynamic-update-slice_fusion.2.refs_4_), channel_id=1, source_target_pairs={{0,24},{8,16},{16,8},{24,0},{1,25},{9,17},{17,9},{25,1},{2,26},{10... | collective-permute-start | bytes 393224 | tf_op jit(solution)/shard_map/ppermute | solution.py:25
  48.2 1.3 copy-start.15
  48.2 15.9 %collective-permute-start.16 = (bf16[256,256]{1,0:T(8,128)(2,1)S(1)}, bf16[256,256]{1,0:T(8,128)(2,1)S(1)}, u32[]{:S(2)}, u32[]{:S(2)}) collective-permute-start(bf16[256,256]{1,0:T(8,128)(2,1)S(1)} %constant_dynamic-update-slice_fusion.2.refs_4_), channel_id=1, source_target_pairs={{0,16},{8,24},{16,0},{24,8},{1,17},{9,25},{17,1},{25,9},{2,18},{10... | collective-permute-start | bytes 393224 | tf_op jit(solution)/shard_map/ppermute | solution.py:25
  48.9 15.1 %collective-permute-start.15 = (bf16[256,256]{1,0:T(8,128)(2,1)S(1)}, bf16[256,256]{1,0:T(8,128)(2,1)S(1)}, u32[]{:S(2)}, u32[]{:S(2)}) collective-permute-start(bf16[256,256]{1,0:T(8,128)(2,1)S(1)} %constant_dynamic-update-slice_fusion.2.refs_4_), channel_id=1, source_target_pairs={{0,8},{8,0},{16,24},{24,16},{1,9},{9,1},{17,25},{25,17},{2,10},{10... | collective-permute-start | bytes 393224 | tf_op jit(solution)/shard_map/ppermute | solution.py:25
  64.0 0.7 copy-start.6
  64.0 0.7 copy-start.7
  64.8 0.7 copy-start.8
  68.5 5.2 %copy-start.21 = (bf16[256,128]{1,0:T(8,128)(2,1)S(1)}, bf16[256,128]{1,0:T(8,128)(2,1)}, u32[]{:S(2)}) copy-start(bf16[256,128]{1,0:T(8,128)(2,1)} %get-tuple-element.13) | copy-start | bytes 196612
  68.5 7.4 %copy-start.18 = (bf16[256,128]{1,0:T(8,128)(2,1)S(1)}, bf16[256,128]{1,0:T(8,128)(2,1)}, u32[]{:S(2)}) copy-start(bf16[256,128]{1,0:T(8,128)(2,1)} %get-tuple-element.12) | copy-start | bytes 196612
  68.5 37.4 %collective-permute-start.20 = (bf16[1024,256]{1,0:T(8,128)(2,1)}, bf16[1024,256]{1,0:T(8,128)(2,1)S(1)}, u32[]{:S(2)}, u32[]{:S(2)}) collective-permute-start(bf16[1024,256]{1,0:T(8,128)(2,1)} %project.7), channel_id=1, source_target_pairs={{0,2},{1,3},{2,0},{3,1},{4,6},{5,7},{6,4},{7,5},{8,10},{9,11},{10,... | collective-permute-start | bytes 1572872 | tf_op jit(solution)/shard_map/ppermute | solution.py:25
  71.8 40.1 %collective-permute-start.18 = (bf16[1024,256]{1,0:T(8,128)(2,1)}, bf16[1024,256]{1,0:T(8,128)(2,1)S(1)}, u32[]{:S(2)}, u32[]{:S(2)}) collective-permute-start(bf16[1024,256]{1,0:T(8,128)(2,1)} %project.5), channel_id=1, source_target_pairs={{0,2},{1,3},{2,0},{3,1},{4,6},{5,7},{6,4},{7,5},{8,10},{9,11},{10,... | collective-permute-start | bytes 1572872 | tf_op jit(solution)/shard_map/ppermute | solution.py:25
  73.6 17.2 %collective-permute-start.9 = (bf16[256,128]{1,0:T(8,128)(2,1)S(1)}, bf16[256,128]{1,0:T(8,128)(2,1)S(1)}, u32[]{:S(2)}, u32[]{:S(2)}) collective-permute-start(bf16[256,128]{1,0:T(8,128)(2,1)S(1)} %copy-done.21), channel_id=1, source_target_pairs={{0,4},{1,5},{2,6},{3,7},{4,0},{5,1},{6,2},{7,3},{8,12},{9,13},{10,... | collective-permute-start | bytes 196616 | tf_op jit(solution)/shard_map/ppermute | solution.py:25
  90.8 7.5 %copy-start.4 = (bf16[256,256]{1,0:T(8,128)(2,1)}, bf16[256,256]{1,0:T(8,128)(2,1)S(1)}, u32[]{:S(2)}) copy-start(bf16[256,256]{1,0:T(8,128)(2,1)S(1)} %constant_dynamic-update-slice_fusion.refs_4_) | copy-start | bytes 393220
  90.8 5.9 %collective-permute-start.12 = (bf16[256,256]{1,0:T(8,128)(2,1)S(1)}, bf16[256,256]{1,0:T(8,128)(2,1)S(1)}, u32[]{:S(2)}, u32[]{:S(2)}) collective-permute-start(bf16[256,256]{1,0:T(8,128)(2,1)S(1)} %constant_dynamic-update-slice_fusion.refs_4_), channel_id=1, source_target_pairs={{0,24},{8,16},{16,8},{24,0},{1,25},{9,17},{17,9},{25,1},{2,26},{10... | collective-permute-start | bytes 393224 | tf_op jit(solution)/shard_map/ppermute | solution.py:25
  93.0 5.2 %collective-permute-start.11 = (bf16[256,256]{1,0:T(8,128)(2,1)S(1)}, bf16[256,256]{1,0:T(8,128)(2,1)S(1)}, u32[]{:S(2)}, u32[]{:S(2)}) collective-permute-start(bf16[256,256]{1,0:T(8,128)(2,1)S(1)} %constant_dynamic-update-slice_fusion.refs_4_), channel_id=1, source_target_pairs={{0,16},{8,24},{16,0},{24,8},{1,17},{9,25},{17,1},{25,9},{2,18},{10... | collective-permute-start | bytes 393224 | tf_op jit(solution)/shard_map/ppermute | solution.py:25
  93.4 5.0 %collective-permute-start.10 = (bf16[256,256]{1,0:T(8,128)(2,1)S(1)}, bf16[256,256]{1,0:T(8,128)(2,1)S(1)}, u32[]{:S(2)}, u32[]{:S(2)}) collective-permute-start(bf16[256,256]{1,0:T(8,128)(2,1)S(1)} %constant_dynamic-update-slice_fusion.refs_4_), channel_id=1, source_target_pairs={{0,8},{8,0},{16,24},{24,16},{1,9},{9,1},{17,25},{25,17},{2,10},{10... | collective-permute-start | bytes 393224 | tf_op jit(solution)/shard_map/ppermute | solution.py:25
  96.8 1.6 %copy-start.9 = (bf16[256,256]{1,0:T(8,128)(2,1)}, bf16[256,256]{1,0:T(8,128)(2,1)S(1)}, u32[]{:S(2)}) copy-start(bf16[256,256]{1,0:T(8,128)(2,1)S(1)} %collective-permute-done.12.refs_7_) | copy-start | bytes 393220
  98.2 0.7 copy-start.10
  98.8 0.7 copy-start.11
  105.9 0.8 copy-start
  108.5 20.2 %collective-permute-start.21 = (bf16[1024,128]{1,0:T(8,128)(2,1)}, bf16[1024,128]{1,0:T(8,128)(2,1)S(1)}, u32[]{:S(2)}, u32[]{:S(2)}) collective-permute-start(bf16[1024,128]{1,0:T(8,128)(2,1)} %add_columns.3), channel_id=1, source_target_pairs={{0,4},{1,5},{2,6},{3,7},{4,0},{5,1},{6,2},{7,3},{8,12},{9,13},{10,... | collective-permute-start | bytes 786440 | tf_op jit(solution)/shard_map/ppermute | solution.py:25
  111.9 0.8 copy-start.1
  114.5 17.0 %collective-permute-start.19 = (bf16[1024,128]{1,0:T(8,128)(2,1)}, bf16[1024,128]{1,0:T(8,128)(2,1)S(1)}, u32[]{:S(2)}, u32[]{:S(2)}) collective-permute-start(bf16[1024,128]{1,0:T(8,128)(2,1)} %add_columns.2), channel_id=1, source_target_pairs={{0,4},{1,5},{2,6},{3,7},{4,0},{5,1},{6,2},{7,3},{8,12},{9,13},{10,... | collective-permute-start | bytes 786440 | tf_op jit(solution)/shard_map/ppermute | solution.py:25
  128.7 0.7 copy-start.17
  131.5 0.7 copy-start.16

commit v3 on v1

v3 whole, which is shorter than its diff:
```python
import functools
import math

import jax
import jax.numpy as jnp
from jax import lax
from jax.experimental import pallas as pl
from jax.experimental.pallas import tpu as pltpu
from jax.sharding import PartitionSpec as P

F32 = jnp.float32
BF16 = jnp.bfloat16
VMEM_LIMIT = 36 * 2**20
IN_ORDER = pltpu.CompilerParams(
    vmem_limit_bytes=VMEM_LIMIT, dimension_semantics=("arbitrary",)
)


def cost(flops, moved, exponents=0):
    return pl.CostEstimate(flops=flops, bytes_accessed=moved, transcendentals=exponents)


def swap(value, axis, mask):
    pairs = [(source, source ^ mask) for source in range(lax.axis_size(axis))]
    return lax.ppermute(value, axis, pairs)


def dot(left, right, left_dim, right_dim):
    dims = (((left_dim,), (right_dim,)), ((), ()))
    return lax.dot_general(left, right, dims, preferred_element_type=F32)


def attention_kernel(height, own_ref, other_ref, q_ref, up_ref, dq_ref, mine_ref, theirs_ref, k_ref, v_ref, dk_ref, dv_ref):
    length, depth = q_ref.shape
    factor = depth**-0.5
    power = factor * math.log2(math.e)
    head = pl.program_id(0)
    is_even = lax.axis_index("tensor") % 2 == 0

    @pl.when(head == 0)
    def _():
        k_ref[...] = jnp.where(is_even, own_ref[...], other_ref[...])
        v_ref[...] = jnp.where(is_even, other_ref[...], own_ref[...])
        dk_ref[...] = jnp.zeros_like(dk_ref)
        dv_ref[...] = jnp.zeros_like(dv_ref)

    half = height // 2
    key_place = lax.broadcasted_iota(jnp.int32, (half, half), 0)
    query_place = lax.broadcasted_iota(jnp.int32, (half, half), 1)
    visible = key_place <= query_place

    def merge(reduce, join, long, short):
        long = reduce(long, axis=0, keepdims=True)
        short = reduce(short, axis=0, keepdims=True)
        return jnp.concatenate([long[:, :half], join(long[:, half:], short)], 1)

    for block in reversed(range(length // height)):
        first = block * height
        middle = first + half
        finish = first + height
        query, upstream = q_ref[first:finish], up_ref[first:finish]
        query_end, upstream_end = query[half:], upstream[half:]
        keys, values = k_ref[:middle], v_ref[:middle]
        keys_end, values_end = k_ref[middle:finish], v_ref[middle:finish]
        scores = dot(keys, query, 1, 1)
        scores_end = dot(keys_end, query_end, 1, 1)
        product = dot(values, upstream, 1, 1)
        product_end = dot(values_end, upstream_end, 1, 1)
        corner = jnp.where(visible, scores[first:, :half], -jnp.inf)
        corner = jnp.concatenate([corner, scores[first:, half:]], 1)
        scores = corner if block == 0 else jnp.concatenate([scores[:first], corner], 0)
        scores_end = jnp.where(visible, scores_end, -jnp.inf)
        biggest = merge(jnp.max, jnp.maximum, scores, scores_end)
        weights = jnp.exp2((scores - biggest) * power)
        weights_end = jnp.exp2((scores_end - biggest[:, half:]) * power)
        scale = 1.0 / merge(jnp.sum, jnp.add, weights, weights_end)
        center = merge(jnp.sum, jnp.add, weights * product, weights_end * product_end) * scale
        weights = weights * scale
        weights_end = weights_end * scale[:, half:]
        grad = (weights * (product - center) * factor).astype(BF16)
        grad_end = (weights_end * (product_end - center[:, half:]) * factor).astype(BF16)
        dv_ref[:middle] += dot(weights.astype(BF16), upstream, 1, 0)
        dv_ref[middle:finish] += dot(weights_end.astype(BF16), upstream_end, 1, 0)
        dk_ref[:middle] += dot(grad, query, 1, 0)
        dk_ref[middle:finish] += dot(grad_end, query_end, 1, 0)
        query_grad = dot(grad, keys, 0, 0)
        dq_ref[first:middle] = query_grad[:half].astype(BF16)
        dq_ref[middle:finish] = (query_grad[half:] + dot(grad_end, keys_end, 0, 0)).astype(BF16)

    @pl.when(head == pl.num_programs(0) - 1)
    def _():
        mine_ref[...] = jnp.where(is_even, dk_ref[...], dv_ref[...])
        theirs_ref[...] = jnp.where(is_even, dv_ref[...], dk_ref[...])


def attention(own, other, queries, out_grad):
    length, width = queries.shape
    depth = own.shape[1]
    height = min(512, length)
    column = pl.BlockSpec((length, depth), lambda h: (0, h))
    whole = pl.BlockSpec((length, depth), lambda h: (0, 0))
    sums = jax.ShapeDtypeStruct((length, depth), F32)
    return pl.pallas_call(
        functools.partial(attention_kernel, height),
        grid=(width // depth,),
        in_specs=[whole, whole, column, column],
        out_specs=[column, whole, whole],
        out_shape=[jax.ShapeDtypeStruct((length, width), BF16), sums, sums],
        scratch_shapes=[
            pltpu.VMEM((length, depth), BF16),
            pltpu.VMEM((length, depth), BF16),
            pltpu.VMEM((length, depth), F32),
            pltpu.VMEM((length, depth), F32),
        ],
        compiler_params=IN_ORDER,
        cost_estimate=cost(
            20 * length * length * width,
            6 * queries.nbytes,
            length * length * width // depth,
        ),
        name="attention",
    )(own, other, queries, out_grad)


def kv_kernel(rows, mine_ref, arrived_ref, mask_ref, *out_refs):
    place = lax.axis_index("tensor")
    chip, core = place // 2, place % 2
    for step, out_ref in enumerate(out_refs):
        for half in range(2):
            start = ((chip ^ step) * 2 + (core ^ half)) * rows
            span = pl.ds(pl.multiple_of(start, rows), rows)
            total = mine_ref[span, :] + arrived_ref[span, :].astype(F32)
            keep = mask_ref[span, :].astype(F32)
            out_ref[half * rows : (half + 1) * rows, :] = (total * keep).astype(BF16)


def kv_blocks(mine, arrived, mask, rows):
    length, depth = mine.shape
    count = length // (2 * rows)
    return pl.pallas_call(
        functools.partial(kv_kernel, rows),
        out_shape=[jax.ShapeDtypeStruct((2 * rows, depth), BF16)] * count,
        compiler_params=pltpu.CompilerParams(vmem_limit_bytes=8 * 2**20),
        cost_estimate=cost(0, 2 * mine.nbytes),
        name="kv_blocks",
    )(mine, arrived, mask)


def per_device(inputs, queries, keys_values, out_grad, weight_mask, clip_mask):
    depth = keys_values.shape[1]
    rows = inputs.shape[0]
    groups = lax.axis_size("dp")
    chips = lax.axis_size("tensor") // 2
    block = weight_mask.shape[0]
    row_place = lax.axis_index("dp")

    other = swap(keys_values, "tensor", 1)
    parts = []
    for step in range(groups):
        start = (row_place ^ step) * block
        part = lax.dynamic_slice(inputs, (0, start), (rows, block))
        parts.append(part if step == 0 else swap(part, "dp", step))

    query_grad, mine, theirs = attention(keys_values, other, queries, out_grad)
    arrived = swap(theirs, "tensor", 1)
    arrived, *parts = lax.optimization_barrier((arrived, *parts))
    pieces = [piece for part in parts for piece in (part, swap(part, "tensor", 1))]
    blocks = kv_blocks(mine, arrived, clip_mask, rows)

    blocks = [b if s == 0 else swap(b, "tensor", 2 * s) for s, b in enumerate(blocks)]
    blocks = lax.optimization_barrier(blocks)
    order = sorted(range(chips), key=lambda s: [(s >> b) & 1 for b in range(8)])
    evens, odds = order[: chips // 2], order[chips // 2 :]

    def gather(steps):
        stacked = jnp.concatenate([blocks[s] for s in steps], 1)
        parts = [stacked if s == 0 else swap(stacked, "dp", s) for s in range(groups)]
        return jnp.concatenate(parts, 0)

    grads_odd = gather(odds)
    grads_even = gather(evens)

    wide = block // 2
    near = jnp.concatenate([p[:, :wide] for p in pieces], 0)
    far = jnp.concatenate([p[:, wide:] for p in pieces], 0)

    def column(step):
        group = evens if step in evens else odds
        place = group.index(step) * depth
        return (grads_even if step in evens else grads_odd)[:, place : place + depth]

    sent = swap(dot(near, grads_odd, 0, 0).astype(BF16), "tensor", 2)
    straight = [
        swap(dot(far, column(step), 0, 0).astype(BF16), "tensor", 2 * step)
        for step in odds + evens[1:]
    ]
    terms = [dot(near, grads_even, 0, 0), sent]
    columns, bit = chips // 2 * depth, 2
    while columns > depth:
        columns, bit = columns // 2, bit * 2
        away = sum(t[:, columns : 2 * columns].astype(F32) for t in terms).astype(BF16)
        terms.append(swap(away, "tensor", bit))
    upper = sum(t[:, :depth].astype(F32) for t in terms)
    lower = dot(far, column(0), 0, 0) + sum(t.astype(F32) for t in straight)
    summed = jnp.concatenate([upper, lower], 0)
    weight_grad = jnp.where(weight_mask == 1, summed, 0.0)
    return (query_grad, weight_grad)


def solution(mesh):
    spec = P("dp", "tensor")
    in_specs = (P(("dp", "tensor"), None), spec, spec, spec, spec, spec)
    return jax.shard_map(
        per_device, mesh=mesh, in_specs=in_specs, out_specs=(spec, spec), check_vma=False
    )
```

time: 132 us -> 104 us (0.79)
  Pallas kernels: 39.3 us -> 17.1 us
  waiting for transfers between devices: 57.1 us -> 46.2 us
  matrix products: 0 us -> 4.52 us
  starting transfers between devices: 23.1 us -> 26.3 us
  other arithmetic: 3.69 us -> 1.28 us
  local copies, waits for them, and re-layouts: 7.12 us -> 5.52 us
    pallas_call x5 -> x1, Pallas kernels: 19.6 us -> 0.21 us  [kv_blocks(): pl.pallas_call(functools.partial(kv_kernel, rows), out_shape=[jax.ShapeDt...]
    ppermute x19 -> x23, waiting for transfers between devices: 57.1 us -> 46.2 us  [swap(): return lax.ppermute(value, axis, pairs)]
    dot_general x0 -> x6, matrix products: none -> 4.52 us  [dot(): return lax.dot_general(left, right, dims, preferred_element_type=F32)]
    ppermute x19 -> x23, starting transfers between devices: 23.1 us -> 26.3 us  [swap(): return lax.ppermute(value, axis, pairs)]
    pallas_call x1, Pallas kernels: 19.7 us -> 16.9 us  [attention(): pl.pallas_call(functools.partial(attention_kernel, height), grid=(width /...]
    dynamic_slice x1, local copies, waits for them, and re-layouts: 0.14 us -> 2.86 us  [per_device(): part = lax.dynamic_slice(inputs, (0, start), (rows, block))]
    concatenate x4 -> x2, other arithmetic: 2.34 us -> 0.07 us  [gather(): return jnp.concatenate(parts, 0)]
    slice x5 -> x0, local copies, waits for them, and re-layouts: 2.19 us -> none  [the longest x3 2.15 us: per_device(): g[half:]]
  transfers between devices with their start and end apart: 19 -> 23, of which waited for: 11 -> 10; matrix products, arithmetic and copies ran while one was open for 4% -> 8% of each run, Pallas kernels for 9% -> 17%
where the time goes in v3:
time: 104 us; the launch traced here: 102 us
  waiting for transfers between devices  46.2 us (44%)
  starting transfers between devices  26.3 us (25%)
  Pallas kernels  17.1 us (16%)
  local copies, waits for them, and re-layouts  5.52 us (5%)
  matrix products  4.52 us (4%)
  other arithmetic  1.28 us (1%)
    ppermute x23, waiting for transfers between devices, swap(): return lax.ppermute(value, axis, pairs)  46.2 us
    ppermute x23, starting transfers between devices, swap(): return lax.ppermute(value, axis, pairs)  26.3 us
    pallas_call x1, Pallas kernels, attention(): pl.pallas_call(functools.partial(attention_kernel, height), grid=(width /...  16.9 us
    dot_general x6, matrix products, dot(): return lax.dot_general(left, right, dims, preferred_element_type=F32)  4.52 us
    dynamic_slice x1, local copies, waits for them, and re-layouts, per_device(): part = lax.dynamic_slice(inputs, (0, start), (rows, block))  2.86 us
    unnamed x20, local copies, waits for them, and re-layouts  2.58 us
  transfers between devices with their start and end apart: 23, of which 10 were waited for; matrix products, arithmetic and copies ran while one was open for 8% of the time, Pallas kernels for 17%

profile of v3, /device:TPU:0, one launch (start us, length us, event | category | flops | bytes accessed | tf_op | source)
XLA Modules:
  0.0 101.8 jit_solution(10213571236505562422)
XLA Ops:
  0.6 0.5 collective-permute-start
  1.2 2.9 %constant_dynamic-slice_fusion = (bf16[128,2048]{1,0:T(8,128)(2,1)}, bf16[128,2048]{1,0:T(8,128)(2,1)}, bf16[128,2048]{1,0:T(8,128)(2,1)S(1)}, bf16[128,2048]{1,0:T(8,128)(2,1)}) fusion(bf16[128,8192]{1,0:T(8,128)(2,1)} %param.6, s32[]{:T(128)S(6)} %select_n.19, s32[]{:T(128)S(6)} %select_n.17, s32[]{:T(128)S(6)} %select_n.16, s32[]{:T(128)S(6)} %select_n.18), kind=kLoop, calls=%fused_computation.36 | loop fusion | bytes 4194320 | tf_op jit(solution)/shard_map/dynamic_slice | solution.py:161
  4.0 2.6 %collective-permute-start.2 = (bf16[128,2048]{1,0:T(8,128)(2,1)}, bf16[128,2048]{1,0:T(8,128)(2,1)}, u32[]{:S(2)}, u32[]{:S(2)}) collective-permute-start(bf16[128,2048]{1,0:T(8,128)(2,1)} %get-tuple-element.35), channel_id=1, source_target_pairs={{0,8},{8,0},{16,24},{24,16},{1,9},{9,1},{17,25},{25,17},{2,10},{10... | collective-permute-start | bytes 1572872 | tf_op jit(solution)/shard_map/ppermute | solution.py:25
  6.6 1.5 %collective-permute-start.3 = (bf16[128,2048]{1,0:T(8,128)(2,1)}, bf16[128,2048]{1,0:T(8,128)(2,1)}, u32[]{:S(2)}, u32[]{:S(2)}) collective-permute-start(bf16[128,2048]{1,0:T(8,128)(2,1)} %get-tuple-element.37), channel_id=1, source_target_pairs={{0,16},{8,24},{16,0},{24,8},{1,17},{9,25},{17,1},{25,9},{2,18},{10... | collective-permute-start | bytes 1572872 | tf_op jit(solution)/shard_map/ppermute | solution.py:25
  8.1 0.0 collective-permute-start.4
  8.1 0.0 collective-permute-done.other_ref
  8.1 16.9 %attention.1 = (bf16[1024,768]{1,0:T(8,128)(2,1)}, f32[1024,128]{1,0:T(8,128)S(1)}, f32[1024,128]{1,0:T(8,128)S(1)}) custom-call(bf16[1024,128]{1,0:T(8,128)(2,1)S(1)} %copy-done.2, bf16[1024,128]{1,0:T(8,128)(2,1)S(1)} %collective-permute-done.other_ref, bf16[1024,768]{1,0:T(8,128)(2,1)S(1)} %copy-done, bf16[1024,768]{1,0:T(8,128)(2,1)S(1)} %copy-done.1), custom_call_target="tpu_custom_call" | custom-call | flops 16106127360 | bytes 9437184 | tf_op jit(solution)/shard_map/attention/pallas_call | solution.py:103
  25.0 0.2 copy.8.mask_ref
  25.3 6.8 %collective-permute-done.3 = bf16[128,2048]{1,0:T(8,128)(2,1)} collective-permute-done((bf16[128,2048]{1,0:T(8,128)(2,1)}, bf16[128,2048]{1,0:T(8,128)(2,1)}, u32[]{:S(2)}, u32[]{:S(2)}) %collective-permute-start.3) | collective-permute-done | bytes 524320 | tf_op jit(solution)/shard_map/ppermute | solution.py:25
  32.1 0.2 kv_blocks.1
  32.3 2.7 %collective-permute-start.10 = (bf16[256,128]{1,0:T(8,128)(2,1)S(1)}, bf16[256,128]{1,0:T(8,128)(2,1)S(1)}, u32[]{:S(2)}, u32[]{:S(2)}) collective-permute-start(bf16[256,128]{1,0:T(8,128)(2,1)S(1)} %get-tuple-element.28), channel_id=1, source_target_pairs={{0,4},{1,5},{2,6},{3,7},{4,0},{5,1},{6,2},{7,3},{8,12},{9,13},{10,... | collective-permute-start | bytes 196616 | tf_op jit(solution)/shard_map/ppermute | solution.py:25
  35.0 1.3 %collective-permute-start.11 = (bf16[256,128]{1,0:T(8,128)(2,1)S(1)}, bf16[256,128]{1,0:T(8,128)(2,1)S(1)}, u32[]{:S(2)}, u32[]{:S(2)}) collective-permute-start(bf16[256,128]{1,0:T(8,128)(2,1)S(1)} %get-tuple-element.29), channel_id=1, source_target_pairs={{0,6},{1,7},{2,4},{3,5},{4,2},{5,3},{6,0},{7,1},{8,14},{9,15},{10,... | collective-permute-start | bytes 196616 | tf_op jit(solution)/shard_map/ppermute | solution.py:25
  36.3 0.2 collective-permute-start.9
  36.6 1.1 %collective-permute-done.10 = bf16[256,128]{1,0:T(8,128)(2,1)S(1)} collective-permute-done((bf16[256,128]{1,0:T(8,128)(2,1)S(1)}, bf16[256,128]{1,0:T(8,128)(2,1)S(1)}, u32[]{:S(2)}, u32[]{:S(2)}) %collective-permute-start.10) | collective-permute-done | bytes 65568 | tf_op jit(solution)/shard_map/ppermute | solution.py:25
  37.6 3.6 %collective-permute-done.11 = bf16[256,128]{1,0:T(8,128)(2,1)S(1)} collective-permute-done((bf16[256,128]{1,0:T(8,128)(2,1)S(1)}, bf16[256,128]{1,0:T(8,128)(2,1)S(1)}, u32[]{:S(2)}, u32[]{:S(2)}) %collective-permute-start.11) | collective-permute-done | bytes 65568 | tf_op jit(solution)/shard_map/ppermute | solution.py:25
  41.2 0.1 collective-permute-done.9
  41.3 1.2 %collective-permute-start.15 = (bf16[256,256]{1,0:T(8,128)(2,1)S(1)}, bf16[256,256]{1,0:T(8,128)(2,1)S(1)}, u32[]{:S(2)}, u32[]{:S(2)}) collective-permute-start(bf16[256,256]{1,0:T(8,128)(2,1)S(1)} %constant_dynamic-update-slice_fusion.2), channel_id=1, source_target_pairs={{0,8},{8,0},{16,24},{24,16},{1,9},{9,1},{17,25},{25,17},{2,10},{10... | collective-permute-start | bytes 393224 | tf_op jit(solution)/shard_map/ppermute | solution.py:25
  42.5 0.9 collective-permute-start.16
  43.5 1.4 %collective-permute-start.17 = (bf16[256,256]{1,0:T(8,128)(2,1)S(1)}, bf16[256,256]{1,0:T(8,128)(2,1)S(1)}, u32[]{:S(2)}, u32[]{:S(2)}) collective-permute-start(bf16[256,256]{1,0:T(8,128)(2,1)S(1)} %constant_dynamic-update-slice_fusion.2), channel_id=1, source_target_pairs={{0,24},{8,16},{16,8},{24,0},{1,25},{9,17},{17,9},{25,1},{2,26},{10... | collective-permute-start | bytes 393224 | tf_op jit(solution)/shard_map/ppermute | solution.py:25
  44.9 1.2 %collective-permute-start.12 = (bf16[256,256]{1,0:T(8,128)(2,1)S(1)}, bf16[256,256]{1,0:T(8,128)(2,1)S(1)}, u32[]{:S(2)}, u32[]{:S(2)}) collective-permute-start(bf16[256,256]{1,0:T(8,128)(2,1)S(1)} %constant_dynamic-update-slice_fusion), channel_id=1, source_target_pairs={{0,8},{8,0},{16,24},{24,16},{1,9},{9,1},{17,25},{25,17},{2,10},{10... | collective-permute-start | bytes 393224 | tf_op jit(solution)/shard_map/ppermute | solution.py:25
  46.1 1.6 %collective-permute-done.15 = bf16[256,256]{1,0:T(8,128)(2,1)S(1)} collective-permute-done((bf16[256,256]{1,0:T(8,128)(2,1)S(1)}, bf16[256,256]{1,0:T(8,128)(2,1)S(1)}, u32[]{:S(2)}, u32[]{:S(2)}) %collective-permute-start.15) | collective-permute-done | bytes 131104 | tf_op jit(solution)/shard_map/ppermute | solution.py:25
  47.8 1.4 %collective-permute-start.13 = (bf16[256,256]{1,0:T(8,128)(2,1)S(1)}, bf16[256,256]{1,0:T(8,128)(2,1)S(1)}, u32[]{:S(2)}, u32[]{:S(2)}) collective-permute-start(bf16[256,256]{1,0:T(8,128)(2,1)S(1)} %constant_dynamic-update-slice_fusion), channel_id=1, source_target_pairs={{0,16},{8,24},{16,0},{24,8},{1,17},{9,25},{17,1},{25,9},{2,18},{10... | collective-permute-start | bytes 393224 | tf_op jit(solution)/shard_map/ppermute | solution.py:25
  49.1 3.0 %collective-permute-start.14 = (bf16[256,256]{1,0:T(8,128)(2,1)S(1)}, bf16[256,256]{1,0:T(8,128)(2,1)S(1)}, u32[]{:S(2)}, u32[]{:S(2)}) collective-permute-start(bf16[256,256]{1,0:T(8,128)(2,1)S(1)} %constant_dynamic-update-slice_fusion), channel_id=1, source_target_pairs={{0,24},{8,16},{16,8},{24,0},{1,25},{9,17},{17,9},{25,1},{2,26},{10... | collective-permute-start | bytes 393224 | tf_op jit(solution)/shard_map/ppermute | solution.py:25
  52.2 0.1 collective-permute-start.6
  52.3 0.2 collective-permute-done.12
  52.5 0.3 collective-permute-start.7
  52.9 0.2 collective-permute-start.8
  53.0 2.0 %collective-permute-done.14 = bf16[256,256]{1,0:T(8,128)(2,1)S(1)} collective-permute-done((bf16[256,256]{1,0:T(8,128)(2,1)S(1)}, bf16[256,256]{1,0:T(8,128)(2,1)S(1)}, u32[]{:S(2)}, u32[]{:S(2)}) %collective-permute-start.14) | collective-permute-done | bytes 131104 | tf_op jit(solution)/shard_map/ppermute | solution.py:25
  55.2 1.1 %slice_dynamic-update-slice_fusion.14 = (bf16[1024,1024]{1,0:T(8,128)(2,1)S(1)}, bf16[1024,1024]{1,0:T(8,128)(2,1)S(1)}) fusion(bf16[1024,1024]{1,0:T(8,128)(2,1)S(1)} %get-tuple-element.50, bf16[128,2048]{1,0:T(8,128)(2,1)} %collective-permute-done.2, bf16[1024,1024]{1,0:T(8,128)(2,1)S(1)} %get-tuple-element.51), kind=kLoop, calls=%fused_computation.30 | loop fusion | bytes 1048576
  56.3 1.1 %slice_dynamic-update-slice_fusion.13 = (bf16[1024,1024]{1,0:T(8,128)(2,1)S(1)}, bf16[1024,1024]{1,0:T(8,128)(2,1)S(1)}) fusion(bf16[1024,1024]{1,0:T(8,128)(2,1)S(1)} %get-tuple-element.46, bf16[128,2048]{1,0:T(8,128)(2,1)} %collective-permute-done.3, bf16[1024,1024]{1,0:T(8,128)(2,1)S(1)} %get-tuple-element.47), kind=kLoop, calls=%fused_computation.29 | loop fusion | bytes 1048576
  57.5 0.8 convolution_convert_fusion.3
  58.3 0.8 convolution_convert_fusion.2
  59.0 0.8 convolution_convert_fusion
  59.8 2.8 %collective-permute-start.18 = (bf16[1024,256]{1,0:T(8,128)(2,1)S(1)}, bf16[1024,256]{1,0:T(8,128)(2,1)S(1)}, u32[]{:S(2)}, u32[]{:S(2)}) collective-permute-start(bf16[1024,256]{1,0:T(8,128)(2,1)S(1)} %convolution_convert_fusion), channel_id=1, source_target_pairs={{0,2},{1,3},{2,0},{3,1},{4,6},{5,7},{6,4},{7,5},{8,10},{9,11},{10,... | collective-permute-start | bytes 1572872 | tf_op jit(solution)/shard_map/ppermute | solution.py:25
  62.6 0.1 collective-permute-start.20
  62.7 3.5 %collective-permute-start.21 = (bf16[1024,128]{1,0:T(8,128)(2,1)S(1)}, bf16[1024,128]{1,0:T(8,128)(2,1)S(1)}, u32[]{:S(2)}, u32[]{:S(2)}) collective-permute-start(bf16[1024,128]{1,0:T(8,128)(2,1)S(1)} %convolution_convert_fusion.2), channel_id=1, source_target_pairs={{0,6},{1,7},{2,4},{3,5},{4,2},{5,3},{6,0},{7,1},{8,14},{9,15},{10,... | collective-permute-start | bytes 786440 | tf_op jit(solution)/shard_map/ppermute | solution.py:25
  66.2 0.8 convolution_convert_fusion.1
  67.0 0.1 collective-permute-start.22
  67.1 0.7 fusion.6
  67.8 21.7 %collective-permute-done.18 = bf16[1024,256]{1,0:T(8,128)(2,1)S(1)} collective-permute-done((bf16[1024,256]{1,0:T(8,128)(2,1)S(1)}, bf16[1024,256]{1,0:T(8,128)(2,1)S(1)}, u32[]{:S(2)}, u32[]{:S(2)}) %collective-permute-start.18) | collective-permute-done | bytes 524320 | tf_op jit(solution)/shard_map/ppermute | solution.py:25
  89.5 0.1 fusion
  89.6 1.3 %collective-permute-start.19 = (bf16[1024,128]{1,0:T(8,128)(2,1)S(1)}, bf16[1024,128]{1,0:T(8,128)(2,1)S(1)}, u32[]{:S(2)}, u32[]{:S(2)}) collective-permute-start(bf16[1024,128]{1,0:T(8,128)(2,1)S(1)} %fusion), channel_id=1, source_target_pairs={{0,4},{1,5},{2,6},{3,7},{4,0},{5,1},{6,2},{7,3},{8,12},{9,13},{10,... | collective-permute-start | bytes 786440 | tf_op jit(solution)/shard_map/ppermute | solution.py:25
  90.9 1.5 %collective-permute-done.20 = bf16[1024,128]{1,0:T(8,128)(2,1)S(1)} collective-permute-done((bf16[1024,128]{1,0:T(8,128)(2,1)S(1)}, bf16[1024,128]{1,0:T(8,128)(2,1)S(1)}, u32[]{:S(2)}, u32[]{:S(2)}) %collective-permute-start.20) | collective-permute-done | bytes 262176 | tf_op jit(solution)/shard_map/ppermute | solution.py:25
  92.4 0.7 convolution_add_fusion
  93.2 0.0 copy-start.3
  93.2 7.5 %collective-permute-done.19 = bf16[1024,128]{1,0:T(8,128)(2,1)S(1)} collective-permute-done((bf16[1024,128]{1,0:T(8,128)(2,1)S(1)}, bf16[1024,128]{1,0:T(8,128)(2,1)S(1)}, u32[]{:S(2)}, u32[]{:S(2)}) %collective-permute-start.19) | collective-permute-done | bytes 262176 | tf_op jit(solution)/shard_map/ppermute | solution.py:25
  100.7 0.1 fusion.1
  100.8 1.1 %maximum_select_fusion = f32[2048,128]{1,0:T(8,128)} fusion(f32[1024,128]{1,0:T(8,128)S(1)} %convolution_add_fusion, f32[1024,128]{1,0:T(8,128)S(1)} %fusion.1, s32[2048,128]{1,0:T(8,128)S(1)} %copy-done.3), kind=kLoop, calls=%fused_computation.5 | loop fusion | flops 786432 | bytes 3145728 | tf_op jit(solution)/shard_map/jit(_where)/select_n | solution.py:206
  (35 shorter events, 0.4 us)
Async XLA Ops:
  0.6 7.5 %collective-permute-start = (bf16[1024,128]{1,0:T(8,128)(2,1)}, bf16[1024,128]{1,0:T(8,128)(2,1)S(1)}, u32[]{:S(2)}, u32[]{:S(2)}) collective-permute-start(bf16[1024,128]{1,0:T(8,128)(2,1)} %own_ref.1), channel_id=1, source_target_pairs={{0,1},{1,0},{2,3},{3,2},{4,5},{5,4},{6,7},{7,6},{8,9},{9,8},{10,11... | collective-permute-start | bytes 786440 | tf_op jit(solution)/shard_map/ppermute | solution.py:25
  1.1 7.0 %copy-start = (bf16[1024,768]{1,0:T(8,128)(2,1)S(1)}, bf16[1024,768]{1,0:T(8,128)(2,1)}, u32[]{:S(2)}) copy-start(bf16[1024,768]{1,0:T(8,128)(2,1)} %q_ref.1) | copy-start | bytes 4718596
  1.2 7.0 %copy-start.1 = (bf16[1024,768]{1,0:T(8,128)(2,1)S(1)}, bf16[1024,768]{1,0:T(8,128)(2,1)}, u32[]{:S(2)}) copy-start(bf16[1024,768]{1,0:T(8,128)(2,1)} %up_ref.1) | copy-start | bytes 4718596
  1.2 7.0 %copy-start.2 = (bf16[1024,128]{1,0:T(8,128)(2,1)S(1)}, bf16[1024,128]{1,0:T(8,128)(2,1)}, u32[]{:S(2)}) copy-start(bf16[1024,128]{1,0:T(8,128)(2,1)} %own_ref.1) | copy-start | bytes 786436
  4.0 21.2 %collective-permute-start.2 = (bf16[128,2048]{1,0:T(8,128)(2,1)}, bf16[128,2048]{1,0:T(8,128)(2,1)}, u32[]{:S(2)}, u32[]{:S(2)}) collective-permute-start(bf16[128,2048]{1,0:T(8,128)(2,1)} %get-tuple-element.35), channel_id=1, source_target_pairs={{0,8},{8,0},{16,24},{24,16},{1,9},{9,1},{17,25},{25,17},{2,10},{10... | collective-permute-start | bytes 1572872 | tf_op jit(solution)/shard_map/ppermute | solution.py:25
  6.6 25.5 %collective-permute-start.3 = (bf16[128,2048]{1,0:T(8,128)(2,1)}, bf16[128,2048]{1,0:T(8,128)(2,1)}, u32[]{:S(2)}, u32[]{:S(2)}) collective-permute-start(bf16[128,2048]{1,0:T(8,128)(2,1)} %get-tuple-element.37), channel_id=1, source_target_pairs={{0,16},{8,24},{16,0},{24,8},{1,17},{9,25},{17,1},{25,9},{2,18},{10... | collective-permute-start | bytes 1572872 | tf_op jit(solution)/shard_map/ppermute | solution.py:25
  8.1 16.9 %copy-start.4 = (s32[1024,1]{0,1:T(1,128)S(1)}, s32[1024,1]{0,1:T(1,128)}, u32[]{:S(2)}) copy-start(s32[1024,1]{0,1:T(1,128)} %param.11) | copy-start | bytes 12292
  8.1 24.0 %collective-permute-start.4 = (bf16[128,2048]{1,0:T(8,128)(2,1)}, bf16[128,2048]{1,0:T(8,128)(2,1)S(1)}, u32[]{:S(2)}, u32[]{:S(2)}) collective-permute-start(bf16[128,2048]{1,0:T(8,128)(2,1)} %get-tuple-element.34), channel_id=1, source_target_pairs={{0,24},{8,16},{16,8},{24,0},{1,25},{9,17},{17,9},{25,1},{2,26},{10... | collective-permute-start | bytes 1572872 | tf_op jit(solution)/shard_map/ppermute | solution.py:25
  25.0 7.1 %collective-permute-start.1 = (f32[1024,128]{1,0:T(8,128)S(1)}, f32[1024,128]{1,0:T(8,128)S(1)}, u32[]{:S(2)}, u32[]{:S(2)}) collective-permute-start(f32[1024,128]{1,0:T(8,128)S(1)} %get-tuple-element.19), channel_id=1, source_target_pairs={{0,1},{1,0},{2,3},{3,2},{4,5},{5,4},{6,7},{7,6},{8,9},{9,8},{10,11... | collective-permute-start | bytes 1572872 | tf_op jit(solution)/shard_map/ppermute | solution.py:25
  32.3 5.3 %collective-permute-start.10 = (bf16[256,128]{1,0:T(8,128)(2,1)S(1)}, bf16[256,128]{1,0:T(8,128)(2,1)S(1)}, u32[]{:S(2)}, u32[]{:S(2)}) collective-permute-start(bf16[256,128]{1,0:T(8,128)(2,1)S(1)} %get-tuple-element.28), channel_id=1, source_target_pairs={{0,4},{1,5},{2,6},{3,7},{4,0},{5,1},{6,2},{7,3},{8,12},{9,13},{10,... | collective-permute-start | bytes 196616 | tf_op jit(solution)/shard_map/ppermute | solution.py:25
  35.0 6.2 %collective-permute-start.11 = (bf16[256,128]{1,0:T(8,128)(2,1)S(1)}, bf16[256,128]{1,0:T(8,128)(2,1)S(1)}, u32[]{:S(2)}, u32[]{:S(2)}) collective-permute-start(bf16[256,128]{1,0:T(8,128)(2,1)S(1)} %get-tuple-element.29), channel_id=1, source_target_pairs={{0,6},{1,7},{2,4},{3,5},{4,2},{5,3},{6,0},{7,1},{8,14},{9,15},{10,... | collective-permute-start | bytes 196616 | tf_op jit(solution)/shard_map/ppermute | solution.py:25
  36.3 5.0 %collective-permute-start.9 = (bf16[256,128]{1,0:T(8,128)(2,1)S(1)}, bf16[256,128]{1,0:T(8,128)(2,1)S(1)}, u32[]{:S(2)}, u32[]{:S(2)}) collective-permute-start(bf16[256,128]{1,0:T(8,128)(2,1)S(1)} %get-tuple-element.27), channel_id=1, source_target_pairs={{0,2},{1,3},{2,0},{3,1},{4,6},{5,7},{6,4},{7,5},{8,10},{9,11},{10,... | collective-permute-start | bytes 196616 | tf_op jit(solution)/shard_map/ppermute | solution.py:25
  36.6 18.5 %collective-permute-start.5 = (bf16[128,2048]{1,0:T(8,128)(2,1)S(1)}, bf16[128,2048]{1,0:T(8,128)(2,1)S(1)}, u32[]{:S(2)}, u32[]{:S(2)}) collective-permute-start(bf16[128,2048]{1,0:T(8,128)(2,1)S(1)} %get-tuple-element.20), channel_id=1, source_target_pairs={{0,1},{1,0},{2,3},{3,2},{4,5},{5,4},{6,7},{7,6},{8,9},{9,8},{10,11... | collective-permute-start | bytes 1572872 | tf_op jit(solution)/shard_map/ppermute | solution.py:25
  41.3 6.4 %collective-permute-start.15 = (bf16[256,256]{1,0:T(8,128)(2,1)S(1)}, bf16[256,256]{1,0:T(8,128)(2,1)S(1)}, u32[]{:S(2)}, u32[]{:S(2)}) collective-permute-start(bf16[256,256]{1,0:T(8,128)(2,1)S(1)} %constant_dynamic-update-slice_fusion.2), channel_id=1, source_target_pairs={{0,8},{8,0},{16,24},{24,16},{1,9},{9,1},{17,25},{25,17},{2,10},{10... | collective-permute-start | bytes 393224 | tf_op jit(solution)/shard_map/ppermute | solution.py:25
  42.5 6.6 %collective-permute-start.16 = (bf16[256,256]{1,0:T(8,128)(2,1)S(1)}, bf16[256,256]{1,0:T(8,128)(2,1)S(1)}, u32[]{:S(2)}, u32[]{:S(2)}) collective-permute-start(bf16[256,256]{1,0:T(8,128)(2,1)S(1)} %constant_dynamic-update-slice_fusion.2), channel_id=1, source_target_pairs={{0,16},{8,24},{16,0},{24,8},{1,17},{9,25},{17,1},{25,9},{2,18},{10... | collective-permute-start | bytes 393224 | tf_op jit(solution)/shard_map/ppermute | solution.py:25
  43.5 8.7 %collective-permute-start.17 = (bf16[256,256]{1,0:T(8,128)(2,1)S(1)}, bf16[256,256]{1,0:T(8,128)(2,1)S(1)}, u32[]{:S(2)}, u32[]{:S(2)}) collective-permute-start(bf16[256,256]{1,0:T(8,128)(2,1)S(1)} %constant_dynamic-update-slice_fusion.2), channel_id=1, source_target_pairs={{0,24},{8,16},{16,8},{24,0},{1,25},{9,17},{17,9},{25,1},{2,26},{10... | collective-permute-start | bytes 393224 | tf_op jit(solution)/shard_map/ppermute | solution.py:25
  44.9 7.6 %collective-permute-start.12 = (bf16[256,256]{1,0:T(8,128)(2,1)S(1)}, bf16[256,256]{1,0:T(8,128)(2,1)S(1)}, u32[]{:S(2)}, u32[]{:S(2)}) collective-permute-start(bf16[256,256]{1,0:T(8,128)(2,1)S(1)} %constant_dynamic-update-slice_fusion), channel_id=1, source_target_pairs={{0,8},{8,0},{16,24},{24,16},{1,9},{9,1},{17,25},{25,17},{2,10},{10... | collective-permute-start | bytes 393224 | tf_op jit(solution)/shard_map/ppermute | solution.py:25
  47.8 5.1 %collective-permute-start.13 = (bf16[256,256]{1,0:T(8,128)(2,1)S(1)}, bf16[256,256]{1,0:T(8,128)(2,1)S(1)}, u32[]{:S(2)}, u32[]{:S(2)}) collective-permute-start(bf16[256,256]{1,0:T(8,128)(2,1)S(1)} %constant_dynamic-update-slice_fusion), channel_id=1, source_target_pairs={{0,16},{8,24},{16,0},{24,8},{1,17},{9,25},{17,1},{25,9},{2,18},{10... | collective-permute-start | bytes 393224 | tf_op jit(solution)/shard_map/ppermute | solution.py:25
  49.1 5.9 %collective-permute-start.14 = (bf16[256,256]{1,0:T(8,128)(2,1)S(1)}, bf16[256,256]{1,0:T(8,128)(2,1)S(1)}, u32[]{:S(2)}, u32[]{:S(2)}) collective-permute-start(bf16[256,256]{1,0:T(8,128)(2,1)S(1)} %constant_dynamic-update-slice_fusion), channel_id=1, source_target_pairs={{0,24},{8,16},{16,8},{24,0},{1,25},{9,17},{17,9},{25,1},{2,26},{10... | collective-permute-start | bytes 393224 | tf_op jit(solution)/shard_map/ppermute | solution.py:25
  52.2 4.1 %collective-permute-start.6 = (bf16[128,2048]{1,0:T(8,128)(2,1)}, bf16[128,2048]{1,0:T(8,128)(2,1)S(1)}, u32[]{:S(2)}, u32[]{:S(2)}) collective-permute-start(bf16[128,2048]{1,0:T(8,128)(2,1)} %collective-permute-done.2), channel_id=1, source_target_pairs={{0,1},{1,0},{2,3},{3,2},{4,5},{5,4},{6,7},{7,6},{8,9},{9,8},{10,11... | collective-permute-start | bytes 1572872 | tf_op jit(solution)/shard_map/ppermute | solution.py:25
  52.5 4.8 %collective-permute-start.7 = (bf16[128,2048]{1,0:T(8,128)(2,1)}, bf16[128,2048]{1,0:T(8,128)(2,1)S(1)}, u32[]{:S(2)}, u32[]{:S(2)}) collective-permute-start(bf16[128,2048]{1,0:T(8,128)(2,1)} %collective-permute-done.3), channel_id=1, source_target_pairs={{0,1},{1,0},{2,3},{3,2},{4,5},{5,4},{6,7},{7,6},{8,9},{9,8},{10,11... | collective-permute-start | bytes 1572872 | tf_op jit(solution)/shard_map/ppermute | solution.py:25
  52.9 4.6 %collective-permute-start.8 = (bf16[128,2048]{1,0:T(8,128)(2,1)S(1)}, bf16[128,2048]{1,0:T(8,128)(2,1)S(1)}, u32[]{:S(2)}, u32[]{:S(2)}) collective-permute-start(bf16[128,2048]{1,0:T(8,128)(2,1)S(1)} %collective-permute-done.4), channel_id=1, source_target_pairs={{0,1},{1,0},{2,3},{3,2},{4,5},{5,4},{6,7},{7,6},{8,9},{9,8},{10,11... | collective-permute-start | bytes 1572872 | tf_op jit(solution)/shard_map/ppermute | solution.py:25
  59.8 29.7 %collective-permute-start.18 = (bf16[1024,256]{1,0:T(8,128)(2,1)S(1)}, bf16[1024,256]{1,0:T(8,128)(2,1)S(1)}, u32[]{:S(2)}, u32[]{:S(2)}) collective-permute-start(bf16[1024,256]{1,0:T(8,128)(2,1)S(1)} %convolution_convert_fusion), channel_id=1, source_target_pairs={{0,2},{1,3},{2,0},{3,1},{4,6},{5,7},{6,4},{7,5},{8,10},{9,11},{10,... | collective-permute-start | bytes 1572872 | tf_op jit(solution)/shard_map/ppermute | solution.py:25
  62.6 29.8 %collective-permute-start.20 = (bf16[1024,128]{1,0:T(8,128)(2,1)S(1)}, bf16[1024,128]{1,0:T(8,128)(2,1)S(1)}, u32[]{:S(2)}, u32[]{:S(2)}) collective-permute-start(bf16[1024,128]{1,0:T(8,128)(2,1)S(1)} %convolution_convert_fusion.3), channel_id=1, source_target_pairs={{0,2},{1,3},{2,0},{3,1},{4,6},{5,7},{6,4},{7,5},{8,10},{9,11},{10,... | collective-permute-start | bytes 786440 | tf_op jit(solution)/shard_map/ppermute | solution.py:25
  62.7 29.7 %collective-permute-start.21 = (bf16[1024,128]{1,0:T(8,128)(2,1)S(1)}, bf16[1024,128]{1,0:T(8,128)(2,1)S(1)}, u32[]{:S(2)}, u32[]{:S(2)}) collective-permute-start(bf16[1024,128]{1,0:T(8,128)(2,1)S(1)} %convolution_convert_fusion.2), channel_id=1, source_target_pairs={{0,6},{1,7},{2,4},{3,5},{4,2},{5,3},{6,0},{7,1},{8,14},{9,15},{10,... | collective-permute-start | bytes 786440 | tf_op jit(solution)/shard_map/ppermute | solution.py:25
  67.0 25.4 %collective-permute-start.22 = (bf16[1024,128]{1,0:T(8,128)(2,1)S(1)}, bf16[1024,128]{1,0:T(8,128)(2,1)S(1)}, u32[]{:S(2)}, u32[]{:S(2)}) collective-permute-start(bf16[1024,128]{1,0:T(8,128)(2,1)S(1)} %convolution_convert_fusion.1), channel_id=1, source_target_pairs={{0,4},{1,5},{2,6},{3,7},{4,0},{5,1},{6,2},{7,3},{8,12},{9,13},{10,... | collective-permute-start | bytes 786440 | tf_op jit(solution)/shard_map/ppermute | solution.py:25
  89.6 11.1 %collective-permute-start.19 = (bf16[1024,128]{1,0:T(8,128)(2,1)S(1)}, bf16[1024,128]{1,0:T(8,128)(2,1)S(1)}, u32[]{:S(2)}, u32[]{:S(2)}) collective-permute-start(bf16[1024,128]{1,0:T(8,128)(2,1)S(1)} %fusion), channel_id=1, source_target_pairs={{0,4},{1,5},{2,6},{3,7},{4,0},{5,1},{6,2},{7,3},{8,12},{9,13},{10,... | collective-permute-start | bytes 786440 | tf_op jit(solution)/shard_map/ppermute | solution.py:25
  93.2 7.6 %copy-start.3 = (s32[2048,128]{1,0:T(8,128)S(1)}, s32[2048,128]{1,0:T(8,128)}, u32[]{:S(2)}) copy-start(s32[2048,128]{1,0:T(8,128)} %param.10) | copy-start | bytes 3145732

commit v4 on v3

--- a/solution.py
+++ b/solution.py
@@ -122,6 +122,60 @@
     )(own, other, queries, out_grad)
 
 
+def spread_kernel(plan, source_ref, *refs):
+    out_refs, sems = refs[:-1], refs[-1]
+    wide = out_refs[0].shape[1]
+    place = lax.axis_index("dp")
+    copies = []
+    for index, (out, first, step, low, high) in enumerate(plan):
+        start = pl.multiple_of((place ^ step) * wide, wide)
+        copy = pltpu.make_async_copy(
+            source_ref.at[low:high, pl.ds(start, wide)],
+            out_refs[out].at[first : first + high - low],
+            sems.at[index],
+        )
+        copy.start()
+        copies.append(copy)
+    for copy in copies:
+        copy.wait()
+
+
+def spread(source, wide, plan):
+    heights = {}
+    for out, first, _, low, high in plan:
+        heights[out] = max(heights.get(out, 0), first + high - low)
+    anywhere = pl.BlockSpec(memory_space=pl.ANY)
+    return pl.pallas_call(
+        functools.partial(spread_kernel, plan),
+        in_specs=[anywhere],
+        out_specs=[anywhere] * len(heights),
+        out_shape=[
+            jax.ShapeDtypeStruct((heights[out], wide), source.dtype) for out in sorted(heights)
+        ],
+        scratch_shapes=[pltpu.SemaphoreType.DMA((len(plan),))],
+        cost_estimate=cost(0, 2 * source.nbytes),
+        name="spread",
+    )(source)
+
+
+def exchange_rows(inputs, wide):
+    rows = inputs.shape[0]
+    groups = lax.axis_size("dp")
+    if groups != 4:
+        parts = spread(inputs, wide, [(s, 0, s, 0, rows) for s in range(groups)])
+        return [part if s == 0 else swap(part, "dp", s) for s, part in enumerate(parts)]
+    half = rows // 2
+    own, left, right = spread(
+        inputs,
+        wide,
+        [(0, 0, 0, 0, rows), (1, 0, 1, 0, rows), (1, rows, 3, 0, half), (2, 0, 2, 0, rows),
+         (2, rows, 3, half, rows)],
+    )
+    left, right = swap(left, "dp", 1), swap(right, "dp", 2)
+    upper, lower = swap(left[rows:], "dp", 2), swap(right[rows:], "dp", 1)
+    return [own, left[:rows], right[:rows], jnp.concatenate([upper, lower], 0)]
+
+
 def kv_kernel(rows, mine_ref, arrived_ref, mask_ref, *out_refs):
     place = lax.axis_index("tensor")
     chip, core = place // 2, place % 2
@@ -152,56 +206,53 @@
     groups = lax.axis_size("dp")
     chips = lax.axis_size("tensor") // 2
     block = weight_mask.shape[0]
-    row_place = lax.axis_index("dp")
 
     other = swap(keys_values, "tensor", 1)
-    parts = []
-    for step in range(groups):
-        start = (row_place ^ step) * block
-        part = lax.dynamic_slice(inputs, (0, start), (rows, block))
-        parts.append(part if step == 0 else swap(part, "dp", step))
-
+    parts = exchange_rows(inputs, block)
     query_grad, mine, theirs = attention(keys_values, other, queries, out_grad)
     arrived = swap(theirs, "tensor", 1)
-    arrived, *parts = lax.optimization_barrier((arrived, *parts))
-    pieces = [piece for part in parts for piece in (part, swap(part, "tensor", 1))]
     blocks = kv_blocks(mine, arrived, clip_mask, rows)
 
     blocks = [b if s == 0 else swap(b, "tensor", 2 * s) for s, b in enumerate(blocks)]
-    blocks = lax.optimization_barrier(blocks)
+    blocks, parts = lax.optimization_barrier((blocks, parts))
     order = sorted(range(chips), key=lambda s: [(s >> b) & 1 for b in range(8)])
     evens, odds = order[: chips // 2], order[chips // 2 :]
 
-    def gather(steps):
-        stacked = jnp.concatenate([blocks[s] for s in steps], 1)
-        parts = [stacked if s == 0 else swap(stacked, "dp", s) for s in range(groups)]
-        return jnp.concatenate(parts, 0)
-
-    grads_odd = gather(odds)
-    grads_even = gather(evens)
+    def gather(stacked):
+        found = [stacked if s == 0 else swap(stacked, "dp", s) for s in range(groups)]
+        return [jnp.concatenate([f[h * rows : (h + 1) * rows] for f in found], 0) for h in (0, 1)]
 
     wide = block // 2
-    near = jnp.concatenate([p[:, :wide] for p in pieces], 0)
-    far = jnp.concatenate([p[:, wide:] for p in pieces], 0)
-
-    def column(step):
-        group = evens if step in evens else odds
-        place = group.index(step) * depth
-        return (grads_even if step in evens else grads_odd)[:, place : place + depth]
-
-    sent = swap(dot(near, grads_odd, 0, 0).astype(BF16), "tensor", 2)
-    straight = [
-        swap(dot(far, column(step), 0, 0).astype(BF16), "tensor", 2 * step)
-        for step in odds + evens[1:]
-    ]
-    terms = [dot(near, grads_even, 0, 0), sent]
-    columns, bit = chips // 2 * depth, 2
+    cuts = []
+    for cut in range(2):
+        own = jnp.concatenate([p[:, cut * wide : (cut + 1) * wide] for p in parts], 0)
+        cuts.append((own, swap(own, "tensor", 1)))
+    near, far = cuts
+
+    def product(pair, grads, place=None):
+        if place is not None:
+            grads = [g[:, place * depth : (place + 1) * depth] for g in grads]
+        return dot(pair[0], grads[0], 0, 0) + dot(pair[1], grads[1], 0, 0)
+
+    def send(value, step):
+        return swap(value.astype(BF16), "tensor", 2 * step)
+
+    grads = gather(jnp.concatenate([blocks[s] for s in order], 1))
+    half = chips // 2 * depth
+    even, odd = [g[:, :half] for g in grads], [g[:, half:] for g in grads]
+    sent = send(product(near, odd), 1)
+    late = {s: product(far, odd, odds.index(s)).astype(BF16) for s in odds}
+    late.update({s: product(far, even, evens.index(s)).astype(BF16) for s in evens[1:]})
+    straight = [send(late[s], s) for s in range(2, chips)]
+    nearest, straight = lax.optimization_barrier((late[1], straight))
+    terms = [product(near, even), sent]
+    columns, bit = chips // 2 * depth, 1
     while columns > depth:
         columns, bit = columns // 2, bit * 2
-        away = sum(t[:, columns : 2 * columns].astype(F32) for t in terms).astype(BF16)
-        terms.append(swap(away, "tensor", bit))
+        terms.append(send(sum(t[:, columns : 2 * columns].astype(F32) for t in terms), bit))
+    straight.append(send(nearest, 1))
     upper = sum(t[:, :depth].astype(F32) for t in terms)
-    lower = dot(far, column(0), 0, 0) + sum(t.astype(F32) for t in straight)
+    lower = product(far, even, 0) + sum(t.astype(F32) for t in straight)
     summed = jnp.concatenate([upper, lower], 0)
     weight_grad = jnp.where(weight_mask == 1, summed, 0.0)
     return (query_grad, weight_grad)

time: 104 us -> 159 us (1.53); the launches traced: 102 us -> 159 us
  Pallas kernels: 17.1 us -> 81.8 us
  waiting for transfers between devices: 46.2 us -> 41.6 us
  local copies, waits for them, and re-layouts: 5.52 us -> 2.86 us
    pallas_call x0 -> x1, Pallas kernels: none -> 64.7 us  [spread(): pl.pallas_call(functools.partial(spread_kernel, plan), in_specs=[anywhere...]
    ppermute x23 -> x19, waiting for transfers between devices: 46.2 us -> 41.6 us  [swap(): return lax.ppermute(value, axis, pairs)]
    dynamic_slice x1 -> x0, local copies, waits for them, and re-layouts: 2.86 us -> none  [per_device(): part = lax.dynamic_slice(inputs, (0, start), (rows, block))]
    ppermute x23 -> x19, starting transfers between devices: 26.3 us -> 24.9 us  [swap(): return lax.ppermute(value, axis, pairs)]
    dot_general x6 -> x12, matrix products: 4.52 us -> 5.78 us  [dot(): return lax.dot_general(left, right, dims, preferred_element_type=F32)]
  transfers between devices with their start and end apart: 23 -> 19, of which waited for: 10 -> 10; matrix products, arithmetic and copies ran while one was open for 8% -> 4% of each run, Pallas kernels for 17% -> 51%
where the time goes in v4:
time: 159 us
  Pallas kernels  81.8 us (51%)
  waiting for transfers between devices  41.6 us (26%)
  starting transfers between devices  24.9 us (16%)
  matrix products  5.78 us (4%)
  local copies, waits for them, and re-layouts  2.86 us (2%)
    pallas_call x1, Pallas kernels, spread(): pl.pallas_call(functools.partial(spread_kernel, plan), in_specs=[anywhere...  64.7 us
    ppermute x19, waiting for transfers between devices, swap(): return lax.ppermute(value, axis, pairs)  41.6 us
    ppermute x19, starting transfers between devices, swap(): return lax.ppermute(value, axis, pairs)  24.9 us
    pallas_call x1, Pallas kernels, attention(): pl.pallas_call(functools.partial(attention_kernel, height), grid=(width /...  16.9 us
    dot_general x12, matrix products, dot(): return lax.dot_general(left, right, dims, preferred_element_type=F32)  5.78 us
  transfers between devices with their start and end apart: 19, of which 10 were waited for; matrix products, arithmetic and copies ran while one was open for 4% of the time, Pallas kernels for 51%

profile of v4, /device:TPU:0, one launch (start us, length us, event | category | flops | bytes accessed | tf_op | source)
XLA Modules:
  0.0 159.3 jit_solution(2965205638001171310)
XLA Ops:
  0.6 0.5 collective-permute-start
  1.2 64.7 %spread.1 = (bf16[128,2048]{1,0:T(8,128)(2,1)}, bf16[192,2048]{1,0:T(8,128)(2,1)}, bf16[192,2048]{1,0:T(8,128)(2,1)}) custom-call(bf16[128,8192]{1,0:T(8,128)(2,1)} %source_ref.1), custom_call_target="tpu_custom_call" | custom-call | bytes 4194304 | tf_op jit(solution)/shard_map/spread/pallas_call | solution.py:148
  65.8 2.6 %collective-permute-start.5 = (bf16[192,2048]{1,0:T(8,128)(2,1)}, bf16[192,2048]{1,0:T(8,128)(2,1)S(1)}, u32[]{:S(2)}, u32[]{:S(2)}) collective-permute-start(bf16[192,2048]{1,0:T(8,128)(2,1)} %get-tuple-element.31), channel_id=1, source_target_pairs={{0,8},{8,0},{16,24},{24,16},{1,9},{9,1},{17,25},{25,17},{2,10},{10... | collective-permute-start | bytes 2359304 | tf_op jit(solution)/shard_map/ppermute | solution.py:25
  68.4 1.5 collective-permute-start.6
  70.0 1.4 copy-done.1
  71.4 16.9 %attention.1 = (bf16[1024,768]{1,0:T(8,128)(2,1)}, f32[1024,128]{1,0:T(8,128)S(1)}, f32[1024,128]{1,0:T(8,128)S(1)}) custom-call(bf16[1024,128]{1,0:T(8,128)(2,1)S(1)} %copy-done.2, bf16[1024,128]{1,0:T(8,128)(2,1)S(1)} %collective-permute-done.other_ref, bf16[1024,768]{1,0:T(8,128)(2,1)S(1)} %copy-done, bf16[1024,768]{1,0:T(8,128)(2,1)S(1)} %copy-done.1), custom_call_target="tpu_custom_call" | custom-call | flops 16106127360 | bytes 9437184 | tf_op jit(solution)/shard_map/attention/pallas_call | solution.py:103
  88.3 0.6 collective-permute-start.8
  88.9 0.3 copy-done.4
  89.2 0.6 copy-done.3
  89.8 1.5 collective-permute-start.7
  91.3 0.2 copy.8.mask_ref
  91.6 0.2 kv_blocks.1
  91.8 1.6 %collective-permute-start.2 = (bf16[256,128]{1,0:T(8,128)(2,1)S(1)}, bf16[256,128]{1,0:T(8,128)(2,1)S(1)}, u32[]{:S(2)}, u32[]{:S(2)}) collective-permute-start(bf16[256,128]{1,0:T(8,128)(2,1)S(1)} %get-tuple-element.27), channel_id=1, source_target_pairs={{0,2},{1,3},{2,0},{3,1},{4,6},{5,7},{6,4},{7,5},{8,10},{9,11},{10,... | collective-permute-start | bytes 196616 | tf_op jit(solution)/shard_map/ppermute | solution.py:25
  93.4 2.6 %collective-permute-start.3 = (bf16[256,128]{1,0:T(8,128)(2,1)S(1)}, bf16[256,128]{1,0:T(8,128)(2,1)S(1)}, u32[]{:S(2)}, u32[]{:S(2)}) collective-permute-start(bf16[256,128]{1,0:T(8,128)(2,1)S(1)} %get-tuple-element.28), channel_id=1, source_target_pairs={{0,4},{1,5},{2,6},{3,7},{4,0},{5,1},{6,2},{7,3},{8,12},{9,13},{10,... | collective-permute-start | bytes 196616 | tf_op jit(solution)/shard_map/ppermute | solution.py:25
  96.0 0.2 collective-permute-start.4
  96.2 0.8 collective-permute-done.8
  97.1 1.1 collective-permute-done.7
  98.2 1.8 %collective-permute-done.3 = bf16[256,128]{1,0:T(8,128)(2,1)S(1)} collective-permute-done((bf16[256,128]{1,0:T(8,128)(2,1)S(1)}, bf16[256,128]{1,0:T(8,128)(2,1)S(1)}, u32[]{:S(2)}, u32[]{:S(2)}) %collective-permute-start.3) | collective-permute-done | bytes 65568 | tf_op jit(solution)/shard_map/ppermute | solution.py:25
  100.0 2.1 %collective-permute-done.4 = bf16[256,128]{1,0:T(8,128)(2,1)S(1)} collective-permute-done((bf16[256,128]{1,0:T(8,128)(2,1)S(1)}, bf16[256,128]{1,0:T(8,128)(2,1)S(1)}, u32[]{:S(2)}, u32[]{:S(2)}) %collective-permute-start.4) | collective-permute-done | bytes 65568 | tf_op jit(solution)/shard_map/ppermute | solution.py:25
  102.2 1.6 %collective-permute-start.11 = (bf16[256,512]{1,0:T(8,128)(2,1)S(1)}, bf16[256,512]{1,0:T(8,128)(2,1)S(1)}, u32[]{:S(2)}, u32[]{:S(2)}) collective-permute-start(bf16[256,512]{1,0:T(8,128)(2,1)S(1)} %constant_dynamic-update-slice_fusion), channel_id=1, source_target_pairs={{0,24},{8,16},{16,8},{24,0},{1,25},{9,17},{17,9},{25,1},{2,26},{10... | collective-permute-start | bytes 786440 | tf_op jit(solution)/shard_map/ppermute | solution.py:25
  103.8 1.4 collective-permute-start.10
  105.2 0.5 collective-permute-start.9
  105.8 0.1 fusion.25
  106.2 0.6 collective-permute-start.12
  106.8 4.9 %collective-permute-done.11 = bf16[256,512]{1,0:T(8,128)(2,1)S(1)} collective-permute-done((bf16[256,512]{1,0:T(8,128)(2,1)S(1)}, bf16[256,512]{1,0:T(8,128)(2,1)S(1)}, u32[]{:S(2)}, u32[]{:S(2)}) %collective-permute-start.11) | collective-permute-done | bytes 262176 | tf_op jit(solution)/shard_map/ppermute | solution.py:25
  111.7 2.7 %collective-permute-done.10 = bf16[256,512]{1,0:T(8,128)(2,1)S(1)} collective-permute-done((bf16[256,512]{1,0:T(8,128)(2,1)S(1)}, bf16[256,512]{1,0:T(8,128)(2,1)S(1)}, u32[]{:S(2)}, u32[]{:S(2)}) %collective-permute-start.10) | collective-permute-done | bytes 262176 | tf_op jit(solution)/shard_map/ppermute | solution.py:25
  114.5 0.5 fusion.16
  115.0 0.5 fusion.3
  115.5 2.1 %collective-permute-start.16 = (bf16[1024,128]{1,0:T(8,128)(2,1)S(1)}, bf16[1024,128]{1,0:T(8,128)(2,1)S(1)}, u32[]{:S(2)}, u32[]{:S(2)}) collective-permute-start(bf16[1024,128]{1,0:T(8,128)(2,1)S(1)} %fusion.3), channel_id=1, source_target_pairs={{0,4},{1,5},{2,6},{3,7},{4,0},{5,1},{6,2},{7,3},{8,12},{9,13},{10,... | collective-permute-start | bytes 786440 | tf_op jit(solution)/shard_map/ppermute | solution.py:25
  117.5 0.5 fusion.13
  118.0 0.5 fusion.4
  118.5 1.2 collective-permute-start.17
  119.7 0.5 fusion.10
  120.2 0.5 convolution_add_fusion.1
  120.7 0.5 fusion.7
  121.2 0.5 fusion
  121.7 0.4 collective-permute-start.13
  122.1 0.5 fusion.19
  122.6 0.5 fusion.2
  123.1 12.4 %collective-permute-done.16 = bf16[1024,128]{1,0:T(8,128)(2,1)S(1)} collective-permute-done((bf16[1024,128]{1,0:T(8,128)(2,1)S(1)}, bf16[1024,128]{1,0:T(8,128)(2,1)S(1)}, u32[]{:S(2)}, u32[]{:S(2)}) %collective-permute-start.16) | collective-permute-done | bytes 262176 | tf_op jit(solution)/shard_map/ppermute | solution.py:25
  135.5 5.5 %collective-permute-start.18 = (bf16[1024,128]{1,0:T(8,128)(2,1)S(1)}, bf16[1024,128]{1,0:T(8,128)(2,1)S(1)}, u32[]{:S(2)}, u32[]{:S(2)}) collective-permute-start(bf16[1024,128]{1,0:T(8,128)(2,1)S(1)} %fusion.2), channel_id=1, source_target_pairs={{0,2},{1,3},{2,0},{3,1},{4,6},{5,7},{6,4},{7,5},{8,10},{9,11},{10,... | collective-permute-start | bytes 786440 | tf_op jit(solution)/shard_map/ppermute | solution.py:25
  141.0 0.5 fusion.22
  141.5 4.3 %collective-permute-done.13 = bf16[1024,256]{1,0:T(8,128)(2,1)S(1)} collective-permute-done((bf16[1024,256]{1,0:T(8,128)(2,1)S(1)}, bf16[1024,256]{1,0:T(8,128)(2,1)S(1)}, u32[]{:S(2)}, u32[]{:S(2)}) %collective-permute-start.13) | collective-permute-done | bytes 524320 | tf_op jit(solution)/shard_map/ppermute | solution.py:25
  145.9 0.4 collective-permute-start.14
  146.2 5.5 %collective-permute-done.18 = bf16[1024,128]{1,0:T(8,128)(2,1)S(1)} collective-permute-done((bf16[1024,128]{1,0:T(8,128)(2,1)S(1)}, bf16[1024,128]{1,0:T(8,128)(2,1)S(1)}, u32[]{:S(2)}, u32[]{:S(2)}) %collective-permute-start.18) | collective-permute-done | bytes 262176 | tf_op jit(solution)/shard_map/ppermute | solution.py:25
  151.7 0.5 fusion.1
  152.2 5.9 %collective-permute-done.14 = bf16[1024,128]{1,0:T(8,128)(2,1)S(1)} collective-permute-done((bf16[1024,128]{1,0:T(8,128)(2,1)S(1)}, bf16[1024,128]{1,0:T(8,128)(2,1)S(1)}, u32[]{:S(2)}, u32[]{:S(2)}) %collective-permute-start.14) | collective-permute-done | bytes 262176 | tf_op jit(solution)/shard_map/ppermute | solution.py:25
  158.2 1.1 maximum_select_fusion
  (45 shorter events, 0.8 us)
Async XLA Ops:
  0.6 69.3 %copy-start.2 = (bf16[1024,128]{1,0:T(8,128)(2,1)S(1)}, bf16[1024,128]{1,0:T(8,128)(2,1)}, u32[]{:S(2)}) copy-start(bf16[1024,128]{1,0:T(8,128)(2,1)} %own_ref.1) | copy-start | bytes 786436
  0.6 69.3 %copy-start = (bf16[1024,768]{1,0:T(8,128)(2,1)S(1)}, bf16[1024,768]{1,0:T(8,128)(2,1)}, u32[]{:S(2)}) copy-start(bf16[1024,768]{1,0:T(8,128)(2,1)} %q_ref.1) | copy-start | bytes 4718596
  0.6 69.3 %collective-permute-start = (bf16[1024,128]{1,0:T(8,128)(2,1)}, bf16[1024,128]{1,0:T(8,128)(2,1)S(1)}, u32[]{:S(2)}, u32[]{:S(2)}) collective-permute-start(bf16[1024,128]{1,0:T(8,128)(2,1)} %own_ref.1), channel_id=1, source_target_pairs={{0,1},{1,0},{2,3},{3,2},{4,5},{5,4},{6,7},{7,6},{8,9},{9,8},{10,11... | collective-permute-start | bytes 786440 | tf_op jit(solution)/shard_map/ppermute | solution.py:25
  65.8 23.0 %collective-permute-start.5 = (bf16[192,2048]{1,0:T(8,128)(2,1)}, bf16[192,2048]{1,0:T(8,128)(2,1)S(1)}, u32[]{:S(2)}, u32[]{:S(2)}) collective-permute-start(bf16[192,2048]{1,0:T(8,128)(2,1)} %get-tuple-element.31), channel_id=1, source_target_pairs={{0,8},{8,0},{16,24},{24,16},{1,9},{9,1},{17,25},{25,17},{2,10},{10... | collective-permute-start | bytes 2359304 | tf_op jit(solution)/shard_map/ppermute | solution.py:25
  68.4 19.9 %collective-permute-start.6 = (bf16[192,2048]{1,0:T(8,128)(2,1)}, bf16[192,2048]{1,0:T(8,128)(2,1)S(1)}, u32[]{:S(2)}, u32[]{:S(2)}) collective-permute-start(bf16[192,2048]{1,0:T(8,128)(2,1)} %get-tuple-element.32), channel_id=1, source_target_pairs={{0,16},{8,24},{16,0},{24,8},{1,17},{9,25},{17,1},{25,9},{2,18},{10... | collective-permute-start | bytes 2359304 | tf_op jit(solution)/shard_map/ppermute | solution.py:25
  70.0 1.4 copy-start.1
  71.4 19.9 %copy-start.7 = (s32[1024,1]{0,1:T(1,128)S(1)}, s32[1024,1]{0,1:T(1,128)}, u32[]{:S(2)}) copy-start(s32[1024,1]{0,1:T(1,128)} %param.11) | copy-start | bytes 12292
  88.2 3.3 %collective-permute-start.1 = (f32[1024,128]{1,0:T(8,128)S(1)}, f32[1024,128]{1,0:T(8,128)S(1)}, u32[]{:S(2)}, u32[]{:S(2)}) collective-permute-start(f32[1024,128]{1,0:T(8,128)S(1)} %get-tuple-element.25), channel_id=1, source_target_pairs={{0,1},{1,0},{2,3},{3,2},{4,5},{5,4},{6,7},{7,6},{8,9},{9,8},{10,11... | collective-permute-start | bytes 1572872 | tf_op jit(solution)/shard_map/ppermute | solution.py:25
  88.3 0.9 copy-start.4
  88.3 8.7 %collective-permute-start.8 = (bf16[64,2048]{1,0:T(8,128)(2,1)S(1)}, bf16[64,2048]{1,0:T(8,128)(2,1)S(1)}, u32[]{:S(2)}, u32[]{:S(2)}) collective-permute-start(bf16[64,2048]{1,0:T(8,128)(2,1)S(1)} %slice.155), channel_id=1, source_target_pairs={{0,8},{8,0},{16,24},{24,16},{1,9},{9,1},{17,25},{25,17},{2,10},{10... | collective-permute-start | bytes 786440 | tf_op jit(solution)/shard_map/ppermute | solution.py:25
  88.9 0.9 copy-start.3
  89.8 8.4 %collective-permute-start.7 = (bf16[64,2048]{1,0:T(8,128)(2,1)S(1)}, bf16[64,2048]{1,0:T(8,128)(2,1)S(1)}, u32[]{:S(2)}, u32[]{:S(2)}) collective-permute-start(bf16[64,2048]{1,0:T(8,128)(2,1)S(1)} %slice.154), channel_id=1, source_target_pairs={{0,16},{8,24},{16,0},{24,8},{1,17},{9,25},{17,1},{25,9},{2,18},{10... | collective-permute-start | bytes 786440 | tf_op jit(solution)/shard_map/ppermute | solution.py:25
  91.8 14.0 %slice-start.1 = ((bf16[192,2048]{1,0:T(8,128)(2,1)}), bf16[128,2048]{1,0:T(8,128)(2,1)S(1)}, s32[]{:S(2)}) async-start(bf16[192,2048]{1,0:T(8,128)(2,1)} %copy-done.4), calls=%async_computation.1 | async-start | bytes 1048576 | tf_op jit(solution)/shard_map/slice | solution.py:176
  91.8 6.5 %collective-permute-start.2 = (bf16[256,128]{1,0:T(8,128)(2,1)S(1)}, bf16[256,128]{1,0:T(8,128)(2,1)S(1)}, u32[]{:S(2)}, u32[]{:S(2)}) collective-permute-start(bf16[256,128]{1,0:T(8,128)(2,1)S(1)} %get-tuple-element.27), channel_id=1, source_target_pairs={{0,2},{1,3},{2,0},{3,1},{4,6},{5,7},{6,4},{7,5},{8,10},{9,11},{10,... | collective-permute-start | bytes 196616 | tf_op jit(solution)/shard_map/ppermute | solution.py:25
  93.4 6.6 %collective-permute-start.3 = (bf16[256,128]{1,0:T(8,128)(2,1)S(1)}, bf16[256,128]{1,0:T(8,128)(2,1)S(1)}, u32[]{:S(2)}, u32[]{:S(2)}) collective-permute-start(bf16[256,128]{1,0:T(8,128)(2,1)S(1)} %get-tuple-element.28), channel_id=1, source_target_pairs={{0,4},{1,5},{2,6},{3,7},{4,0},{5,1},{6,2},{7,3},{8,12},{9,13},{10,... | collective-permute-start | bytes 196616 | tf_op jit(solution)/shard_map/ppermute | solution.py:25
  96.0 6.1 %collective-permute-start.4 = (bf16[256,128]{1,0:T(8,128)(2,1)S(1)}, bf16[256,128]{1,0:T(8,128)(2,1)S(1)}, u32[]{:S(2)}, u32[]{:S(2)}) collective-permute-start(bf16[256,128]{1,0:T(8,128)(2,1)S(1)} %get-tuple-element.29), channel_id=1, source_target_pairs={{0,6},{1,7},{2,4},{3,5},{4,2},{5,3},{6,0},{7,1},{8,14},{9,15},{10,... | collective-permute-start | bytes 196616 | tf_op jit(solution)/shard_map/ppermute | solution.py:25
  96.2 9.6 %slice-start = ((bf16[192,2048]{1,0:T(8,128)(2,1)}), bf16[128,2048]{1,0:T(8,128)(2,1)S(1)}, s32[]{:S(2)}) async-start(bf16[192,2048]{1,0:T(8,128)(2,1)} %copy-done.3), calls=%async_computation | async-start | bytes 1048576 | tf_op jit(solution)/shard_map/slice | solution.py:176
  96.2 9.6 %copy-start.6 = (bf16[128,2048]{1,0:T(8,128)(2,1)S(1)}, bf16[128,2048]{1,0:T(8,128)(2,1)}, u32[]{:S(2)}) copy-start(bf16[128,2048]{1,0:T(8,128)(2,1)} %get-tuple-element.33) | copy-start | bytes 1572868
  102.2 9.5 %collective-permute-start.11 = (bf16[256,512]{1,0:T(8,128)(2,1)S(1)}, bf16[256,512]{1,0:T(8,128)(2,1)S(1)}, u32[]{:S(2)}, u32[]{:S(2)}) collective-permute-start(bf16[256,512]{1,0:T(8,128)(2,1)S(1)} %constant_dynamic-update-slice_fusion), channel_id=1, source_target_pairs={{0,24},{8,16},{16,8},{24,0},{1,25},{9,17},{17,9},{25,1},{2,26},{10... | collective-permute-start | bytes 786440 | tf_op jit(solution)/shard_map/ppermute | solution.py:25
  103.8 10.6 %collective-permute-start.10 = (bf16[256,512]{1,0:T(8,128)(2,1)S(1)}, bf16[256,512]{1,0:T(8,128)(2,1)S(1)}, u32[]{:S(2)}, u32[]{:S(2)}) collective-permute-start(bf16[256,512]{1,0:T(8,128)(2,1)S(1)} %constant_dynamic-update-slice_fusion), channel_id=1, source_target_pairs={{0,16},{8,24},{16,0},{24,8},{1,17},{9,25},{17,1},{25,9},{2,18},{10... | collective-permute-start | bytes 786440 | tf_op jit(solution)/shard_map/ppermute | solution.py:25
  105.2 9.2 %collective-permute-start.9 = (bf16[256,512]{1,0:T(8,128)(2,1)S(1)}, bf16[256,512]{1,0:T(8,128)(2,1)S(1)}, u32[]{:S(2)}, u32[]{:S(2)}) collective-permute-start(bf16[256,512]{1,0:T(8,128)(2,1)S(1)} %constant_dynamic-update-slice_fusion), channel_id=1, source_target_pairs={{0,8},{8,0},{16,24},{24,16},{1,9},{9,1},{17,25},{25,17},{2,10},{10... | collective-permute-start | bytes 786440 | tf_op jit(solution)/shard_map/ppermute | solution.py:25
  106.0 8.5 %collective-permute-start.15 = (bf16[512,1024]{1,0:T(8,128)(2,1)S(1)}, bf16[512,1024]{1,0:T(8,128)(2,1)S(1)}, u32[]{:S(2)}, u32[]{:S(2)}) collective-permute-start(bf16[512,1024]{1,0:T(8,128)(2,1)S(1)} %pad_maximum_fusion.1), channel_id=1, source_target_pairs={{0,1},{1,0},{2,3},{3,2},{4,5},{5,4},{6,7},{7,6},{8,9},{9,8},{10,11... | collective-permute-start | bytes 3145736 | tf_op jit(solution)/shard_map/ppermute | solution.py:25
  106.2 13.5 %collective-permute-start.12 = (bf16[512,1024]{1,0:T(8,128)(2,1)S(1)}, bf16[512,1024]{1,0:T(8,128)(2,1)S(1)}, u32[]{:S(2)}, u32[]{:S(2)}) collective-permute-start(bf16[512,1024]{1,0:T(8,128)(2,1)S(1)} %pad_maximum_fusion), channel_id=1, source_target_pairs={{0,1},{1,0},{2,3},{3,2},{4,5},{5,4},{6,7},{7,6},{8,9},{9,8},{10,11... | collective-permute-start | bytes 3145736 | tf_op jit(solution)/shard_map/ppermute | solution.py:25
  115.5 20.0 %collective-permute-start.16 = (bf16[1024,128]{1,0:T(8,128)(2,1)S(1)}, bf16[1024,128]{1,0:T(8,128)(2,1)S(1)}, u32[]{:S(2)}, u32[]{:S(2)}) collective-permute-start(bf16[1024,128]{1,0:T(8,128)(2,1)S(1)} %fusion.3), channel_id=1, source_target_pairs={{0,4},{1,5},{2,6},{3,7},{4,0},{5,1},{6,2},{7,3},{8,12},{9,13},{10,... | collective-permute-start | bytes 786440 | tf_op jit(solution)/shard_map/ppermute | solution.py:25
  118.5 17.0 %collective-permute-start.17 = (bf16[1024,128]{1,0:T(8,128)(2,1)S(1)}, bf16[1024,128]{1,0:T(8,128)(2,1)S(1)}, u32[]{:S(2)}, u32[]{:S(2)}) collective-permute-start(bf16[1024,128]{1,0:T(8,128)(2,1)S(1)} %fusion.4), channel_id=1, source_target_pairs={{0,6},{1,7},{2,4},{3,5},{4,2},{5,3},{6,0},{7,1},{8,14},{9,15},{10,... | collective-permute-start | bytes 786440 | tf_op jit(solution)/shard_map/ppermute | solution.py:25
  121.7 24.1 %collective-permute-start.13 = (bf16[1024,256]{1,0:T(8,128)(2,1)S(1)}, bf16[1024,256]{1,0:T(8,128)(2,1)S(1)}, u32[]{:S(2)}, u32[]{:S(2)}) collective-permute-start(bf16[1024,256]{1,0:T(8,128)(2,1)S(1)} %fusion), channel_id=1, source_target_pairs={{0,2},{1,3},{2,0},{3,1},{4,6},{5,7},{6,4},{7,5},{8,10},{9,11},{10,... | collective-permute-start | bytes 1572872 | tf_op jit(solution)/shard_map/ppermute | solution.py:25
  135.5 16.2 %collective-permute-start.18 = (bf16[1024,128]{1,0:T(8,128)(2,1)S(1)}, bf16[1024,128]{1,0:T(8,128)(2,1)S(1)}, u32[]{:S(2)}, u32[]{:S(2)}) collective-permute-start(bf16[1024,128]{1,0:T(8,128)(2,1)S(1)} %fusion.2), channel_id=1, source_target_pairs={{0,2},{1,3},{2,0},{3,1},{4,6},{5,7},{6,4},{7,5},{8,10},{9,11},{10,... | collective-permute-start | bytes 786440 | tf_op jit(solution)/shard_map/ppermute | solution.py:25
  145.8 12.4 %copy-start.5 = (s32[2048,128]{1,0:T(8,128)S(1)}, s32[2048,128]{1,0:T(8,128)}, u32[]{:S(2)}) copy-start(s32[2048,128]{1,0:T(8,128)} %param.10) | copy-start | bytes 3145732
  145.9 12.3 %collective-permute-start.14 = (bf16[1024,128]{1,0:T(8,128)(2,1)S(1)}, bf16[1024,128]{1,0:T(8,128)(2,1)S(1)}, u32[]{:S(2)}, u32[]{:S(2)}) collective-permute-start(bf16[1024,128]{1,0:T(8,128)(2,1)S(1)} %fusion.5), channel_id=1, source_target_pairs={{0,4},{1,5},{2,6},{3,7},{4,0},{5,1},{6,2},{7,3},{8,12},{9,13},{10,... | collective-permute-start | bytes 786440 | tf_op jit(solution)/shard_map/ppermute | solution.py:25

commit v5 on v4

--- a/solution.py
+++ b/solution.py
@@ -122,37 +122,24 @@
     )(own, other, queries, out_grad)
 
 
-def spread_kernel(plan, source_ref, *refs):
-    out_refs, sems = refs[:-1], refs[-1]
+def spread_kernel(plan, source_ref, *out_refs):
     wide = out_refs[0].shape[1]
     place = lax.axis_index("dp")
-    copies = []
-    for index, (out, first, step, low, high) in enumerate(plan):
+    for out, first, step, low, high in plan:
         start = pl.multiple_of((place ^ step) * wide, wide)
-        copy = pltpu.make_async_copy(
-            source_ref.at[low:high, pl.ds(start, wide)],
-            out_refs[out].at[first : first + high - low],
-            sems.at[index],
-        )
-        copy.start()
-        copies.append(copy)
-    for copy in copies:
-        copy.wait()
+        out_refs[out][first : first + high - low] = source_ref[low:high, pl.ds(start, wide)]
 
 
 def spread(source, wide, plan):
     heights = {}
     for out, first, _, low, high in plan:
         heights[out] = max(heights.get(out, 0), first + high - low)
-    anywhere = pl.BlockSpec(memory_space=pl.ANY)
     return pl.pallas_call(
         functools.partial(spread_kernel, plan),
-        in_specs=[anywhere],
-        out_specs=[anywhere] * len(heights),
         out_shape=[
             jax.ShapeDtypeStruct((heights[out], wide), source.dtype) for out in sorted(heights)
         ],
-        scratch_shapes=[pltpu.SemaphoreType.DMA((len(plan),))],
+        compiler_params=pltpu.CompilerParams(vmem_limit_bytes=16 * 2**20),
         cost_estimate=cost(0, 2 * source.nbytes),
         name="spread",
     )(source)
@@ -244,12 +231,13 @@
     late = {s: product(far, odd, odds.index(s)).astype(BF16) for s in odds}
     late.update({s: product(far, even, evens.index(s)).astype(BF16) for s in evens[1:]})
     straight = [send(late[s], s) for s in range(2, chips)]
-    nearest, straight = lax.optimization_barrier((late[1], straight))
     terms = [product(near, even), sent]
-    columns, bit = chips // 2 * depth, 1
+    columns, bit = half, 1
     while columns > depth:
         columns, bit = columns // 2, bit * 2
-        terms.append(send(sum(t[:, columns : 2 * columns].astype(F32) for t in terms), bit))
+        away = sum(t[:, columns : 2 * columns].astype(F32) for t in terms).astype(BF16)
+        terms.append(send(away, bit))
+    nearest, straight, _ = lax.optimization_barrier((late[1], straight, away))
     straight.append(send(nearest, 1))
     upper = sum(t[:, :depth].astype(F32) for t in terms)
     lower = product(far, even, 0) + sum(t.astype(F32) for t in straight)

time: 159 us -> 95.3 us (0.60)
  Pallas kernels: 81.8 us -> 17.2 us
  starting transfers between devices: 24.9 us -> 22.2 us
  local copies, waits for them, and re-layouts: 2.86 us -> 5.08 us
    pallas_call x1, Pallas kernels: 64.7 us -> 0.14 us  [spread(): pl.pallas_call(functools.partial(spread_kernel, plan), out_shape=[jax.Sha...]
    ppermute x19, starting transfers between devices: 24.9 us -> 22.2 us  [swap(): return lax.ppermute(value, axis, pairs)]
  transfers between devices with their start and end apart: 19 -> 19, of which waited for: 10 -> 10; matrix products, arithmetic and copies ran while one was open for 4% -> 9% of each run, Pallas kernels for 51% -> 18%
where the time goes in v5:
time: 95.3 us; the launch traced here: 95.1 us
  waiting for transfers between devices  41.4 us (43%)
  starting transfers between devices  22.2 us (23%)
  Pallas kernels  17.2 us (18%)
  matrix products  5.77 us (6%)
  local copies, waits for them, and re-layouts  5.08 us (5%)
  other arithmetic  2.49 us (3%)
    ppermute x19, waiting for transfers between devices, swap(): return lax.ppermute(value, axis, pairs)  41.4 us
    ppermute x19, starting transfers between devices, swap(): return lax.ppermute(value, axis, pairs)  22.2 us
    pallas_call x1, Pallas kernels, attention(): pl.pallas_call(functools.partial(attention_kernel, height), grid=(width /...  16.9 us
    dot_general x12, matrix products, dot(): return lax.dot_general(left, right, dims, preferred_element_type=F32)  5.77 us
    unnamed x20, local copies, waits for them, and re-layouts  3.29 us
  transfers between devices with their start and end apart: 19, of which 10 were waited for; matrix products, arithmetic and copies ran while one was open for 9% of the time, Pallas kernels for 18%

profile of v5, /device:TPU:0, one launch (start us, length us, event | category | flops | bytes accessed | tf_op | source)
XLA Modules:
  0.0 95.1 jit_solution(3568114911775370382)
XLA Ops:
  0.6 0.5 collective-permute-start
  1.1 1.6 %copy-done = bf16[128,8192]{1,0:T(8,128)(2,1)S(1)} copy-done((bf16[128,8192]{1,0:T(8,128)(2,1)S(1)}, bf16[128,8192]{1,0:T(8,128)(2,1)}, u32[]{:S(2)}) %copy-start) | copy-done | bytes 2097176
  2.7 0.1 spread.1
  2.9 2.6 %collective-permute-start.5 = (bf16[192,2048]{1,0:T(8,128)(2,1)S(1)}, bf16[192,2048]{1,0:T(8,128)(2,1)S(1)}, u32[]{:S(2)}, u32[]{:S(2)}) collective-permute-start(bf16[192,2048]{1,0:T(8,128)(2,1)S(1)} %get-tuple-element.31), channel_id=1, source_target_pairs={{0,8},{8,0},{16,24},{24,16},{1,9},{9,1},{17,25},{25,17},{2,10},{10... | collective-permute-start | bytes 2359304 | tf_op jit(solution)/shard_map/ppermute | solution.py:25
  5.4 1.5 %collective-permute-start.6 = (bf16[192,2048]{1,0:T(8,128)(2,1)S(1)}, bf16[192,2048]{1,0:T(8,128)(2,1)S(1)}, u32[]{:S(2)}, u32[]{:S(2)}) collective-permute-start(bf16[192,2048]{1,0:T(8,128)(2,1)S(1)} %get-tuple-element.32), channel_id=1, source_target_pairs={{0,16},{8,24},{16,0},{24,8},{1,17},{9,25},{17,1},{25,9},{2,18},{10... | collective-permute-start | bytes 2359304 | tf_op jit(solution)/shard_map/ppermute | solution.py:25
  7.0 1.4 %copy-done.2 = bf16[1024,768]{1,0:T(8,128)(2,1)S(1)} copy-done((bf16[1024,768]{1,0:T(8,128)(2,1)S(1)}, bf16[1024,768]{1,0:T(8,128)(2,1)}, u32[]{:S(2)}) %copy-start.2) | copy-done | bytes 1572888
  8.4 16.9 %attention.1 = (bf16[1024,768]{1,0:T(8,128)(2,1)}, f32[1024,128]{1,0:T(8,128)S(1)}, f32[1024,128]{1,0:T(8,128)S(1)}) custom-call(bf16[1024,128]{1,0:T(8,128)(2,1)S(1)} %copy-done.3, bf16[1024,128]{1,0:T(8,128)(2,1)S(1)} %collective-permute-done.other_ref, bf16[1024,768]{1,0:T(8,128)(2,1)S(1)} %copy-done.1, bf16[1024,768]{1,0:T(8,128)(2,1)S(1)} %copy-done.2), custom_call_target="tpu_custom_call" | custom-call | flops 16106127360 | bytes 9437184 | tf_op jit(solution)/shard_map/attention/pallas_call | solution.py:103
  25.3 0.8 slice.154
  26.0 0.5 collective-permute-start.7
  26.5 0.8 slice.155
  27.3 1.2 %collective-permute-start.8 = (bf16[64,2048]{1,0:T(8,128)(2,1)}, bf16[64,2048]{1,0:T(8,128)(2,1)}, u32[]{:S(2)}, u32[]{:S(2)}) collective-permute-start(bf16[64,2048]{1,0:T(8,128)(2,1)} %slice.155), channel_id=1, source_target_pairs={{0,8},{8,0},{16,24},{24,16},{1,9},{9,1},{17,25},{25,17},{2,10},{10... | collective-permute-start | bytes 786440 | tf_op jit(solution)/shard_map/ppermute | solution.py:25
  28.5 0.2 copy.8.mask_ref
  28.8 0.2 kv_blocks.1
  29.0 1.6 %collective-permute-start.2 = (bf16[256,128]{1,0:T(8,128)(2,1)S(1)}, bf16[256,128]{1,0:T(8,128)(2,1)S(1)}, u32[]{:S(2)}, u32[]{:S(2)}) collective-permute-start(bf16[256,128]{1,0:T(8,128)(2,1)S(1)} %get-tuple-element.27), channel_id=1, source_target_pairs={{0,2},{1,3},{2,0},{3,1},{4,6},{5,7},{6,4},{7,5},{8,10},{9,11},{10,... | collective-permute-start | bytes 196616 | tf_op jit(solution)/shard_map/ppermute | solution.py:25
  30.6 2.6 %collective-permute-start.3 = (bf16[256,128]{1,0:T(8,128)(2,1)S(1)}, bf16[256,128]{1,0:T(8,128)(2,1)S(1)}, u32[]{:S(2)}, u32[]{:S(2)}) collective-permute-start(bf16[256,128]{1,0:T(8,128)(2,1)S(1)} %get-tuple-element.28), channel_id=1, source_target_pairs={{0,4},{1,5},{2,6},{3,7},{4,0},{5,1},{6,2},{7,3},{8,12},{9,13},{10,... | collective-permute-start | bytes 196616 | tf_op jit(solution)/shard_map/ppermute | solution.py:25
  33.2 0.2 collective-permute-start.4
  33.4 1.6 %collective-permute-done.7 = bf16[64,2048]{1,0:T(8,128)(2,1)} collective-permute-done((bf16[64,2048]{1,0:T(8,128)(2,1)}, bf16[64,2048]{1,0:T(8,128)(2,1)}, u32[]{:S(2)}, u32[]{:S(2)}) %collective-permute-start.7) | collective-permute-done | bytes 262176 | tf_op jit(solution)/shard_map/ppermute | solution.py:25
  35.1 1.0 %collective-permute-done.8 = bf16[64,2048]{1,0:T(8,128)(2,1)} collective-permute-done((bf16[64,2048]{1,0:T(8,128)(2,1)}, bf16[64,2048]{1,0:T(8,128)(2,1)}, u32[]{:S(2)}, u32[]{:S(2)}) %collective-permute-start.8) | collective-permute-done | bytes 262176 | tf_op jit(solution)/shard_map/ppermute | solution.py:25
  36.1 1.1 %pad_maximum_fusion.2 = bf16[128,2048]{1,0:T(8,128)(2,1)S(1)} fusion(bf16[64,2048]{1,0:T(8,128)(2,1)} %collective-permute-done.8, bf16[64,2048]{1,0:T(8,128)(2,1)} %collective-permute-done.7), kind=kLoop, calls=%fused_computation.18 | loop fusion | flops 1048576 | bytes 1048576 | tf_op jit(solution)/shard_map/concatenate | solution.py:163
  37.2 0.4 collective-permute-done.3
  37.5 1.8 %collective-permute-done.4 = bf16[256,128]{1,0:T(8,128)(2,1)S(1)} collective-permute-done((bf16[256,128]{1,0:T(8,128)(2,1)S(1)}, bf16[256,128]{1,0:T(8,128)(2,1)S(1)}, u32[]{:S(2)}, u32[]{:S(2)}) %collective-permute-start.4) | collective-permute-done | bytes 65568 | tf_op jit(solution)/shard_map/ppermute | solution.py:25
  39.4 1.0 %collective-permute-start.9 = (bf16[256,512]{1,0:T(8,128)(2,1)S(1)}, bf16[256,512]{1,0:T(8,128)(2,1)S(1)}, u32[]{:S(2)}, u32[]{:S(2)}) collective-permute-start(bf16[256,512]{1,0:T(8,128)(2,1)S(1)} %constant_dynamic-update-slice_fusion), channel_id=1, source_target_pairs={{0,8},{8,0},{16,24},{24,16},{1,9},{9,1},{17,25},{25,17},{2,10},{10... | collective-permute-start | bytes 786440 | tf_op jit(solution)/shard_map/ppermute | solution.py:25
  40.4 1.5 %collective-permute-start.10 = (bf16[256,512]{1,0:T(8,128)(2,1)S(1)}, bf16[256,512]{1,0:T(8,128)(2,1)S(1)}, u32[]{:S(2)}, u32[]{:S(2)}) collective-permute-start(bf16[256,512]{1,0:T(8,128)(2,1)S(1)} %constant_dynamic-update-slice_fusion), channel_id=1, source_target_pairs={{0,16},{8,24},{16,0},{24,8},{1,17},{9,25},{17,1},{25,9},{2,18},{10... | collective-permute-start | bytes 786440 | tf_op jit(solution)/shard_map/ppermute | solution.py:25
  41.9 1.0 %collective-permute-start.11 = (bf16[256,512]{1,0:T(8,128)(2,1)S(1)}, bf16[256,512]{1,0:T(8,128)(2,1)S(1)}, u32[]{:S(2)}, u32[]{:S(2)}) collective-permute-start(bf16[256,512]{1,0:T(8,128)(2,1)S(1)} %constant_dynamic-update-slice_fusion), channel_id=1, source_target_pairs={{0,24},{8,16},{16,8},{24,0},{1,25},{9,17},{17,9},{25,1},{2,26},{10... | collective-permute-start | bytes 786440 | tf_op jit(solution)/shard_map/ppermute | solution.py:25
  43.4 0.6 collective-permute-start.15
  43.9 4.3 %collective-permute-done.9 = bf16[256,512]{1,0:T(8,128)(2,1)S(1)} collective-permute-done((bf16[256,512]{1,0:T(8,128)(2,1)S(1)}, bf16[256,512]{1,0:T(8,128)(2,1)S(1)}, u32[]{:S(2)}, u32[]{:S(2)}) %collective-permute-start.9) | collective-permute-done | bytes 262176 | tf_op jit(solution)/shard_map/ppermute | solution.py:25
  48.2 3.9 %collective-permute-done.10 = bf16[256,512]{1,0:T(8,128)(2,1)S(1)} collective-permute-done((bf16[256,512]{1,0:T(8,128)(2,1)S(1)}, bf16[256,512]{1,0:T(8,128)(2,1)S(1)}, u32[]{:S(2)}, u32[]{:S(2)}) %collective-permute-start.10) | collective-permute-done | bytes 262176 | tf_op jit(solution)/shard_map/ppermute | solution.py:25
  52.3 0.5 fusion.7
  52.8 0.5 fusion
  53.3 1.0 %collective-permute-start.13 = (bf16[1024,256]{1,0:T(8,128)(2,1)S(1)}, bf16[1024,256]{1,0:T(8,128)(2,1)S(1)}, u32[]{:S(2)}, u32[]{:S(2)}) collective-permute-start(bf16[1024,256]{1,0:T(8,128)(2,1)S(1)} %fusion), channel_id=1, source_target_pairs={{0,2},{1,3},{2,0},{3,1},{4,6},{5,7},{6,4},{7,5},{8,10},{9,11},{10,... | collective-permute-start | bytes 1572872 | tf_op jit(solution)/shard_map/ppermute | solution.py:25
  54.3 0.5 fusion.13
  54.8 0.5 fusion.4
  55.3 2.6 %collective-permute-start.17 = (bf16[1024,128]{1,0:T(8,128)(2,1)S(1)}, bf16[1024,128]{1,0:T(8,128)(2,1)S(1)}, u32[]{:S(2)}, u32[]{:S(2)}) collective-permute-start(bf16[1024,128]{1,0:T(8,128)(2,1)S(1)} %fusion.4), channel_id=1, source_target_pairs={{0,6},{1,7},{2,4},{3,5},{4,2},{5,3},{6,0},{7,1},{8,14},{9,15},{10,... | collective-permute-start | bytes 786440 | tf_op jit(solution)/shard_map/ppermute | solution.py:25
  57.9 0.5 fusion.16
  58.3 0.5 fusion.3
  59.0 0.5 fusion.10
  59.4 0.5 fusion.19
  59.9 0.5 fusion.2
  60.4 0.5 convolution_add_fusion.1
  60.9 12.2 %collective-permute-done.13 = bf16[1024,256]{1,0:T(8,128)(2,1)S(1)} collective-permute-done((bf16[1024,256]{1,0:T(8,128)(2,1)S(1)}, bf16[1024,256]{1,0:T(8,128)(2,1)S(1)}, u32[]{:S(2)}, u32[]{:S(2)}) %collective-permute-start.13) | collective-permute-done | bytes 524320 | tf_op jit(solution)/shard_map/ppermute | solution.py:25
  73.2 2.0 %collective-permute-start.14 = (bf16[1024,128]{1,0:T(8,128)(2,1)S(1)}, bf16[1024,128]{1,0:T(8,128)(2,1)S(1)}, u32[]{:S(2)}, u32[]{:S(2)}) collective-permute-start(bf16[1024,128]{1,0:T(8,128)(2,1)S(1)} %fusion.5), channel_id=1, source_target_pairs={{0,4},{1,5},{2,6},{3,7},{4,0},{5,1},{6,2},{7,3},{8,12},{9,13},{10,... | collective-permute-start | bytes 786440 | tf_op jit(solution)/shard_map/ppermute | solution.py:25
  75.2 0.5 fusion.22
  75.7 10.5 %collective-permute-done.16 = bf16[1024,128]{1,0:T(8,128)(2,1)S(1)} collective-permute-done((bf16[1024,128]{1,0:T(8,128)(2,1)S(1)}, bf16[1024,128]{1,0:T(8,128)(2,1)S(1)}, u32[]{:S(2)}, u32[]{:S(2)}) %collective-permute-start.16) | collective-permute-done | bytes 262176 | tf_op jit(solution)/shard_map/ppermute | solution.py:25
  86.2 1.5 %collective-permute-start.18 = (bf16[1024,128]{1,0:T(8,128)(2,1)S(1)}, bf16[1024,128]{1,0:T(8,128)(2,1)S(1)}, u32[]{:S(2)}, u32[]{:S(2)}) collective-permute-start(bf16[1024,128]{1,0:T(8,128)(2,1)S(1)} %fusion.2), channel_id=1, source_target_pairs={{0,2},{1,3},{2,0},{3,1},{4,6},{5,7},{6,4},{7,5},{8,10},{9,11},{10,... | collective-permute-start | bytes 786440 | tf_op jit(solution)/shard_map/ppermute | solution.py:25
  87.7 3.0 %collective-permute-done.14 = bf16[1024,128]{1,0:T(8,128)(2,1)S(1)} collective-permute-done((bf16[1024,128]{1,0:T(8,128)(2,1)S(1)}, bf16[1024,128]{1,0:T(8,128)(2,1)S(1)}, u32[]{:S(2)}, u32[]{:S(2)}) %collective-permute-start.14) | collective-permute-done | bytes 262176 | tf_op jit(solution)/shard_map/ppermute | solution.py:25
  90.9 2.6 %collective-permute-done.18 = bf16[1024,128]{1,0:T(8,128)(2,1)S(1)} collective-permute-done((bf16[1024,128]{1,0:T(8,128)(2,1)S(1)}, bf16[1024,128]{1,0:T(8,128)(2,1)S(1)}, u32[]{:S(2)}, u32[]{:S(2)}) %collective-permute-start.18) | collective-permute-done | bytes 262176 | tf_op jit(solution)/shard_map/ppermute | solution.py:25
  93.5 0.5 fusion.1
  94.0 1.1 %maximum_select_fusion = f32[2048,128]{1,0:T(8,128)} fusion(f32[1024,128]{1,0:T(8,128)S(1)} %fusion.1, f32[1024,128]{1,0:T(8,128)S(1)} %fusion.6, s32[2048,128]{1,0:T(8,128)S(1)} %copy-done.6), kind=kLoop, calls=%fused_computation.13 | loop fusion | flops 786432 | bytes 3145728 | tf_op jit(solution)/shard_map/jit(_where)/select_n | solution.py:245
  (45 shorter events, 0.9 us)
Async XLA Ops:
  0.6 6.3 %collective-permute-start = (bf16[1024,128]{1,0:T(8,128)(2,1)}, bf16[1024,128]{1,0:T(8,128)(2,1)S(1)}, u32[]{:S(2)}, u32[]{:S(2)}) collective-permute-start(bf16[1024,128]{1,0:T(8,128)(2,1)} %own_ref.1), channel_id=1, source_target_pairs={{0,1},{1,0},{2,3},{3,2},{4,5},{5,4},{6,7},{7,6},{8,9},{9,8},{10,11... | collective-permute-start | bytes 786440 | tf_op jit(solution)/shard_map/ppermute | solution.py:25
  1.1 1.6 %copy-start = (bf16[128,8192]{1,0:T(8,128)(2,1)S(1)}, bf16[128,8192]{1,0:T(8,128)(2,1)}, u32[]{:S(2)}) copy-start(bf16[128,8192]{1,0:T(8,128)(2,1)} %source_ref.1) | copy-start | bytes 6291460
  2.7 4.2 %copy-start.1 = (bf16[1024,768]{1,0:T(8,128)(2,1)S(1)}, bf16[1024,768]{1,0:T(8,128)(2,1)}, u32[]{:S(2)}) copy-start(bf16[1024,768]{1,0:T(8,128)(2,1)} %q_ref.1) | copy-start | bytes 4718596
  2.7 4.2 %copy-start.3 = (bf16[1024,128]{1,0:T(8,128)(2,1)S(1)}, bf16[1024,128]{1,0:T(8,128)(2,1)}, u32[]{:S(2)}) copy-start(bf16[1024,128]{1,0:T(8,128)(2,1)} %own_ref.1) | copy-start | bytes 786436
  2.9 22.4 %collective-permute-start.5 = (bf16[192,2048]{1,0:T(8,128)(2,1)S(1)}, bf16[192,2048]{1,0:T(8,128)(2,1)S(1)}, u32[]{:S(2)}, u32[]{:S(2)}) collective-permute-start(bf16[192,2048]{1,0:T(8,128)(2,1)S(1)} %get-tuple-element.31), channel_id=1, source_target_pairs={{0,8},{8,0},{16,24},{24,16},{1,9},{9,1},{17,25},{25,17},{2,10},{10... | collective-permute-start | bytes 2359304 | tf_op jit(solution)/shard_map/ppermute | solution.py:25
  5.4 21.1 %collective-permute-start.6 = (bf16[192,2048]{1,0:T(8,128)(2,1)S(1)}, bf16[192,2048]{1,0:T(8,128)(2,1)S(1)}, u32[]{:S(2)}, u32[]{:S(2)}) collective-permute-start(bf16[192,2048]{1,0:T(8,128)(2,1)S(1)} %get-tuple-element.32), channel_id=1, source_target_pairs={{0,16},{8,24},{16,0},{24,8},{1,17},{9,25},{17,1},{25,9},{2,18},{10... | collective-permute-start | bytes 2359304 | tf_op jit(solution)/shard_map/ppermute | solution.py:25
  7.0 1.4 %copy-start.2 = (bf16[1024,768]{1,0:T(8,128)(2,1)S(1)}, bf16[1024,768]{1,0:T(8,128)(2,1)}, u32[]{:S(2)}) copy-start(bf16[1024,768]{1,0:T(8,128)(2,1)} %up_ref.1) | copy-start | bytes 4718596
  8.4 20.1 %copy-start.7 = (s32[1024,1]{0,1:T(1,128)S(1)}, s32[1024,1]{0,1:T(1,128)}, u32[]{:S(2)}) copy-start(s32[1024,1]{0,1:T(1,128)} %param.11) | copy-start | bytes 12292
  25.3 3.5 %collective-permute-start.1 = (f32[1024,128]{1,0:T(8,128)S(1)}, f32[1024,128]{1,0:T(8,128)S(1)}, u32[]{:S(2)}, u32[]{:S(2)}) collective-permute-start(f32[1024,128]{1,0:T(8,128)S(1)} %get-tuple-element.25), channel_id=1, source_target_pairs={{0,1},{1,0},{2,3},{3,2},{4,5},{5,4},{6,7},{7,6},{8,9},{9,8},{10,11... | collective-permute-start | bytes 1572872 | tf_op jit(solution)/shard_map/ppermute | solution.py:25
  25.3 2.0 %copy-start.5 = (bf16[192,2048]{1,0:T(8,128)(2,1)}, bf16[192,2048]{1,0:T(8,128)(2,1)S(1)}, u32[]{:S(2)}) copy-start(bf16[192,2048]{1,0:T(8,128)(2,1)S(1)} %collective-permute-done.5) | copy-start | bytes 2359300
  26.0 9.0 %collective-permute-start.7 = (bf16[64,2048]{1,0:T(8,128)(2,1)}, bf16[64,2048]{1,0:T(8,128)(2,1)}, u32[]{:S(2)}, u32[]{:S(2)}) collective-permute-start(bf16[64,2048]{1,0:T(8,128)(2,1)} %slice.154), channel_id=1, source_target_pairs={{0,16},{8,24},{16,0},{24,8},{1,17},{9,25},{17,1},{25,9},{2,18},{10... | collective-permute-start | bytes 786440 | tf_op jit(solution)/shard_map/ppermute | solution.py:25
  26.5 6.9 %copy-start.4 = (bf16[192,2048]{1,0:T(8,128)(2,1)}, bf16[192,2048]{1,0:T(8,128)(2,1)S(1)}, u32[]{:S(2)}) copy-start(bf16[192,2048]{1,0:T(8,128)(2,1)S(1)} %collective-permute-done.6) | copy-start | bytes 2359300
  27.3 8.8 %collective-permute-start.8 = (bf16[64,2048]{1,0:T(8,128)(2,1)}, bf16[64,2048]{1,0:T(8,128)(2,1)}, u32[]{:S(2)}, u32[]{:S(2)}) collective-permute-start(bf16[64,2048]{1,0:T(8,128)(2,1)} %slice.155), channel_id=1, source_target_pairs={{0,8},{8,0},{16,24},{24,16},{1,9},{9,1},{17,25},{25,17},{2,10},{10... | collective-permute-start | bytes 786440 | tf_op jit(solution)/shard_map/ppermute | solution.py:25
  29.0 14.0 %slice-start.1 = ((bf16[192,2048]{1,0:T(8,128)(2,1)}), bf16[128,2048]{1,0:T(8,128)(2,1)S(1)}, s32[]{:S(2)}) async-start(bf16[192,2048]{1,0:T(8,128)(2,1)} %copy-done.5), calls=%async_computation.1 | async-start | bytes 1048576 | tf_op jit(solution)/shard_map/slice | solution.py:163
  29.0 8.2 %collective-permute-start.2 = (bf16[256,128]{1,0:T(8,128)(2,1)S(1)}, bf16[256,128]{1,0:T(8,128)(2,1)S(1)}, u32[]{:S(2)}, u32[]{:S(2)}) collective-permute-start(bf16[256,128]{1,0:T(8,128)(2,1)S(1)} %get-tuple-element.27), channel_id=1, source_target_pairs={{0,2},{1,3},{2,0},{3,1},{4,6},{5,7},{6,4},{7,5},{8,10},{9,11},{10,... | collective-permute-start | bytes 196616 | tf_op jit(solution)/shard_map/ppermute | solution.py:25
  30.6 6.9 %collective-permute-start.3 = (bf16[256,128]{1,0:T(8,128)(2,1)S(1)}, bf16[256,128]{1,0:T(8,128)(2,1)S(1)}, u32[]{:S(2)}, u32[]{:S(2)}) collective-permute-start(bf16[256,128]{1,0:T(8,128)(2,1)S(1)} %get-tuple-element.28), channel_id=1, source_target_pairs={{0,4},{1,5},{2,6},{3,7},{4,0},{5,1},{6,2},{7,3},{8,12},{9,13},{10,... | collective-permute-start | bytes 196616 | tf_op jit(solution)/shard_map/ppermute | solution.py:25
  33.2 6.1 %collective-permute-start.4 = (bf16[256,128]{1,0:T(8,128)(2,1)S(1)}, bf16[256,128]{1,0:T(8,128)(2,1)S(1)}, u32[]{:S(2)}, u32[]{:S(2)}) collective-permute-start(bf16[256,128]{1,0:T(8,128)(2,1)S(1)} %get-tuple-element.29), channel_id=1, source_target_pairs={{0,6},{1,7},{2,4},{3,5},{4,2},{5,3},{6,0},{7,1},{8,14},{9,15},{10,... | collective-permute-start | bytes 196616 | tf_op jit(solution)/shard_map/ppermute | solution.py:25
  35.1 8.0 %slice-start = ((bf16[192,2048]{1,0:T(8,128)(2,1)}), bf16[128,2048]{1,0:T(8,128)(2,1)S(1)}, s32[]{:S(2)}) async-start(bf16[192,2048]{1,0:T(8,128)(2,1)} %copy-done.4), calls=%async_computation | async-start | bytes 1048576 | tf_op jit(solution)/shard_map/slice | solution.py:163
  39.4 8.8 %collective-permute-start.9 = (bf16[256,512]{1,0:T(8,128)(2,1)S(1)}, bf16[256,512]{1,0:T(8,128)(2,1)S(1)}, u32[]{:S(2)}, u32[]{:S(2)}) collective-permute-start(bf16[256,512]{1,0:T(8,128)(2,1)S(1)} %constant_dynamic-update-slice_fusion), channel_id=1, source_target_pairs={{0,8},{8,0},{16,24},{24,16},{1,9},{9,1},{17,25},{25,17},{2,10},{10... | collective-permute-start | bytes 786440 | tf_op jit(solution)/shard_map/ppermute | solution.py:25
  40.4 11.8 %collective-permute-start.10 = (bf16[256,512]{1,0:T(8,128)(2,1)S(1)}, bf16[256,512]{1,0:T(8,128)(2,1)S(1)}, u32[]{:S(2)}, u32[]{:S(2)}) collective-permute-start(bf16[256,512]{1,0:T(8,128)(2,1)S(1)} %constant_dynamic-update-slice_fusion), channel_id=1, source_target_pairs={{0,16},{8,24},{16,0},{24,8},{1,17},{9,25},{17,1},{25,9},{2,18},{10... | collective-permute-start | bytes 786440 | tf_op jit(solution)/shard_map/ppermute | solution.py:25
  41.9 10.3 %collective-permute-start.11 = (bf16[256,512]{1,0:T(8,128)(2,1)S(1)}, bf16[256,512]{1,0:T(8,128)(2,1)S(1)}, u32[]{:S(2)}, u32[]{:S(2)}) collective-permute-start(bf16[256,512]{1,0:T(8,128)(2,1)S(1)} %constant_dynamic-update-slice_fusion), channel_id=1, source_target_pairs={{0,24},{8,16},{16,8},{24,0},{1,25},{9,17},{17,9},{25,1},{2,26},{10... | collective-permute-start | bytes 786440 | tf_op jit(solution)/shard_map/ppermute | solution.py:25
  43.2 9.1 %collective-permute-start.12 = (bf16[512,1024]{1,0:T(8,128)(2,1)S(1)}, bf16[512,1024]{1,0:T(8,128)(2,1)S(1)}, u32[]{:S(2)}, u32[]{:S(2)}) collective-permute-start(bf16[512,1024]{1,0:T(8,128)(2,1)S(1)} %pad_maximum_fusion), channel_id=1, source_target_pairs={{0,1},{1,0},{2,3},{3,2},{4,5},{5,4},{6,7},{7,6},{8,9},{9,8},{10,11... | collective-permute-start | bytes 3145736 | tf_op jit(solution)/shard_map/ppermute | solution.py:25
  43.4 10.9 %collective-permute-start.15 = (bf16[512,1024]{1,0:T(8,128)(2,1)S(1)}, bf16[512,1024]{1,0:T(8,128)(2,1)S(1)}, u32[]{:S(2)}, u32[]{:S(2)}) collective-permute-start(bf16[512,1024]{1,0:T(8,128)(2,1)S(1)} %pad_maximum_fusion.1), channel_id=1, source_target_pairs={{0,1},{1,0},{2,3},{3,2},{4,5},{5,4},{6,7},{7,6},{8,9},{9,8},{10,11... | collective-permute-start | bytes 3145736 | tf_op jit(solution)/shard_map/ppermute | solution.py:25
  53.3 19.8 %collective-permute-start.13 = (bf16[1024,256]{1,0:T(8,128)(2,1)S(1)}, bf16[1024,256]{1,0:T(8,128)(2,1)S(1)}, u32[]{:S(2)}, u32[]{:S(2)}) collective-permute-start(bf16[1024,256]{1,0:T(8,128)(2,1)S(1)} %fusion), channel_id=1, source_target_pairs={{0,2},{1,3},{2,0},{3,1},{4,6},{5,7},{6,4},{7,5},{8,10},{9,11},{10,... | collective-permute-start | bytes 1572872 | tf_op jit(solution)/shard_map/ppermute | solution.py:25
  55.3 20.4 %collective-permute-start.17 = (bf16[1024,128]{1,0:T(8,128)(2,1)S(1)}, bf16[1024,128]{1,0:T(8,128)(2,1)S(1)}, u32[]{:S(2)}, u32[]{:S(2)}) collective-permute-start(bf16[1024,128]{1,0:T(8,128)(2,1)S(1)} %fusion.4), channel_id=1, source_target_pairs={{0,6},{1,7},{2,4},{3,5},{4,2},{5,3},{6,0},{7,1},{8,14},{9,15},{10,... | collective-permute-start | bytes 786440 | tf_op jit(solution)/shard_map/ppermute | solution.py:25
  58.8 27.4 %collective-permute-start.16 = (bf16[1024,128]{1,0:T(8,128)(2,1)S(1)}, bf16[1024,128]{1,0:T(8,128)(2,1)S(1)}, u32[]{:S(2)}, u32[]{:S(2)}) collective-permute-start(bf16[1024,128]{1,0:T(8,128)(2,1)S(1)} %fusion.3), channel_id=1, source_target_pairs={{0,4},{1,5},{2,6},{3,7},{4,0},{5,1},{6,2},{7,3},{8,12},{9,13},{10,... | collective-permute-start | bytes 786440 | tf_op jit(solution)/shard_map/ppermute | solution.py:25
  73.2 17.6 %collective-permute-start.14 = (bf16[1024,128]{1,0:T(8,128)(2,1)S(1)}, bf16[1024,128]{1,0:T(8,128)(2,1)S(1)}, u32[]{:S(2)}, u32[]{:S(2)}) collective-permute-start(bf16[1024,128]{1,0:T(8,128)(2,1)S(1)} %fusion.5), channel_id=1, source_target_pairs={{0,4},{1,5},{2,6},{3,7},{4,0},{5,1},{6,2},{7,3},{8,12},{9,13},{10,... | collective-permute-start | bytes 786440 | tf_op jit(solution)/shard_map/ppermute | solution.py:25
  86.2 7.3 %collective-permute-start.18 = (bf16[1024,128]{1,0:T(8,128)(2,1)S(1)}, bf16[1024,128]{1,0:T(8,128)(2,1)S(1)}, u32[]{:S(2)}, u32[]{:S(2)}) collective-permute-start(bf16[1024,128]{1,0:T(8,128)(2,1)S(1)} %fusion.2), channel_id=1, source_target_pairs={{0,2},{1,3},{2,0},{3,1},{4,6},{5,7},{6,4},{7,5},{8,10},{9,11},{10,... | collective-permute-start | bytes 786440 | tf_op jit(solution)/shard_map/ppermute | solution.py:25
  90.8 3.1 %copy-start.6 = (s32[2048,128]{1,0:T(8,128)S(1)}, s32[2048,128]{1,0:T(8,128)}, u32[]{:S(2)}) copy-start(s32[2048,128]{1,0:T(8,128)} %param.10) | copy-start | bytes 3145732

commit v6 on v5

--- a/solution.py
+++ b/solution.py
@@ -10,7 +10,7 @@
 
 F32 = jnp.float32
 BF16 = jnp.bfloat16
-VMEM_LIMIT = 36 * 2**20
+VMEM_LIMIT = 50 * 2**20
 IN_ORDER = pltpu.CompilerParams(
     vmem_limit_bytes=VMEM_LIMIT, dimension_semantics=("arbitrary",)
 )
@@ -201,13 +201,24 @@
     blocks = kv_blocks(mine, arrived, clip_mask, rows)
 
     blocks = [b if s == 0 else swap(b, "tensor", 2 * s) for s, b in enumerate(blocks)]
-    blocks, parts = lax.optimization_barrier((blocks, parts))
+    blocks[-1], parts = lax.optimization_barrier((blocks[-1], parts))
     order = sorted(range(chips), key=lambda s: [(s >> b) & 1 for b in range(8)])
     evens, odds = order[: chips // 2], order[chips // 2 :]
 
-    def gather(stacked):
-        found = [stacked if s == 0 else swap(stacked, "dp", s) for s in range(groups)]
-        return [jnp.concatenate([f[h * rows : (h + 1) * rows] for f in found], 0) for h in (0, 1)]
+    groups_of = (range(chips // 2), range(chips // 2, chips))
+    found = []
+    for steps in groups_of:
+        stacked = jnp.concatenate([blocks[s] for s in steps], 1)
+        found.append([stacked if s == 0 else swap(stacked, "dp", s) for s in range(groups)])
+    found = lax.optimization_barrier(found)
+    grads = [None] * chips
+    for steps, group in zip(groups_of, found):
+        for place, step in enumerate(steps):
+            columns = slice(place * depth, (place + 1) * depth)
+            grads[step] = [
+                jnp.concatenate([f[h * rows : (h + 1) * rows, columns] for f in group], 0)
+                for h in (0, 1)
+            ]
 
     wide = block // 2
     cuts = []
@@ -216,31 +227,29 @@
         cuts.append((own, swap(own, "tensor", 1)))
     near, far = cuts
 
-    def product(pair, grads, place=None):
-        if place is not None:
-            grads = [g[:, place * depth : (place + 1) * depth] for g in grads]
+    def product(pair, grads):
         return dot(pair[0], grads[0], 0, 0) + dot(pair[1], grads[1], 0, 0)
 
     def send(value, step):
         return swap(value.astype(BF16), "tensor", 2 * step)
 
-    grads = gather(jnp.concatenate([blocks[s] for s in order], 1))
-    half = chips // 2 * depth
-    even, odd = [g[:, :half] for g in grads], [g[:, half:] for g in grads]
+    def joined(steps):
+        return [jnp.concatenate([grads[s][h] for s in steps], 1) for h in (0, 1)]
+
+    odd, even = joined(odds), joined(evens)
+    straight = [send(product(far, grads[s]), s) for s in range(2, chips)]
     sent = send(product(near, odd), 1)
-    late = {s: product(far, odd, odds.index(s)).astype(BF16) for s in odds}
-    late.update({s: product(far, even, evens.index(s)).astype(BF16) for s in evens[1:]})
-    straight = [send(late[s], s) for s in range(2, chips)]
+    sent, straight = lax.optimization_barrier((sent, straight))
     terms = [product(near, even), sent]
-    columns, bit = half, 1
+    columns, bit = chips // 2 * depth, 1
     while columns > depth:
         columns, bit = columns // 2, bit * 2
         away = sum(t[:, columns : 2 * columns].astype(F32) for t in terms).astype(BF16)
         terms.append(send(away, bit))
-    nearest, straight, _ = lax.optimization_barrier((late[1], straight, away))
+    nearest, _ = lax.optimization_barrier((product(far, grads[1]).astype(BF16), away))
     straight.append(send(nearest, 1))
     upper = sum(t[:, :depth].astype(F32) for t in terms)
-    lower = product(far, even, 0) + sum(t.astype(F32) for t in straight)
+    lower = product(far, grads[0]) + sum(t.astype(F32) for t in straight)
     summed = jnp.concatenate([upper, lower], 0)
     weight_grad = jnp.where(weight_mask == 1, summed, 0.0)
     return (query_grad, weight_grad)

time: 95.3 us -> 98.8 us (1.037)
  starting transfers between devices: 22.2 us -> 24 us
  Pallas kernels: 17.2 us -> 18.8 us
  local copies, waits for them, and re-layouts: 5.08 us -> 6.34 us
  other arithmetic: 2.49 us -> 1.41 us
    slice x4 -> x2, local copies, waits for them, and re-layouts: 0.01 us -> 2.16 us  [exchange_rows(): return [own, left[:rows], right[:rows], jnp.concatenate([upper, lower], 0)]]
    ppermute x19 -> x22, starting transfers between devices: 22.2 us -> 24 us  [swap(): return lax.ppermute(value, axis, pairs)]
    unnamed x20 -> x13, local copies, waits for them, and re-layouts: 3.29 us -> 1.85 us
    concatenate x1, other arithmetic: 1.07 us -> 0.04 us  [exchange_rows(): return [own, left[:rows], right[:rows], jnp.concatenate([upper, lower], 0)]]
    ppermute x19 -> x22, waiting for transfers between devices: 41.4 us -> 41.3 us  [swap(): return lax.ppermute(value, axis, pairs)]
  transfers between devices with their start and end apart: 19 -> 22, of which waited for: 10 -> 12; matrix products, arithmetic and copies ran while one was open for 9% -> 10% of each run, Pallas kernels for 18% -> 19%
where the time goes in v6:
time: 98.8 us; the launch traced here: 98.5 us
  waiting for transfers between devices  41.3 us (42%)
  starting transfers between devices  24 us (24%)
  Pallas kernels  18.8 us (19%)
  local copies, waits for them, and re-layouts  6.34 us (6%)
  matrix products  5.74 us (6%)
  other arithmetic  1.41 us (1%)
    ppermute x22, waiting for transfers between devices, swap(): return lax.ppermute(value, axis, pairs)  41.3 us
    ppermute x22, starting transfers between devices, swap(): return lax.ppermute(value, axis, pairs)  24 us
    pallas_call x1, Pallas kernels, attention(): pl.pallas_call(functools.partial(attention_kernel, height), grid=(width /...  17.5 us
    dot_general x12, matrix products, dot(): return lax.dot_general(left, right, dims, preferred_element_type=F32)  5.74 us
    slice x2, local copies, waits for them, and re-layouts, exchange_rows(): return [own, left[:rows], right[:rows], jnp.concatenate([upper, lower], 0)]  2.16 us
  transfers between devices with their start and end apart: 22, of which 12 were waited for; matrix products, arithmetic and copies ran while one was open for 10% of the time, Pallas kernels for 19%

profile of v6, /device:TPU:0, one launch (start us, length us, event | category | flops | bytes accessed | tf_op | source)
XLA Modules:
  0.0 98.5 jit_solution(3694014573333327185)
XLA Ops:
  0.6 0.5 collective-permute-start
  1.1 1.6 %copy-done = bf16[128,8192]{1,0:T(8,128)(2,1)S(1)} copy-done((bf16[128,8192]{1,0:T(8,128)(2,1)S(1)}, bf16[128,8192]{1,0:T(8,128)(2,1)}, u32[]{:S(2)}) %copy-start) | copy-done | bytes 2097176
  2.7 1.0 %spread.1 = (bf16[128,2048]{1,0:T(8,128)(2,1)S(1)}, bf16[192,2048]{1,0:T(8,128)(2,1)}, bf16[192,2048]{1,0:T(8,128)(2,1)S(1)}) custom-call(bf16[128,8192]{1,0:T(8,128)(2,1)S(1)} %copy-done), custom_call_target="tpu_custom_call" | custom-call | bytes 4194304 | tf_op jit(solution)/shard_map/spread/pallas_call | solution.py:137
  3.8 2.5 %collective-permute-start.3 = (bf16[192,2048]{1,0:T(8,128)(2,1)}, bf16[192,2048]{1,0:T(8,128)(2,1)}, u32[]{:S(2)}, u32[]{:S(2)}) collective-permute-start(bf16[192,2048]{1,0:T(8,128)(2,1)} %get-tuple-element.34), channel_id=1, source_target_pairs={{0,8},{8,0},{16,24},{24,16},{1,9},{9,1},{17,25},{25,17},{2,10},{10... | collective-permute-start | bytes 2359304 | tf_op jit(solution)/shard_map/ppermute | solution.py:25
  6.3 1.5 %collective-permute-start.4 = (bf16[192,2048]{1,0:T(8,128)(2,1)S(1)}, bf16[192,2048]{1,0:T(8,128)(2,1)}, u32[]{:S(2)}, u32[]{:S(2)}) collective-permute-start(bf16[192,2048]{1,0:T(8,128)(2,1)S(1)} %get-tuple-element.35), channel_id=1, source_target_pairs={{0,16},{8,24},{16,0},{24,8},{1,17},{9,25},{17,1},{25,9},{2,18},{10... | collective-permute-start | bytes 2359304 | tf_op jit(solution)/shard_map/ppermute | solution.py:25
  7.8 17.5 %attention.1 = (bf16[1024,768]{1,0:T(8,128)(2,1)}, f32[1024,128]{1,0:T(8,128)S(1)}, f32[1024,128]{1,0:T(8,128)S(1)}) custom-call(bf16[1024,128]{1,0:T(8,128)(2,1)S(1)} %copy-done.2, bf16[1024,128]{1,0:T(8,128)(2,1)S(1)} %collective-permute-done.other_ref, bf16[1024,768]{1,0:T(8,128)(2,1)S(1)} %copy-done.1, bf16[1024,768]{1,0:T(8,128)(2,1)} %up_ref.1), custom_call_target="tpu_custom_call" | custom-call | flops 16106127360 | bytes 9437184 | tf_op jit(solution)/shard_map/attention/pallas_call | solution.py:103
  25.6 1.7 %collective-permute-done.1.arrived_ref = f32[1024,128]{1,0:T(8,128)S(1)} collective-permute-done((f32[1024,128]{1,0:T(8,128)S(1)}, f32[1024,128]{1,0:T(8,128)S(1)}, u32[]{:S(2)}, u32[]{:S(2)}) %collective-permute-start.1) | collective-permute-done | bytes 524320 | tf_op jit(solution)/shard_map/ppermute | solution.py:25
  27.4 3.7 %collective-permute-start.2 = (bf16[256,128]{1,0:T(8,128)(2,1)S(1)}, bf16[256,128]{1,0:T(8,128)(2,1)S(1)}, u32[]{:S(2)}, u32[]{:S(2)}) collective-permute-start(bf16[256,128]{1,0:T(8,128)(2,1)S(1)} %get-tuple-element.32), channel_id=1, source_target_pairs={{0,6},{1,7},{2,4},{3,5},{4,2},{5,3},{6,0},{7,1},{8,14},{9,15},{10,... | collective-permute-start | bytes 196616 | tf_op jit(solution)/shard_map/ppermute | solution.py:25
  31.1 0.8 collective-permute-start.7
  31.9 1.0 slice.194
  32.9 0.6 collective-permute-start.5
  33.4 1.0 slice.195
  34.4 0.5 collective-permute-start.6
  34.9 1.1 %slice.192 = bf16[128,2048]{1,0:T(8,128)(2,1)S(1)} slice(bf16[192,2048]{1,0:T(8,128)(2,1)} %collective-permute-done.3), slice={[0:128], [0:2048]} | slice | bytes 1048576 | tf_op jit(solution)/shard_map/slice | solution.py:163
  36.0 1.1 %slice.193 = bf16[128,2048]{1,0:T(8,128)(2,1)S(1)} slice(bf16[192,2048]{1,0:T(8,128)(2,1)} %collective-permute-done.4), slice={[0:128], [0:2048]} | slice | bytes 1048576 | tf_op jit(solution)/shard_map/slice | solution.py:163
  37.1 2.7 %collective-permute-start.10 = (bf16[256,256]{1,0:T(8,128)(2,1)S(1)}, bf16[256,256]{1,0:T(8,128)(2,1)S(1)}, u32[]{:S(2)}, u32[]{:S(2)}) collective-permute-start(bf16[256,256]{1,0:T(8,128)(2,1)S(1)} %constant_dynamic-update-slice_fusion), channel_id=1, source_target_pairs={{0,24},{8,16},{16,8},{24,0},{1,25},{9,17},{17,9},{25,1},{2,26},{10... | collective-permute-start | bytes 393224 | tf_op jit(solution)/shard_map/ppermute | solution.py:25
  39.8 0.5 collective-permute-start.8
  40.3 0.3 collective-permute-done.5
  40.6 0.5 collective-permute-start.9
  41.1 2.6 %collective-permute-done.6 = bf16[64,2048]{1,0:T(8,128)(2,1)S(1)} collective-permute-done((bf16[64,2048]{1,0:T(8,128)(2,1)S(1)}, bf16[64,2048]{1,0:T(8,128)(2,1)S(1)}, u32[]{:S(2)}, u32[]{:S(2)}) %collective-permute-start.6) | collective-permute-done | bytes 262176 | tf_op jit(solution)/shard_map/ppermute | solution.py:25
  43.9 2.0 %collective-permute-start.13 = (bf16[256,256]{1,0:T(8,128)(2,1)S(1)}, bf16[256,256]{1,0:T(8,128)(2,1)S(1)}, u32[]{:S(2)}, u32[]{:S(2)}) collective-permute-start(bf16[256,256]{1,0:T(8,128)(2,1)S(1)} %constant_dynamic-update-slice_fusion.2), channel_id=1, source_target_pairs={{0,16},{8,24},{16,0},{24,8},{1,17},{9,25},{17,1},{25,9},{2,18},{10... | collective-permute-start | bytes 393224 | tf_op jit(solution)/shard_map/ppermute | solution.py:25
  46.2 1.3 %collective-permute-done.10 = bf16[256,256]{1,0:T(8,128)(2,1)S(1)} collective-permute-done((bf16[256,256]{1,0:T(8,128)(2,1)S(1)}, bf16[256,256]{1,0:T(8,128)(2,1)S(1)}, u32[]{:S(2)}, u32[]{:S(2)}) %collective-permute-start.10) | collective-permute-done | bytes 131104 | tf_op jit(solution)/shard_map/ppermute | solution.py:25
  47.8 1.6 %collective-permute-done.8 = bf16[256,256]{1,0:T(8,128)(2,1)S(1)} collective-permute-done((bf16[256,256]{1,0:T(8,128)(2,1)S(1)}, bf16[256,256]{1,0:T(8,128)(2,1)S(1)}, u32[]{:S(2)}, u32[]{:S(2)}) %collective-permute-start.8) | collective-permute-done | bytes 131104 | tf_op jit(solution)/shard_map/ppermute | solution.py:25
  49.4 0.5 collective-permute-start.15
  49.9 1.8 %collective-permute-done.12 = bf16[256,256]{1,0:T(8,128)(2,1)S(1)} collective-permute-done((bf16[256,256]{1,0:T(8,128)(2,1)S(1)}, bf16[256,256]{1,0:T(8,128)(2,1)S(1)}, u32[]{:S(2)}, u32[]{:S(2)}) %collective-permute-start.12) | collective-permute-done | bytes 131104 | tf_op jit(solution)/shard_map/ppermute | solution.py:25
  51.7 2.4 %collective-permute-done.14 = bf16[256,256]{1,0:T(8,128)(2,1)S(1)} collective-permute-done((bf16[256,256]{1,0:T(8,128)(2,1)S(1)}, bf16[256,256]{1,0:T(8,128)(2,1)S(1)}, u32[]{:S(2)}, u32[]{:S(2)}) %collective-permute-start.14) | collective-permute-done | bytes 131104 | tf_op jit(solution)/shard_map/ppermute | solution.py:25
  54.3 0.5 fusion.38
  54.7 0.5 fusion.7
  55.2 0.5 fusion.107
  55.7 0.5 fusion.77
  56.2 0.5 fusion.99
  56.6 0.5 fusion.69
  57.1 0.5 fusion.3
  57.6 3.5 %collective-permute-start.19 = (bf16[1024,128]{1,0:T(8,128)(2,1)S(1)}, bf16[1024,128]{1,0:T(8,128)(2,1)S(1)}, u32[]{:S(2)}, u32[]{:S(2)}) collective-permute-start(bf16[1024,128]{1,0:T(8,128)(2,1)S(1)} %fusion.3), channel_id=1, source_target_pairs={{0,6},{1,7},{2,4},{3,5},{4,2},{5,3},{6,0},{7,1},{8,14},{9,15},{10,... | collective-permute-start | bytes 786440 | tf_op jit(solution)/shard_map/ppermute | solution.py:25
  61.1 0.5 fusion
  61.7 0.5 fusion.2
  62.2 1.0 collective-permute-start.18
  63.2 0.5 convolution_add_fusion.1
  63.7 5.1 %collective-permute-done.19 = bf16[1024,128]{1,0:T(8,128)(2,1)S(1)} collective-permute-done((bf16[1024,128]{1,0:T(8,128)(2,1)S(1)}, bf16[1024,128]{1,0:T(8,128)(2,1)S(1)}, u32[]{:S(2)}, u32[]{:S(2)}) %collective-permute-start.19) | collective-permute-done | bytes 262176 | tf_op jit(solution)/shard_map/ppermute | solution.py:25
  68.7 12.8 %collective-permute-done.18 = bf16[1024,128]{1,0:T(8,128)(2,1)S(1)} collective-permute-done((bf16[1024,128]{1,0:T(8,128)(2,1)S(1)}, bf16[1024,128]{1,0:T(8,128)(2,1)S(1)}, u32[]{:S(2)}, u32[]{:S(2)}) %collective-permute-start.18) | collective-permute-done | bytes 262176 | tf_op jit(solution)/shard_map/ppermute | solution.py:25
  81.6 1.0 %collective-permute-done.16 = bf16[1024,256]{1,0:T(8,128)(2,1)S(1)} collective-permute-done((bf16[1024,256]{1,0:T(8,128)(2,1)S(1)}, bf16[1024,256]{1,0:T(8,128)(2,1)S(1)}, u32[]{:S(2)}, u32[]{:S(2)}) %collective-permute-start.16) | collective-permute-done | bytes 524320 | tf_op jit(solution)/shard_map/ppermute | solution.py:25
  82.6 2.4 %collective-permute-start.20 = (bf16[1024,128]{1,0:T(8,128)(2,1)S(1)}, bf16[1024,128]{1,0:T(8,128)(2,1)S(1)}, u32[]{:S(2)}, u32[]{:S(2)}) collective-permute-start(bf16[1024,128]{1,0:T(8,128)(2,1)S(1)} %fusion.5), channel_id=1, source_target_pairs={{0,4},{1,5},{2,6},{3,7},{4,0},{5,1},{6,2},{7,3},{8,12},{9,13},{10,... | collective-permute-start | bytes 786440 | tf_op jit(solution)/shard_map/ppermute | solution.py:25
  85.1 0.5 fusion.4
  85.6 0.5 collective-permute-start.21
  86.0 9.9 %collective-permute-done.20 = bf16[1024,128]{1,0:T(8,128)(2,1)S(1)} collective-permute-done((bf16[1024,128]{1,0:T(8,128)(2,1)S(1)}, bf16[1024,128]{1,0:T(8,128)(2,1)S(1)}, u32[]{:S(2)}, u32[]{:S(2)}) %collective-permute-start.20) | collective-permute-done | bytes 262176 | tf_op jit(solution)/shard_map/ppermute | solution.py:25
  96.1 0.8 collective-permute-done.21
  96.9 0.5 fusion.1
  97.4 1.1 %maximum_select_fusion = f32[2048,128]{1,0:T(8,128)} fusion(f32[1024,128]{1,0:T(8,128)S(1)} %fusion.1, f32[1024,128]{1,0:T(8,128)S(1)} %fusion.6, s32[2048,128]{1,0:T(8,128)S(1)} %copy-done.3), kind=kLoop, calls=%fused_computation.13 | loop fusion | flops 786432 | bytes 3145728 | tf_op jit(solution)/shard_map/jit(_where)/select_n | solution.py:254
  (42 shorter events, 1.6 us)
Async XLA Ops:
  0.6 7.2 %collective-permute-start = (bf16[1024,128]{1,0:T(8,128)(2,1)}, bf16[1024,128]{1,0:T(8,128)(2,1)S(1)}, u32[]{:S(2)}, u32[]{:S(2)}) collective-permute-start(bf16[1024,128]{1,0:T(8,128)(2,1)} %own_ref.1), channel_id=1, source_target_pairs={{0,1},{1,0},{2,3},{3,2},{4,5},{5,4},{6,7},{7,6},{8,9},{9,8},{10,11... | collective-permute-start | bytes 786440 | tf_op jit(solution)/shard_map/ppermute | solution.py:25
  1.1 1.6 %copy-start = (bf16[128,8192]{1,0:T(8,128)(2,1)S(1)}, bf16[128,8192]{1,0:T(8,128)(2,1)}, u32[]{:S(2)}) copy-start(bf16[128,8192]{1,0:T(8,128)(2,1)} %source_ref.1) | copy-start | bytes 6291460
  2.7 5.0 %copy-start.1 = (bf16[1024,768]{1,0:T(8,128)(2,1)S(1)}, bf16[1024,768]{1,0:T(8,128)(2,1)}, u32[]{:S(2)}) copy-start(bf16[1024,768]{1,0:T(8,128)(2,1)} %q_ref.1) | copy-start | bytes 4718596
  2.7 5.0 %copy-start.2 = (bf16[1024,128]{1,0:T(8,128)(2,1)S(1)}, bf16[1024,128]{1,0:T(8,128)(2,1)}, u32[]{:S(2)}) copy-start(bf16[1024,128]{1,0:T(8,128)(2,1)} %own_ref.1) | copy-start | bytes 786436
  3.8 28.1 %collective-permute-start.3 = (bf16[192,2048]{1,0:T(8,128)(2,1)}, bf16[192,2048]{1,0:T(8,128)(2,1)}, u32[]{:S(2)}, u32[]{:S(2)}) collective-permute-start(bf16[192,2048]{1,0:T(8,128)(2,1)} %get-tuple-element.34), channel_id=1, source_target_pairs={{0,8},{8,0},{16,24},{24,16},{1,9},{9,1},{17,25},{25,17},{2,10},{10... | collective-permute-start | bytes 2359304 | tf_op jit(solution)/shard_map/ppermute | solution.py:25
  6.3 19.1 %copy-start.4 = (s32[1024,1]{0,1:T(1,128)S(1)}, s32[1024,1]{0,1:T(1,128)}, u32[]{:S(2)}) copy-start(s32[1024,1]{0,1:T(1,128)} %param.11) | copy-start | bytes 12292
  6.3 27.2 %collective-permute-start.4 = (bf16[192,2048]{1,0:T(8,128)(2,1)S(1)}, bf16[192,2048]{1,0:T(8,128)(2,1)}, u32[]{:S(2)}, u32[]{:S(2)}) collective-permute-start(bf16[192,2048]{1,0:T(8,128)(2,1)S(1)} %get-tuple-element.35), channel_id=1, source_target_pairs={{0,16},{8,24},{16,0},{24,8},{1,17},{9,25},{17,1},{25,9},{2,18},{10... | collective-permute-start | bytes 2359304 | tf_op jit(solution)/shard_map/ppermute | solution.py:25
  25.3 1.9 %collective-permute-start.1 = (f32[1024,128]{1,0:T(8,128)S(1)}, f32[1024,128]{1,0:T(8,128)S(1)}, u32[]{:S(2)}, u32[]{:S(2)}) collective-permute-start(f32[1024,128]{1,0:T(8,128)S(1)} %get-tuple-element.31), channel_id=1, source_target_pairs={{0,1},{1,0},{2,3},{3,2},{4,5},{5,4},{6,7},{7,6},{8,9},{9,8},{10,11... | collective-permute-start | bytes 1572872 | tf_op jit(solution)/shard_map/ppermute | solution.py:25
  27.4 16.3 %collective-permute-start.2 = (bf16[256,128]{1,0:T(8,128)(2,1)S(1)}, bf16[256,128]{1,0:T(8,128)(2,1)S(1)}, u32[]{:S(2)}, u32[]{:S(2)}) collective-permute-start(bf16[256,128]{1,0:T(8,128)(2,1)S(1)} %get-tuple-element.32), channel_id=1, source_target_pairs={{0,6},{1,7},{2,4},{3,5},{4,2},{5,3},{6,0},{7,1},{8,14},{9,15},{10,... | collective-permute-start | bytes 196616 | tf_op jit(solution)/shard_map/ppermute | solution.py:25
  31.1 8.7 %collective-permute-start.11 = (bf16[256,128]{1,0:T(8,128)(2,1)S(1)}, bf16[256,128]{1,0:T(8,128)(2,1)S(1)}, u32[]{:S(2)}, u32[]{:S(2)}) collective-permute-start(bf16[256,128]{1,0:T(8,128)(2,1)S(1)} %get-tuple-element.42), channel_id=1, source_target_pairs={{0,4},{1,5},{2,6},{3,7},{4,0},{5,1},{6,2},{7,3},{8,12},{9,13},{10,... | collective-permute-start | bytes 196616 | tf_op jit(solution)/shard_map/ppermute | solution.py:25
  31.1 6.0 %collective-permute-start.7 = (bf16[256,128]{1,0:T(8,128)(2,1)S(1)}, bf16[256,128]{1,0:T(8,128)(2,1)S(1)}, u32[]{:S(2)}, u32[]{:S(2)}) collective-permute-start(bf16[256,128]{1,0:T(8,128)(2,1)S(1)} %get-tuple-element.41), channel_id=1, source_target_pairs={{0,2},{1,3},{2,0},{3,1},{4,6},{5,7},{6,4},{7,5},{8,10},{9,11},{10,... | collective-permute-start | bytes 196616 | tf_op jit(solution)/shard_map/ppermute | solution.py:25
  32.9 7.7 %collective-permute-start.5 = (bf16[64,2048]{1,0:T(8,128)(2,1)S(1)}, bf16[64,2048]{1,0:T(8,128)(2,1)S(1)}, u32[]{:S(2)}, u32[]{:S(2)}) collective-permute-start(bf16[64,2048]{1,0:T(8,128)(2,1)S(1)} %slice.194), channel_id=1, source_target_pairs={{0,16},{8,24},{16,0},{24,8},{1,17},{9,25},{17,1},{25,9},{2,18},{10... | collective-permute-start | bytes 786440 | tf_op jit(solution)/shard_map/ppermute | solution.py:25
  34.4 9.3 %collective-permute-start.6 = (bf16[64,2048]{1,0:T(8,128)(2,1)S(1)}, bf16[64,2048]{1,0:T(8,128)(2,1)S(1)}, u32[]{:S(2)}, u32[]{:S(2)}) collective-permute-start(bf16[64,2048]{1,0:T(8,128)(2,1)S(1)} %slice.195), channel_id=1, source_target_pairs={{0,8},{8,0},{16,24},{24,16},{1,9},{9,1},{17,25},{25,17},{2,10},{10... | collective-permute-start | bytes 786440 | tf_op jit(solution)/shard_map/ppermute | solution.py:25
  37.1 10.4 %collective-permute-start.10 = (bf16[256,256]{1,0:T(8,128)(2,1)S(1)}, bf16[256,256]{1,0:T(8,128)(2,1)S(1)}, u32[]{:S(2)}, u32[]{:S(2)}) collective-permute-start(bf16[256,256]{1,0:T(8,128)(2,1)S(1)} %constant_dynamic-update-slice_fusion), channel_id=1, source_target_pairs={{0,24},{8,16},{16,8},{24,0},{1,25},{9,17},{17,9},{25,1},{2,26},{10... | collective-permute-start | bytes 393224 | tf_op jit(solution)/shard_map/ppermute | solution.py:25
  39.8 9.6 %collective-permute-start.8 = (bf16[256,256]{1,0:T(8,128)(2,1)S(1)}, bf16[256,256]{1,0:T(8,128)(2,1)S(1)}, u32[]{:S(2)}, u32[]{:S(2)}) collective-permute-start(bf16[256,256]{1,0:T(8,128)(2,1)S(1)} %constant_dynamic-update-slice_fusion), channel_id=1, source_target_pairs={{0,8},{8,0},{16,24},{24,16},{1,9},{9,1},{17,25},{25,17},{2,10},{10... | collective-permute-start | bytes 393224 | tf_op jit(solution)/shard_map/ppermute | solution.py:25
  40.6 8.8 %collective-permute-start.9 = (bf16[256,256]{1,0:T(8,128)(2,1)S(1)}, bf16[256,256]{1,0:T(8,128)(2,1)S(1)}, u32[]{:S(2)}, u32[]{:S(2)}) collective-permute-start(bf16[256,256]{1,0:T(8,128)(2,1)S(1)} %constant_dynamic-update-slice_fusion), channel_id=1, source_target_pairs={{0,16},{8,24},{16,0},{24,8},{1,17},{9,25},{17,1},{25,9},{2,18},{10... | collective-permute-start | bytes 393224 | tf_op jit(solution)/shard_map/ppermute | solution.py:25
  43.8 7.9 %collective-permute-start.12 = (bf16[256,256]{1,0:T(8,128)(2,1)S(1)}, bf16[256,256]{1,0:T(8,128)(2,1)S(1)}, u32[]{:S(2)}, u32[]{:S(2)}) collective-permute-start(bf16[256,256]{1,0:T(8,128)(2,1)S(1)} %constant_dynamic-update-slice_fusion.2), channel_id=1, source_target_pairs={{0,8},{8,0},{16,24},{24,16},{1,9},{9,1},{17,25},{25,17},{2,10},{10... | collective-permute-start | bytes 393224 | tf_op jit(solution)/shard_map/ppermute | solution.py:25
  43.9 7.8 %collective-permute-start.13 = (bf16[256,256]{1,0:T(8,128)(2,1)S(1)}, bf16[256,256]{1,0:T(8,128)(2,1)S(1)}, u32[]{:S(2)}, u32[]{:S(2)}) collective-permute-start(bf16[256,256]{1,0:T(8,128)(2,1)S(1)} %constant_dynamic-update-slice_fusion.2), channel_id=1, source_target_pairs={{0,16},{8,24},{16,0},{24,8},{1,17},{9,25},{17,1},{25,9},{2,18},{10... | collective-permute-start | bytes 393224 | tf_op jit(solution)/shard_map/ppermute | solution.py:25
  47.5 6.5 %collective-permute-start.14 = (bf16[256,256]{1,0:T(8,128)(2,1)S(1)}, bf16[256,256]{1,0:T(8,128)(2,1)S(1)}, u32[]{:S(2)}, u32[]{:S(2)}) collective-permute-start(bf16[256,256]{1,0:T(8,128)(2,1)S(1)} %constant_dynamic-update-slice_fusion.2), channel_id=1, source_target_pairs={{0,24},{8,16},{16,8},{24,0},{1,25},{9,17},{17,9},{25,1},{2,26},{10... | collective-permute-start | bytes 393224 | tf_op jit(solution)/shard_map/ppermute | solution.py:25
  49.3 7.8 %collective-permute-start.17 = (bf16[512,1024]{1,0:T(8,128)(2,1)S(1)}, bf16[512,1024]{1,0:T(8,128)(2,1)S(1)}, u32[]{:S(2)}, u32[]{:S(2)}) collective-permute-start(bf16[512,1024]{1,0:T(8,128)(2,1)S(1)} %pad_maximum_fusion.1), channel_id=1, source_target_pairs={{0,1},{1,0},{2,3},{3,2},{4,5},{5,4},{6,7},{7,6},{8,9},{9,8},{10,11... | collective-permute-start | bytes 3145736 | tf_op jit(solution)/shard_map/ppermute | solution.py:25
  49.4 11.8 %collective-permute-start.15 = (bf16[512,1024]{1,0:T(8,128)(2,1)S(1)}, bf16[512,1024]{1,0:T(8,128)(2,1)S(1)}, u32[]{:S(2)}, u32[]{:S(2)}) collective-permute-start(bf16[512,1024]{1,0:T(8,128)(2,1)S(1)} %pad_maximum_fusion), channel_id=1, source_target_pairs={{0,1},{1,0},{2,3},{3,2},{4,5},{5,4},{6,7},{7,6},{8,9},{9,8},{10,11... | collective-permute-start | bytes 3145736 | tf_op jit(solution)/shard_map/ppermute | solution.py:25
  57.6 11.1 %collective-permute-start.19 = (bf16[1024,128]{1,0:T(8,128)(2,1)S(1)}, bf16[1024,128]{1,0:T(8,128)(2,1)S(1)}, u32[]{:S(2)}, u32[]{:S(2)}) collective-permute-start(bf16[1024,128]{1,0:T(8,128)(2,1)S(1)} %fusion.3), channel_id=1, source_target_pairs={{0,6},{1,7},{2,4},{3,5},{4,2},{5,3},{6,0},{7,1},{8,14},{9,15},{10,... | collective-permute-start | bytes 786440 | tf_op jit(solution)/shard_map/ppermute | solution.py:25
  61.6 20.9 %collective-permute-start.16 = (bf16[1024,256]{1,0:T(8,128)(2,1)S(1)}, bf16[1024,256]{1,0:T(8,128)(2,1)S(1)}, u32[]{:S(2)}, u32[]{:S(2)}) collective-permute-start(bf16[1024,256]{1,0:T(8,128)(2,1)S(1)} %fusion), channel_id=1, source_target_pairs={{0,2},{1,3},{2,0},{3,1},{4,6},{5,7},{6,4},{7,5},{8,10},{9,11},{10,... | collective-permute-start | bytes 1572872 | tf_op jit(solution)/shard_map/ppermute | solution.py:25
  62.2 19.3 %collective-permute-start.18 = (bf16[1024,128]{1,0:T(8,128)(2,1)S(1)}, bf16[1024,128]{1,0:T(8,128)(2,1)S(1)}, u32[]{:S(2)}, u32[]{:S(2)}) collective-permute-start(bf16[1024,128]{1,0:T(8,128)(2,1)S(1)} %fusion.2), channel_id=1, source_target_pairs={{0,4},{1,5},{2,6},{3,7},{4,0},{5,1},{6,2},{7,3},{8,12},{9,13},{10,... | collective-permute-start | bytes 786440 | tf_op jit(solution)/shard_map/ppermute | solution.py:25
  82.6 13.3 %collective-permute-start.20 = (bf16[1024,128]{1,0:T(8,128)(2,1)S(1)}, bf16[1024,128]{1,0:T(8,128)(2,1)S(1)}, u32[]{:S(2)}, u32[]{:S(2)}) collective-permute-start(bf16[1024,128]{1,0:T(8,128)(2,1)S(1)} %fusion.5), channel_id=1, source_target_pairs={{0,4},{1,5},{2,6},{3,7},{4,0},{5,1},{6,2},{7,3},{8,12},{9,13},{10,... | collective-permute-start | bytes 786440 | tf_op jit(solution)/shard_map/ppermute | solution.py:25
  85.6 11.8 %copy-start.3 = (s32[2048,128]{1,0:T(8,128)S(1)}, s32[2048,128]{1,0:T(8,128)}, u32[]{:S(2)}) copy-start(s32[2048,128]{1,0:T(8,128)} %param.10) | copy-start | bytes 3145732
  85.6 11.3 %collective-permute-start.21 = (bf16[1024,128]{1,0:T(8,128)(2,1)S(1)}, bf16[1024,128]{1,0:T(8,128)(2,1)S(1)}, u32[]{:S(2)}, u32[]{:S(2)}) collective-permute-start(bf16[1024,128]{1,0:T(8,128)(2,1)S(1)} %fusion.4), channel_id=1, source_target_pairs={{0,2},{1,3},{2,0},{3,1},{4,6},{5,7},{6,4},{7,5},{8,10},{9,11},{10,... | collective-permute-start | bytes 786440 | tf_op jit(solution)/shard_map/ppermute | solution.py:25

commit v7 on v5

--- a/solution.py
+++ b/solution.py
@@ -10,10 +10,13 @@
 
 F32 = jnp.float32
 BF16 = jnp.bfloat16
-VMEM_LIMIT = 36 * 2**20
+VMEM_LIMIT = 50 * 2**20
 IN_ORDER = pltpu.CompilerParams(
     vmem_limit_bytes=VMEM_LIMIT, dimension_semantics=("arbitrary",)
 )
+
+
+SMALL = pltpu.CompilerParams(vmem_limit_bytes=16 * 2**20)
 
 
 def cost(flops, moved, exponents=0):
@@ -139,13 +142,30 @@
         out_shape=[
             jax.ShapeDtypeStruct((heights[out], wide), source.dtype) for out in sorted(heights)
         ],
-        compiler_params=pltpu.CompilerParams(vmem_limit_bytes=16 * 2**20),
+        compiler_params=SMALL,
         cost_estimate=cost(0, 2 * source.nbytes),
         name="spread",
     )(source)
 
 
-def exchange_rows(inputs, wide):
+def lay(sources, outputs):
+    def kernel(*refs):
+        for out_ref, (_, entries) in zip(refs[len(sources) :], outputs):
+            for source, rows, columns, first in entries:
+                height = rows.stop - rows.start
+                out_ref[first : first + height] = refs[source][rows, columns]
+
+    moved = sum(2 * math.prod(shape) * 2 for shape, _ in outputs)
+    return pl.pallas_call(
+        kernel,
+        out_shape=[jax.ShapeDtypeStruct(shape, sources[0].dtype) for shape, _ in outputs],
+        compiler_params=SMALL,
+        cost_estimate=cost(0, moved),
+        name="lay",
+    )(*sources)
+
+
+def send_rows(inputs, wide):
     rows = inputs.shape[0]
     groups = lax.axis_size("dp")
     if groups != 4:
@@ -158,9 +178,59 @@
         [(0, 0, 0, 0, rows), (1, 0, 1, 0, rows), (1, rows, 3, 0, half), (2, 0, 2, 0, rows),
          (2, rows, 3, half, rows)],
     )
-    left, right = swap(left, "dp", 1), swap(right, "dp", 2)
-    upper, lower = swap(left[rows:], "dp", 2), swap(right[rows:], "dp", 1)
-    return [own, left[:rows], right[:rows], jnp.concatenate([upper, lower], 0)]
+    return [own, swap(left, "dp", 1), swap(right, "dp", 2)]
+
+
+def pass_rows(parts, wide):
+    rows = parts[0].shape[0]
+    groups = lax.axis_size("dp")
+    if groups != 4:
+        return parts, [[(s, slice(0, rows))] for s in range(groups)]
+    own, left, right = parts
+    half = rows // 2
+    tail = slice(rows, rows + half)
+    every = slice(None)
+    upper, lower = lay(
+        [left, right],
+        [((half, wide), [(0, tail, every, 0)]), ((half, wide), [(1, tail, every, 0)])],
+    )
+    upper, lower = swap(upper, "dp", 2), swap(lower, "dp", 1)
+    whole, part = slice(0, rows), slice(0, half)
+    places = [[(0, whole)], [(1, whole)], [(2, whole)], [(3, part), (4, part)]]
+    return [own, left, right, upper, lower], places
+
+
+def product_kernel(jobs, depth, groups, own_ref, other_ref, *refs):
+    found, out_refs = refs[:groups], refs[groups:]
+    rows = found[0].shape[0] // 2
+
+    def pick(step, half):
+        columns = slice(step * depth, (step + 1) * depth)
+        return jnp.concatenate([f[half * rows : (half + 1) * rows, columns] for f in found], 0)
+
+    for steps, out_ref in zip(jobs, out_refs):
+        total = None
+        for half, ref in enumerate((own_ref, other_ref)):
+            grads = jnp.concatenate([pick(step, half) for step in steps], 1)
+            term = dot(ref[...], grads, 0, 0)
+            total = term if total is None else total + term
+        out_ref[...] = total.astype(out_ref.dtype)
+
+
+def products(pair, found, depth, jobs, dtypes):
+    groups = len(found)
+    tokens, wide = pair[0].shape
+    count = sum(len(steps) for steps in jobs)
+    return pl.pallas_call(
+        functools.partial(product_kernel, jobs, depth, groups),
+        out_shape=[
+            jax.ShapeDtypeStruct((wide, len(steps) * depth), dtype)
+            for steps, dtype in zip(jobs, dtypes)
+        ],
+        compiler_params=SMALL,
+        cost_estimate=cost(4 * tokens * wide * count * depth, 4 * tokens * wide),
+        name="products",
+    )(*pair, *found)
 
 
 def kv_kernel(rows, mine_ref, arrived_ref, mask_ref, *out_refs):
@@ -181,7 +251,7 @@
     return pl.pallas_call(
         functools.partial(kv_kernel, rows),
         out_shape=[jax.ShapeDtypeStruct((2 * rows, depth), BF16)] * count,
-        compiler_params=pltpu.CompilerParams(vmem_limit_bytes=8 * 2**20),
+        compiler_params=SMALL,
         cost_estimate=cost(0, 2 * mine.nbytes),
         name="kv_blocks",
     )(mine, arrived, mask)
@@ -195,52 +265,55 @@
     block = weight_mask.shape[0]
 
     other = swap(keys_values, "tensor", 1)
-    parts = exchange_rows(inputs, block)
+    parts = send_rows(inputs, block)
+
     query_grad, mine, theirs = attention(keys_values, other, queries, out_grad)
+    mine, parts = lax.optimization_barrier((mine, parts))
     arrived = swap(theirs, "tensor", 1)
     blocks = kv_blocks(mine, arrived, clip_mask, rows)
 
     blocks = [b if s == 0 else swap(b, "tensor", 2 * s) for s, b in enumerate(blocks)]
+    parts, places = pass_rows(parts, block)
     blocks, parts = lax.optimization_barrier((blocks, parts))
     order = sorted(range(chips), key=lambda s: [(s >> b) & 1 for b in range(8)])
     evens, odds = order[: chips // 2], order[chips // 2 :]
 
-    def gather(stacked):
-        found = [stacked if s == 0 else swap(stacked, "dp", s) for s in range(groups)]
-        return [jnp.concatenate([f[h * rows : (h + 1) * rows] for f in found], 0) for h in (0, 1)]
-
     wide = block // 2
-    cuts = []
+    outputs = []
     for cut in range(2):
-        own = jnp.concatenate([p[:, cut * wide : (cut + 1) * wide] for p in parts], 0)
-        cuts.append((own, swap(own, "tensor", 1)))
-    near, far = cuts
-
-    def product(pair, grads, place=None):
-        if place is not None:
-            grads = [g[:, place * depth : (place + 1) * depth] for g in grads]
-        return dot(pair[0], grads[0], 0, 0) + dot(pair[1], grads[1], 0, 0)
+        columns, entries, first = slice(cut * wide, (cut + 1) * wide), [], 0
+        for source in places:
+            for array, span in source:
+                entries.append((array, span, columns, first))
+                first += span.stop - span.start
+        outputs.append(((groups * rows, wide), entries))
+    near, far = [(own, swap(own, "tensor", 1)) for own in lay(parts, outputs)]
+
+    stacked = jnp.concatenate(blocks, 1)
+    found = [stacked if s == 0 else swap(stacked, "dp", s) for s in range(groups)]
 
     def send(value, step):
         return swap(value.astype(BF16), "tensor", 2 * step)
 
-    grads = gather(jnp.concatenate([blocks[s] for s in order], 1))
-    half = chips // 2 * depth
-    even, odd = [g[:, :half] for g in grads], [g[:, half:] for g in grads]
-    sent = send(product(near, odd), 1)
-    late = {s: product(far, odd, odds.index(s)).astype(BF16) for s in odds}
-    late.update({s: product(far, even, evens.index(s)).astype(BF16) for s in evens[1:]})
-    straight = [send(late[s], s) for s in range(2, chips)]
-    terms = [product(near, even), sent]
-    columns, bit = half, 1
+    away = list(range(2, chips))
+    straight = products(far, found, depth, [(s,) for s in away], [BF16] * len(away))
+    straight, found = lax.optimization_barrier((straight, found))
+    straight = [send(value, s) for value, s in zip(straight, away)]
+    (first,) = products(near, found, depth, [tuple(odds)], [BF16])
+    sent = send(first, 1)
+    (even,) = products(near, found, depth, [tuple(evens)], [F32])
+    own, nearest = products(far, found, depth, [(0,), (1,)], [F32, BF16])
+    sent, straight = lax.optimization_barrier((sent, straight))
+    terms = [even, sent]
+    columns, bit = chips // 2 * depth, 1
     while columns > depth:
         columns, bit = columns // 2, bit * 2
         away = sum(t[:, columns : 2 * columns].astype(F32) for t in terms).astype(BF16)
         terms.append(send(away, bit))
-    nearest, straight, _ = lax.optimization_barrier((late[1], straight, away))
+    nearest, _ = lax.optimization_barrier((nearest, away))
     straight.append(send(nearest, 1))
     upper = sum(t[:, :depth].astype(F32) for t in terms)
-    lower = product(far, even, 0) + sum(t.astype(F32) for t in straight)
+    lower = own + sum(t.astype(F32) for t in straight)
     summed = jnp.concatenate([upper, lower], 0)
     weight_grad = jnp.where(weight_mask == 1, summed, 0.0)
     return (query_grad, weight_grad)

time: 95.3 us -> 98.5 us (1.034)
  Pallas kernels: 17.2 us -> 25.2 us
  matrix products: 5.77 us -> 0 us
  waiting for transfers between devices: 41.4 us -> 44.7 us
  local copies, waits for them, and re-layouts: 5.08 us -> 1.9 us
  starting transfers between devices: 22.2 us -> 24.3 us
  other arithmetic: 2.49 us -> 1.32 us
    pallas_call x0 -> x6, Pallas kernels: none -> 6.1 us  [the longest x4 4.18 us: products(): pl.pallas_call(functools.partial(product_kernel, jobs, depth, groups), ou...]
    dot_general x12 -> x0, matrix products: 5.77 us -> none  [dot(): return lax.dot_general(left, right, dims, preferred_element_type=F32)]
    ppermute x19, waiting for transfers between devices: 41.4 us -> 44.7 us  [swap(): return lax.ppermute(value, axis, pairs)]
    ppermute x19, starting transfers between devices: 22.2 us -> 24.3 us  [swap(): return lax.ppermute(value, axis, pairs)]
    slice x12 -> x0, local copies, waits for them, and re-layouts: 1.77 us -> none  [the longest x2 1.52 us: exchange_rows(): upper, lower = (swap(left[rows:], 'dp', 2), swap(right[rows:], 'dp', 1))]
    unnamed x20 -> x14, local copies, waits for them, and re-layouts: 3.29 us -> 1.88 us
    concatenate x4 -> x0, other arithmetic: 1.28 us -> none  [the longest x1 1.07 us: exchange_rows(): return [own, left[:rows], right[:rows], jnp.concatenate([upper, lower], 0)]]
    pallas_call x1, Pallas kernels: 0.22 us -> 1.24 us  [kv_blocks(): pl.pallas_call(functools.partial(kv_kernel, rows), out_shape=[jax.ShapeDt...]
  transfers between devices with their start and end apart: 19 -> 19, of which waited for: 10 -> 10; matrix products, arithmetic and copies ran while one was open for 9% -> 0% of each run, Pallas kernels for 18% -> 24%
where the time goes in v7:
time: 98.5 us; the launch traced here: 98.2 us
  waiting for transfers between devices  44.7 us (45%)
  Pallas kernels  25.2 us (26%)
  starting transfers between devices  24.3 us (25%)
  local copies, waits for them, and re-layouts  1.9 us (2%)
  other arithmetic  1.32 us (1%)
    ppermute x19, waiting for transfers between devices, swap(): return lax.ppermute(value, axis, pairs)  44.7 us
    ppermute x19, starting transfers between devices, swap(): return lax.ppermute(value, axis, pairs)  24.3 us
    pallas_call x1, Pallas kernels, attention(): pl.pallas_call(functools.partial(attention_kernel, height), grid=(width /...  17.7 us
    pallas_call x4, Pallas kernels, products(): pl.pallas_call(functools.partial(product_kernel, jobs, depth, groups), ou...  4.18 us
  transfers between devices with their start and end apart: 19, of which 10 were waited for; matrix products, arithmetic and copies ran while one was open for 0% of the time, Pallas kernels for 24%

profile of v7, /device:TPU:0, one launch (start us, length us, event | category | flops | bytes accessed | tf_op | source)
XLA Modules:
  0.0 98.2 jit_solution(15046988387717395240)
XLA Ops:
  0.6 0.5 collective-permute-start
  1.1 1.6 %copy-done = bf16[128,8192]{1,0:T(8,128)(2,1)S(1)} copy-done((bf16[128,8192]{1,0:T(8,128)(2,1)S(1)}, bf16[128,8192]{1,0:T(8,128)(2,1)}, u32[]{:S(2)}) %copy-start) | copy-done | bytes 2097176
  2.7 0.1 spread.1
  2.9 2.6 %collective-permute-start.1 = (bf16[192,2048]{1,0:T(8,128)(2,1)S(1)}, bf16[192,2048]{1,0:T(8,128)(2,1)S(1)}, u32[]{:S(2)}, u32[]{:S(2)}) collective-permute-start(bf16[192,2048]{1,0:T(8,128)(2,1)S(1)} %get-tuple-element.46), channel_id=1, source_target_pairs={{0,8},{8,0},{16,24},{24,16},{1,9},{9,1},{17,25},{25,17},{2,10},{10... | collective-permute-start | bytes 2359304 | tf_op jit(solution)/shard_map/ppermute | solution.py:28
  5.4 1.5 %collective-permute-start.2 = (bf16[192,2048]{1,0:T(8,128)(2,1)S(1)}, bf16[192,2048]{1,0:T(8,128)(2,1)S(1)}, u32[]{:S(2)}, u32[]{:S(2)}) collective-permute-start(bf16[192,2048]{1,0:T(8,128)(2,1)S(1)} %get-tuple-element.47), channel_id=1, source_target_pairs={{0,16},{8,24},{16,0},{24,8},{1,17},{9,25},{17,1},{25,9},{2,18},{10... | collective-permute-start | bytes 2359304 | tf_op jit(solution)/shard_map/ppermute | solution.py:28
  7.0 0.0 collective-permute-done.other_ref
  7.0 17.7 %attention.1 = (bf16[1024,768]{1,0:T(8,128)(2,1)}, f32[1024,128]{1,0:T(8,128)S(1)}, f32[1024,128]{1,0:T(8,128)}) custom-call(bf16[1024,128]{1,0:T(8,128)(2,1)S(1)} %copy-done.2, bf16[1024,128]{1,0:T(8,128)(2,1)S(1)} %collective-permute-done.other_ref, bf16[1024,768]{1,0:T(8,128)(2,1)S(1)} %copy-done.1, bf16[1024,768]{1,0:T(8,128)(2,1)} %up_ref.1), custom_call_target="tpu_custom_call" | custom-call | flops 16106127360 | bytes 9437184 | tf_op jit(solution)/shard_map/attention/pallas_call | solution.py:106
  24.7 0.0 collective-permute-start.3
  24.7 0.4 collective-permute-done.2.refs_1_.refs_2_
  25.1 0.8 lay.2
  26.0 1.5 %collective-permute-start.7 = (bf16[64,2048]{1,0:T(8,128)(2,1)}, bf16[64,2048]{1,0:T(8,128)(2,1)S(1)}, u32[]{:S(2)}, u32[]{:S(2)}) collective-permute-start(bf16[64,2048]{1,0:T(8,128)(2,1)} %get-tuple-element.57), channel_id=1, source_target_pairs={{0,16},{8,24},{16,0},{24,8},{1,17},{9,25},{17,1},{25,9},{2,18},{10... | collective-permute-start | bytes 786440 | tf_op jit(solution)/shard_map/ppermute | solution.py:28
  27.5 0.5 collective-permute-start.8
  28.0 0.2 copy.8.mask_ref
  28.2 1.2 %kv_blocks.1 = (bf16[256,128]{1,0:T(8,128)(2,1)S(1)}, bf16[256,128]{1,0:T(8,128)(2,1)S(1)}, bf16[256,128]{1,0:T(8,128)(2,1)S(1)}, bf16[256,128]{1,0:T(8,128)(2,1)S(1)}) custom-call(f32[1024,128]{1,0:T(8,128)S(1)} %get-tuple-element.48.mine_ref, f32[1024,128]{1,0:T(8,128)} %collective-permute-done.3.arrived_ref, s32[1024,1]{1,0:T(8,128)S(1)} %copy.8.mask_ref), custom_call_target="tpu_custom_call" | custom-call | bytes 1048576 | tf_op jit(solution)/shard_map/kv_blocks/pallas_call | solution.py:251
  29.5 1.6 %collective-permute-start.4 = (bf16[256,128]{1,0:T(8,128)(2,1)S(1)}, bf16[256,128]{1,0:T(8,128)(2,1)S(1)}, u32[]{:S(2)}, u32[]{:S(2)}) collective-permute-start(bf16[256,128]{1,0:T(8,128)(2,1)S(1)} %get-tuple-element.51), channel_id=1, source_target_pairs={{0,2},{1,3},{2,0},{3,1},{4,6},{5,7},{6,4},{7,5},{8,10},{9,11},{10,... | collective-permute-start | bytes 196616 | tf_op jit(solution)/shard_map/ppermute | solution.py:28
  31.1 2.6 %collective-permute-start.5 = (bf16[256,128]{1,0:T(8,128)(2,1)S(1)}, bf16[256,128]{1,0:T(8,128)(2,1)S(1)}, u32[]{:S(2)}, u32[]{:S(2)}) collective-permute-start(bf16[256,128]{1,0:T(8,128)(2,1)S(1)} %get-tuple-element.52), channel_id=1, source_target_pairs={{0,4},{1,5},{2,6},{3,7},{4,0},{5,1},{6,2},{7,3},{8,12},{9,13},{10,... | collective-permute-start | bytes 196616 | tf_op jit(solution)/shard_map/ppermute | solution.py:28
  33.7 0.2 collective-permute-start.6
  33.9 0.5 collective-permute-done.4
  34.5 3.2 %collective-permute-done.5 = bf16[256,128]{1,0:T(8,128)(2,1)S(1)} collective-permute-done((bf16[256,128]{1,0:T(8,128)(2,1)S(1)}, bf16[256,128]{1,0:T(8,128)(2,1)S(1)}, u32[]{:S(2)}, u32[]{:S(2)}) %collective-permute-start.5) | collective-permute-done | bytes 65568 | tf_op jit(solution)/shard_map/ppermute | solution.py:28
  37.7 2.1 %collective-permute-done.6 = bf16[256,128]{1,0:T(8,128)(2,1)S(1)} collective-permute-done((bf16[256,128]{1,0:T(8,128)(2,1)S(1)}, bf16[256,128]{1,0:T(8,128)(2,1)S(1)}, u32[]{:S(2)}, u32[]{:S(2)}) %collective-permute-start.6) | collective-permute-done | bytes 65568 | tf_op jit(solution)/shard_map/ppermute | solution.py:28
  39.8 0.0 collective-permute-done.7.refs_3_
  39.8 0.0 collective-permute-done.8.refs_4_
  39.8 1.1 %lay.3 = (bf16[512,1024]{1,0:T(8,128)(2,1)S(1)}, bf16[512,1024]{1,0:T(8,128)(2,1)S(1)}) custom-call(bf16[128,2048]{1,0:T(8,128)(2,1)S(1)} %get-tuple-element.59.refs_0_, bf16[192,2048]{1,0:T(8,128)(2,1)S(1)} %collective-permute-done.1.refs_0_.refs_1_, bf16[192,2048]{1,0:T(8,128)(2,1)S(1)} %collective-permute-done.2.refs_1_.refs_2_, ...), custom_call_target="tpu_custom_call" | custom-call | bytes 4194304 | tf_op jit(solution)/shard_map/lay/pallas_call | solution.py:159
  40.9 0.1 collective-permute-start.10
  41.0 0.5 collective-permute-start.9
  41.6 1.6 %collective-permute-start.11 = (bf16[256,512]{1,0:T(8,128)(2,1)S(1)}, bf16[256,512]{1,0:T(8,128)(2,1)S(1)}, u32[]{:S(2)}, u32[]{:S(2)}) collective-permute-start(bf16[256,512]{1,0:T(8,128)(2,1)S(1)} %constant_dynamic-update-slice_fusion.refs_0_), channel_id=1, source_target_pairs={{0,8},{8,0},{16,24},{24,16},{1,9},{9,1},{17,25},{25,17},{2,10},{10... | collective-permute-start | bytes 786440 | tf_op jit(solution)/shard_map/ppermute | solution.py:28
  43.1 0.5 collective-permute-start.12
  43.6 1.5 %collective-permute-start.13 = (bf16[256,512]{1,0:T(8,128)(2,1)S(1)}, bf16[256,512]{1,0:T(8,128)(2,1)S(1)}, u32[]{:S(2)}, u32[]{:S(2)}) collective-permute-start(bf16[256,512]{1,0:T(8,128)(2,1)S(1)} %constant_dynamic-update-slice_fusion.refs_0_), channel_id=1, source_target_pairs={{0,24},{8,16},{16,8},{24,0},{1,25},{9,17},{17,9},{25,1},{2,26},{10... | collective-permute-start | bytes 786440 | tf_op jit(solution)/shard_map/ppermute | solution.py:28
  45.1 5.7 %collective-permute-done.11.refs_1_ = bf16[256,512]{1,0:T(8,128)(2,1)S(1)} collective-permute-done((bf16[256,512]{1,0:T(8,128)(2,1)S(1)}, bf16[256,512]{1,0:T(8,128)(2,1)S(1)}, u32[]{:S(2)}, u32[]{:S(2)}) %collective-permute-start.11) | collective-permute-done | bytes 262176 | tf_op jit(solution)/shard_map/ppermute | solution.py:28
  50.8 6.0 %collective-permute-done.12.refs_2_ = bf16[256,512]{1,0:T(8,128)(2,1)S(1)} collective-permute-done((bf16[256,512]{1,0:T(8,128)(2,1)S(1)}, bf16[256,512]{1,0:T(8,128)(2,1)S(1)}, u32[]{:S(2)}, u32[]{:S(2)}) %collective-permute-start.12) | collective-permute-done | bytes 262176 | tf_op jit(solution)/shard_map/ppermute | solution.py:28
  56.7 1.3 %products.4 = (bf16[1024,128]{1,0:T(8,128)(2,1)S(1)}, bf16[1024,128]{1,0:T(8,128)(2,1)S(1)}) custom-call(bf16[512,1024]{1,0:T(8,128)(2,1)S(1)} %get-tuple-element.65.own_ref, bf16[512,1024]{1,0:T(8,128)(2,1)S(1)} %collective-permute-done.10.other_ref, bf16[256,512]{1,0:T(8,128)(2,1)S(1)} %constant_dynamic-update-slice_fusion.refs_0_, ...), custom_call_target="tpu_custom_call" | custom-call | flops 536870912 | bytes 2097152 | tf_op jit(solution)/shard_map/products/pallas_call | solution.py:224
  58.1 0.8 products.6
  58.9 0.1 collective-permute-start.14
  58.9 1.5 %collective-permute-start.15 = (bf16[1024,128]{1,0:T(8,128)(2,1)S(1)}, bf16[1024,128]{1,0:T(8,128)(2,1)S(1)}, u32[]{:S(2)}, u32[]{:S(2)}) collective-permute-start(bf16[1024,128]{1,0:T(8,128)(2,1)S(1)} %get-tuple-element.76), channel_id=1, source_target_pairs={{0,4},{1,5},{2,6},{3,7},{4,0},{5,1},{6,2},{7,3},{8,12},{9,13},{10,... | collective-permute-start | bytes 786440 | tf_op jit(solution)/shard_map/ppermute | solution.py:28
  60.4 2.9 %collective-permute-start.16 = (bf16[1024,128]{1,0:T(8,128)(2,1)S(1)}, bf16[1024,128]{1,0:T(8,128)(2,1)S(1)}, u32[]{:S(2)}, u32[]{:S(2)}) collective-permute-start(bf16[1024,128]{1,0:T(8,128)(2,1)S(1)} %get-tuple-element.77), channel_id=1, source_target_pairs={{0,6},{1,7},{2,4},{3,5},{4,2},{5,3},{6,0},{7,1},{8,14},{9,15},{10,... | collective-permute-start | bytes 786440 | tf_op jit(solution)/shard_map/ppermute | solution.py:28
  63.3 0.8 products.5
  64.1 12.9 %collective-permute-done.15 = bf16[1024,128]{1,0:T(8,128)(2,1)S(1)} collective-permute-done((bf16[1024,128]{1,0:T(8,128)(2,1)S(1)}, bf16[1024,128]{1,0:T(8,128)(2,1)S(1)}, u32[]{:S(2)}, u32[]{:S(2)}) %collective-permute-start.15) | collective-permute-done | bytes 262176 | tf_op jit(solution)/shard_map/ppermute | solution.py:28
  77.0 6.1 %collective-permute-done.16 = bf16[1024,128]{1,0:T(8,128)(2,1)S(1)} collective-permute-done((bf16[1024,128]{1,0:T(8,128)(2,1)S(1)}, bf16[1024,128]{1,0:T(8,128)(2,1)S(1)}, u32[]{:S(2)}, u32[]{:S(2)}) %collective-permute-start.16) | collective-permute-done | bytes 262176 | tf_op jit(solution)/shard_map/ppermute | solution.py:28
  83.1 0.1 fusion
  83.2 4.6 %collective-permute-start.17 = (bf16[1024,128]{1,0:T(8,128)(2,1)S(1)}, bf16[1024,128]{1,0:T(8,128)(2,1)S(1)}, u32[]{:S(2)}, u32[]{:S(2)}) collective-permute-start(bf16[1024,128]{1,0:T(8,128)(2,1)S(1)} %fusion), channel_id=1, source_target_pairs={{0,4},{1,5},{2,6},{3,7},{4,0},{5,1},{6,2},{7,3},{8,12},{9,13},{10,... | collective-permute-start | bytes 786440 | tf_op jit(solution)/shard_map/ppermute | solution.py:28
  87.8 1.3 %products.7 = (f32[1024,128]{1,0:T(8,128)S(1)}, bf16[1024,128]{1,0:T(8,128)(2,1)S(1)}) custom-call(bf16[512,1024]{1,0:T(8,128)(2,1)S(1)} %get-tuple-element.65.own_ref, bf16[512,1024]{1,0:T(8,128)(2,1)S(1)} %collective-permute-done.10.other_ref, bf16[256,512]{1,0:T(8,128)(2,1)S(1)} %constant_dynamic-update-slice_fusion.refs_0_, ...), custom_call_target="tpu_custom_call" | custom-call | flops 536870912 | bytes 2097152 | tf_op jit(solution)/shard_map/products/pallas_call | solution.py:224
  89.0 0.0 copy-start.3
  89.1 0.1 collective-permute-start.18
  89.1 5.9 %collective-permute-done.17 = bf16[1024,128]{1,0:T(8,128)(2,1)S(1)} collective-permute-done((bf16[1024,128]{1,0:T(8,128)(2,1)S(1)}, bf16[1024,128]{1,0:T(8,128)(2,1)S(1)}, u32[]{:S(2)}, u32[]{:S(2)}) %collective-permute-start.17) | collective-permute-done | bytes 262176 | tf_op jit(solution)/shard_map/ppermute | solution.py:28
  95.1 0.1 fusion.1
  95.1 1.9 %collective-permute-done.18 = bf16[1024,128]{1,0:T(8,128)(2,1)S(1)} collective-permute-done((bf16[1024,128]{1,0:T(8,128)(2,1)S(1)}, bf16[1024,128]{1,0:T(8,128)(2,1)S(1)}, u32[]{:S(2)}, u32[]{:S(2)}) %collective-permute-start.18) | collective-permute-done | bytes 262176 | tf_op jit(solution)/shard_map/ppermute | solution.py:28
  97.0 0.1 add_add_fusion
  97.1 1.1 %maximum_select_fusion = f32[2048,128]{1,0:T(8,128)} fusion(f32[1024,128]{1,0:T(8,128)S(1)} %add_add_fusion, f32[1024,128]{1,0:T(8,128)S(1)} %fusion.1, s32[2048,128]{1,0:T(8,128)S(1)} %copy-done.3), kind=kLoop, calls=%fused_computation | loop fusion | flops 786432 | bytes 3145728 | tf_op jit(solution)/shard_map/jit(_where)/select_n | solution.py:318
  (18 shorter events, 0.1 us)
Async XLA Ops:
  0.6 6.3 %collective-permute-start = (bf16[1024,128]{1,0:T(8,128)(2,1)}, bf16[1024,128]{1,0:T(8,128)(2,1)S(1)}, u32[]{:S(2)}, u32[]{:S(2)}) collective-permute-start(bf16[1024,128]{1,0:T(8,128)(2,1)} %own_ref.1), channel_id=1, source_target_pairs={{0,1},{1,0},{2,3},{3,2},{4,5},{5,4},{6,7},{7,6},{8,9},{9,8},{10,11... | collective-permute-start | bytes 786440 | tf_op jit(solution)/shard_map/ppermute | solution.py:28
  1.1 1.6 %copy-start = (bf16[128,8192]{1,0:T(8,128)(2,1)S(1)}, bf16[128,8192]{1,0:T(8,128)(2,1)}, u32[]{:S(2)}) copy-start(bf16[128,8192]{1,0:T(8,128)(2,1)} %source_ref.1) | copy-start | bytes 6291460
  2.7 4.2 %copy-start.1 = (bf16[1024,768]{1,0:T(8,128)(2,1)S(1)}, bf16[1024,768]{1,0:T(8,128)(2,1)}, u32[]{:S(2)}) copy-start(bf16[1024,768]{1,0:T(8,128)(2,1)} %q_ref.1) | copy-start | bytes 4718596
  2.7 4.2 %copy-start.2 = (bf16[1024,128]{1,0:T(8,128)(2,1)S(1)}, bf16[1024,128]{1,0:T(8,128)(2,1)}, u32[]{:S(2)}) copy-start(bf16[1024,128]{1,0:T(8,128)(2,1)} %own_ref.1) | copy-start | bytes 786436
  2.9 21.8 %collective-permute-start.1 = (bf16[192,2048]{1,0:T(8,128)(2,1)S(1)}, bf16[192,2048]{1,0:T(8,128)(2,1)S(1)}, u32[]{:S(2)}, u32[]{:S(2)}) collective-permute-start(bf16[192,2048]{1,0:T(8,128)(2,1)S(1)} %get-tuple-element.46), channel_id=1, source_target_pairs={{0,8},{8,0},{16,24},{24,16},{1,9},{9,1},{17,25},{25,17},{2,10},{10... | collective-permute-start | bytes 2359304 | tf_op jit(solution)/shard_map/ppermute | solution.py:28
  5.4 19.7 %collective-permute-start.2 = (bf16[192,2048]{1,0:T(8,128)(2,1)S(1)}, bf16[192,2048]{1,0:T(8,128)(2,1)S(1)}, u32[]{:S(2)}, u32[]{:S(2)}) collective-permute-start(bf16[192,2048]{1,0:T(8,128)(2,1)S(1)} %get-tuple-element.47), channel_id=1, source_target_pairs={{0,16},{8,24},{16,0},{24,8},{1,17},{9,25},{17,1},{25,9},{2,18},{10... | collective-permute-start | bytes 2359304 | tf_op jit(solution)/shard_map/ppermute | solution.py:28
  24.7 3.3 %copy-start.4 = (s32[1024,1]{0,1:T(1,128)S(1)}, s32[1024,1]{0,1:T(1,128)}, u32[]{:S(2)}) copy-start(s32[1024,1]{0,1:T(1,128)} %param.11) | copy-start | bytes 12292
  24.7 3.5 %collective-permute-start.3 = (f32[1024,128]{1,0:T(8,128)}, f32[1024,128]{1,0:T(8,128)}, u32[]{:S(2)}, u32[]{:S(2)}) collective-permute-start(f32[1024,128]{1,0:T(8,128)} %get-tuple-element.49), channel_id=1, source_target_pairs={{0,1},{1,0},{2,3},{3,2},{4,5},{5,4},{6,7},{7,6},{8,9},{9,8},{10,11... | collective-permute-start | bytes 1572872 | tf_op jit(solution)/shard_map/ppermute | solution.py:28
  26.0 13.8 %collective-permute-start.7 = (bf16[64,2048]{1,0:T(8,128)(2,1)}, bf16[64,2048]{1,0:T(8,128)(2,1)S(1)}, u32[]{:S(2)}, u32[]{:S(2)}) collective-permute-start(bf16[64,2048]{1,0:T(8,128)(2,1)} %get-tuple-element.57), channel_id=1, source_target_pairs={{0,16},{8,24},{16,0},{24,8},{1,17},{9,25},{17,1},{25,9},{2,18},{10... | collective-permute-start | bytes 786440 | tf_op jit(solution)/shard_map/ppermute | solution.py:28
  27.5 12.3 %collective-permute-start.8 = (bf16[64,2048]{1,0:T(8,128)(2,1)}, bf16[64,2048]{1,0:T(8,128)(2,1)}, u32[]{:S(2)}, u32[]{:S(2)}) collective-permute-start(bf16[64,2048]{1,0:T(8,128)(2,1)} %get-tuple-element.58), channel_id=1, source_target_pairs={{0,8},{8,0},{16,24},{24,16},{1,9},{9,1},{17,25},{25,17},{2,10},{10... | collective-permute-start | bytes 786440 | tf_op jit(solution)/shard_map/ppermute | solution.py:28
  29.5 5.0 %collective-permute-start.4 = (bf16[256,128]{1,0:T(8,128)(2,1)S(1)}, bf16[256,128]{1,0:T(8,128)(2,1)S(1)}, u32[]{:S(2)}, u32[]{:S(2)}) collective-permute-start(bf16[256,128]{1,0:T(8,128)(2,1)S(1)} %get-tuple-element.51), channel_id=1, source_target_pairs={{0,2},{1,3},{2,0},{3,1},{4,6},{5,7},{6,4},{7,5},{8,10},{9,11},{10,... | collective-permute-start | bytes 196616 | tf_op jit(solution)/shard_map/ppermute | solution.py:28
  31.1 6.6 %collective-permute-start.5 = (bf16[256,128]{1,0:T(8,128)(2,1)S(1)}, bf16[256,128]{1,0:T(8,128)(2,1)S(1)}, u32[]{:S(2)}, u32[]{:S(2)}) collective-permute-start(bf16[256,128]{1,0:T(8,128)(2,1)S(1)} %get-tuple-element.52), channel_id=1, source_target_pairs={{0,4},{1,5},{2,6},{3,7},{4,0},{5,1},{6,2},{7,3},{8,12},{9,13},{10,... | collective-permute-start | bytes 196616 | tf_op jit(solution)/shard_map/ppermute | solution.py:28
  33.7 6.1 %collective-permute-start.6 = (bf16[256,128]{1,0:T(8,128)(2,1)S(1)}, bf16[256,128]{1,0:T(8,128)(2,1)S(1)}, u32[]{:S(2)}, u32[]{:S(2)}) collective-permute-start(bf16[256,128]{1,0:T(8,128)(2,1)S(1)} %get-tuple-element.53), channel_id=1, source_target_pairs={{0,6},{1,7},{2,4},{3,5},{4,2},{5,3},{6,0},{7,1},{8,14},{9,15},{10,... | collective-permute-start | bytes 196616 | tf_op jit(solution)/shard_map/ppermute | solution.py:28
  40.9 15.9 %collective-permute-start.10 = (bf16[512,1024]{1,0:T(8,128)(2,1)S(1)}, bf16[512,1024]{1,0:T(8,128)(2,1)S(1)}, u32[]{:S(2)}, u32[]{:S(2)}) collective-permute-start(bf16[512,1024]{1,0:T(8,128)(2,1)S(1)} %get-tuple-element.65.own_ref), channel_id=1, source_target_pairs={{0,1},{1,0},{2,3},{3,2},{4,5},{5,4},{6,7},{7,6},{8,9},{9,8},{10,11... | collective-permute-start | bytes 3145736 | tf_op jit(solution)/shard_map/ppermute | solution.py:28
  41.0 17.1 %collective-permute-start.9 = (bf16[512,1024]{1,0:T(8,128)(2,1)S(1)}, bf16[512,1024]{1,0:T(8,128)(2,1)S(1)}, u32[]{:S(2)}, u32[]{:S(2)}) collective-permute-start(bf16[512,1024]{1,0:T(8,128)(2,1)S(1)} %get-tuple-element.64.own_ref), channel_id=1, source_target_pairs={{0,1},{1,0},{2,3},{3,2},{4,5},{5,4},{6,7},{7,6},{8,9},{9,8},{10,11... | collective-permute-start | bytes 3145736 | tf_op jit(solution)/shard_map/ppermute | solution.py:28
  41.6 9.2 %collective-permute-start.11 = (bf16[256,512]{1,0:T(8,128)(2,1)S(1)}, bf16[256,512]{1,0:T(8,128)(2,1)S(1)}, u32[]{:S(2)}, u32[]{:S(2)}) collective-permute-start(bf16[256,512]{1,0:T(8,128)(2,1)S(1)} %constant_dynamic-update-slice_fusion.refs_0_), channel_id=1, source_target_pairs={{0,8},{8,0},{16,24},{24,16},{1,9},{9,1},{17,25},{25,17},{2,10},{10... | collective-permute-start | bytes 786440 | tf_op jit(solution)/shard_map/ppermute | solution.py:28
  43.1 13.6 %collective-permute-start.12 = (bf16[256,512]{1,0:T(8,128)(2,1)S(1)}, bf16[256,512]{1,0:T(8,128)(2,1)S(1)}, u32[]{:S(2)}, u32[]{:S(2)}) collective-permute-start(bf16[256,512]{1,0:T(8,128)(2,1)S(1)} %constant_dynamic-update-slice_fusion.refs_0_), channel_id=1, source_target_pairs={{0,16},{8,24},{16,0},{24,8},{1,17},{9,25},{17,1},{25,9},{2,18},{10... | collective-permute-start | bytes 786440 | tf_op jit(solution)/shard_map/ppermute | solution.py:28
  43.6 13.1 %collective-permute-start.13 = (bf16[256,512]{1,0:T(8,128)(2,1)S(1)}, bf16[256,512]{1,0:T(8,128)(2,1)S(1)}, u32[]{:S(2)}, u32[]{:S(2)}) collective-permute-start(bf16[256,512]{1,0:T(8,128)(2,1)S(1)} %constant_dynamic-update-slice_fusion.refs_0_), channel_id=1, source_target_pairs={{0,24},{8,16},{16,8},{24,0},{1,25},{9,17},{17,9},{25,1},{2,26},{10... | collective-permute-start | bytes 786440 | tf_op jit(solution)/shard_map/ppermute | solution.py:28
  58.9 24.2 %collective-permute-start.14 = (bf16[1024,256]{1,0:T(8,128)(2,1)S(1)}, bf16[1024,256]{1,0:T(8,128)(2,1)S(1)}, u32[]{:S(2)}, u32[]{:S(2)}) collective-permute-start(bf16[1024,256]{1,0:T(8,128)(2,1)S(1)} %products.6), channel_id=1, source_target_pairs={{0,2},{1,3},{2,0},{3,1},{4,6},{5,7},{6,4},{7,5},{8,10},{9,11},{10,... | collective-permute-start | bytes 1572872 | tf_op jit(solution)/shard_map/ppermute | solution.py:28
  58.9 18.0 %collective-permute-start.15 = (bf16[1024,128]{1,0:T(8,128)(2,1)S(1)}, bf16[1024,128]{1,0:T(8,128)(2,1)S(1)}, u32[]{:S(2)}, u32[]{:S(2)}) collective-permute-start(bf16[1024,128]{1,0:T(8,128)(2,1)S(1)} %get-tuple-element.76), channel_id=1, source_target_pairs={{0,4},{1,5},{2,6},{3,7},{4,0},{5,1},{6,2},{7,3},{8,12},{9,13},{10,... | collective-permute-start | bytes 786440 | tf_op jit(solution)/shard_map/ppermute | solution.py:28
  60.4 22.7 %collective-permute-start.16 = (bf16[1024,128]{1,0:T(8,128)(2,1)S(1)}, bf16[1024,128]{1,0:T(8,128)(2,1)S(1)}, u32[]{:S(2)}, u32[]{:S(2)}) collective-permute-start(bf16[1024,128]{1,0:T(8,128)(2,1)S(1)} %get-tuple-element.77), channel_id=1, source_target_pairs={{0,6},{1,7},{2,4},{3,5},{4,2},{5,3},{6,0},{7,1},{8,14},{9,15},{10,... | collective-permute-start | bytes 786440 | tf_op jit(solution)/shard_map/ppermute | solution.py:28
  83.2 11.9 %collective-permute-start.17 = (bf16[1024,128]{1,0:T(8,128)(2,1)S(1)}, bf16[1024,128]{1,0:T(8,128)(2,1)S(1)}, u32[]{:S(2)}, u32[]{:S(2)}) collective-permute-start(bf16[1024,128]{1,0:T(8,128)(2,1)S(1)} %fusion), channel_id=1, source_target_pairs={{0,4},{1,5},{2,6},{3,7},{4,0},{5,1},{6,2},{7,3},{8,12},{9,13},{10,... | collective-permute-start | bytes 786440 | tf_op jit(solution)/shard_map/ppermute | solution.py:28
  89.0 8.1 %copy-start.3 = (s32[2048,128]{1,0:T(8,128)S(1)}, s32[2048,128]{1,0:T(8,128)}, u32[]{:S(2)}) copy-start(s32[2048,128]{1,0:T(8,128)} %param.10) | copy-start | bytes 3145732
  89.1 8.0 %collective-permute-start.18 = (bf16[1024,128]{1,0:T(8,128)(2,1)S(1)}, bf16[1024,128]{1,0:T(8,128)(2,1)S(1)}, u32[]{:S(2)}, u32[]{:S(2)}) collective-permute-start(bf16[1024,128]{1,0:T(8,128)(2,1)S(1)} %get-tuple-element.83), channel_id=1, source_target_pairs={{0,2},{1,3},{2,0},{3,1},{4,6},{5,7},{6,4},{7,5},{8,10},{9,11},{10,... | collective-permute-start | bytes 786440 | tf_op jit(solution)/shard_map/ppermute | solution.py:28

commit v8 on v7

--- a/solution.py
+++ b/solution.py
@@ -11,6 +11,7 @@
 F32 = jnp.float32
 BF16 = jnp.bfloat16
 VMEM_LIMIT = 50 * 2**20
+SHARE = 4
 IN_ORDER = pltpu.CompilerParams(
     vmem_limit_bytes=VMEM_LIMIT, dimension_semantics=("arbitrary",)
 )
@@ -21,6 +22,9 @@
 
 def cost(flops, moved, exponents=0):
     return pl.CostEstimate(flops=flops, bytes_accessed=moved, transcendentals=exponents)
+
+
+TINY = cost(0, 2**16)
 
 
 def swap(value, axis, mask):
@@ -125,25 +129,25 @@
     )(own, other, queries, out_grad)
 
 
-def spread_kernel(plan, source_ref, *out_refs):
+def spread_kernel(plan, stride, source_ref, *out_refs):
     wide = out_refs[0].shape[1]
     place = lax.axis_index("dp")
     for out, first, step, low, high in plan:
-        start = pl.multiple_of((place ^ step) * wide, wide)
+        start = pl.multiple_of((place ^ step) * stride, 128)
         out_refs[out][first : first + high - low] = source_ref[low:high, pl.ds(start, wide)]
 
 
-def spread(source, wide, plan):
+def spread(source, stride, wide, plan):
     heights = {}
     for out, first, _, low, high in plan:
         heights[out] = max(heights.get(out, 0), first + high - low)
     return pl.pallas_call(
-        functools.partial(spread_kernel, plan),
+        functools.partial(spread_kernel, plan, stride),
         out_shape=[
             jax.ShapeDtypeStruct((heights[out], wide), source.dtype) for out in sorted(heights)
         ],
         compiler_params=SMALL,
-        cost_estimate=cost(0, 2 * source.nbytes),
+        cost_estimate=TINY,
         name="spread",
     )(source)
 
@@ -155,25 +159,25 @@
                 height = rows.stop - rows.start
                 out_ref[first : first + height] = refs[source][rows, columns]
 
-    moved = sum(2 * math.prod(shape) * 2 for shape, _ in outputs)
     return pl.pallas_call(
         kernel,
         out_shape=[jax.ShapeDtypeStruct(shape, sources[0].dtype) for shape, _ in outputs],
         compiler_params=SMALL,
-        cost_estimate=cost(0, moved),
+        cost_estimate=TINY,
         name="lay",
     )(*sources)
 
 
-def send_rows(inputs, wide):
+def send_rows(inputs, stride, wide):
     rows = inputs.shape[0]
     groups = lax.axis_size("dp")
     if groups != 4:
-        parts = spread(inputs, wide, [(s, 0, s, 0, rows) for s in range(groups)])
+        parts = spread(inputs, stride, wide, [(s, 0, s, 0, rows) for s in range(groups)])
         return [part if s == 0 else swap(part, "dp", s) for s, part in enumerate(parts)]
     half = rows // 2
     own, left, right = spread(
         inputs,
+        stride,
         wide,
         [(0, 0, 0, 0, rows), (1, 0, 1, 0, rows), (1, rows, 3, 0, half), (2, 0, 2, 0, rows),
          (2, rows, 3, half, rows)],
@@ -208,41 +212,40 @@
         columns = slice(step * depth, (step + 1) * depth)
         return jnp.concatenate([f[half * rows : (half + 1) * rows, columns] for f in found], 0)
 
-    for steps, out_ref in zip(jobs, out_refs):
+    for (steps, low, high, _), out_ref in zip(jobs, out_refs):
         total = None
         for half, ref in enumerate((own_ref, other_ref)):
             grads = jnp.concatenate([pick(step, half) for step in steps], 1)
-            term = dot(ref[...], grads, 0, 0)
+            term = dot(ref[:, low:high], grads, 0, 0)
             total = term if total is None else total + term
         out_ref[...] = total.astype(out_ref.dtype)
 
 
-def products(pair, found, depth, jobs, dtypes):
-    groups = len(found)
-    tokens, wide = pair[0].shape
-    count = sum(len(steps) for steps in jobs)
-    return pl.pallas_call(
-        functools.partial(product_kernel, jobs, depth, groups),
+def products(pair, found, depth, jobs):
+    tokens = pair[0].shape[0]
+    count = sum(len(steps) * (high - low) for steps, low, high, _ in jobs)
+    return pl.pallas_call(
+        functools.partial(product_kernel, jobs, depth, len(found)),
         out_shape=[
-            jax.ShapeDtypeStruct((wide, len(steps) * depth), dtype)
-            for steps, dtype in zip(jobs, dtypes)
+            jax.ShapeDtypeStruct((high - low, len(steps) * depth), dtype)
+            for steps, low, high, dtype in jobs
         ],
         compiler_params=SMALL,
-        cost_estimate=cost(4 * tokens * wide * count * depth, 4 * tokens * wide),
+        cost_estimate=cost(4 * tokens * count * depth, 2**20),
         name="products",
     )(*pair, *found)
 
 
-def kv_kernel(rows, mine_ref, arrived_ref, mask_ref, *out_refs):
+def kv_kernel(rows, mine_ref, arrived_ref, mask_ref, whole_ref, *out_refs):
     place = lax.axis_index("tensor")
     chip, core = place // 2, place % 2
+    keep = mask_ref[...].astype(F32)
+    whole_ref[...] = ((mine_ref[...] + arrived_ref[...]) * keep).astype(BF16)
     for step, out_ref in enumerate(out_refs):
         for half in range(2):
             start = ((chip ^ step) * 2 + (core ^ half)) * rows
             span = pl.ds(pl.multiple_of(start, rows), rows)
-            total = mine_ref[span, :] + arrived_ref[span, :].astype(F32)
-            keep = mask_ref[span, :].astype(F32)
-            out_ref[half * rows : (half + 1) * rows, :] = (total * keep).astype(BF16)
+            out_ref[half * rows : (half + 1) * rows, :] = whole_ref[span, :]
 
 
 def kv_blocks(mine, arrived, mask, rows):
@@ -250,11 +253,34 @@
     count = length // (2 * rows)
     return pl.pallas_call(
         functools.partial(kv_kernel, rows),
-        out_shape=[jax.ShapeDtypeStruct((2 * rows, depth), BF16)] * count,
+        out_shape=[jax.ShapeDtypeStruct((length, depth), BF16)]
+        + [jax.ShapeDtypeStruct((2 * rows, depth), BF16)] * count,
         compiler_params=SMALL,
-        cost_estimate=cost(0, 2 * mine.nbytes),
+        cost_estimate=TINY,
         name="kv_blocks",
     )(mine, arrived, mask)
+
+
+def own_kernel(wide, rows_ref, grads_ref, *out_refs):
+    place = lax.axis_index("dp")
+    for step, out_ref in enumerate(out_refs):
+        start = pl.multiple_of((place ^ step) * wide, wide)
+        part = rows_ref[:, pl.ds(start, wide)]
+        out_ref[...] = dot(part, grads_ref[...], 0, 0).astype(out_ref.dtype)
+
+
+def own_products(gathered, grads, groups):
+    wide = gathered.shape[1] // groups
+    depth = grads.shape[1]
+    return pl.pallas_call(
+        functools.partial(own_kernel, wide),
+        out_shape=[
+            jax.ShapeDtypeStruct((wide, depth), BF16 if step else F32) for step in range(groups)
+        ],
+        compiler_params=pltpu.CompilerParams(vmem_limit_bytes=32 * 2**20),
+        cost_estimate=cost(2 * math.prod(gathered.shape) * depth, gathered.nbytes),
+        name="own_products",
+    )(gathered, grads)
 
 
 def per_device(inputs, queries, keys_values, out_grad, weight_mask, clip_mask):
@@ -264,46 +290,52 @@
     chips = lax.axis_size("tensor") // 2
     block = weight_mask.shape[0]
 
+    extra = block // SHARE // 128 * 128
+    wide = (block - extra) // 2
+    tails = [inputs[:, g * block + 2 * wide : (g + 1) * block] for g in range(groups)]
+    gathered = lax.all_gather(jnp.concatenate(tails, 1), "tensor", axis=0, tiled=True)
+
     other = swap(keys_values, "tensor", 1)
-    parts = send_rows(inputs, block)
+    parts = send_rows(inputs, block, 2 * wide)
 
     query_grad, mine, theirs = attention(keys_values, other, queries, out_grad)
     mine, parts = lax.optimization_barrier((mine, parts))
     arrived = swap(theirs, "tensor", 1)
-    blocks = kv_blocks(mine, arrived, clip_mask, rows)
+    grads, *blocks = kv_blocks(mine, arrived, clip_mask, rows)
 
     blocks = [b if s == 0 else swap(b, "tensor", 2 * s) for s, b in enumerate(blocks)]
-    parts, places = pass_rows(parts, block)
+    parts, places = pass_rows(parts, 2 * wide)
     blocks, parts = lax.optimization_barrier((blocks, parts))
     order = sorted(range(chips), key=lambda s: [(s >> b) & 1 for b in range(8)])
     evens, odds = order[: chips // 2], order[chips // 2 :]
-
-    wide = block // 2
-    outputs = []
-    for cut in range(2):
-        columns, entries, first = slice(cut * wide, (cut + 1) * wide), [], 0
-        for source in places:
-            for array, span in source:
-                entries.append((array, span, columns, first))
-                first += span.stop - span.start
-        outputs.append(((groups * rows, wide), entries))
-    near, far = [(own, swap(own, "tensor", 1)) for own in lay(parts, outputs)]
-
     stacked = jnp.concatenate(blocks, 1)
     found = [stacked if s == 0 else swap(stacked, "dp", s) for s in range(groups)]
 
+    entries, first = [], 0
+    for source in places:
+        for array, span in source:
+            entries.append((array, span, slice(None), first))
+            first += span.stop - span.start
+    (packed,) = lay(parts, [((first, 2 * wide), entries)])
+    pair = (packed, swap(packed, "tensor", 1))
+
     def send(value, step):
         return swap(value.astype(BF16), "tensor", 2 * step)
 
+    far, near = (wide, 2 * wide), (0, wide)
     away = list(range(2, chips))
-    straight = products(far, found, depth, [(s,) for s in away], [BF16] * len(away))
+    straight = products(pair, found, depth, [((s,), *far, BF16) for s in away])
     straight, found = lax.optimization_barrier((straight, found))
     straight = [send(value, s) for value, s in zip(straight, away)]
-    (first,) = products(near, found, depth, [tuple(odds)], [BF16])
+    (first,) = products(pair, found, depth, [(tuple(odds), *near, BF16)])
     sent = send(first, 1)
-    (even,) = products(near, found, depth, [tuple(evens)], [F32])
-    own, nearest = products(far, found, depth, [(0,), (1,)], [F32, BF16])
-    sent, straight = lax.optimization_barrier((sent, straight))
+    found, grads, _ = lax.optimization_barrier((found, grads, first))
+    even, own, nearest = products(
+        pair, found, depth, [(tuple(evens), *near, F32), ((0,), *far, F32), ((1,), *far, BF16)]
+    )
+    ends = own_products(gathered, grads, groups)
+    ends = [e if s == 0 else swap(e, "dp", s) for s, e in enumerate(ends)]
+    sent, straight, ends = lax.optimization_barrier((sent, straight, ends))
     terms = [even, sent]
     columns, bit = chips // 2 * depth, 1
     while columns > depth:
@@ -314,7 +346,8 @@
     straight.append(send(nearest, 1))
     upper = sum(t[:, :depth].astype(F32) for t in terms)
     lower = own + sum(t.astype(F32) for t in straight)
-    summed = jnp.concatenate([upper, lower], 0)
+    last = sum(e.astype(F32) for e in ends)
+    summed = jnp.concatenate([upper, lower, last], 0)
     weight_grad = jnp.where(weight_mask == 1, summed, 0.0)
     return (query_grad, weight_grad)
 

time: 98.5 us -> 115 us (1.17)
  between operations: 0.8 us -> 14.2 us
  waiting for transfers between devices: 44.7 us -> 35.2 us
  starting transfers between devices: 24.3 us -> 30.7 us
  other arithmetic: 1.32 us -> 5.05 us
  local copies, waits for them, and re-layouts: 1.9 us -> 4.78 us
    ppermute x19 -> x21, waiting for transfers between devices: 44.7 us -> 35.2 us  [swap(): return lax.ppermute(value, axis, pairs)]
    ppermute x19 -> x21, starting transfers between devices: 24.3 us -> 30.6 us  [swap(): return lax.ppermute(value, axis, pairs)]
    pallas_call x5, Pallas kernels: 4.31 us -> 6.05 us  [the longest x3 4.58 us: products(): pl.pallas_call(functools.partial(product_kernel, jobs, depth, len(found))...]
    unnamed x14 -> x32, local copies, waits for them, and re-layouts: 1.88 us -> 3.46 us
    slice x0 -> x1, local copies, waits for them, and re-layouts: none -> 1.3 us  [per_device(): inputs[:, g * block + 2 * wide:(g + 1) * block]]
  transfers between devices with their start and end apart: 19 -> 22, of which waited for: 10 -> 10; matrix products, arithmetic and copies ran while one was open for 0% -> 1% of each run, Pallas kernels for 24% -> 22%
where the time goes in v8:
time: 115 us
  waiting for transfers between devices  35.2 us (31%)
  starting transfers between devices  30.7 us (27%)
  Pallas kernels  24.9 us (22%)
  between operations  14.2 us (12%)
  other arithmetic  5.05 us (4%)
  local copies, waits for them, and re-layouts  4.78 us (4%)
    ppermute x21, waiting for transfers between devices, swap(): return lax.ppermute(value, axis, pairs)  35.2 us
    ppermute x21, starting transfers between devices, swap(): return lax.ppermute(value, axis, pairs)  30.6 us
    pallas_call x1, Pallas kernels, attention(): pl.pallas_call(functools.partial(attention_kernel, height), grid=(width /...  17.7 us
    pallas_call x3, Pallas kernels, products(): pl.pallas_call(functools.partial(product_kernel, jobs, depth, len(found))...  4.58 us
    unnamed x32, local copies, waits for them, and re-layouts  3.46 us
  transfers between devices with their start and end apart: 22, of which 10 were waited for; matrix products, arithmetic and copies ran while one was open for 1% of the time, Pallas kernels for 22%

profile of v8, /device:TPU:0, one launch (start us, length us, event | category | flops | bytes accessed | tf_op | source)
XLA Modules:
  0.0 114.8 jit_solution(4226280699492712551)
XLA Ops:
  7.2 1.3 %fusion = (bf16[128,512]{1,0:T(8,128)(2,1)S(1)}, bf16[128,512]{1,0:T(8,128)(2,1)S(1)}, bf16[128,512]{1,0:T(8,128)(2,1)S(1)}, bf16[128,512]{1,0:T(8,128)(2,1)S(1)}) fusion(bf16[128,8192]{1,0:T(8,128)(2,1)} %source_ref.1), kind=kLoop, calls=%fused_computation.10 | loop fusion | bytes 1048576 | tf_op jit(solution)/shard_map/slice | solution.py:295
  8.5 0.8 pad_maximum_fusion
  9.4 0.5 collective-permute-start
  10.0 0.1 spread.1
  10.1 2.6 %collective-permute-start.1 = (bf16[192,1536]{1,0:T(8,128)(2,1)S(1)}, bf16[192,1536]{1,0:T(8,128)(2,1)S(1)}, u32[]{:S(2)}, u32[]{:S(2)}) collective-permute-start(bf16[192,1536]{1,0:T(8,128)(2,1)S(1)} %get-tuple-element.59), channel_id=1, source_target_pairs={{0,8},{8,0},{16,24},{24,16},{1,9},{9,1},{17,25},{25,17},{2,10},{10... | collective-permute-start | bytes 1769480 | tf_op jit(solution)/shard_map/ppermute | solution.py:32
  12.6 1.5 %collective-permute-start.2 = (bf16[192,1536]{1,0:T(8,128)(2,1)S(1)}, bf16[192,1536]{1,0:T(8,128)(2,1)S(1)}, u32[]{:S(2)}, u32[]{:S(2)}) collective-permute-start(bf16[192,1536]{1,0:T(8,128)(2,1)S(1)} %get-tuple-element.60), channel_id=1, source_target_pairs={{0,16},{8,24},{16,0},{24,8},{1,17},{9,25},{17,1},{25,9},{2,18},{10... | collective-permute-start | bytes 1769480 | tf_op jit(solution)/shard_map/ppermute | solution.py:32
  14.2 17.7 %attention.1 = (bf16[1024,768]{1,0:T(8,128)(2,1)}, f32[1024,128]{1,0:T(8,128)S(1)}, f32[1024,128]{1,0:T(8,128)}) custom-call(bf16[1024,128]{1,0:T(8,128)(2,1)S(1)} %copy-done.11, bf16[1024,128]{1,0:T(8,128)(2,1)S(1)} %collective-permute-done.other_ref, bf16[1024,768]{1,0:T(8,128)(2,1)S(1)} %copy-done.10, bf16[1024,768]{1,0:T(8,128)(2,1)} %up_ref.1), custom_call_target="tpu_custom_call" | custom-call | flops 16106127360 | bytes 9437184 | tf_op jit(solution)/shard_map/attention/pallas_call | solution.py:110
  31.9 0.8 lay.2
  32.7 0.5 collective-permute-start.7
  33.2 0.9 collective-permute-start.8
  34.2 0.2 copy.8.mask_ref
  34.4 0.2 kv_blocks.1
  34.6 1.6 %collective-permute-start.4 = (bf16[256,128]{1,0:T(8,128)(2,1)S(1)}, bf16[256,128]{1,0:T(8,128)(2,1)S(1)}, u32[]{:S(2)}, u32[]{:S(2)}) collective-permute-start(bf16[256,128]{1,0:T(8,128)(2,1)S(1)} %get-tuple-element.64), channel_id=1, source_target_pairs={{0,2},{1,3},{2,0},{3,1},{4,6},{5,7},{6,4},{7,5},{8,10},{9,11},{10,... | collective-permute-start | bytes 196616 | tf_op jit(solution)/shard_map/ppermute | solution.py:32
  36.3 2.6 %collective-permute-start.5 = (bf16[256,128]{1,0:T(8,128)(2,1)S(1)}, bf16[256,128]{1,0:T(8,128)(2,1)S(1)}, u32[]{:S(2)}, u32[]{:S(2)}) collective-permute-start(bf16[256,128]{1,0:T(8,128)(2,1)S(1)} %get-tuple-element.65), channel_id=1, source_target_pairs={{0,4},{1,5},{2,6},{3,7},{4,0},{5,1},{6,2},{7,3},{8,12},{9,13},{10,... | collective-permute-start | bytes 196616 | tf_op jit(solution)/shard_map/ppermute | solution.py:32
  38.9 0.2 collective-permute-start.6
  39.1 1.1 collective-permute-done.7.refs_3_
  40.2 0.2 collective-permute-done.8.refs_4_
  40.4 3.8 %collective-permute-done.4 = bf16[256,128]{1,0:T(8,128)(2,1)S(1)} collective-permute-done((bf16[256,128]{1,0:T(8,128)(2,1)S(1)}, bf16[256,128]{1,0:T(8,128)(2,1)S(1)}, u32[]{:S(2)}, u32[]{:S(2)}) %collective-permute-start.4) | collective-permute-done | bytes 65568 | tf_op jit(solution)/shard_map/ppermute | solution.py:32
  44.2 3.4 %collective-permute-done.5 = bf16[256,128]{1,0:T(8,128)(2,1)S(1)} collective-permute-done((bf16[256,128]{1,0:T(8,128)(2,1)S(1)}, bf16[256,128]{1,0:T(8,128)(2,1)S(1)}, u32[]{:S(2)}, u32[]{:S(2)}) %collective-permute-start.5) | collective-permute-done | bytes 65568 | tf_op jit(solution)/shard_map/ppermute | solution.py:32
  47.6 0.7 collective-permute-done.6
  48.3 0.1 lay.3.own_ref
  48.4 0.1 collective-permute-start.9
  48.6 1.2 %collective-permute-start.10 = (bf16[256,512]{1,0:T(8,128)(2,1)S(1)}, bf16[256,512]{1,0:T(8,128)(2,1)S(1)}, u32[]{:S(2)}, u32[]{:S(2)}) collective-permute-start(bf16[256,512]{1,0:T(8,128)(2,1)S(1)} %constant_dynamic-update-slice_fusion.refs_0_), channel_id=1, source_target_pairs={{0,8},{8,0},{16,24},{24,16},{1,9},{9,1},{17,25},{25,17},{2,10},{10... | collective-permute-start | bytes 786440 | tf_op jit(solution)/shard_map/ppermute | solution.py:32
  49.8 1.5 %collective-permute-start.11 = (bf16[256,512]{1,0:T(8,128)(2,1)S(1)}, bf16[256,512]{1,0:T(8,128)(2,1)S(1)}, u32[]{:S(2)}, u32[]{:S(2)}) collective-permute-start(bf16[256,512]{1,0:T(8,128)(2,1)S(1)} %constant_dynamic-update-slice_fusion.refs_0_), channel_id=1, source_target_pairs={{0,16},{8,24},{16,0},{24,8},{1,17},{9,25},{17,1},{25,9},{2,18},{10... | collective-permute-start | bytes 786440 | tf_op jit(solution)/shard_map/ppermute | solution.py:32
  51.3 0.8 collective-permute-start.12
  52.1 5.6 %collective-permute-done.10.refs_1_ = bf16[256,512]{1,0:T(8,128)(2,1)S(1)} collective-permute-done((bf16[256,512]{1,0:T(8,128)(2,1)S(1)}, bf16[256,512]{1,0:T(8,128)(2,1)S(1)}, u32[]{:S(2)}, u32[]{:S(2)}) %collective-permute-start.10) | collective-permute-done | bytes 262176 | tf_op jit(solution)/shard_map/ppermute | solution.py:32
  57.8 6.1 %collective-permute-done.11.refs_2_ = bf16[256,512]{1,0:T(8,128)(2,1)S(1)} collective-permute-done((bf16[256,512]{1,0:T(8,128)(2,1)S(1)}, bf16[256,512]{1,0:T(8,128)(2,1)S(1)}, u32[]{:S(2)}, u32[]{:S(2)}) %collective-permute-start.11) | collective-permute-done | bytes 262176 | tf_op jit(solution)/shard_map/ppermute | solution.py:32
  63.8 1.8 %products.3 = (bf16[768,128]{1,0:T(8,128)(2,1)}, bf16[768,128]{1,0:T(8,128)(2,1)}) custom-call(bf16[512,1536]{1,0:T(8,128)(2,1)S(1)} %lay.3.own_ref, bf16[512,1536]{1,0:T(8,128)(2,1)S(1)} %collective-permute-done.9.other_ref, bf16[256,512]{1,0:T(8,128)(2,1)S(1)} %constant_dynamic-update-slice_fusion.refs_0_, ...), custom_call_target="tpu_custom_call" | custom-call | flops 402653184 | bytes 1048576 | tf_op jit(solution)/shard_map/products/pallas_call | solution.py:227
  65.6 1.4 %products.4 = bf16[768,256]{1,0:T(8,128)(2,1)} custom-call(bf16[512,1536]{1,0:T(8,128)(2,1)S(1)} %lay.3.own_ref, bf16[512,1536]{1,0:T(8,128)(2,1)S(1)} %collective-permute-done.9.other_ref, bf16[256,512]{1,0:T(8,128)(2,1)S(1)} %constant_dynamic-update-slice_fusion.refs_0_, bf16[256,512]{1,0:T(8,128)(2,1)S(1)} %collective-permute-done.10.refs_1_, ...), custom_call_target="tpu_custom_call" | custom-call | flops 402653184 | bytes 1048576 | tf_op jit(solution)/shard_map/products/pallas_call | solution.py:227
  67.0 5.7 %collective-permute-start.13 = (bf16[768,256]{1,0:T(8,128)(2,1)}, bf16[768,256]{1,0:T(8,128)(2,1)}, u32[]{:S(2)}, u32[]{:S(2)}) collective-permute-start(bf16[768,256]{1,0:T(8,128)(2,1)} %products.4), channel_id=1, source_target_pairs={{0,2},{1,3},{2,0},{3,1},{4,6},{5,7},{6,4},{7,5},{8,10},{9,11},{10,... | collective-permute-start | bytes 1179656 | tf_op jit(solution)/shard_map/ppermute | solution.py:32
  72.7 1.8 %collective-permute-start.14 = (bf16[768,128]{1,0:T(8,128)(2,1)}, bf16[768,128]{1,0:T(8,128)(2,1)}, u32[]{:S(2)}, u32[]{:S(2)}) collective-permute-start(bf16[768,128]{1,0:T(8,128)(2,1)} %get-tuple-element.93), channel_id=1, source_target_pairs={{0,4},{1,5},{2,6},{3,7},{4,0},{5,1},{6,2},{7,3},{8,12},{9,13},{10,... | collective-permute-start | bytes 589832 | tf_op jit(solution)/shard_map/ppermute | solution.py:32
  74.5 1.5 %collective-permute-start.15 = (bf16[768,128]{1,0:T(8,128)(2,1)}, bf16[768,128]{1,0:T(8,128)(2,1)}, u32[]{:S(2)}, u32[]{:S(2)}) collective-permute-start(bf16[768,128]{1,0:T(8,128)(2,1)} %get-tuple-element.94), channel_id=1, source_target_pairs={{0,6},{1,7},{2,4},{3,5},{4,2},{5,3},{6,0},{7,1},{8,14},{9,15},{10,... | collective-permute-start | bytes 589832 | tf_op jit(solution)/shard_map/ppermute | solution.py:32
  76.0 2.2 %copy-done = bf16[1024,2048]{1,0:T(8,128)(2,1)S(1)} copy-done((bf16[1024,2048]{1,0:T(8,128)(2,1)S(1)}, bf16[1024,2048]{1,0:T(8,128)(2,1)}, u32[]{:S(2)}) %copy-start) | copy-done | bytes 4194328
  78.2 0.9 copy-done.9
  79.1 1.4 %own_products.1 = (f32[512,128]{1,0:T(8,128)S(1)}, bf16[512,128]{1,0:T(8,128)(2,1)S(1)}, bf16[512,128]{1,0:T(8,128)(2,1)S(1)}, bf16[512,128]{1,0:T(8,128)(2,1)S(1)}) custom-call(bf16[1024,2048]{1,0:T(8,128)(2,1)S(1)} %copy-done, bf16[1024,128]{1,0:T(8,128)(2,1)S(1)} %copy-done.9), custom_call_target="tpu_custom_call" | custom-call | flops 536870912 | bytes 4194304 | tf_op jit(solution)/shard_map/own_products/pallas_call | solution.py:275
  80.5 1.3 %collective-permute-start.16 = (bf16[512,128]{1,0:T(8,128)(2,1)S(1)}, bf16[512,128]{1,0:T(8,128)(2,1)S(1)}, u32[]{:S(2)}, u32[]{:S(2)}) collective-permute-start(bf16[512,128]{1,0:T(8,128)(2,1)S(1)} %get-tuple-element.97), channel_id=1, source_target_pairs={{0,8},{8,0},{16,24},{24,16},{1,9},{9,1},{17,25},{25,17},{2,10},{10... | collective-permute-start | bytes 393224 | tf_op jit(solution)/shard_map/ppermute | solution.py:32
  81.8 0.8 collective-permute-start.17
  82.6 4.2 %collective-permute-done.14 = bf16[768,128]{1,0:T(8,128)(2,1)} collective-permute-done((bf16[768,128]{1,0:T(8,128)(2,1)}, bf16[768,128]{1,0:T(8,128)(2,1)}, u32[]{:S(2)}, u32[]{:S(2)}) %collective-permute-start.14) | collective-permute-done | bytes 196640 | tf_op jit(solution)/shard_map/ppermute | solution.py:32
  86.9 1.5 %collective-permute-start.18 = (bf16[512,128]{1,0:T(8,128)(2,1)S(1)}, bf16[512,128]{1,0:T(8,128)(2,1)S(1)}, u32[]{:S(2)}, u32[]{:S(2)}) collective-permute-start(bf16[512,128]{1,0:T(8,128)(2,1)S(1)} %get-tuple-element.99), channel_id=1, source_target_pairs={{0,24},{8,16},{16,8},{24,0},{1,25},{9,17},{17,9},{25,1},{2,26},{10... | collective-permute-start | bytes 393224 | tf_op jit(solution)/shard_map/ppermute | solution.py:32
  88.4 1.4 %products.5 = (f32[768,256]{1,0:T(8,128)S(1)}, f32[768,128]{1,0:T(8,128)S(1)}, bf16[768,128]{1,0:T(8,128)(2,1)S(1)}) custom-call(bf16[512,1536]{1,0:T(8,128)(2,1)S(1)} %lay.3.own_ref, bf16[512,1536]{1,0:T(8,128)(2,1)S(1)} %collective-permute-done.9.other_ref, bf16[256,512]{1,0:T(8,128)(2,1)S(1)} %constant_dynamic-update-slice_fusion.refs_0_, ...), custom_call_target="tpu_custom_call" | custom-call | flops 805306368 | bytes 1048576 | tf_op jit(solution)/shard_map/products/pallas_call | solution.py:227
  89.8 3.4 %collective-permute-done.15 = bf16[768,128]{1,0:T(8,128)(2,1)} collective-permute-done((bf16[768,128]{1,0:T(8,128)(2,1)}, bf16[768,128]{1,0:T(8,128)(2,1)}, u32[]{:S(2)}, u32[]{:S(2)}) %collective-permute-start.15) | collective-permute-done | bytes 196640 | tf_op jit(solution)/shard_map/ppermute | solution.py:32
  93.2 1.0 add_convert_fusion
  94.2 3.0 %collective-permute-start.19 = (bf16[768,128]{1,0:T(8,128)(2,1)S(1)}, bf16[768,128]{1,0:T(8,128)(2,1)S(1)}, u32[]{:S(2)}, u32[]{:S(2)}) collective-permute-start(bf16[768,128]{1,0:T(8,128)(2,1)S(1)} %add_convert_fusion), channel_id=1, source_target_pairs={{0,4},{1,5},{2,6},{3,7},{4,0},{5,1},{6,2},{7,3},{8,12},{9,13},{10,... | collective-permute-start | bytes 589832 | tf_op jit(solution)/shard_map/ppermute | solution.py:32
  97.2 0.9 collective-permute-start.20
  98.2 6.6 %collective-permute-done.19 = bf16[768,128]{1,0:T(8,128)(2,1)S(1)} collective-permute-done((bf16[768,128]{1,0:T(8,128)(2,1)S(1)}, bf16[768,128]{1,0:T(8,128)(2,1)S(1)}, u32[]{:S(2)}, u32[]{:S(2)}) %collective-permute-start.19) | collective-permute-done | bytes 196640 | tf_op jit(solution)/shard_map/ppermute | solution.py:32
  104.8 1.0 convert_add_fusion
  105.8 1.1 add_add_fusion
  106.9 1.1 maximum_select_fusion
  (46 shorter events, 0.3 us)
Async XLA Ops:
  7.2 2.8 %copy-start.1 = (bf16[128,8192]{1,0:T(8,128)(2,1)S(1)}, bf16[128,8192]{1,0:T(8,128)(2,1)}, u32[]{:S(2)}) copy-start(bf16[128,8192]{1,0:T(8,128)(2,1)} %source_ref.1) | copy-start | bytes 6291460
  7.2 2.2 %copy-start.11 = (bf16[1024,128]{1,0:T(8,128)(2,1)S(1)}, bf16[1024,128]{1,0:T(8,128)(2,1)}, u32[]{:S(2)}) copy-start(bf16[1024,128]{1,0:T(8,128)(2,1)} %own_ref.1) | copy-start | bytes 786436
  7.2 68.8 %all-gather.2.cloned.1.call-start = ((), (), s32[]{:S(2)}) async-start(), calls=%async_computation | async-start | bytes 4718592 | tf_op jit(solution)/shard_map/all_gather | solution.py:296
  9.4 4.8 %copy-start.10 = (bf16[1024,768]{1,0:T(8,128)(2,1)S(1)}, bf16[1024,768]{1,0:T(8,128)(2,1)}, u32[]{:S(2)}) copy-start(bf16[1024,768]{1,0:T(8,128)(2,1)} %q_ref.1) | copy-start | bytes 4718596
  9.4 4.7 %collective-permute-start = (bf16[1024,128]{1,0:T(8,128)(2,1)S(1)}, bf16[1024,128]{1,0:T(8,128)(2,1)S(1)}, u32[]{:S(2)}, u32[]{:S(2)}) collective-permute-start(bf16[1024,128]{1,0:T(8,128)(2,1)S(1)} %copy-done.11), channel_id=1, source_target_pairs={{0,1},{1,0},{2,3},{3,2},{4,5},{5,4},{6,7},{7,6},{8,9},{9,8},{10,11... | collective-permute-start | bytes 786440 | tf_op jit(solution)/shard_map/ppermute | solution.py:32
  10.1 21.8 %collective-permute-start.1 = (bf16[192,1536]{1,0:T(8,128)(2,1)S(1)}, bf16[192,1536]{1,0:T(8,128)(2,1)S(1)}, u32[]{:S(2)}, u32[]{:S(2)}) collective-permute-start(bf16[192,1536]{1,0:T(8,128)(2,1)S(1)} %get-tuple-element.59), channel_id=1, source_target_pairs={{0,8},{8,0},{16,24},{24,16},{1,9},{9,1},{17,25},{25,17},{2,10},{10... | collective-permute-start | bytes 1769480 | tf_op jit(solution)/shard_map/ppermute | solution.py:32
  12.6 21.5 %copy-start.13 = (s32[1024,1]{0,1:T(1,128)S(1)}, s32[1024,1]{0,1:T(1,128)}, u32[]{:S(2)}) copy-start(s32[1024,1]{0,1:T(1,128)} %param.11) | copy-start | bytes 12292
  12.6 19.3 %collective-permute-start.2 = (bf16[192,1536]{1,0:T(8,128)(2,1)S(1)}, bf16[192,1536]{1,0:T(8,128)(2,1)S(1)}, u32[]{:S(2)}, u32[]{:S(2)}) collective-permute-start(bf16[192,1536]{1,0:T(8,128)(2,1)S(1)} %get-tuple-element.60), channel_id=1, source_target_pairs={{0,16},{8,24},{16,0},{24,8},{1,17},{9,25},{17,1},{25,9},{2,18},{10... | collective-permute-start | bytes 1769480 | tf_op jit(solution)/shard_map/ppermute | solution.py:32
  31.9 2.5 %collective-permute-start.3 = (f32[1024,128]{1,0:T(8,128)}, f32[1024,128]{1,0:T(8,128)S(1)}, u32[]{:S(2)}, u32[]{:S(2)}) collective-permute-start(f32[1024,128]{1,0:T(8,128)} %get-tuple-element.62), channel_id=1, source_target_pairs={{0,1},{1,0},{2,3},{3,2},{4,5},{5,4},{6,7},{7,6},{8,9},{9,8},{10,11... | collective-permute-start | bytes 1572872 | tf_op jit(solution)/shard_map/ppermute | solution.py:32
  32.7 7.5 %collective-permute-start.7 = (bf16[64,1536]{1,0:T(8,128)(2,1)}, bf16[64,1536]{1,0:T(8,128)(2,1)S(1)}, u32[]{:S(2)}, u32[]{:S(2)}) collective-permute-start(bf16[64,1536]{1,0:T(8,128)(2,1)} %get-tuple-element.70), channel_id=1, source_target_pairs={{0,16},{8,24},{16,0},{24,8},{1,17},{9,25},{17,1},{25,9},{2,18},{10... | collective-permute-start | bytes 589832 | tf_op jit(solution)/shard_map/ppermute | solution.py:32
  33.2 7.2 %collective-permute-start.8 = (bf16[64,1536]{1,0:T(8,128)(2,1)}, bf16[64,1536]{1,0:T(8,128)(2,1)S(1)}, u32[]{:S(2)}, u32[]{:S(2)}) collective-permute-start(bf16[64,1536]{1,0:T(8,128)(2,1)} %get-tuple-element.71), channel_id=1, source_target_pairs={{0,8},{8,0},{16,24},{24,16},{1,9},{9,1},{17,25},{25,17},{2,10},{10... | collective-permute-start | bytes 589832 | tf_op jit(solution)/shard_map/ppermute | solution.py:32
  34.6 13.8 %copy-start.8 = (bf16[1024,128]{1,0:T(8,128)(2,1)}, bf16[1024,128]{1,0:T(8,128)(2,1)S(1)}, u32[]{:S(2)}) copy-start(bf16[1024,128]{1,0:T(8,128)(2,1)S(1)} %get-tuple-element.95.grads_ref) | copy-start | bytes 786436
  34.6 9.6 %collective-permute-start.4 = (bf16[256,128]{1,0:T(8,128)(2,1)S(1)}, bf16[256,128]{1,0:T(8,128)(2,1)S(1)}, u32[]{:S(2)}, u32[]{:S(2)}) collective-permute-start(bf16[256,128]{1,0:T(8,128)(2,1)S(1)} %get-tuple-element.64), channel_id=1, source_target_pairs={{0,2},{1,3},{2,0},{3,1},{4,6},{5,7},{6,4},{7,5},{8,10},{9,11},{10,... | collective-permute-start | bytes 196616 | tf_op jit(solution)/shard_map/ppermute | solution.py:32
  36.3 11.3 %collective-permute-start.5 = (bf16[256,128]{1,0:T(8,128)(2,1)S(1)}, bf16[256,128]{1,0:T(8,128)(2,1)S(1)}, u32[]{:S(2)}, u32[]{:S(2)}) collective-permute-start(bf16[256,128]{1,0:T(8,128)(2,1)S(1)} %get-tuple-element.65), channel_id=1, source_target_pairs={{0,4},{1,5},{2,6},{3,7},{4,0},{5,1},{6,2},{7,3},{8,12},{9,13},{10,... | collective-permute-start | bytes 196616 | tf_op jit(solution)/shard_map/ppermute | solution.py:32
  38.9 9.4 %collective-permute-start.6 = (bf16[256,128]{1,0:T(8,128)(2,1)S(1)}, bf16[256,128]{1,0:T(8,128)(2,1)S(1)}, u32[]{:S(2)}, u32[]{:S(2)}) collective-permute-start(bf16[256,128]{1,0:T(8,128)(2,1)S(1)} %get-tuple-element.66), channel_id=1, source_target_pairs={{0,6},{1,7},{2,4},{3,5},{4,2},{5,3},{6,0},{7,1},{8,14},{9,15},{10,... | collective-permute-start | bytes 196616 | tf_op jit(solution)/shard_map/ppermute | solution.py:32
  48.4 15.4 %collective-permute-start.9 = (bf16[512,1536]{1,0:T(8,128)(2,1)S(1)}, bf16[512,1536]{1,0:T(8,128)(2,1)S(1)}, u32[]{:S(2)}, u32[]{:S(2)}) collective-permute-start(bf16[512,1536]{1,0:T(8,128)(2,1)S(1)} %lay.3.own_ref), channel_id=1, source_target_pairs={{0,1},{1,0},{2,3},{3,2},{4,5},{5,4},{6,7},{7,6},{8,9},{9,8},{10,11... | collective-permute-start | bytes 4718600 | tf_op jit(solution)/shard_map/ppermute | solution.py:32
  48.6 9.2 %collective-permute-start.10 = (bf16[256,512]{1,0:T(8,128)(2,1)S(1)}, bf16[256,512]{1,0:T(8,128)(2,1)S(1)}, u32[]{:S(2)}, u32[]{:S(2)}) collective-permute-start(bf16[256,512]{1,0:T(8,128)(2,1)S(1)} %constant_dynamic-update-slice_fusion.refs_0_), channel_id=1, source_target_pairs={{0,8},{8,0},{16,24},{24,16},{1,9},{9,1},{17,25},{25,17},{2,10},{10... | collective-permute-start | bytes 786440 | tf_op jit(solution)/shard_map/ppermute | solution.py:32
  49.8 14.0 %collective-permute-start.11 = (bf16[256,512]{1,0:T(8,128)(2,1)S(1)}, bf16[256,512]{1,0:T(8,128)(2,1)S(1)}, u32[]{:S(2)}, u32[]{:S(2)}) collective-permute-start(bf16[256,512]{1,0:T(8,128)(2,1)S(1)} %constant_dynamic-update-slice_fusion.refs_0_), channel_id=1, source_target_pairs={{0,16},{8,24},{16,0},{24,8},{1,17},{9,25},{17,1},{25,9},{2,18},{10... | collective-permute-start | bytes 786440 | tf_op jit(solution)/shard_map/ppermute | solution.py:32
  51.3 12.5 %collective-permute-start.12 = (bf16[256,512]{1,0:T(8,128)(2,1)S(1)}, bf16[256,512]{1,0:T(8,128)(2,1)S(1)}, u32[]{:S(2)}, u32[]{:S(2)}) collective-permute-start(bf16[256,512]{1,0:T(8,128)(2,1)S(1)} %constant_dynamic-update-slice_fusion.refs_0_), channel_id=1, source_target_pairs={{0,24},{8,16},{16,8},{24,0},{1,25},{9,17},{17,9},{25,1},{2,26},{10... | collective-permute-start | bytes 786440 | tf_op jit(solution)/shard_map/ppermute | solution.py:32
  57.7 7.9 %copy-start.2 = (bf16[256,512]{1,0:T(8,128)(2,1)}, bf16[256,512]{1,0:T(8,128)(2,1)S(1)}, u32[]{:S(2)}) copy-start(bf16[256,512]{1,0:T(8,128)(2,1)S(1)} %collective-permute-done.10.refs_1_) | copy-start | bytes 786436
  63.8 1.8 %copy-start.4 = (bf16[256,512]{1,0:T(8,128)(2,1)}, bf16[256,512]{1,0:T(8,128)(2,1)S(1)}, u32[]{:S(2)}) copy-start(bf16[256,512]{1,0:T(8,128)(2,1)S(1)} %collective-permute-done.11.refs_2_) | copy-start | bytes 786436
  63.8 1.8 %copy-start.6 = (bf16[256,512]{1,0:T(8,128)(2,1)}, bf16[256,512]{1,0:T(8,128)(2,1)S(1)}, u32[]{:S(2)}) copy-start(bf16[256,512]{1,0:T(8,128)(2,1)S(1)} %collective-permute-done.12.refs_3_) | copy-start | bytes 786436
  67.0 26.2 %collective-permute-start.13 = (bf16[768,256]{1,0:T(8,128)(2,1)}, bf16[768,256]{1,0:T(8,128)(2,1)}, u32[]{:S(2)}, u32[]{:S(2)}) collective-permute-start(bf16[768,256]{1,0:T(8,128)(2,1)} %products.4), channel_id=1, source_target_pairs={{0,2},{1,3},{2,0},{3,1},{4,6},{5,7},{6,4},{7,5},{8,10},{9,11},{10,... | collective-permute-start | bytes 1179656 | tf_op jit(solution)/shard_map/ppermute | solution.py:32
  72.7 14.1 %collective-permute-start.14 = (bf16[768,128]{1,0:T(8,128)(2,1)}, bf16[768,128]{1,0:T(8,128)(2,1)}, u32[]{:S(2)}, u32[]{:S(2)}) collective-permute-start(bf16[768,128]{1,0:T(8,128)(2,1)} %get-tuple-element.93), channel_id=1, source_target_pairs={{0,4},{1,5},{2,6},{3,7},{4,0},{5,1},{6,2},{7,3},{8,12},{9,13},{10,... | collective-permute-start | bytes 589832 | tf_op jit(solution)/shard_map/ppermute | solution.py:32
  74.5 18.7 %collective-permute-start.15 = (bf16[768,128]{1,0:T(8,128)(2,1)}, bf16[768,128]{1,0:T(8,128)(2,1)}, u32[]{:S(2)}, u32[]{:S(2)}) collective-permute-start(bf16[768,128]{1,0:T(8,128)(2,1)} %get-tuple-element.94), channel_id=1, source_target_pairs={{0,6},{1,7},{2,4},{3,5},{4,2},{5,3},{6,0},{7,1},{8,14},{9,15},{10,... | collective-permute-start | bytes 589832 | tf_op jit(solution)/shard_map/ppermute | solution.py:32
  76.0 2.2 %copy-start = (bf16[1024,2048]{1,0:T(8,128)(2,1)S(1)}, bf16[1024,2048]{1,0:T(8,128)(2,1)}, u32[]{:S(2)}) copy-start(bf16[1024,2048]{1,0:T(8,128)(2,1)} %all-gather.2.cloned.1.call-done.rows_ref) | copy-start | bytes 12582916
  78.2 0.9 copy-start.9
  79.1 9.2 %copy-start.3 = (bf16[256,512]{1,0:T(8,128)(2,1)S(1)}, bf16[256,512]{1,0:T(8,128)(2,1)}, u32[]{:S(2)}) copy-start(bf16[256,512]{1,0:T(8,128)(2,1)} %copy-done.2) | copy-start | bytes 786436
  79.1 9.2 %copy-start.5 = (bf16[256,512]{1,0:T(8,128)(2,1)S(1)}, bf16[256,512]{1,0:T(8,128)(2,1)}, u32[]{:S(2)}) copy-start(bf16[256,512]{1,0:T(8,128)(2,1)} %copy-done.4) | copy-start | bytes 786436
  79.1 9.2 %copy-start.7 = (bf16[256,512]{1,0:T(8,128)(2,1)S(1)}, bf16[256,512]{1,0:T(8,128)(2,1)}, u32[]{:S(2)}) copy-start(bf16[256,512]{1,0:T(8,128)(2,1)} %copy-done.6) | copy-start | bytes 786436
  80.5 12.7 %collective-permute-start.16 = (bf16[512,128]{1,0:T(8,128)(2,1)S(1)}, bf16[512,128]{1,0:T(8,128)(2,1)S(1)}, u32[]{:S(2)}, u32[]{:S(2)}) collective-permute-start(bf16[512,128]{1,0:T(8,128)(2,1)S(1)} %get-tuple-element.97), channel_id=1, source_target_pairs={{0,8},{8,0},{16,24},{24,16},{1,9},{9,1},{17,25},{25,17},{2,10},{10... | collective-permute-start | bytes 393224 | tf_op jit(solution)/shard_map/ppermute | solution.py:32
  81.8 11.4 %collective-permute-start.17 = (bf16[512,128]{1,0:T(8,128)(2,1)S(1)}, bf16[512,128]{1,0:T(8,128)(2,1)S(1)}, u32[]{:S(2)}, u32[]{:S(2)}) collective-permute-start(bf16[512,128]{1,0:T(8,128)(2,1)S(1)} %get-tuple-element.98), channel_id=1, source_target_pairs={{0,16},{8,24},{16,0},{24,8},{1,17},{9,25},{17,1},{25,9},{2,18},{10... | collective-permute-start | bytes 393224 | tf_op jit(solution)/shard_map/ppermute | solution.py:32
  86.9 6.4 %collective-permute-start.18 = (bf16[512,128]{1,0:T(8,128)(2,1)S(1)}, bf16[512,128]{1,0:T(8,128)(2,1)S(1)}, u32[]{:S(2)}, u32[]{:S(2)}) collective-permute-start(bf16[512,128]{1,0:T(8,128)(2,1)S(1)} %get-tuple-element.99), channel_id=1, source_target_pairs={{0,24},{8,16},{16,8},{24,0},{1,25},{9,17},{17,9},{25,1},{2,26},{10... | collective-permute-start | bytes 393224 | tf_op jit(solution)/shard_map/ppermute | solution.py:32
  94.2 10.5 %collective-permute-start.19 = (bf16[768,128]{1,0:T(8,128)(2,1)S(1)}, bf16[768,128]{1,0:T(8,128)(2,1)S(1)}, u32[]{:S(2)}, u32[]{:S(2)}) collective-permute-start(bf16[768,128]{1,0:T(8,128)(2,1)S(1)} %add_convert_fusion), channel_id=1, source_target_pairs={{0,4},{1,5},{2,6},{3,7},{4,0},{5,1},{6,2},{7,3},{8,12},{9,13},{10,... | collective-permute-start | bytes 589832 | tf_op jit(solution)/shard_map/ppermute | solution.py:32
  97.2 9.7 %copy-start.12 = (s32[2048,128]{1,0:T(8,128)S(1)}, s32[2048,128]{1,0:T(8,128)}, u32[]{:S(2)}) copy-start(s32[2048,128]{1,0:T(8,128)} %param.10) | copy-start | bytes 3145732
  97.2 8.5 %collective-permute-start.20 = (bf16[768,128]{1,0:T(8,128)(2,1)S(1)}, bf16[768,128]{1,0:T(8,128)(2,1)S(1)}, u32[]{:S(2)}, u32[]{:S(2)}) collective-permute-start(bf16[768,128]{1,0:T(8,128)(2,1)S(1)} %get-tuple-element.105), channel_id=1, source_target_pairs={{0,2},{1,3},{2,0},{3,1},{4,6},{5,7},{6,4},{7,5},{8,10},{9,11},{10,... | collective-permute-start | bytes 589832 | tf_op jit(solution)/shard_map/ppermute | solution.py:32
Sparse Core Ops, SparseCore 0:
  9.6 55.3 all-gather.1

commit v9 on v7

--- a/solution.py
+++ b/solution.py
@@ -21,6 +21,9 @@
 
 def cost(flops, moved, exponents=0):
     return pl.CostEstimate(flops=flops, bytes_accessed=moved, transcendentals=exponents)
+
+
+TINY = cost(0, 2**10)
 
 
 def swap(value, axis, mask):
@@ -143,7 +146,7 @@
             jax.ShapeDtypeStruct((heights[out], wide), source.dtype) for out in sorted(heights)
         ],
         compiler_params=SMALL,
-        cost_estimate=cost(0, 2 * source.nbytes),
+        cost_estimate=TINY,
         name="spread",
     )(source)
 
@@ -155,12 +158,11 @@
                 height = rows.stop - rows.start
                 out_ref[first : first + height] = refs[source][rows, columns]
 
-    moved = sum(2 * math.prod(shape) * 2 for shape, _ in outputs)
     return pl.pallas_call(
         kernel,
         out_shape=[jax.ShapeDtypeStruct(shape, sources[0].dtype) for shape, _ in outputs],
         compiler_params=SMALL,
-        cost_estimate=cost(0, moved),
+        cost_estimate=TINY,
         name="lay",
     )(*sources)
 
@@ -200,37 +202,41 @@
     return [own, left, right, upper, lower], places
 
 
-def product_kernel(jobs, depth, groups, own_ref, other_ref, *refs):
-    found, out_refs = refs[:groups], refs[groups:]
+def product_kernel(jobs, depth, held, groups, own_ref, other_ref, *refs):
+    count = len(held) * groups
+    found, out_refs = refs[:count], refs[count:]
     rows = found[0].shape[0] // 2
 
     def pick(step, half):
-        columns = slice(step * depth, (step + 1) * depth)
-        return jnp.concatenate([f[half * rows : (half + 1) * rows, columns] for f in found], 0)
-
-    for steps, out_ref in zip(jobs, out_refs):
+        for index, steps in enumerate(held):
+            if step in steps:
+                place = steps.index(step) * depth
+                part = found[index * groups : (index + 1) * groups]
+        span = slice(half * rows, (half + 1) * rows)
+        return jnp.concatenate([f[span, place : place + depth] for f in part], 0)
+
+    for (steps, low, high, _), out_ref in zip(jobs, out_refs):
         total = None
         for half, ref in enumerate((own_ref, other_ref)):
             grads = jnp.concatenate([pick(step, half) for step in steps], 1)
-            term = dot(ref[...], grads, 0, 0)
+            term = dot(ref[:, low:high], grads, 0, 0)
             total = term if total is None else total + term
         out_ref[...] = total.astype(out_ref.dtype)
 
 
-def products(pair, found, depth, jobs, dtypes):
-    groups = len(found)
-    tokens, wide = pair[0].shape
-    count = sum(len(steps) for steps in jobs)
-    return pl.pallas_call(
-        functools.partial(product_kernel, jobs, depth, groups),
+def products(pair, depth, found, jobs):
+    held = [steps for steps, _ in found]
+    groups = len(found[0][1])
+    return pl.pallas_call(
+        functools.partial(product_kernel, jobs, depth, held, groups),
         out_shape=[
-            jax.ShapeDtypeStruct((wide, len(steps) * depth), dtype)
-            for steps, dtype in zip(jobs, dtypes)
+            jax.ShapeDtypeStruct((high - low, len(steps) * depth), dtype)
+            for steps, low, high, dtype in jobs
         ],
         compiler_params=SMALL,
-        cost_estimate=cost(4 * tokens * wide * count * depth, 4 * tokens * wide),
+        cost_estimate=TINY,
         name="products",
-    )(*pair, *found)
+    )(*pair, *[array for _, arrays in found for array in arrays])
 
 
 def kv_kernel(rows, mine_ref, arrived_ref, mask_ref, *out_refs):
@@ -240,7 +246,7 @@
         for half in range(2):
             start = ((chip ^ step) * 2 + (core ^ half)) * rows
             span = pl.ds(pl.multiple_of(start, rows), rows)
-            total = mine_ref[span, :] + arrived_ref[span, :].astype(F32)
+            total = mine_ref[span, :] + arrived_ref[span, :]
             keep = mask_ref[span, :].astype(F32)
             out_ref[half * rows : (half + 1) * rows, :] = (total * keep).astype(BF16)
 
@@ -252,7 +258,7 @@
         functools.partial(kv_kernel, rows),
         out_shape=[jax.ShapeDtypeStruct((2 * rows, depth), BF16)] * count,
         compiler_params=SMALL,
-        cost_estimate=cost(0, 2 * mine.nbytes),
+        cost_estimate=TINY,
         name="kv_blocks",
     )(mine, arrived, mask)
 
@@ -264,6 +270,7 @@
     chips = lax.axis_size("tensor") // 2
     block = weight_mask.shape[0]
 
+    wide = block // 2
     other = swap(keys_values, "tensor", 1)
     parts = send_rows(inputs, block)
 
@@ -278,42 +285,49 @@
     order = sorted(range(chips), key=lambda s: [(s >> b) & 1 for b in range(8)])
     evens, odds = order[: chips // 2], order[chips // 2 :]
 
-    wide = block // 2
-    outputs = []
-    for cut in range(2):
-        columns, entries, first = slice(cut * wide, (cut + 1) * wide), [], 0
-        for source in places:
-            for array, span in source:
-                entries.append((array, span, columns, first))
-                first += span.stop - span.start
-        outputs.append(((groups * rows, wide), entries))
-    near, far = [(own, swap(own, "tensor", 1)) for own in lay(parts, outputs)]
-
-    stacked = jnp.concatenate(blocks, 1)
-    found = [stacked if s == 0 else swap(stacked, "dp", s) for s in range(groups)]
+    def gather(steps, values):
+        stacked = jnp.concatenate(values, 1)
+        return steps, [stacked if s == 0 else swap(stacked, "dp", s) for s in range(groups)]
+
+    entries, first = [], 0
+    for source in places:
+        for array, span in source:
+            entries.append((array, span, slice(None), first))
+            first += span.stop - span.start
+    (packed,) = lay(parts, [((first, 2 * wide), entries)])
+    pair = (packed, swap(packed, "tensor", 1))
 
     def send(value, step):
         return swap(value.astype(BF16), "tensor", 2 * step)
 
-    away = list(range(2, chips))
-    straight = products(far, found, depth, [(s,) for s in away], [BF16] * len(away))
-    straight, found = lax.optimization_barrier((straight, found))
-    straight = [send(value, s) for value, s in zip(straight, away)]
-    (first,) = products(near, found, depth, [tuple(odds)], [BF16])
+    far, near = (wide, 2 * wide), (0, wide)
+    away, close = list(range(2, chips)), [0, 1]
+    far_found = gather(away, [blocks[s] for s in away])
+    straight = products(pair, depth, [far_found], [((s,), *far, BF16) for s in away])
+    values, straight = lax.optimization_barrier(([blocks[s] for s in close], straight))
+    arrived = []
+    for value, step in zip(straight, away):
+        if arrived:
+            value, arrived[-1] = lax.optimization_barrier((value, arrived[-1]))
+        arrived.append(send(value, step))
+    found = [far_found, gather(close, values)]
+    (first,) = products(pair, depth, found, [(tuple(odds), *near, BF16)])
     sent = send(first, 1)
-    (even,) = products(near, found, depth, [tuple(evens)], [F32])
-    own, nearest = products(far, found, depth, [(0,), (1,)], [F32, BF16])
-    sent, straight = lax.optimization_barrier((sent, straight))
+    arrays, _ = lax.optimization_barrier(([arrays for _, arrays in found], first))
+    found = [(away, arrays[0]), (close, arrays[1])]
+    even, own, nearest = products(
+        pair, depth, found, [(tuple(evens), *near, F32), ((0,), *far, F32), ((1,), *far, BF16)]
+    )
     terms = [even, sent]
     columns, bit = chips // 2 * depth, 1
     while columns > depth:
         columns, bit = columns // 2, bit * 2
         away = sum(t[:, columns : 2 * columns].astype(F32) for t in terms).astype(BF16)
         terms.append(send(away, bit))
-    nearest, _ = lax.optimization_barrier((nearest, away))
-    straight.append(send(nearest, 1))
+    nearest, arrived[-1] = lax.optimization_barrier((nearest, arrived[-1]))
+    arrived.append(send(nearest, 1))
     upper = sum(t[:, :depth].astype(F32) for t in terms)
-    lower = own + sum(t.astype(F32) for t in straight)
+    lower = own + sum(t.astype(F32) for t in arrived)
     summed = jnp.concatenate([upper, lower], 0)
     weight_grad = jnp.where(weight_mask == 1, summed, 0.0)
     return (query_grad, weight_grad)

time: 98.5 us -> 101 us (1.025)
  waiting for transfers between devices: 44.7 us -> 50.1 us
  starting transfers between devices: 24.3 us -> 21.9 us
    ppermute x19 -> x21, waiting for transfers between devices: 44.7 us -> 50.1 us  [swap(): return lax.ppermute(value, axis, pairs)]
    ppermute x19 -> x21, starting transfers between devices: 24.3 us -> 21.9 us  [swap(): return lax.ppermute(value, axis, pairs)]
    pallas_call x4 -> x3, Pallas kernels: 4.18 us -> 3.94 us  [products(): pl.pallas_call(functools.partial(product_kernel, jobs, depth, held, group...]
  transfers between devices with their start and end apart: 19 -> 21, of which waited for: 10 -> 13; matrix products, arithmetic and copies ran while one was open for 0% -> 0% of each run, Pallas kernels for 24% -> 22%
where the time goes in v9:
time: 101 us
  waiting for transfers between devices  50.1 us (50%)
  Pallas kernels  25 us (25%)
  starting transfers between devices  21.9 us (22%)
  local copies, waits for them, and re-layouts  1.89 us (2%)
  other arithmetic  1.32 us (1%)
    ppermute x21, waiting for transfers between devices, swap(): return lax.ppermute(value, axis, pairs)  50.1 us
    ppermute x21, starting transfers between devices, swap(): return lax.ppermute(value, axis, pairs)  21.9 us
    pallas_call x1, Pallas kernels, attention(): pl.pallas_call(functools.partial(attention_kernel, height), grid=(width /...  17.7 us
    pallas_call x3, Pallas kernels, products(): pl.pallas_call(functools.partial(product_kernel, jobs, depth, held, group...  3.94 us
  transfers between devices with their start and end apart: 21, of which 13 were waited for; matrix products, arithmetic and copies ran while one was open for 0% of the time, Pallas kernels for 22%

profile of v9, /device:TPU:0, one launch (start us, length us, event | category | flops | bytes accessed | tf_op | source)
XLA Modules:
  0.0 100.9 jit_solution(768995944257163296)
XLA Ops:
  0.6 0.5 collective-permute-start
  1.1 1.6 %copy-done = bf16[128,8192]{1,0:T(8,128)(2,1)S(1)} copy-done((bf16[128,8192]{1,0:T(8,128)(2,1)S(1)}, bf16[128,8192]{1,0:T(8,128)(2,1)}, u32[]{:S(2)}) %copy-start) | copy-done | bytes 2097176
  2.7 0.1 spread.1
  2.9 2.6 %collective-permute-start.1 = (bf16[192,2048]{1,0:T(8,128)(2,1)S(1)}, bf16[192,2048]{1,0:T(8,128)(2,1)S(1)}, u32[]{:S(2)}, u32[]{:S(2)}) collective-permute-start(bf16[192,2048]{1,0:T(8,128)(2,1)S(1)} %get-tuple-element.51), channel_id=1, source_target_pairs={{0,8},{8,0},{16,24},{24,16},{1,9},{9,1},{17,25},{25,17},{2,10},{10... | collective-permute-start | bytes 2359304 | tf_op jit(solution)/shard_map/ppermute | solution.py:31
  5.5 1.5 %collective-permute-start.2 = (bf16[192,2048]{1,0:T(8,128)(2,1)S(1)}, bf16[192,2048]{1,0:T(8,128)(2,1)S(1)}, u32[]{:S(2)}, u32[]{:S(2)}) collective-permute-start(bf16[192,2048]{1,0:T(8,128)(2,1)S(1)} %get-tuple-element.52), channel_id=1, source_target_pairs={{0,16},{8,24},{16,0},{24,8},{1,17},{9,25},{17,1},{25,9},{2,18},{10... | collective-permute-start | bytes 2359304 | tf_op jit(solution)/shard_map/ppermute | solution.py:31
  7.0 0.0 collective-permute-done.other_ref
  7.0 17.7 %attention.1 = (bf16[1024,768]{1,0:T(8,128)(2,1)}, f32[1024,128]{1,0:T(8,128)S(1)}, f32[1024,128]{1,0:T(8,128)}) custom-call(bf16[1024,128]{1,0:T(8,128)(2,1)S(1)} %copy-done.2, bf16[1024,128]{1,0:T(8,128)(2,1)S(1)} %collective-permute-done.other_ref, bf16[1024,768]{1,0:T(8,128)(2,1)S(1)} %copy-done.1, bf16[1024,768]{1,0:T(8,128)(2,1)} %up_ref.1), custom_call_target="tpu_custom_call" | custom-call | flops 16106127360 | bytes 9437184 | tf_op jit(solution)/shard_map/attention/pallas_call | solution.py:109
  24.7 0.0 collective-permute-done.1.refs_0_.refs_1_
  24.7 0.4 collective-permute-done.2.refs_1_.refs_2_
  25.1 0.9 lay.2
  26.0 1.5 %collective-permute-start.7 = (bf16[64,2048]{1,0:T(8,128)(2,1)}, bf16[64,2048]{1,0:T(8,128)(2,1)S(1)}, u32[]{:S(2)}, u32[]{:S(2)}) collective-permute-start(bf16[64,2048]{1,0:T(8,128)(2,1)} %get-tuple-element.62), channel_id=1, source_target_pairs={{0,16},{8,24},{16,0},{24,8},{1,17},{9,25},{17,1},{25,9},{2,18},{10... | collective-permute-start | bytes 786440 | tf_op jit(solution)/shard_map/ppermute | solution.py:31
  27.5 0.5 collective-permute-start.8
  28.0 0.2 copy.8.mask_ref
  28.3 1.2 %kv_blocks.1 = (bf16[256,128]{1,0:T(8,128)(2,1)S(1)}, bf16[256,128]{1,0:T(8,128)(2,1)S(1)}, bf16[256,128]{1,0:T(8,128)(2,1)S(1)}, bf16[256,128]{1,0:T(8,128)(2,1)S(1)}) custom-call(f32[1024,128]{1,0:T(8,128)S(1)} %get-tuple-element.53.mine_ref, f32[1024,128]{1,0:T(8,128)} %collective-permute-done.3.arrived_ref, s32[1024,1]{1,0:T(8,128)S(1)} %copy.8.mask_ref), custom_call_target="tpu_custom_call" | custom-call | bytes 1024 | tf_op jit(solution)/shard_map/kv_blocks/pallas_call | solution.py:257
  29.5 1.6 %collective-permute-start.4 = (bf16[256,128]{1,0:T(8,128)(2,1)S(1)}, bf16[256,128]{1,0:T(8,128)(2,1)S(1)}, u32[]{:S(2)}, u32[]{:S(2)}) collective-permute-start(bf16[256,128]{1,0:T(8,128)(2,1)S(1)} %get-tuple-element.56), channel_id=1, source_target_pairs={{0,2},{1,3},{2,0},{3,1},{4,6},{5,7},{6,4},{7,5},{8,10},{9,11},{10,... | collective-permute-start | bytes 196616 | tf_op jit(solution)/shard_map/ppermute | solution.py:31
  31.2 2.6 %collective-permute-start.5 = (bf16[256,128]{1,0:T(8,128)(2,1)S(1)}, bf16[256,128]{1,0:T(8,128)(2,1)S(1)}, u32[]{:S(2)}, u32[]{:S(2)}) collective-permute-start(bf16[256,128]{1,0:T(8,128)(2,1)S(1)} %get-tuple-element.57), channel_id=1, source_target_pairs={{0,4},{1,5},{2,6},{3,7},{4,0},{5,1},{6,2},{7,3},{8,12},{9,13},{10,... | collective-permute-start | bytes 196616 | tf_op jit(solution)/shard_map/ppermute | solution.py:31
  33.7 0.2 collective-permute-start.6
  34.0 0.5 collective-permute-done.4
  34.5 3.2 %collective-permute-done.5 = bf16[256,128]{1,0:T(8,128)(2,1)S(1)} collective-permute-done((bf16[256,128]{1,0:T(8,128)(2,1)S(1)}, bf16[256,128]{1,0:T(8,128)(2,1)S(1)}, u32[]{:S(2)}, u32[]{:S(2)}) %collective-permute-start.5) | collective-permute-done | bytes 65568 | tf_op jit(solution)/shard_map/ppermute | solution.py:31
  37.7 2.1 %collective-permute-done.6 = bf16[256,128]{1,0:T(8,128)(2,1)S(1)} collective-permute-done((bf16[256,128]{1,0:T(8,128)(2,1)S(1)}, bf16[256,128]{1,0:T(8,128)(2,1)S(1)}, u32[]{:S(2)}, u32[]{:S(2)}) %collective-permute-start.6) | collective-permute-done | bytes 65568 | tf_op jit(solution)/shard_map/ppermute | solution.py:31
  39.8 1.1 %lay.3.own_ref = bf16[512,2048]{1,0:T(8,128)(2,1)S(1)} custom-call(bf16[128,2048]{1,0:T(8,128)(2,1)S(1)} %get-tuple-element.64.refs_0_, bf16[192,2048]{1,0:T(8,128)(2,1)S(1)} %collective-permute-done.1.refs_0_.refs_1_, bf16[192,2048]{1,0:T(8,128)(2,1)S(1)} %collective-permute-done.2.refs_1_.refs_2_, bf16[64,2048]{1,0:T(8,128)(2,1)S(1)} %collective-permute-done.7.refs_3_, ...), custom_call_target="tpu_custom_call" | custom-call | bytes 1024 | tf_op jit(solution)/shard_map/lay/pallas_call | solution.py:161
  40.9 0.1 collective-permute-start.9
  41.0 1.5 %collective-permute-start.12 = (bf16[256,256]{1,0:T(8,128)(2,1)S(1)}, bf16[256,256]{1,0:T(8,128)(2,1)S(1)}, u32[]{:S(2)}, u32[]{:S(2)}) collective-permute-start(bf16[256,256]{1,0:T(8,128)(2,1)S(1)} %constant_dynamic-update-slice_fusion.refs_0_), channel_id=1, source_target_pairs={{0,24},{8,16},{16,8},{24,0},{1,25},{9,17},{17,9},{25,1},{2,26},{10... | collective-permute-start | bytes 393224 | tf_op jit(solution)/shard_map/ppermute | solution.py:31
  42.5 1.5 %collective-permute-start.11 = (bf16[256,256]{1,0:T(8,128)(2,1)S(1)}, bf16[256,256]{1,0:T(8,128)(2,1)S(1)}, u32[]{:S(2)}, u32[]{:S(2)}) collective-permute-start(bf16[256,256]{1,0:T(8,128)(2,1)S(1)} %constant_dynamic-update-slice_fusion.refs_0_), channel_id=1, source_target_pairs={{0,16},{8,24},{16,0},{24,8},{1,17},{9,25},{17,1},{25,9},{2,18},{10... | collective-permute-start | bytes 393224 | tf_op jit(solution)/shard_map/ppermute | solution.py:31
  44.0 0.5 collective-permute-start.10
  44.6 3.7 %collective-permute-done.12.refs_3_ = bf16[256,256]{1,0:T(8,128)(2,1)S(1)} collective-permute-done((bf16[256,256]{1,0:T(8,128)(2,1)S(1)}, bf16[256,256]{1,0:T(8,128)(2,1)S(1)}, u32[]{:S(2)}, u32[]{:S(2)}) %collective-permute-start.12) | collective-permute-done | bytes 131104 | tf_op jit(solution)/shard_map/ppermute | solution.py:31
  48.3 2.4 %collective-permute-done.11.refs_2_ = bf16[256,256]{1,0:T(8,128)(2,1)S(1)} collective-permute-done((bf16[256,256]{1,0:T(8,128)(2,1)S(1)}, bf16[256,256]{1,0:T(8,128)(2,1)S(1)}, u32[]{:S(2)}, u32[]{:S(2)}) %collective-permute-start.11) | collective-permute-done | bytes 131104 | tf_op jit(solution)/shard_map/ppermute | solution.py:31
  50.7 1.3 %products.3 = (bf16[1024,128]{1,0:T(8,128)(2,1)S(1)}, bf16[1024,128]{1,0:T(8,128)(2,1)S(1)}) custom-call(bf16[512,2048]{1,0:T(8,128)(2,1)S(1)} %lay.3.own_ref, bf16[512,2048]{1,0:T(8,128)(2,1)S(1)} %collective-permute-done.9.other_ref, bf16[256,256]{1,0:T(8,128)(2,1)S(1)} %constant_dynamic-update-slice_fusion.refs_0_, ...), custom_call_target="tpu_custom_call" | custom-call | bytes 1024 | tf_op jit(solution)/shard_map/products/pallas_call | solution.py:230
  52.1 1.6 %collective-permute-start.15 = (bf16[256,256]{1,0:T(8,128)(2,1)S(1)}, bf16[256,256]{1,0:T(8,128)(2,1)S(1)}, u32[]{:S(2)}, u32[]{:S(2)}) collective-permute-start(bf16[256,256]{1,0:T(8,128)(2,1)S(1)} %constant_dynamic-update-slice_fusion.2.refs_4_), channel_id=1, source_target_pairs={{0,24},{8,16},{16,8},{24,0},{1,25},{9,17},{17,9},{25,1},{2,26},{10... | collective-permute-start | bytes 393224 | tf_op jit(solution)/shard_map/ppermute | solution.py:31
  53.7 0.7 collective-permute-start.14
  54.4 1.2 %collective-permute-start.13 = (bf16[256,256]{1,0:T(8,128)(2,1)S(1)}, bf16[256,256]{1,0:T(8,128)(2,1)S(1)}, u32[]{:S(2)}, u32[]{:S(2)}) collective-permute-start(bf16[256,256]{1,0:T(8,128)(2,1)S(1)} %constant_dynamic-update-slice_fusion.2.refs_4_), channel_id=1, source_target_pairs={{0,8},{8,0},{16,24},{24,16},{1,9},{9,1},{17,25},{25,17},{2,10},{10... | collective-permute-start | bytes 393224 | tf_op jit(solution)/shard_map/ppermute | solution.py:31
  55.6 0.7 collective-permute-start.18
  56.3 3.1 %collective-permute-done.15.refs_7_ = bf16[256,256]{1,0:T(8,128)(2,1)S(1)} collective-permute-done((bf16[256,256]{1,0:T(8,128)(2,1)S(1)}, bf16[256,256]{1,0:T(8,128)(2,1)S(1)}, u32[]{:S(2)}, u32[]{:S(2)}) %collective-permute-start.15) | collective-permute-done | bytes 131104 | tf_op jit(solution)/shard_map/ppermute | solution.py:31
  59.4 1.9 %collective-permute-done.14.refs_6_ = bf16[256,256]{1,0:T(8,128)(2,1)S(1)} collective-permute-done((bf16[256,256]{1,0:T(8,128)(2,1)S(1)}, bf16[256,256]{1,0:T(8,128)(2,1)S(1)}, u32[]{:S(2)}, u32[]{:S(2)}) %collective-permute-start.14) | collective-permute-done | bytes 131104 | tf_op jit(solution)/shard_map/ppermute | solution.py:31
  61.3 0.8 products.4
  62.1 0.1 collective-permute-start.16
  62.2 6.1 %collective-permute-done.18 = bf16[1024,128]{1,0:T(8,128)(2,1)S(1)} collective-permute-done((bf16[1024,128]{1,0:T(8,128)(2,1)S(1)}, bf16[1024,128]{1,0:T(8,128)(2,1)S(1)}, u32[]{:S(2)}, u32[]{:S(2)}) %collective-permute-start.18) | collective-permute-done | bytes 262176 | tf_op jit(solution)/shard_map/ppermute | solution.py:31
  68.3 2.3 %collective-permute-start.19 = (bf16[1024,128]{1,0:T(8,128)(2,1)S(1)}, bf16[1024,128]{1,0:T(8,128)(2,1)S(1)}, u32[]{:S(2)}, u32[]{:S(2)}) collective-permute-start(bf16[1024,128]{1,0:T(8,128)(2,1)S(1)} %get-tuple-element.91), channel_id=1, source_target_pairs={{0,6},{1,7},{2,4},{3,5},{4,2},{5,3},{6,0},{7,1},{8,14},{9,15},{10,... | collective-permute-start | bytes 786440 | tf_op jit(solution)/shard_map/ppermute | solution.py:31
  70.6 1.9 %products.5 = (f32[1024,256]{1,0:T(8,128)S(1)}, f32[1024,128]{1,0:T(8,128)S(1)}, bf16[1024,128]{1,0:T(8,128)(2,1)S(1)}) custom-call(bf16[512,2048]{1,0:T(8,128)(2,1)S(1)} %lay.3.own_ref, bf16[512,2048]{1,0:T(8,128)(2,1)S(1)} %collective-permute-done.9.other_ref, bf16[256,256]{1,0:T(8,128)(2,1)S(1)} %constant_dynamic-update-slice_fusion.refs_0_, ...), custom_call_target="tpu_custom_call" | custom-call | bytes 1024 | tf_op jit(solution)/shard_map/products/pallas_call | solution.py:230
  72.4 9.4 %collective-permute-done.19 = bf16[1024,128]{1,0:T(8,128)(2,1)S(1)} collective-permute-done((bf16[1024,128]{1,0:T(8,128)(2,1)S(1)}, bf16[1024,128]{1,0:T(8,128)(2,1)S(1)}, u32[]{:S(2)}, u32[]{:S(2)}) %collective-permute-start.19) | collective-permute-done | bytes 262176 | tf_op jit(solution)/shard_map/ppermute | solution.py:31
  81.9 3.2 %collective-permute-done.16 = bf16[1024,256]{1,0:T(8,128)(2,1)S(1)} collective-permute-done((bf16[1024,256]{1,0:T(8,128)(2,1)S(1)}, bf16[1024,256]{1,0:T(8,128)(2,1)S(1)}, u32[]{:S(2)}, u32[]{:S(2)}) %collective-permute-start.16) | collective-permute-done | bytes 524320 | tf_op jit(solution)/shard_map/ppermute | solution.py:31
  85.1 0.1 add_convert_fusion
  85.2 0.5 collective-permute-start.17
  85.6 6.2 %collective-permute-done.20 = bf16[1024,128]{1,0:T(8,128)(2,1)S(1)} collective-permute-done((bf16[1024,128]{1,0:T(8,128)(2,1)S(1)}, bf16[1024,128]{1,0:T(8,128)(2,1)S(1)}, u32[]{:S(2)}, u32[]{:S(2)}) %collective-permute-start.20) | collective-permute-done | bytes 262176 | tf_op jit(solution)/shard_map/ppermute | solution.py:31
  91.9 0.1 add_add_fusion
  92.0 7.8 %collective-permute-done.17 = bf16[1024,128]{1,0:T(8,128)(2,1)S(1)} collective-permute-done((bf16[1024,128]{1,0:T(8,128)(2,1)S(1)}, bf16[1024,128]{1,0:T(8,128)(2,1)S(1)}, u32[]{:S(2)}, u32[]{:S(2)}) %collective-permute-start.17) | collective-permute-done | bytes 262176 | tf_op jit(solution)/shard_map/ppermute | solution.py:31
  99.8 0.1 convert_add_fusion
  99.8 1.1 %maximum_select_fusion = f32[2048,128]{1,0:T(8,128)} fusion(f32[1024,128]{1,0:T(8,128)S(1)} %add_add_fusion, f32[1024,128]{1,0:T(8,128)S(1)} %convert_add_fusion, s32[2048,128]{1,0:T(8,128)S(1)} %copy-done.3), kind=kLoop, calls=%fused_computation | loop fusion | flops 786432 | bytes 3145728 | tf_op jit(solution)/shard_map/jit(_where)/select_n | solution.py:332
  (21 shorter events, 0.1 us)
Async XLA Ops:
  0.6 6.3 %collective-permute-start = (bf16[1024,128]{1,0:T(8,128)(2,1)}, bf16[1024,128]{1,0:T(8,128)(2,1)S(1)}, u32[]{:S(2)}, u32[]{:S(2)}) collective-permute-start(bf16[1024,128]{1,0:T(8,128)(2,1)} %own_ref.1), channel_id=1, source_target_pairs={{0,1},{1,0},{2,3},{3,2},{4,5},{5,4},{6,7},{7,6},{8,9},{9,8},{10,11... | collective-permute-start | bytes 786440 | tf_op jit(solution)/shard_map/ppermute | solution.py:31
  1.1 1.6 %copy-start = (bf16[128,8192]{1,0:T(8,128)(2,1)S(1)}, bf16[128,8192]{1,0:T(8,128)(2,1)}, u32[]{:S(2)}) copy-start(bf16[128,8192]{1,0:T(8,128)(2,1)} %source_ref.1) | copy-start | bytes 6291460
  2.7 4.2 %copy-start.1 = (bf16[1024,768]{1,0:T(8,128)(2,1)S(1)}, bf16[1024,768]{1,0:T(8,128)(2,1)}, u32[]{:S(2)}) copy-start(bf16[1024,768]{1,0:T(8,128)(2,1)} %q_ref.1) | copy-start | bytes 4718596
  2.7 4.2 %copy-start.2 = (bf16[1024,128]{1,0:T(8,128)(2,1)S(1)}, bf16[1024,128]{1,0:T(8,128)(2,1)}, u32[]{:S(2)}) copy-start(bf16[1024,128]{1,0:T(8,128)(2,1)} %own_ref.1) | copy-start | bytes 786436
  2.9 21.8 %collective-permute-start.1 = (bf16[192,2048]{1,0:T(8,128)(2,1)S(1)}, bf16[192,2048]{1,0:T(8,128)(2,1)S(1)}, u32[]{:S(2)}, u32[]{:S(2)}) collective-permute-start(bf16[192,2048]{1,0:T(8,128)(2,1)S(1)} %get-tuple-element.51), channel_id=1, source_target_pairs={{0,8},{8,0},{16,24},{24,16},{1,9},{9,1},{17,25},{25,17},{2,10},{10... | collective-permute-start | bytes 2359304 | tf_op jit(solution)/shard_map/ppermute | solution.py:31
  5.4 22.6 %copy-start.4 = (s32[1024,1]{0,1:T(1,128)S(1)}, s32[1024,1]{0,1:T(1,128)}, u32[]{:S(2)}) copy-start(s32[1024,1]{0,1:T(1,128)} %param.11) | copy-start | bytes 12292
  5.5 19.7 %collective-permute-start.2 = (bf16[192,2048]{1,0:T(8,128)(2,1)S(1)}, bf16[192,2048]{1,0:T(8,128)(2,1)S(1)}, u32[]{:S(2)}, u32[]{:S(2)}) collective-permute-start(bf16[192,2048]{1,0:T(8,128)(2,1)S(1)} %get-tuple-element.52), channel_id=1, source_target_pairs={{0,16},{8,24},{16,0},{24,8},{1,17},{9,25},{17,1},{25,9},{2,18},{10... | collective-permute-start | bytes 2359304 | tf_op jit(solution)/shard_map/ppermute | solution.py:31
  24.7 3.5 %collective-permute-start.3 = (f32[1024,128]{1,0:T(8,128)}, f32[1024,128]{1,0:T(8,128)}, u32[]{:S(2)}, u32[]{:S(2)}) collective-permute-start(f32[1024,128]{1,0:T(8,128)} %get-tuple-element.54), channel_id=1, source_target_pairs={{0,1},{1,0},{2,3},{3,2},{4,5},{5,4},{6,7},{7,6},{8,9},{9,8},{10,11... | collective-permute-start | bytes 1572872 | tf_op jit(solution)/shard_map/ppermute | solution.py:31
  26.0 13.8 %collective-permute-start.7 = (bf16[64,2048]{1,0:T(8,128)(2,1)}, bf16[64,2048]{1,0:T(8,128)(2,1)S(1)}, u32[]{:S(2)}, u32[]{:S(2)}) collective-permute-start(bf16[64,2048]{1,0:T(8,128)(2,1)} %get-tuple-element.62), channel_id=1, source_target_pairs={{0,16},{8,24},{16,0},{24,8},{1,17},{9,25},{17,1},{25,9},{2,18},{10... | collective-permute-start | bytes 786440 | tf_op jit(solution)/shard_map/ppermute | solution.py:31
  27.5 12.3 %collective-permute-start.8 = (bf16[64,2048]{1,0:T(8,128)(2,1)}, bf16[64,2048]{1,0:T(8,128)(2,1)}, u32[]{:S(2)}, u32[]{:S(2)}) collective-permute-start(bf16[64,2048]{1,0:T(8,128)(2,1)} %get-tuple-element.63), channel_id=1, source_target_pairs={{0,8},{8,0},{16,24},{24,16},{1,9},{9,1},{17,25},{25,17},{2,10},{10... | collective-permute-start | bytes 786440 | tf_op jit(solution)/shard_map/ppermute | solution.py:31
  29.5 5.0 %collective-permute-start.4 = (bf16[256,128]{1,0:T(8,128)(2,1)S(1)}, bf16[256,128]{1,0:T(8,128)(2,1)S(1)}, u32[]{:S(2)}, u32[]{:S(2)}) collective-permute-start(bf16[256,128]{1,0:T(8,128)(2,1)S(1)} %get-tuple-element.56), channel_id=1, source_target_pairs={{0,2},{1,3},{2,0},{3,1},{4,6},{5,7},{6,4},{7,5},{8,10},{9,11},{10,... | collective-permute-start | bytes 196616 | tf_op jit(solution)/shard_map/ppermute | solution.py:31
  31.2 6.6 %collective-permute-start.5 = (bf16[256,128]{1,0:T(8,128)(2,1)S(1)}, bf16[256,128]{1,0:T(8,128)(2,1)S(1)}, u32[]{:S(2)}, u32[]{:S(2)}) collective-permute-start(bf16[256,128]{1,0:T(8,128)(2,1)S(1)} %get-tuple-element.57), channel_id=1, source_target_pairs={{0,4},{1,5},{2,6},{3,7},{4,0},{5,1},{6,2},{7,3},{8,12},{9,13},{10,... | collective-permute-start | bytes 196616 | tf_op jit(solution)/shard_map/ppermute | solution.py:31
  33.7 6.1 %collective-permute-start.6 = (bf16[256,128]{1,0:T(8,128)(2,1)S(1)}, bf16[256,128]{1,0:T(8,128)(2,1)S(1)}, u32[]{:S(2)}, u32[]{:S(2)}) collective-permute-start(bf16[256,128]{1,0:T(8,128)(2,1)S(1)} %get-tuple-element.58), channel_id=1, source_target_pairs={{0,6},{1,7},{2,4},{3,5},{4,2},{5,3},{6,0},{7,1},{8,14},{9,15},{10,... | collective-permute-start | bytes 196616 | tf_op jit(solution)/shard_map/ppermute | solution.py:31
  40.9 9.8 %collective-permute-start.9 = (bf16[512,2048]{1,0:T(8,128)(2,1)S(1)}, bf16[512,2048]{1,0:T(8,128)(2,1)S(1)}, u32[]{:S(2)}, u32[]{:S(2)}) collective-permute-start(bf16[512,2048]{1,0:T(8,128)(2,1)S(1)} %lay.3.own_ref), channel_id=1, source_target_pairs={{0,1},{1,0},{2,3},{3,2},{4,5},{5,4},{6,7},{7,6},{8,9},{9,8},{10,11... | collective-permute-start | bytes 6291464 | tf_op jit(solution)/shard_map/ppermute | solution.py:31
  41.0 7.3 %collective-permute-start.12 = (bf16[256,256]{1,0:T(8,128)(2,1)S(1)}, bf16[256,256]{1,0:T(8,128)(2,1)S(1)}, u32[]{:S(2)}, u32[]{:S(2)}) collective-permute-start(bf16[256,256]{1,0:T(8,128)(2,1)S(1)} %constant_dynamic-update-slice_fusion.refs_0_), channel_id=1, source_target_pairs={{0,24},{8,16},{16,8},{24,0},{1,25},{9,17},{17,9},{25,1},{2,26},{10... | collective-permute-start | bytes 393224 | tf_op jit(solution)/shard_map/ppermute | solution.py:31
  42.5 8.2 %collective-permute-start.11 = (bf16[256,256]{1,0:T(8,128)(2,1)S(1)}, bf16[256,256]{1,0:T(8,128)(2,1)S(1)}, u32[]{:S(2)}, u32[]{:S(2)}) collective-permute-start(bf16[256,256]{1,0:T(8,128)(2,1)S(1)} %constant_dynamic-update-slice_fusion.refs_0_), channel_id=1, source_target_pairs={{0,16},{8,24},{16,0},{24,8},{1,17},{9,25},{17,1},{25,9},{2,18},{10... | collective-permute-start | bytes 393224 | tf_op jit(solution)/shard_map/ppermute | solution.py:31
  44.0 6.7 %collective-permute-start.10 = (bf16[256,256]{1,0:T(8,128)(2,1)S(1)}, bf16[256,256]{1,0:T(8,128)(2,1)S(1)}, u32[]{:S(2)}, u32[]{:S(2)}) collective-permute-start(bf16[256,256]{1,0:T(8,128)(2,1)S(1)} %constant_dynamic-update-slice_fusion.refs_0_), channel_id=1, source_target_pairs={{0,8},{8,0},{16,24},{24,16},{1,9},{9,1},{17,25},{25,17},{2,10},{10... | collective-permute-start | bytes 393224 | tf_op jit(solution)/shard_map/ppermute | solution.py:31
  52.1 7.3 %collective-permute-start.15 = (bf16[256,256]{1,0:T(8,128)(2,1)S(1)}, bf16[256,256]{1,0:T(8,128)(2,1)S(1)}, u32[]{:S(2)}, u32[]{:S(2)}) collective-permute-start(bf16[256,256]{1,0:T(8,128)(2,1)S(1)} %constant_dynamic-update-slice_fusion.2.refs_4_), channel_id=1, source_target_pairs={{0,24},{8,16},{16,8},{24,0},{1,25},{9,17},{17,9},{25,1},{2,26},{10... | collective-permute-start | bytes 393224 | tf_op jit(solution)/shard_map/ppermute | solution.py:31
  53.7 7.6 %collective-permute-start.14 = (bf16[256,256]{1,0:T(8,128)(2,1)S(1)}, bf16[256,256]{1,0:T(8,128)(2,1)S(1)}, u32[]{:S(2)}, u32[]{:S(2)}) collective-permute-start(bf16[256,256]{1,0:T(8,128)(2,1)S(1)} %constant_dynamic-update-slice_fusion.2.refs_4_), channel_id=1, source_target_pairs={{0,16},{8,24},{16,0},{24,8},{1,17},{9,25},{17,1},{25,9},{2,18},{10... | collective-permute-start | bytes 393224 | tf_op jit(solution)/shard_map/ppermute | solution.py:31
  54.4 6.9 %collective-permute-start.13 = (bf16[256,256]{1,0:T(8,128)(2,1)S(1)}, bf16[256,256]{1,0:T(8,128)(2,1)S(1)}, u32[]{:S(2)}, u32[]{:S(2)}) collective-permute-start(bf16[256,256]{1,0:T(8,128)(2,1)S(1)} %constant_dynamic-update-slice_fusion.2.refs_4_), channel_id=1, source_target_pairs={{0,8},{8,0},{16,24},{24,16},{1,9},{9,1},{17,25},{25,17},{2,10},{10... | collective-permute-start | bytes 393224 | tf_op jit(solution)/shard_map/ppermute | solution.py:31
  55.6 12.7 %collective-permute-start.18 = (bf16[1024,128]{1,0:T(8,128)(2,1)S(1)}, bf16[1024,128]{1,0:T(8,128)(2,1)S(1)}, u32[]{:S(2)}, u32[]{:S(2)}) collective-permute-start(bf16[1024,128]{1,0:T(8,128)(2,1)S(1)} %get-tuple-element.88), channel_id=1, source_target_pairs={{0,4},{1,5},{2,6},{3,7},{4,0},{5,1},{6,2},{7,3},{8,12},{9,13},{10,... | collective-permute-start | bytes 786440 | tf_op jit(solution)/shard_map/ppermute | solution.py:31
  62.1 23.0 %collective-permute-start.16 = (bf16[1024,256]{1,0:T(8,128)(2,1)S(1)}, bf16[1024,256]{1,0:T(8,128)(2,1)S(1)}, u32[]{:S(2)}, u32[]{:S(2)}) collective-permute-start(bf16[1024,256]{1,0:T(8,128)(2,1)S(1)} %products.4), channel_id=1, source_target_pairs={{0,2},{1,3},{2,0},{3,1},{4,6},{5,7},{6,4},{7,5},{8,10},{9,11},{10,... | collective-permute-start | bytes 1572872 | tf_op jit(solution)/shard_map/ppermute | solution.py:31
  68.3 13.6 %collective-permute-start.19 = (bf16[1024,128]{1,0:T(8,128)(2,1)S(1)}, bf16[1024,128]{1,0:T(8,128)(2,1)S(1)}, u32[]{:S(2)}, u32[]{:S(2)}) collective-permute-start(bf16[1024,128]{1,0:T(8,128)(2,1)S(1)} %get-tuple-element.91), channel_id=1, source_target_pairs={{0,6},{1,7},{2,4},{3,5},{4,2},{5,3},{6,0},{7,1},{8,14},{9,15},{10,... | collective-permute-start | bytes 786440 | tf_op jit(solution)/shard_map/ppermute | solution.py:31
  81.9 10.0 %collective-permute-start.20 = (bf16[1024,128]{1,0:T(8,128)(2,1)S(1)}, bf16[1024,128]{1,0:T(8,128)(2,1)S(1)}, u32[]{:S(2)}, u32[]{:S(2)}) collective-permute-start(bf16[1024,128]{1,0:T(8,128)(2,1)S(1)} %get-tuple-element.93), channel_id=1, source_target_pairs={{0,2},{1,3},{2,0},{3,1},{4,6},{5,7},{6,4},{7,5},{8,10},{9,11},{10,... | collective-permute-start | bytes 786440 | tf_op jit(solution)/shard_map/ppermute | solution.py:31
  85.1 14.7 %copy-start.3 = (s32[2048,128]{1,0:T(8,128)S(1)}, s32[2048,128]{1,0:T(8,128)}, u32[]{:S(2)}) copy-start(s32[2048,128]{1,0:T(8,128)} %param.10) | copy-start | bytes 3145732
  85.2 14.6 %collective-permute-start.17 = (bf16[1024,128]{1,0:T(8,128)(2,1)S(1)}, bf16[1024,128]{1,0:T(8,128)(2,1)S(1)}, u32[]{:S(2)}, u32[]{:S(2)}) collective-permute-start(bf16[1024,128]{1,0:T(8,128)(2,1)S(1)} %add_convert_fusion), channel_id=1, source_target_pairs={{0,4},{1,5},{2,6},{3,7},{4,0},{5,1},{6,2},{7,3},{8,12},{9,13},{10,... | collective-permute-start | bytes 786440 | tf_op jit(solution)/shard_map/ppermute | solution.py:31

commit v10 on v9

v10 whole, which is shorter than its diff:
```python
import functools
import math

import jax
import jax.numpy as jnp
from jax import lax
from jax.experimental import pallas as pl
from jax.experimental.pallas import tpu as pltpu
from jax.sharding import PartitionSpec as P

F32 = jnp.float32
BF16 = jnp.bfloat16
VMEM_LIMIT = 40 * 2**20
IN_ORDER = pltpu.CompilerParams(
    vmem_limit_bytes=VMEM_LIMIT, dimension_semantics=("arbitrary",)
)


SMALL = pltpu.CompilerParams(vmem_limit_bytes=16 * 2**20)


def cost(flops, moved, exponents=0):
    return pl.CostEstimate(flops=flops, bytes_accessed=moved, transcendentals=exponents)


TINY, LONG = cost(0, 2**10), cost(2 * 10**10, 2**20)


def swap(value, axis, mask):
    pairs = [(source, source ^ mask) for source in range(lax.axis_size(axis))]
    return lax.ppermute(value, axis, pairs)


def dot(left, right, left_dim, right_dim):
    dims = (((left_dim,), (right_dim,)), ((), ()))
    return lax.dot_general(left, right, dims, preferred_element_type=F32)


def attention_kernel(
    height, heads, own_ref, other_ref, q_ref, up_ref, dq_ref, mine_ref, theirs_ref,
    k_ref, v_ref, dk_ref, dv_ref,
):
    length, depth = k_ref.shape
    factor = depth**-0.5
    power = factor * math.log2(math.e)
    step = pl.program_id(0)
    is_even = lax.axis_index("tensor") % 2 == 0

    @pl.when(step == 0)
    def _():
        k_ref[...] = jnp.where(is_even, own_ref[...], other_ref[...])
        v_ref[...] = jnp.where(is_even, other_ref[...], own_ref[...])
        dk_ref[...] = jnp.zeros_like(dk_ref)
        dv_ref[...] = jnp.zeros_like(dv_ref)

    half = height // 2
    key_place = lax.broadcasted_iota(jnp.int32, (half, half), 0)
    query_place = lax.broadcasted_iota(jnp.int32, (half, half), 1)
    visible = key_place <= query_place

    def merge(reduce, join, long, short):
        long = reduce(long, axis=0, keepdims=True)
        short = reduce(short, axis=0, keepdims=True)
        return jnp.concatenate([long[:, :half], join(long[:, half:], short)], 1)

    def load(unit):
        head, block = unit
        span = slice(block * height, (block + 1) * height)
        columns = slice(head * depth, (head + 1) * depth)
        middle = block * height + half
        rows, end = slice(0, middle), slice(middle, middle + half)
        return q_ref[span, columns], up_ref[span, columns], rows, end

    def multiply(unit):
        query, upstream, rows, end = load(unit)
        return (
            dot(k_ref[rows], query, 1, 1),
            dot(k_ref[end], query[half:], 1, 1),
            dot(v_ref[rows], upstream, 1, 1),
            dot(v_ref[end], upstream[half:], 1, 1),
        )

    def normalize(unit, scores, scores_end, product, product_end):
        first = unit[1] * height
        corner = jnp.where(visible, scores[first:, :half], -jnp.inf)
        corner = jnp.concatenate([corner, scores[first:, half:]], 1)
        scores = corner if first == 0 else jnp.concatenate([scores[:first], corner], 0)
        scores_end = jnp.where(visible, scores_end, -jnp.inf)
        biggest = merge(jnp.max, jnp.maximum, scores, scores_end)
        weights = jnp.exp2((scores - biggest) * power)
        weights_end = jnp.exp2((scores_end - biggest[:, half:]) * power)
        scale = 1.0 / merge(jnp.sum, jnp.add, weights, weights_end)
        center = merge(jnp.sum, jnp.add, weights * product, weights_end * product_end) * scale
        weights = weights * scale
        weights_end = weights_end * scale[:, half:]
        grad = (weights * (product - center) * factor).astype(BF16)
        grad_end = (weights_end * (product_end - center[:, half:]) * factor).astype(BF16)
        return weights.astype(BF16), weights_end.astype(BF16), grad, grad_end

    def collect(unit, weights, weights_end, grad, grad_end):
        query, upstream, rows, end = load(unit)
        columns = slice(unit[0] * depth, (unit[0] + 1) * depth)
        dv_ref[rows] += dot(weights, upstream, 1, 0)
        dv_ref[end] += dot(weights_end, upstream[half:], 1, 0)
        dk_ref[rows] += dot(grad, query, 1, 0)
        dk_ref[end] += dot(grad_end, query[half:], 1, 0)
        query_grad = dot(grad, k_ref[rows], 0, 0)
        tail = query_grad[half:] + dot(grad_end, k_ref[end], 0, 0)
        dq_ref[rows.stop - half : rows.stop, columns] = query_grad[:half].astype(BF16)
        dq_ref[end, columns] = tail.astype(BF16)

    units = [(h, b) for h in range(heads) for b in reversed(range(length // height))]
    held, last = multiply(units[0]), None
    for index, unit in enumerate(units):
        ahead = multiply(units[index + 1]) if index + 1 < len(units) else None
        ready = normalize(unit, *held)
        if last is not None:
            collect(*last)
        last, held = (unit, *ready), ahead
    collect(*last)

    @pl.when(step == pl.num_programs(0) - 1)
    def _():
        mine_ref[...] = jnp.where(is_even, dk_ref[...], dv_ref[...])
        theirs_ref[...] = jnp.where(is_even, dv_ref[...], dk_ref[...])


def attention(own, other, queries, out_grad):
    length, width = queries.shape
    depth = own.shape[1]
    height = min(512, length)
    heads = 2 if width // depth % 2 == 0 else 1
    column = pl.BlockSpec((length, heads * depth), lambda h: (0, h))
    whole = pl.BlockSpec((length, depth), lambda h: (0, 0))
    sums = jax.ShapeDtypeStruct((length, depth), F32)
    return pl.pallas_call(
        functools.partial(attention_kernel, height, heads),
        grid=(width // (heads * depth),),
        in_specs=[whole, whole, column, column],
        out_specs=[column, whole, whole],
        out_shape=[jax.ShapeDtypeStruct((length, width), BF16), sums, sums],
        scratch_shapes=[
            pltpu.VMEM((length, depth), BF16),
            pltpu.VMEM((length, depth), BF16),
            pltpu.VMEM((length, depth), F32),
            pltpu.VMEM((length, depth), F32),
        ],
        compiler_params=IN_ORDER,
        cost_estimate=cost(
            20 * length * length * width,
            6 * queries.nbytes,
            length * length * width // depth,
        ),
        name="attention",
    )(own, other, queries, out_grad)


def spread_kernel(plan, source_ref, *out_refs):
    wide = out_refs[0].shape[1]
    place = lax.axis_index("dp")
    for out, first, step, low, high in plan:
        start = pl.multiple_of((place ^ step) * wide, wide)
        out_refs[out][first : first + high - low] = source_ref[low:high, pl.ds(start, wide)]


def spread(source, wide, plan):
    heights = {}
    for out, first, _, low, high in plan:
        heights[out] = max(heights.get(out, 0), first + high - low)
    return pl.pallas_call(
        functools.partial(spread_kernel, plan),
        out_shape=[
            jax.ShapeDtypeStruct((heights[out], wide), source.dtype) for out in sorted(heights)
        ],
        compiler_params=SMALL,
        cost_estimate=TINY,
        name="spread",
    )(source)


def lay(sources, outputs, hint=TINY):
    def kernel(*refs):
        for out_ref, (_, entries) in zip(refs[len(sources) :], outputs):
            for source, rows, columns, first in entries:
                height = rows.stop - rows.start
                out_ref[first : first + height] = refs[source][rows, columns]

    return pl.pallas_call(
        kernel,
        out_shape=[jax.ShapeDtypeStruct(shape, sources[0].dtype) for shape, _ in outputs],
        compiler_params=SMALL,
        cost_estimate=hint,
        name="lay",
    )(*sources)


def send_rows(inputs, wide):
    rows = inputs.shape[0]
    groups = lax.axis_size("dp")
    if groups != 4:
        parts = spread(inputs, wide, [(s, 0, s, 0, rows) for s in range(groups)])
        return [part if s == 0 else swap(part, "dp", s) for s, part in enumerate(parts)]
    half = rows // 2
    own, left, right = spread(
        inputs,
        wide,
        [(0, 0, 0, 0, rows), (1, 0, 1, 0, rows), (1, rows, 3, 0, half), (2, 0, 2, 0, rows),
         (2, rows, 3, half, rows)],
    )
    return [own, swap(left, "dp", 1), swap(right, "dp", 2)]


def pass_rows(parts, wide):
    rows = parts[0].shape[0]
    groups = lax.axis_size("dp")
    if groups != 4:
        return parts, [[(s, slice(0, rows))] for s in range(groups)]
    own, left, right = parts
    half = rows // 2
    tail = slice(rows, rows + half)
    every = slice(None)
    upper, lower = lay(
        [left, right],
        [((half, wide), [(0, tail, every, 0)]), ((half, wide), [(1, tail, every, 0)])],
    )
    upper, lower = swap(upper, "dp", 2), swap(lower, "dp", 1)
    whole, part = slice(0, rows), slice(0, half)
    places = [[(0, whole)], [(1, whole)], [(2, whole)], [(3, part), (4, part)]]
    return [own, left, right, upper, lower], places


def product_kernel(jobs, depth, own_ref, other_ref, own_grads_ref, other_grads_ref, *out_refs):
    pairs = ((own_ref, own_grads_ref), (other_ref, other_grads_ref))
    for (places, low, high, _), out_ref in zip(jobs, out_refs):
        columns = slice(places[0] * depth, (places[-1] + 1) * depth)
        total = sum(dot(ref[:, low:high], grads[:, columns], 0, 0) for ref, grads in pairs)
        out_ref[...] = total.astype(out_ref.dtype)


def products(pair, grads, depth, jobs, hint=TINY):
    return pl.pallas_call(
        functools.partial(product_kernel, jobs, depth),
        out_shape=[
            jax.ShapeDtypeStruct((high - low, len(places) * depth), dtype)
            for places, low, high, dtype in jobs
        ],
        compiler_params=SMALL,
        cost_estimate=hint,
        name="products",
    )(*pair, *grads)


def kv_kernel(rows, mine_ref, arrived_ref, mask_ref, *out_refs):
    place = lax.axis_index("tensor")
    chip, core = place // 2, place % 2
    for step, out_ref in enumerate(out_refs):
        for half in range(2):
            start = ((chip ^ step) * 2 + (core ^ half)) * rows
            span = pl.ds(pl.multiple_of(start, rows), rows)
            total = mine_ref[span, :] + arrived_ref[span, :].astype(F32)
            keep = mask_ref[span, :].astype(F32)
            out_ref[half * rows : (half + 1) * rows, :] = (total * keep).astype(BF16)


def kv_blocks(mine, arrived, mask, rows):
    length, depth = mine.shape
    count = length // (2 * rows)
    return pl.pallas_call(
        functools.partial(kv_kernel, rows),
        out_shape=[jax.ShapeDtypeStruct((2 * rows, depth), BF16)] * count,
        compiler_params=SMALL,
        cost_estimate=TINY,
        name="kv_blocks",
    )(mine, arrived, mask)


def per_device(inputs, queries, keys_values, out_grad, weight_mask, clip_mask):
    depth = keys_values.shape[1]
    rows = inputs.shape[0]
    groups = lax.axis_size("dp")
    chips = lax.axis_size("tensor") // 2
    block = weight_mask.shape[0]

    other = swap(keys_values, "tensor", 1)
    parts = send_rows(inputs, block)

    query_grad, mine, theirs = attention(keys_values, other, queries, out_grad)
    mine, parts = lax.optimization_barrier((mine, parts))
    arrived = swap(theirs, "tensor", 1)
    blocks = kv_blocks(mine, arrived, clip_mask, rows)

    blocks = [b if s == 0 else swap(b, "tensor", 2 * s) for s, b in enumerate(blocks)]
    parts, places = pass_rows(parts, block)
    blocks, parts = lax.optimization_barrier((blocks, parts))
    order = sorted(range(chips), key=lambda s: [(s >> b) & 1 for b in range(8)])
    evens, odds = order[: chips // 2], order[chips // 2 :]
    stacked = jnp.concatenate([blocks[s] for s in order], 1)
    found = [stacked if s == 0 else swap(stacked, "dp", s) for s in range(groups)]
    whole = (groups * rows, chips * depth)
    halves = [
        (whole, [(s, slice(h * rows, (h + 1) * rows), slice(None), s * rows) for s in range(groups)])
        for h in (0, 1)
    ]
    grads = lay(found, halves, LONG)

    entries, first = [], 0
    for source in places:
        for array, span in source:
            entries.append((array, span, slice(None), first))
            first += span.stop - span.start
    (packed,) = lay(parts, [((first, block), entries)])
    pair = (packed, swap(packed, "tensor", 1))

    def send(value, step):
        return swap(value.astype(BF16), "tensor", 2 * step)

    wide, half = block // 2, chips // 2
    far, near = (wide, block), (0, wide)
    away = list(range(2, chips))
    direct = products(pair, grads, depth, [((order.index(s),), *far, BF16) for s in away])
    direct, grads = lax.optimization_barrier((direct, grads))
    (first,) = products(pair, grads, depth, [(range(half, chips), *near, BF16)], LONG)
    direct = [send(value, s) for value, s in zip(direct, away)]
    sent = send(first, 1)
    grads, _ = lax.optimization_barrier((grads, first))
    jobs = [(range(half), *near, F32), ((0,), *far, F32), ((order.index(1),), *far, BF16)]
    even, own, nearest = products(pair, grads, depth, jobs)
    sent, direct = lax.optimization_barrier((sent, direct))
    terms = [even, sent]
    columns, bit = half * depth, 1
    while columns > depth:
        columns, bit = columns // 2, bit * 2
        value = sum(t[:, columns : 2 * columns].astype(F32) for t in terms).astype(BF16)
        terms.append(send(value, bit))
    nearest, _ = lax.optimization_barrier((nearest, value))
    direct.append(send(nearest, 1))
    upper = sum(t[:, :depth].astype(F32) for t in terms)
    lower = own + sum(t.astype(F32) for t in direct)
    summed = jnp.concatenate([upper, lower], 0)
    weight_grad = jnp.where(weight_mask == 1, summed, 0.0)
    return (query_grad, weight_grad)


def solution(mesh):
    spec = P("dp", "tensor")
    in_specs = (P(("dp", "tensor"), None), spec, spec, spec, spec, spec)
    return jax.shard_map(
        per_device, mesh=mesh, in_specs=in_specs, out_specs=(spec, spec), check_vma=False
    )
```

time: 101 us -> 92.8 us (0.919)
  waiting for transfers between devices: 50.1 us -> 42 us
  Pallas kernels: 25 us -> 23.1 us
  local copies, waits for them, and re-layouts: 1.89 us -> 3.3 us
    ppermute x21 -> x18, waiting for transfers between devices: 50.1 us -> 42 us  [swap(): return lax.ppermute(value, axis, pairs)]
    pallas_call x4, Pallas kernels: 21.7 us -> 19.7 us  [the longest x1 15.8 us: attention(): pl.pallas_call(functools.partial(attention_kernel, height, heads), grid=(...]
    unnamed x13 -> x16, local copies, waits for them, and re-layouts: 1.85 us -> 3.28 us
    ppermute x21 -> x18, starting transfers between devices: 21.9 us -> 22 us  [swap(): return lax.ppermute(value, axis, pairs)]
  transfers between devices with their start and end apart: 21 -> 18, of which waited for: 13 -> 9; matrix products, arithmetic and copies ran while one was open for 0% -> 0% of each run, Pallas kernels for 22% -> 23%
where the time goes in v10:
time: 92.8 us; the launch traced here: 92.5 us
  waiting for transfers between devices  42 us (45%)
  Pallas kernels  23.1 us (25%)
  starting transfers between devices  22 us (24%)
  local copies, waits for them, and re-layouts  3.3 us (4%)
  other arithmetic  1.33 us (1%)
    ppermute x18, waiting for transfers between devices, swap(): return lax.ppermute(value, axis, pairs)  42 us
    ppermute x18, starting transfers between devices, swap(): return lax.ppermute(value, axis, pairs)  22 us
    pallas_call x1, Pallas kernels, attention(): pl.pallas_call(functools.partial(attention_kernel, height, heads), grid=(...  15.8 us
    pallas_call x3, Pallas kernels, products(): pl.pallas_call(functools.partial(product_kernel, jobs, depth), out_shape=...  3.92 us
    unnamed x16, local copies, waits for them, and re-layouts  3.28 us
    pallas_call x3, Pallas kernels, lay(): pl.pallas_call(kernel, out_shape=[jax.ShapeDtypeStruct(shape, sources[0]....  1.99 us
  transfers between devices with their start and end apart: 18, of which 9 were waited for; matrix products, arithmetic and copies ran while one was open for 0% of the time, Pallas kernels for 23%

profile of v10, /device:TPU:0, one launch (start us, length us, event | category | flops | bytes accessed | tf_op | source)
XLA Modules:
  0.0 92.5 jit_solution(7847176051069948446)
XLA Ops:
  0.6 0.5 collective-permute-start
  1.1 1.6 %copy-done = bf16[128,8192]{1,0:T(8,128)(2,1)S(1)} copy-done((bf16[128,8192]{1,0:T(8,128)(2,1)S(1)}, bf16[128,8192]{1,0:T(8,128)(2,1)}, u32[]{:S(2)}) %copy-start) | copy-done | bytes 2097176
  2.7 0.1 spread.1
  2.9 2.6 %collective-permute-start.1 = (bf16[192,2048]{1,0:T(8,128)(2,1)S(1)}, bf16[192,2048]{1,0:T(8,128)(2,1)S(1)}, u32[]{:S(2)}, u32[]{:S(2)}) collective-permute-start(bf16[192,2048]{1,0:T(8,128)(2,1)S(1)} %get-tuple-element.47), channel_id=1, source_target_pairs={{0,8},{8,0},{16,24},{24,16},{1,9},{9,1},{17,25},{25,17},{2,10},{10... | collective-permute-start | bytes 2359304 | tf_op jit(solution)/shard_map/ppermute | solution.py:31
  5.4 1.5 %collective-permute-start.2 = (bf16[192,2048]{1,0:T(8,128)(2,1)S(1)}, bf16[192,2048]{1,0:T(8,128)(2,1)S(1)}, u32[]{:S(2)}, u32[]{:S(2)}) collective-permute-start(bf16[192,2048]{1,0:T(8,128)(2,1)S(1)} %get-tuple-element.48), channel_id=1, source_target_pairs={{0,16},{8,24},{16,0},{24,8},{1,17},{9,25},{17,1},{25,9},{2,18},{10... | collective-permute-start | bytes 2359304 | tf_op jit(solution)/shard_map/ppermute | solution.py:31
  7.0 0.0 collective-permute-done.other_ref
  7.0 0.0 copy-start.2
  7.0 1.4 %copy-done.2 = bf16[1024,768]{1,0:T(8,128)(2,1)S(1)} copy-done((bf16[1024,768]{1,0:T(8,128)(2,1)S(1)}, bf16[1024,768]{1,0:T(8,128)(2,1)}, u32[]{:S(2)}) %copy-start.2) | copy-done | bytes 1572888
  8.4 15.8 %attention.1 = (bf16[1024,768]{1,0:T(8,128)(2,1)}, f32[1024,128]{1,0:T(8,128)S(1)}, f32[1024,128]{1,0:T(8,128)}) custom-call(bf16[1024,128]{1,0:T(8,128)(2,1)S(1)} %copy-done.3, bf16[1024,128]{1,0:T(8,128)(2,1)S(1)} %collective-permute-done.other_ref, bf16[1024,768]{1,0:T(8,128)(2,1)S(1)} %copy-done.1, bf16[1024,768]{1,0:T(8,128)(2,1)S(1)} %copy-done.2), custom_call_target="tpu_custom_call" | custom-call | flops 16106127360 | bytes 9437184 | tf_op jit(solution)/shard_map/attention/pallas_call | solution.py:136
  24.2 0.9 collective-permute-done.2.refs_1_.refs_2_
  25.1 0.8 lay.3
  26.0 1.5 %collective-permute-start.7 = (bf16[64,2048]{1,0:T(8,128)(2,1)}, bf16[64,2048]{1,0:T(8,128)(2,1)S(1)}, u32[]{:S(2)}, u32[]{:S(2)}) collective-permute-start(bf16[64,2048]{1,0:T(8,128)(2,1)} %get-tuple-element.58), channel_id=1, source_target_pairs={{0,16},{8,24},{16,0},{24,8},{1,17},{9,25},{17,1},{25,9},{2,18},{10... | collective-permute-start | bytes 786440 | tf_op jit(solution)/shard_map/ppermute | solution.py:31
  27.5 0.5 collective-permute-start.8
  28.0 0.2 copy.8.mask_ref
  28.2 1.2 %kv_blocks.1 = (bf16[256,128]{1,0:T(8,128)(2,1)S(1)}, bf16[256,128]{1,0:T(8,128)(2,1)S(1)}, bf16[256,128]{1,0:T(8,128)(2,1)S(1)}, bf16[256,128]{1,0:T(8,128)(2,1)S(1)}) custom-call(f32[1024,128]{1,0:T(8,128)S(1)} %get-tuple-element.49.mine_ref, f32[1024,128]{1,0:T(8,128)} %collective-permute-done.3.arrived_ref, s32[1024,1]{1,0:T(8,128)S(1)} %copy.8.mask_ref), custom_call_target="tpu_custom_call" | custom-call | bytes 1024 | tf_op jit(solution)/shard_map/kv_blocks/pallas_call | solution.py:268
  29.5 1.6 %collective-permute-start.4 = (bf16[256,128]{1,0:T(8,128)(2,1)S(1)}, bf16[256,128]{1,0:T(8,128)(2,1)S(1)}, u32[]{:S(2)}, u32[]{:S(2)}) collective-permute-start(bf16[256,128]{1,0:T(8,128)(2,1)S(1)} %get-tuple-element.52), channel_id=1, source_target_pairs={{0,2},{1,3},{2,0},{3,1},{4,6},{5,7},{6,4},{7,5},{8,10},{9,11},{10,... | collective-permute-start | bytes 196616 | tf_op jit(solution)/shard_map/ppermute | solution.py:31
  31.1 2.6 %collective-permute-start.5 = (bf16[256,128]{1,0:T(8,128)(2,1)S(1)}, bf16[256,128]{1,0:T(8,128)(2,1)S(1)}, u32[]{:S(2)}, u32[]{:S(2)}) collective-permute-start(bf16[256,128]{1,0:T(8,128)(2,1)S(1)} %get-tuple-element.53), channel_id=1, source_target_pairs={{0,4},{1,5},{2,6},{3,7},{4,0},{5,1},{6,2},{7,3},{8,12},{9,13},{10,... | collective-permute-start | bytes 196616 | tf_op jit(solution)/shard_map/ppermute | solution.py:31
  33.7 0.2 collective-permute-start.6
  33.9 0.5 collective-permute-done.4
  34.5 3.2 %collective-permute-done.5 = bf16[256,128]{1,0:T(8,128)(2,1)S(1)} collective-permute-done((bf16[256,128]{1,0:T(8,128)(2,1)S(1)}, bf16[256,128]{1,0:T(8,128)(2,1)S(1)}, u32[]{:S(2)}, u32[]{:S(2)}) %collective-permute-start.5) | collective-permute-done | bytes 65568 | tf_op jit(solution)/shard_map/ppermute | solution.py:31
  37.7 2.1 %collective-permute-done.6 = bf16[256,128]{1,0:T(8,128)(2,1)S(1)} collective-permute-done((bf16[256,128]{1,0:T(8,128)(2,1)S(1)}, bf16[256,128]{1,0:T(8,128)(2,1)S(1)}, u32[]{:S(2)}, u32[]{:S(2)}) %collective-permute-start.6) | collective-permute-done | bytes 65568 | tf_op jit(solution)/shard_map/ppermute | solution.py:31
  39.9 1.5 %collective-permute-start.12 = (bf16[256,512]{1,0:T(8,128)(2,1)S(1)}, bf16[256,512]{1,0:T(8,128)(2,1)S(1)}, u32[]{:S(2)}, u32[]{:S(2)}) collective-permute-start(bf16[256,512]{1,0:T(8,128)(2,1)S(1)} %constant_dynamic-update-slice_fusion.refs_0_), channel_id=1, source_target_pairs={{0,24},{8,16},{16,8},{24,0},{1,25},{9,17},{17,9},{25,1},{2,26},{10... | collective-permute-start | bytes 786440 | tf_op jit(solution)/shard_map/ppermute | solution.py:31
  41.4 1.5 %collective-permute-start.11 = (bf16[256,512]{1,0:T(8,128)(2,1)S(1)}, bf16[256,512]{1,0:T(8,128)(2,1)S(1)}, u32[]{:S(2)}, u32[]{:S(2)}) collective-permute-start(bf16[256,512]{1,0:T(8,128)(2,1)S(1)} %constant_dynamic-update-slice_fusion.refs_0_), channel_id=1, source_target_pairs={{0,16},{8,24},{16,0},{24,8},{1,17},{9,25},{17,1},{25,9},{2,18},{10... | collective-permute-start | bytes 786440 | tf_op jit(solution)/shard_map/ppermute | solution.py:31
  42.9 0.5 collective-permute-start.10
  43.4 1.1 %lay.4.own_ref = bf16[512,2048]{1,0:T(8,128)(2,1)S(1)} custom-call(bf16[128,2048]{1,0:T(8,128)(2,1)S(1)} %get-tuple-element.60.refs_0_, bf16[192,2048]{1,0:T(8,128)(2,1)S(1)} %collective-permute-done.1.refs_0_.refs_1_, bf16[192,2048]{1,0:T(8,128)(2,1)S(1)} %collective-permute-done.2.refs_1_.refs_2_, bf16[64,2048]{1,0:T(8,128)(2,1)S(1)} %collective-permute-done.7.refs_3_, ...), custom_call_target="tpu_custom_call" | custom-call | bytes 1024 | tf_op jit(solution)/shard_map/lay/pallas_call | solution.py:188
  44.5 0.1 collective-permute-start.9
  44.6 4.8 %collective-permute-done.12.refs_3_ = bf16[256,512]{1,0:T(8,128)(2,1)S(1)} collective-permute-done((bf16[256,512]{1,0:T(8,128)(2,1)S(1)}, bf16[256,512]{1,0:T(8,128)(2,1)S(1)}, u32[]{:S(2)}, u32[]{:S(2)}) %collective-permute-start.12) | collective-permute-done | bytes 262176 | tf_op jit(solution)/shard_map/ppermute | solution.py:31
  49.4 2.7 %collective-permute-done.11.refs_2_ = bf16[256,512]{1,0:T(8,128)(2,1)S(1)} collective-permute-done((bf16[256,512]{1,0:T(8,128)(2,1)S(1)}, bf16[256,512]{1,0:T(8,128)(2,1)S(1)}, u32[]{:S(2)}, u32[]{:S(2)}) %collective-permute-start.11) | collective-permute-done | bytes 262176 | tf_op jit(solution)/shard_map/ppermute | solution.py:31
  52.1 0.0 collective-permute-done.10.refs_1_
  52.1 0.1 lay.5
  52.1 0.0 collective-permute-done.9.other_ref
  52.2 1.3 %products.3 = (bf16[1024,128]{1,0:T(8,128)(2,1)S(1)}, bf16[1024,128]{1,0:T(8,128)(2,1)S(1)}) custom-call(bf16[512,2048]{1,0:T(8,128)(2,1)S(1)} %lay.4.own_ref, bf16[512,2048]{1,0:T(8,128)(2,1)S(1)} %collective-permute-done.9.other_ref, bf16[512,512]{1,0:T(8,128)(2,1)S(1)} %get-tuple-element.75.own_grads_ref, ...), custom_call_target="tpu_custom_call" | custom-call | bytes 1024 | tf_op jit(solution)/shard_map/products/pallas_call | solution.py:241
  53.5 0.8 products.4
  54.2 0.1 collective-permute-start.13
  54.3 1.9 %collective-permute-start.14 = (bf16[1024,128]{1,0:T(8,128)(2,1)S(1)}, bf16[1024,128]{1,0:T(8,128)(2,1)S(1)}, u32[]{:S(2)}, u32[]{:S(2)}) collective-permute-start(bf16[1024,128]{1,0:T(8,128)(2,1)S(1)} %get-tuple-element.78), channel_id=1, source_target_pairs={{0,4},{1,5},{2,6},{3,7},{4,0},{5,1},{6,2},{7,3},{8,12},{9,13},{10,... | collective-permute-start | bytes 786440 | tf_op jit(solution)/shard_map/ppermute | solution.py:31
  56.2 2.5 %collective-permute-start.15 = (bf16[1024,128]{1,0:T(8,128)(2,1)S(1)}, bf16[1024,128]{1,0:T(8,128)(2,1)S(1)}, u32[]{:S(2)}, u32[]{:S(2)}) collective-permute-start(bf16[1024,128]{1,0:T(8,128)(2,1)S(1)} %get-tuple-element.79), channel_id=1, source_target_pairs={{0,6},{1,7},{2,4},{3,5},{4,2},{5,3},{6,0},{7,1},{8,14},{9,15},{10,... | collective-permute-start | bytes 786440 | tf_op jit(solution)/shard_map/ppermute | solution.py:31
  58.7 1.8 %products.5 = (f32[1024,256]{1,0:T(8,128)S(1)}, f32[1024,128]{1,0:T(8,128)S(1)}, bf16[1024,128]{1,0:T(8,128)(2,1)S(1)}) custom-call(bf16[512,2048]{1,0:T(8,128)(2,1)S(1)} %lay.4.own_ref, bf16[512,2048]{1,0:T(8,128)(2,1)S(1)} %collective-permute-done.9.other_ref, bf16[512,512]{1,0:T(8,128)(2,1)S(1)} %get-tuple-element.75.own_grads_ref, ...), custom_call_target="tpu_custom_call" | custom-call | bytes 1024 | tf_op jit(solution)/shard_map/products/pallas_call | solution.py:241
  60.6 11.8 %collective-permute-done.14 = bf16[1024,128]{1,0:T(8,128)(2,1)S(1)} collective-permute-done((bf16[1024,128]{1,0:T(8,128)(2,1)S(1)}, bf16[1024,128]{1,0:T(8,128)(2,1)S(1)}, u32[]{:S(2)}, u32[]{:S(2)}) %collective-permute-start.14) | collective-permute-done | bytes 262176 | tf_op jit(solution)/shard_map/ppermute | solution.py:31
  72.4 6.0 %collective-permute-done.15 = bf16[1024,128]{1,0:T(8,128)(2,1)S(1)} collective-permute-done((bf16[1024,128]{1,0:T(8,128)(2,1)S(1)}, bf16[1024,128]{1,0:T(8,128)(2,1)S(1)}, u32[]{:S(2)}, u32[]{:S(2)}) %collective-permute-start.15) | collective-permute-done | bytes 262176 | tf_op jit(solution)/shard_map/ppermute | solution.py:31
  78.4 0.0 collective-permute-done.13
  78.4 0.1 add_convert_fusion
  78.4 1.8 %collective-permute-start.16 = (bf16[1024,128]{1,0:T(8,128)(2,1)S(1)}, bf16[1024,128]{1,0:T(8,128)(2,1)S(1)}, u32[]{:S(2)}, u32[]{:S(2)}) collective-permute-start(bf16[1024,128]{1,0:T(8,128)(2,1)S(1)} %add_convert_fusion), channel_id=1, source_target_pairs={{0,4},{1,5},{2,6},{3,7},{4,0},{5,1},{6,2},{7,3},{8,12},{9,13},{10,... | collective-permute-start | bytes 786440 | tf_op jit(solution)/shard_map/ppermute | solution.py:31
  80.2 1.0 %collective-permute-start.17 = (bf16[1024,128]{1,0:T(8,128)(2,1)S(1)}, bf16[1024,128]{1,0:T(8,128)(2,1)S(1)}, u32[]{:S(2)}, u32[]{:S(2)}) collective-permute-start(bf16[1024,128]{1,0:T(8,128)(2,1)S(1)} %get-tuple-element.85), channel_id=1, source_target_pairs={{0,2},{1,3},{2,0},{3,1},{4,6},{5,7},{6,4},{7,5},{8,10},{9,11},{10,... | collective-permute-start | bytes 786440 | tf_op jit(solution)/shard_map/ppermute | solution.py:31
  81.2 9.9 %collective-permute-done.16 = bf16[1024,128]{1,0:T(8,128)(2,1)S(1)} collective-permute-done((bf16[1024,128]{1,0:T(8,128)(2,1)S(1)}, bf16[1024,128]{1,0:T(8,128)(2,1)S(1)}, u32[]{:S(2)}, u32[]{:S(2)}) %collective-permute-start.16) | collective-permute-done | bytes 262176 | tf_op jit(solution)/shard_map/ppermute | solution.py:31
  91.2 0.1 convert_add_fusion
  91.3 0.0 collective-permute-done.17
  91.3 0.1 add_add_fusion
  91.4 1.1 %maximum_select_fusion = f32[2048,128]{1,0:T(8,128)} fusion(f32[1024,128]{1,0:T(8,128)S(1)} %add_add_fusion, f32[1024,128]{1,0:T(8,128)S(1)} %convert_add_fusion, s32[2048,128]{1,0:T(8,128)S(1)} %copy-done.4), kind=kLoop, calls=%fused_computation | loop fusion | flops 786432 | bytes 3145728 | tf_op jit(solution)/shard_map/jit(_where)/select_n | solution.py:340
  (18 shorter events, 0.1 us)
Async XLA Ops:
  0.6 6.3 %collective-permute-start = (bf16[1024,128]{1,0:T(8,128)(2,1)}, bf16[1024,128]{1,0:T(8,128)(2,1)S(1)}, u32[]{:S(2)}, u32[]{:S(2)}) collective-permute-start(bf16[1024,128]{1,0:T(8,128)(2,1)} %own_ref.1), channel_id=1, source_target_pairs={{0,1},{1,0},{2,3},{3,2},{4,5},{5,4},{6,7},{7,6},{8,9},{9,8},{10,11... | collective-permute-start | bytes 786440 | tf_op jit(solution)/shard_map/ppermute | solution.py:31
  1.1 1.6 %copy-start = (bf16[128,8192]{1,0:T(8,128)(2,1)S(1)}, bf16[128,8192]{1,0:T(8,128)(2,1)}, u32[]{:S(2)}) copy-start(bf16[128,8192]{1,0:T(8,128)(2,1)} %source_ref.1) | copy-start | bytes 6291460
  2.7 4.2 %copy-start.1 = (bf16[1024,768]{1,0:T(8,128)(2,1)S(1)}, bf16[1024,768]{1,0:T(8,128)(2,1)}, u32[]{:S(2)}) copy-start(bf16[1024,768]{1,0:T(8,128)(2,1)} %q_ref.1) | copy-start | bytes 4718596
  2.7 4.2 %copy-start.3 = (bf16[1024,128]{1,0:T(8,128)(2,1)S(1)}, bf16[1024,128]{1,0:T(8,128)(2,1)}, u32[]{:S(2)}) copy-start(bf16[1024,128]{1,0:T(8,128)(2,1)} %own_ref.1) | copy-start | bytes 786436
  2.9 21.3 %collective-permute-start.1 = (bf16[192,2048]{1,0:T(8,128)(2,1)S(1)}, bf16[192,2048]{1,0:T(8,128)(2,1)S(1)}, u32[]{:S(2)}, u32[]{:S(2)}) collective-permute-start(bf16[192,2048]{1,0:T(8,128)(2,1)S(1)} %get-tuple-element.47), channel_id=1, source_target_pairs={{0,8},{8,0},{16,24},{24,16},{1,9},{9,1},{17,25},{25,17},{2,10},{10... | collective-permute-start | bytes 2359304 | tf_op jit(solution)/shard_map/ppermute | solution.py:31
  5.4 19.7 %collective-permute-start.2 = (bf16[192,2048]{1,0:T(8,128)(2,1)S(1)}, bf16[192,2048]{1,0:T(8,128)(2,1)S(1)}, u32[]{:S(2)}, u32[]{:S(2)}) collective-permute-start(bf16[192,2048]{1,0:T(8,128)(2,1)S(1)} %get-tuple-element.48), channel_id=1, source_target_pairs={{0,16},{8,24},{16,0},{24,8},{1,17},{9,25},{17,1},{25,9},{2,18},{10... | collective-permute-start | bytes 2359304 | tf_op jit(solution)/shard_map/ppermute | solution.py:31
  7.0 1.4 %copy-start.2 = (bf16[1024,768]{1,0:T(8,128)(2,1)S(1)}, bf16[1024,768]{1,0:T(8,128)(2,1)}, u32[]{:S(2)}) copy-start(bf16[1024,768]{1,0:T(8,128)(2,1)} %up_ref.1) | copy-start | bytes 4718596
  8.4 19.6 %copy-start.5 = (s32[1024,1]{0,1:T(1,128)S(1)}, s32[1024,1]{0,1:T(1,128)}, u32[]{:S(2)}) copy-start(s32[1024,1]{0,1:T(1,128)} %param.11) | copy-start | bytes 12292
  24.2 4.0 %collective-permute-start.3 = (f32[1024,128]{1,0:T(8,128)}, f32[1024,128]{1,0:T(8,128)}, u32[]{:S(2)}, u32[]{:S(2)}) collective-permute-start(f32[1024,128]{1,0:T(8,128)} %get-tuple-element.50), channel_id=1, source_target_pairs={{0,1},{1,0},{2,3},{3,2},{4,5},{5,4},{6,7},{7,6},{8,9},{9,8},{10,11... | collective-permute-start | bytes 1572872 | tf_op jit(solution)/shard_map/ppermute | solution.py:31
  26.0 13.8 %collective-permute-start.7 = (bf16[64,2048]{1,0:T(8,128)(2,1)}, bf16[64,2048]{1,0:T(8,128)(2,1)S(1)}, u32[]{:S(2)}, u32[]{:S(2)}) collective-permute-start(bf16[64,2048]{1,0:T(8,128)(2,1)} %get-tuple-element.58), channel_id=1, source_target_pairs={{0,16},{8,24},{16,0},{24,8},{1,17},{9,25},{17,1},{25,9},{2,18},{10... | collective-permute-start | bytes 786440 | tf_op jit(solution)/shard_map/ppermute | solution.py:31
  27.5 12.3 %collective-permute-start.8 = (bf16[64,2048]{1,0:T(8,128)(2,1)}, bf16[64,2048]{1,0:T(8,128)(2,1)}, u32[]{:S(2)}, u32[]{:S(2)}) collective-permute-start(bf16[64,2048]{1,0:T(8,128)(2,1)} %get-tuple-element.59), channel_id=1, source_target_pairs={{0,8},{8,0},{16,24},{24,16},{1,9},{9,1},{17,25},{25,17},{2,10},{10... | collective-permute-start | bytes 786440 | tf_op jit(solution)/shard_map/ppermute | solution.py:31
  29.5 5.0 %collective-permute-start.4 = (bf16[256,128]{1,0:T(8,128)(2,1)S(1)}, bf16[256,128]{1,0:T(8,128)(2,1)S(1)}, u32[]{:S(2)}, u32[]{:S(2)}) collective-permute-start(bf16[256,128]{1,0:T(8,128)(2,1)S(1)} %get-tuple-element.52), channel_id=1, source_target_pairs={{0,2},{1,3},{2,0},{3,1},{4,6},{5,7},{6,4},{7,5},{8,10},{9,11},{10,... | collective-permute-start | bytes 196616 | tf_op jit(solution)/shard_map/ppermute | solution.py:31
  31.1 6.6 %collective-permute-start.5 = (bf16[256,128]{1,0:T(8,128)(2,1)S(1)}, bf16[256,128]{1,0:T(8,128)(2,1)S(1)}, u32[]{:S(2)}, u32[]{:S(2)}) collective-permute-start(bf16[256,128]{1,0:T(8,128)(2,1)S(1)} %get-tuple-element.53), channel_id=1, source_target_pairs={{0,4},{1,5},{2,6},{3,7},{4,0},{5,1},{6,2},{7,3},{8,12},{9,13},{10,... | collective-permute-start | bytes 196616 | tf_op jit(solution)/shard_map/ppermute | solution.py:31
  33.7 6.1 %collective-permute-start.6 = (bf16[256,128]{1,0:T(8,128)(2,1)S(1)}, bf16[256,128]{1,0:T(8,128)(2,1)S(1)}, u32[]{:S(2)}, u32[]{:S(2)}) collective-permute-start(bf16[256,128]{1,0:T(8,128)(2,1)S(1)} %get-tuple-element.54), channel_id=1, source_target_pairs={{0,6},{1,7},{2,4},{3,5},{4,2},{5,3},{6,0},{7,1},{8,14},{9,15},{10,... | collective-permute-start | bytes 196616 | tf_op jit(solution)/shard_map/ppermute | solution.py:31
  39.9 9.5 %collective-permute-start.12 = (bf16[256,512]{1,0:T(8,128)(2,1)S(1)}, bf16[256,512]{1,0:T(8,128)(2,1)S(1)}, u32[]{:S(2)}, u32[]{:S(2)}) collective-permute-start(bf16[256,512]{1,0:T(8,128)(2,1)S(1)} %constant_dynamic-update-slice_fusion.refs_0_), channel_id=1, source_target_pairs={{0,24},{8,16},{16,8},{24,0},{1,25},{9,17},{17,9},{25,1},{2,26},{10... | collective-permute-start | bytes 786440 | tf_op jit(solution)/shard_map/ppermute | solution.py:31
  41.4 10.7 %collective-permute-start.11 = (bf16[256,512]{1,0:T(8,128)(2,1)S(1)}, bf16[256,512]{1,0:T(8,128)(2,1)S(1)}, u32[]{:S(2)}, u32[]{:S(2)}) collective-permute-start(bf16[256,512]{1,0:T(8,128)(2,1)S(1)} %constant_dynamic-update-slice_fusion.refs_0_), channel_id=1, source_target_pairs={{0,16},{8,24},{16,0},{24,8},{1,17},{9,25},{17,1},{25,9},{2,18},{10... | collective-permute-start | bytes 786440 | tf_op jit(solution)/shard_map/ppermute | solution.py:31
  42.9 9.2 %collective-permute-start.10 = (bf16[256,512]{1,0:T(8,128)(2,1)S(1)}, bf16[256,512]{1,0:T(8,128)(2,1)S(1)}, u32[]{:S(2)}, u32[]{:S(2)}) collective-permute-start(bf16[256,512]{1,0:T(8,128)(2,1)S(1)} %constant_dynamic-update-slice_fusion.refs_0_), channel_id=1, source_target_pairs={{0,8},{8,0},{16,24},{24,16},{1,9},{9,1},{17,25},{25,17},{2,10},{10... | collective-permute-start | bytes 786440 | tf_op jit(solution)/shard_map/ppermute | solution.py:31
  44.5 7.6 %collective-permute-start.9 = (bf16[512,2048]{1,0:T(8,128)(2,1)S(1)}, bf16[512,2048]{1,0:T(8,128)(2,1)S(1)}, u32[]{:S(2)}, u32[]{:S(2)}) collective-permute-start(bf16[512,2048]{1,0:T(8,128)(2,1)S(1)} %lay.4.own_ref), channel_id=1, source_target_pairs={{0,1},{1,0},{2,3},{3,2},{4,5},{5,4},{6,7},{7,6},{8,9},{9,8},{10,11... | collective-permute-start | bytes 6291464 | tf_op jit(solution)/shard_map/ppermute | solution.py:31
  54.2 24.1 %collective-permute-start.13 = (bf16[1024,256]{1,0:T(8,128)(2,1)S(1)}, bf16[1024,256]{1,0:T(8,128)(2,1)S(1)}, u32[]{:S(2)}, u32[]{:S(2)}) collective-permute-start(bf16[1024,256]{1,0:T(8,128)(2,1)S(1)} %products.4), channel_id=1, source_target_pairs={{0,2},{1,3},{2,0},{3,1},{4,6},{5,7},{6,4},{7,5},{8,10},{9,11},{10,... | collective-permute-start | bytes 1572872 | tf_op jit(solution)/shard_map/ppermute | solution.py:31
  54.3 18.0 %collective-permute-start.14 = (bf16[1024,128]{1,0:T(8,128)(2,1)S(1)}, bf16[1024,128]{1,0:T(8,128)(2,1)S(1)}, u32[]{:S(2)}, u32[]{:S(2)}) collective-permute-start(bf16[1024,128]{1,0:T(8,128)(2,1)S(1)} %get-tuple-element.78), channel_id=1, source_target_pairs={{0,4},{1,5},{2,6},{3,7},{4,0},{5,1},{6,2},{7,3},{8,12},{9,13},{10,... | collective-permute-start | bytes 786440 | tf_op jit(solution)/shard_map/ppermute | solution.py:31
  56.2 22.2 %collective-permute-start.15 = (bf16[1024,128]{1,0:T(8,128)(2,1)S(1)}, bf16[1024,128]{1,0:T(8,128)(2,1)S(1)}, u32[]{:S(2)}, u32[]{:S(2)}) collective-permute-start(bf16[1024,128]{1,0:T(8,128)(2,1)S(1)} %get-tuple-element.79), channel_id=1, source_target_pairs={{0,6},{1,7},{2,4},{3,5},{4,2},{5,3},{6,0},{7,1},{8,14},{9,15},{10,... | collective-permute-start | bytes 786440 | tf_op jit(solution)/shard_map/ppermute | solution.py:31
  78.4 13.1 %copy-start.4 = (s32[2048,128]{1,0:T(8,128)S(1)}, s32[2048,128]{1,0:T(8,128)}, u32[]{:S(2)}) copy-start(s32[2048,128]{1,0:T(8,128)} %param.10) | copy-start | bytes 3145732
  78.4 12.8 %collective-permute-start.16 = (bf16[1024,128]{1,0:T(8,128)(2,1)S(1)}, bf16[1024,128]{1,0:T(8,128)(2,1)S(1)}, u32[]{:S(2)}, u32[]{:S(2)}) collective-permute-start(bf16[1024,128]{1,0:T(8,128)(2,1)S(1)} %add_convert_fusion), channel_id=1, source_target_pairs={{0,4},{1,5},{2,6},{3,7},{4,0},{5,1},{6,2},{7,3},{8,12},{9,13},{10,... | collective-permute-start | bytes 786440 | tf_op jit(solution)/shard_map/ppermute | solution.py:31
  80.2 11.1 %collective-permute-start.17 = (bf16[1024,128]{1,0:T(8,128)(2,1)S(1)}, bf16[1024,128]{1,0:T(8,128)(2,1)S(1)}, u32[]{:S(2)}, u32[]{:S(2)}) collective-permute-start(bf16[1024,128]{1,0:T(8,128)(2,1)S(1)} %get-tuple-element.85), channel_id=1, source_target_pairs={{0,2},{1,3},{2,0},{3,1},{4,6},{5,7},{6,4},{7,5},{8,10},{9,11},{10,... | collective-permute-start | bytes 786440 | tf_op jit(solution)/shard_map/ppermute | solution.py:31

commit v11 on v10

--- a/solution.py
+++ b/solution.py
@@ -10,7 +10,7 @@
 
 F32 = jnp.float32
 BF16 = jnp.bfloat16
-VMEM_LIMIT = 40 * 2**20
+VMEM_LIMIT = 30 * 2**20
 IN_ORDER = pltpu.CompilerParams(
     vmem_limit_bytes=VMEM_LIMIT, dimension_semantics=("arbitrary",)
 )
@@ -194,39 +194,11 @@
     )(*sources)
 
 
-def send_rows(inputs, wide):
+def exchange_rows(inputs, wide):
     rows = inputs.shape[0]
     groups = lax.axis_size("dp")
-    if groups != 4:
-        parts = spread(inputs, wide, [(s, 0, s, 0, rows) for s in range(groups)])
-        return [part if s == 0 else swap(part, "dp", s) for s, part in enumerate(parts)]
-    half = rows // 2
-    own, left, right = spread(
-        inputs,
-        wide,
-        [(0, 0, 0, 0, rows), (1, 0, 1, 0, rows), (1, rows, 3, 0, half), (2, 0, 2, 0, rows),
-         (2, rows, 3, half, rows)],
-    )
-    return [own, swap(left, "dp", 1), swap(right, "dp", 2)]
-
-
-def pass_rows(parts, wide):
-    rows = parts[0].shape[0]
-    groups = lax.axis_size("dp")
-    if groups != 4:
-        return parts, [[(s, slice(0, rows))] for s in range(groups)]
-    own, left, right = parts
-    half = rows // 2
-    tail = slice(rows, rows + half)
-    every = slice(None)
-    upper, lower = lay(
-        [left, right],
-        [((half, wide), [(0, tail, every, 0)]), ((half, wide), [(1, tail, every, 0)])],
-    )
-    upper, lower = swap(upper, "dp", 2), swap(lower, "dp", 1)
-    whole, part = slice(0, rows), slice(0, half)
-    places = [[(0, whole)], [(1, whole)], [(2, whole)], [(3, part), (4, part)]]
-    return [own, left, right, upper, lower], places
+    parts = spread(inputs, wide, [(s, 0, s, 0, rows) for s in range(groups)])
+    return [part if s in (0, groups - 1) else swap(part, "dp", s) for s, part in enumerate(parts)]
 
 
 def product_kernel(jobs, depth, own_ref, other_ref, own_grads_ref, other_grads_ref, *out_refs):
@@ -282,7 +254,7 @@
     block = weight_mask.shape[0]
 
     other = swap(keys_values, "tensor", 1)
-    parts = send_rows(inputs, block)
+    parts = exchange_rows(inputs, block)
 
     query_grad, mine, theirs = attention(keys_values, other, queries, out_grad)
     mine, parts = lax.optimization_barrier((mine, parts))
@@ -290,7 +262,7 @@
     blocks = kv_blocks(mine, arrived, clip_mask, rows)
 
     blocks = [b if s == 0 else swap(b, "tensor", 2 * s) for s, b in enumerate(blocks)]
-    parts, places = pass_rows(parts, block)
+    parts[-1] = swap(parts[-1], "dp", groups - 1)
     blocks, parts = lax.optimization_barrier((blocks, parts))
     order = sorted(range(chips), key=lambda s: [(s >> b) & 1 for b in range(8)])
     evens, odds = order[: chips // 2], order[chips // 2 :]
@@ -303,12 +275,8 @@
     ]
     grads = lay(found, halves, LONG)
 
-    entries, first = [], 0
-    for source in places:
-        for array, span in source:
-            entries.append((array, span, slice(None), first))
-            first += span.stop - span.start
-    (packed,) = lay(parts, [((first, block), entries)])
+    entries = [(p, slice(0, rows), slice(None), p * rows) for p in range(groups)]
+    (packed,) = lay(parts, [((groups * rows, block), entries)])
     pair = (packed, swap(packed, "tensor", 1))
 
     def send(value, step):

time: 92.8 us -> 96.8 us (1.043)
  waiting for transfers between devices: 42 us -> 49.3 us
  starting transfers between devices: 22 us -> 19.7 us
  Pallas kernels: 23.1 us -> 22.1 us
    ppermute x18 -> x17, waiting for transfers between devices: 42 us -> 49.3 us  [swap(): return lax.ppermute(value, axis, pairs)]
    ppermute x18 -> x17, starting transfers between devices: 22 us -> 19.7 us  [swap(): return lax.ppermute(value, axis, pairs)]
    pallas_call x1, Pallas kernels: 1.24 us -> 0.2 us  [kv_blocks(): pl.pallas_call(functools.partial(kv_kernel, rows), out_shape=[jax.ShapeDt...]
    pallas_call x3 -> x2, Pallas kernels: 1.99 us -> 1.24 us  [lay(): pl.pallas_call(kernel, out_shape=[jax.ShapeDtypeStruct(shape, sources[0]....]
  transfers between devices with their start and end apart: 18 -> 17, of which waited for: 9 -> 10; matrix products, arithmetic and copies ran while one was open for 0% -> 0% of each run, Pallas kernels for 23% -> 21%
where the time goes in v11:
time: 96.8 us; the launch traced here: 96.5 us
  waiting for transfers between devices  49.3 us (51%)
  Pallas kernels  22.1 us (23%)
  starting transfers between devices  19.7 us (20%)
  local copies, waits for them, and re-layouts  3.3 us (3%)
  other arithmetic  1.33 us (1%)
    ppermute x17, waiting for transfers between devices, swap(): return lax.ppermute(value, axis, pairs)  49.3 us
    ppermute x17, starting transfers between devices, swap(): return lax.ppermute(value, axis, pairs)  19.7 us
    pallas_call x1, Pallas kernels, attention(): pl.pallas_call(functools.partial(attention_kernel, height, heads), grid=(...  15.8 us
    pallas_call x3, Pallas kernels, products(): pl.pallas_call(functools.partial(product_kernel, jobs, depth), out_shape=...  3.93 us
    unnamed x16, local copies, waits for them, and re-layouts  3.28 us
  transfers between devices with their start and end apart: 17, of which 10 were waited for; matrix products, arithmetic and copies ran while one was open for 0% of the time, Pallas kernels for 21%

profile of v11, /device:TPU:0, one launch (start us, length us, event | category | flops | bytes accessed | tf_op | source)
XLA Modules:
  0.0 96.5 jit_solution(9733613061686098366)
XLA Ops:
  0.6 0.5 collective-permute-start
  1.1 1.6 %copy-done = bf16[128,8192]{1,0:T(8,128)(2,1)S(1)} copy-done((bf16[128,8192]{1,0:T(8,128)(2,1)S(1)}, bf16[128,8192]{1,0:T(8,128)(2,1)}, u32[]{:S(2)}) %copy-start) | copy-done | bytes 2097176
  2.7 0.9 spread.1
  3.7 2.5 %collective-permute-start.1 = (bf16[128,2048]{1,0:T(8,128)(2,1)S(1)}, bf16[128,2048]{1,0:T(8,128)(2,1)S(1)}, u32[]{:S(2)}, u32[]{:S(2)}) collective-permute-start(bf16[128,2048]{1,0:T(8,128)(2,1)S(1)} %get-tuple-element.46), channel_id=1, source_target_pairs={{0,8},{8,0},{16,24},{24,16},{1,9},{9,1},{17,25},{25,17},{2,10},{10... | collective-permute-start | bytes 1572872 | tf_op jit(solution)/shard_map/ppermute | solution.py:31
  6.2 1.5 %collective-permute-start.2 = (bf16[128,2048]{1,0:T(8,128)(2,1)S(1)}, bf16[128,2048]{1,0:T(8,128)(2,1)S(1)}, u32[]{:S(2)}, u32[]{:S(2)}) collective-permute-start(bf16[128,2048]{1,0:T(8,128)(2,1)S(1)} %get-tuple-element.47), channel_id=1, source_target_pairs={{0,16},{8,24},{16,0},{24,8},{1,17},{9,25},{17,1},{25,9},{2,18},{10... | collective-permute-start | bytes 1572872 | tf_op jit(solution)/shard_map/ppermute | solution.py:31
  7.7 0.0 collective-permute-done.other_ref
  7.7 0.0 copy-start.2
  7.7 1.4 %copy-done.2 = bf16[1024,768]{1,0:T(8,128)(2,1)S(1)} copy-done((bf16[1024,768]{1,0:T(8,128)(2,1)S(1)}, bf16[1024,768]{1,0:T(8,128)(2,1)}, u32[]{:S(2)}) %copy-start.2) | copy-done | bytes 1572888
  9.1 15.8 %attention.1 = (bf16[1024,768]{1,0:T(8,128)(2,1)}, f32[1024,128]{1,0:T(8,128)S(1)}, f32[1024,128]{1,0:T(8,128)}) custom-call(bf16[1024,128]{1,0:T(8,128)(2,1)S(1)} %copy-done.3, bf16[1024,128]{1,0:T(8,128)(2,1)S(1)} %collective-permute-done.other_ref, bf16[1024,768]{1,0:T(8,128)(2,1)S(1)} %copy-done.1, bf16[1024,768]{1,0:T(8,128)(2,1)S(1)} %copy-done.2), custom_call_target="tpu_custom_call" | custom-call | flops 16106127360 | bytes 9437184 | tf_op jit(solution)/shard_map/attention/pallas_call | solution.py:136
  25.0 0.0 collective-permute-start.3
  25.0 0.0 collective-permute-done.2.refs_2_
  25.0 0.6 collective-permute-start.7
  25.5 0.2 copy.8.mask_ref
  25.8 1.3 %collective-permute-done.3.arrived_ref = f32[1024,128]{1,0:T(8,128)S(1)} collective-permute-done((f32[1024,128]{1,0:T(8,128)}, f32[1024,128]{1,0:T(8,128)S(1)}, u32[]{:S(2)}, u32[]{:S(2)}) %collective-permute-start.3) | collective-permute-done | bytes 524320 | tf_op jit(solution)/shard_map/ppermute | solution.py:31
  27.1 0.2 kv_blocks.1
  27.3 1.6 %collective-permute-start.4 = (bf16[256,128]{1,0:T(8,128)(2,1)S(1)}, bf16[256,128]{1,0:T(8,128)(2,1)S(1)}, u32[]{:S(2)}, u32[]{:S(2)}) collective-permute-start(bf16[256,128]{1,0:T(8,128)(2,1)S(1)} %get-tuple-element.52), channel_id=1, source_target_pairs={{0,2},{1,3},{2,0},{3,1},{4,6},{5,7},{6,4},{7,5},{8,10},{9,11},{10,... | collective-permute-start | bytes 196616 | tf_op jit(solution)/shard_map/ppermute | solution.py:31
  28.9 2.6 %collective-permute-start.5 = (bf16[256,128]{1,0:T(8,128)(2,1)S(1)}, bf16[256,128]{1,0:T(8,128)(2,1)S(1)}, u32[]{:S(2)}, u32[]{:S(2)}) collective-permute-start(bf16[256,128]{1,0:T(8,128)(2,1)S(1)} %get-tuple-element.53), channel_id=1, source_target_pairs={{0,4},{1,5},{2,6},{3,7},{4,0},{5,1},{6,2},{7,3},{8,12},{9,13},{10,... | collective-permute-start | bytes 196616 | tf_op jit(solution)/shard_map/ppermute | solution.py:31
  31.5 0.2 collective-permute-start.6
  31.7 4.7 %collective-permute-done.5 = bf16[256,128]{1,0:T(8,128)(2,1)S(1)} collective-permute-done((bf16[256,128]{1,0:T(8,128)(2,1)S(1)}, bf16[256,128]{1,0:T(8,128)(2,1)S(1)}, u32[]{:S(2)}, u32[]{:S(2)}) %collective-permute-start.5) | collective-permute-done | bytes 65568 | tf_op jit(solution)/shard_map/ppermute | solution.py:31
  36.5 1.2 %collective-permute-done.6 = bf16[256,128]{1,0:T(8,128)(2,1)S(1)} collective-permute-done((bf16[256,128]{1,0:T(8,128)(2,1)S(1)}, bf16[256,128]{1,0:T(8,128)(2,1)S(1)}, u32[]{:S(2)}, u32[]{:S(2)}) %collective-permute-start.6) | collective-permute-done | bytes 65568 | tf_op jit(solution)/shard_map/ppermute | solution.py:31
  37.7 2.9 %collective-permute-done.7.refs_3_ = bf16[128,2048]{1,0:T(8,128)(2,1)} collective-permute-done((bf16[128,2048]{1,0:T(8,128)(2,1)}, bf16[128,2048]{1,0:T(8,128)(2,1)}, u32[]{:S(2)}, u32[]{:S(2)}) %collective-permute-start.7) | collective-permute-done | bytes 524320 | tf_op jit(solution)/shard_map/ppermute | solution.py:31
  40.6 0.3 collective-permute-start.11
  41.0 1.7 %collective-permute-start.10 = (bf16[256,512]{1,0:T(8,128)(2,1)S(1)}, bf16[256,512]{1,0:T(8,128)(2,1)S(1)}, u32[]{:S(2)}, u32[]{:S(2)}) collective-permute-start(bf16[256,512]{1,0:T(8,128)(2,1)S(1)} %constant_dynamic-update-slice_fusion.refs_0_), channel_id=1, source_target_pairs={{0,16},{8,24},{16,0},{24,8},{1,17},{9,25},{17,1},{25,9},{2,18},{10... | collective-permute-start | bytes 786440 | tf_op jit(solution)/shard_map/ppermute | solution.py:31
  42.7 1.5 %collective-permute-start.9 = (bf16[256,512]{1,0:T(8,128)(2,1)S(1)}, bf16[256,512]{1,0:T(8,128)(2,1)S(1)}, u32[]{:S(2)}, u32[]{:S(2)}) collective-permute-start(bf16[256,512]{1,0:T(8,128)(2,1)S(1)} %constant_dynamic-update-slice_fusion.refs_0_), channel_id=1, source_target_pairs={{0,8},{8,0},{16,24},{24,16},{1,9},{9,1},{17,25},{25,17},{2,10},{10... | collective-permute-start | bytes 786440 | tf_op jit(solution)/shard_map/ppermute | solution.py:31
  44.2 1.2 %lay.2.own_ref = bf16[512,2048]{1,0:T(8,128)(2,1)S(1)} custom-call(bf16[128,2048]{1,0:T(8,128)(2,1)S(1)} %get-tuple-element.59.refs_0_, bf16[128,2048]{1,0:T(8,128)(2,1)S(1)} %collective-permute-done.1.refs_1_, bf16[128,2048]{1,0:T(8,128)(2,1)S(1)} %collective-permute-done.2.refs_2_, bf16[128,2048]{1,0:T(8,128)(2,1)} %collective-permute-done.7.refs_3_), custom_call_target="tpu_custom_call" | custom-call | bytes 1024 | tf_op jit(solution)/shard_map/lay/pallas_call | solution.py:188
  45.4 0.1 collective-permute-start.8
  45.4 5.4 %collective-permute-done.11.refs_3_ = bf16[256,512]{1,0:T(8,128)(2,1)S(1)} collective-permute-done((bf16[256,512]{1,0:T(8,128)(2,1)S(1)}, bf16[256,512]{1,0:T(8,128)(2,1)S(1)}, u32[]{:S(2)}, u32[]{:S(2)}) %collective-permute-start.11) | collective-permute-done | bytes 262176 | tf_op jit(solution)/shard_map/ppermute | solution.py:31
  50.8 3.5 %collective-permute-done.10.refs_2_ = bf16[256,512]{1,0:T(8,128)(2,1)S(1)} collective-permute-done((bf16[256,512]{1,0:T(8,128)(2,1)S(1)}, bf16[256,512]{1,0:T(8,128)(2,1)S(1)}, u32[]{:S(2)}, u32[]{:S(2)}) %collective-permute-start.10) | collective-permute-done | bytes 262176 | tf_op jit(solution)/shard_map/ppermute | solution.py:31
  54.3 0.0 collective-permute-done.9.refs_1_
  54.3 0.1 lay.3
  54.3 0.0 collective-permute-done.8.other_ref
  54.4 1.3 %products.3 = (bf16[1024,128]{1,0:T(8,128)(2,1)S(1)}, bf16[1024,128]{1,0:T(8,128)(2,1)S(1)}) custom-call(bf16[512,2048]{1,0:T(8,128)(2,1)S(1)} %lay.2.own_ref, bf16[512,2048]{1,0:T(8,128)(2,1)S(1)} %collective-permute-done.8.other_ref, bf16[512,512]{1,0:T(8,128)(2,1)S(1)} %get-tuple-element.73.own_grads_ref, ...), custom_call_target="tpu_custom_call" | custom-call | bytes 1024 | tf_op jit(solution)/shard_map/products/pallas_call | solution.py:213
  55.7 0.8 products.4
  56.4 1.7 %collective-permute-start.12 = (bf16[1024,256]{1,0:T(8,128)(2,1)S(1)}, bf16[1024,256]{1,0:T(8,128)(2,1)S(1)}, u32[]{:S(2)}, u32[]{:S(2)}) collective-permute-start(bf16[1024,256]{1,0:T(8,128)(2,1)S(1)} %products.4), channel_id=1, source_target_pairs={{0,2},{1,3},{2,0},{3,1},{4,6},{5,7},{6,4},{7,5},{8,10},{9,11},{10,... | collective-permute-start | bytes 1572872 | tf_op jit(solution)/shard_map/ppermute | solution.py:31
  58.2 2.6 %collective-permute-start.13 = (bf16[1024,128]{1,0:T(8,128)(2,1)S(1)}, bf16[1024,128]{1,0:T(8,128)(2,1)S(1)}, u32[]{:S(2)}, u32[]{:S(2)}) collective-permute-start(bf16[1024,128]{1,0:T(8,128)(2,1)S(1)} %get-tuple-element.76), channel_id=1, source_target_pairs={{0,4},{1,5},{2,6},{3,7},{4,0},{5,1},{6,2},{7,3},{8,12},{9,13},{10,... | collective-permute-start | bytes 786440 | tf_op jit(solution)/shard_map/ppermute | solution.py:31
  60.8 0.1 collective-permute-start.14
  60.9 1.8 %products.5 = (f32[1024,256]{1,0:T(8,128)S(1)}, f32[1024,128]{1,0:T(8,128)S(1)}, bf16[1024,128]{1,0:T(8,128)(2,1)S(1)}) custom-call(bf16[512,2048]{1,0:T(8,128)(2,1)S(1)} %lay.2.own_ref, bf16[512,2048]{1,0:T(8,128)(2,1)S(1)} %collective-permute-done.8.other_ref, bf16[512,512]{1,0:T(8,128)(2,1)S(1)} %get-tuple-element.73.own_grads_ref, ...), custom_call_target="tpu_custom_call" | custom-call | bytes 1024 | tf_op jit(solution)/shard_map/products/pallas_call | solution.py:213
  62.7 13.5 %collective-permute-done.13 = bf16[1024,128]{1,0:T(8,128)(2,1)S(1)} collective-permute-done((bf16[1024,128]{1,0:T(8,128)(2,1)S(1)}, bf16[1024,128]{1,0:T(8,128)(2,1)S(1)}, u32[]{:S(2)}, u32[]{:S(2)}) %collective-permute-start.13) | collective-permute-done | bytes 262176 | tf_op jit(solution)/shard_map/ppermute | solution.py:31
  76.2 6.8 %collective-permute-done.14 = bf16[1024,128]{1,0:T(8,128)(2,1)S(1)} collective-permute-done((bf16[1024,128]{1,0:T(8,128)(2,1)S(1)}, bf16[1024,128]{1,0:T(8,128)(2,1)S(1)}, u32[]{:S(2)}, u32[]{:S(2)}) %collective-permute-start.14) | collective-permute-done | bytes 262176 | tf_op jit(solution)/shard_map/ppermute | solution.py:31
  83.0 0.0 collective-permute-done.12
  83.0 0.1 add_convert_fusion
  83.1 1.7 %collective-permute-start.15 = (bf16[1024,128]{1,0:T(8,128)(2,1)S(1)}, bf16[1024,128]{1,0:T(8,128)(2,1)S(1)}, u32[]{:S(2)}, u32[]{:S(2)}) collective-permute-start(bf16[1024,128]{1,0:T(8,128)(2,1)S(1)} %add_convert_fusion), channel_id=1, source_target_pairs={{0,4},{1,5},{2,6},{3,7},{4,0},{5,1},{6,2},{7,3},{8,12},{9,13},{10,... | collective-permute-start | bytes 786440 | tf_op jit(solution)/shard_map/ppermute | solution.py:31
  84.8 0.3 collective-permute-start.16
  85.2 9.8 %collective-permute-done.15 = bf16[1024,128]{1,0:T(8,128)(2,1)S(1)} collective-permute-done((bf16[1024,128]{1,0:T(8,128)(2,1)S(1)}, bf16[1024,128]{1,0:T(8,128)(2,1)S(1)}, u32[]{:S(2)}, u32[]{:S(2)}) %collective-permute-start.15) | collective-permute-done | bytes 262176 | tf_op jit(solution)/shard_map/ppermute | solution.py:31
  95.0 0.1 convert_add_fusion
  95.1 0.2 collective-permute-done.16
  95.3 0.1 add_add_fusion
  95.4 1.1 %maximum_select_fusion = f32[2048,128]{1,0:T(8,128)} fusion(f32[1024,128]{1,0:T(8,128)S(1)} %add_add_fusion, f32[1024,128]{1,0:T(8,128)S(1)} %convert_add_fusion, s32[2048,128]{1,0:T(8,128)S(1)} %copy-done.4), kind=kLoop, calls=%fused_computation | loop fusion | flops 786432 | bytes 3145728 | tf_op jit(solution)/shard_map/jit(_where)/select_n | solution.py:308
  (15 shorter events, 0.1 us)
Async XLA Ops:
  0.6 7.1 %collective-permute-start = (bf16[1024,128]{1,0:T(8,128)(2,1)}, bf16[1024,128]{1,0:T(8,128)(2,1)S(1)}, u32[]{:S(2)}, u32[]{:S(2)}) collective-permute-start(bf16[1024,128]{1,0:T(8,128)(2,1)} %own_ref.1), channel_id=1, source_target_pairs={{0,1},{1,0},{2,3},{3,2},{4,5},{5,4},{6,7},{7,6},{8,9},{9,8},{10,11... | collective-permute-start | bytes 786440 | tf_op jit(solution)/shard_map/ppermute | solution.py:31
  1.1 1.6 %copy-start = (bf16[128,8192]{1,0:T(8,128)(2,1)S(1)}, bf16[128,8192]{1,0:T(8,128)(2,1)}, u32[]{:S(2)}) copy-start(bf16[128,8192]{1,0:T(8,128)(2,1)} %source_ref.1) | copy-start | bytes 6291460
  2.7 5.0 %copy-start.1 = (bf16[1024,768]{1,0:T(8,128)(2,1)S(1)}, bf16[1024,768]{1,0:T(8,128)(2,1)}, u32[]{:S(2)}) copy-start(bf16[1024,768]{1,0:T(8,128)(2,1)} %q_ref.1) | copy-start | bytes 4718596
  2.7 5.0 %copy-start.3 = (bf16[1024,128]{1,0:T(8,128)(2,1)S(1)}, bf16[1024,128]{1,0:T(8,128)(2,1)}, u32[]{:S(2)}) copy-start(bf16[1024,128]{1,0:T(8,128)(2,1)} %own_ref.1) | copy-start | bytes 786436
  3.7 21.3 %collective-permute-start.1 = (bf16[128,2048]{1,0:T(8,128)(2,1)S(1)}, bf16[128,2048]{1,0:T(8,128)(2,1)S(1)}, u32[]{:S(2)}, u32[]{:S(2)}) collective-permute-start(bf16[128,2048]{1,0:T(8,128)(2,1)S(1)} %get-tuple-element.46), channel_id=1, source_target_pairs={{0,8},{8,0},{16,24},{24,16},{1,9},{9,1},{17,25},{25,17},{2,10},{10... | collective-permute-start | bytes 1572872 | tf_op jit(solution)/shard_map/ppermute | solution.py:31
  6.2 18.8 %collective-permute-start.2 = (bf16[128,2048]{1,0:T(8,128)(2,1)S(1)}, bf16[128,2048]{1,0:T(8,128)(2,1)S(1)}, u32[]{:S(2)}, u32[]{:S(2)}) collective-permute-start(bf16[128,2048]{1,0:T(8,128)(2,1)S(1)} %get-tuple-element.47), channel_id=1, source_target_pairs={{0,16},{8,24},{16,0},{24,8},{1,17},{9,25},{17,1},{25,9},{2,18},{10... | collective-permute-start | bytes 1572872 | tf_op jit(solution)/shard_map/ppermute | solution.py:31
  7.7 1.4 %copy-start.2 = (bf16[1024,768]{1,0:T(8,128)(2,1)S(1)}, bf16[1024,768]{1,0:T(8,128)(2,1)}, u32[]{:S(2)}) copy-start(bf16[1024,768]{1,0:T(8,128)(2,1)} %up_ref.1) | copy-start | bytes 4718596
  9.1 16.4 %copy-start.5 = (s32[1024,1]{0,1:T(1,128)S(1)}, s32[1024,1]{0,1:T(1,128)}, u32[]{:S(2)}) copy-start(s32[1024,1]{0,1:T(1,128)} %param.11) | copy-start | bytes 12292
  25.0 2.1 %collective-permute-start.3 = (f32[1024,128]{1,0:T(8,128)}, f32[1024,128]{1,0:T(8,128)S(1)}, u32[]{:S(2)}, u32[]{:S(2)}) collective-permute-start(f32[1024,128]{1,0:T(8,128)} %get-tuple-element.50), channel_id=1, source_target_pairs={{0,1},{1,0},{2,3},{3,2},{4,5},{5,4},{6,7},{7,6},{8,9},{9,8},{10,11... | collective-permute-start | bytes 1572872 | tf_op jit(solution)/shard_map/ppermute | solution.py:31
  25.0 15.6 %collective-permute-start.7 = (bf16[128,2048]{1,0:T(8,128)(2,1)}, bf16[128,2048]{1,0:T(8,128)(2,1)}, u32[]{:S(2)}, u32[]{:S(2)}) collective-permute-start(bf16[128,2048]{1,0:T(8,128)(2,1)} %get-tuple-element.58), channel_id=1, source_target_pairs={{0,24},{8,16},{16,8},{24,0},{1,25},{9,17},{17,9},{25,1},{2,26},{10... | collective-permute-start | bytes 1572872 | tf_op jit(solution)/shard_map/ppermute | solution.py:31
  27.3 4.5 %collective-permute-start.4 = (bf16[256,128]{1,0:T(8,128)(2,1)S(1)}, bf16[256,128]{1,0:T(8,128)(2,1)S(1)}, u32[]{:S(2)}, u32[]{:S(2)}) collective-permute-start(bf16[256,128]{1,0:T(8,128)(2,1)S(1)} %get-tuple-element.52), channel_id=1, source_target_pairs={{0,2},{1,3},{2,0},{3,1},{4,6},{5,7},{6,4},{7,5},{8,10},{9,11},{10,... | collective-permute-start | bytes 196616 | tf_op jit(solution)/shard_map/ppermute | solution.py:31
  28.9 7.5 %collective-permute-start.5 = (bf16[256,128]{1,0:T(8,128)(2,1)S(1)}, bf16[256,128]{1,0:T(8,128)(2,1)S(1)}, u32[]{:S(2)}, u32[]{:S(2)}) collective-permute-start(bf16[256,128]{1,0:T(8,128)(2,1)S(1)} %get-tuple-element.53), channel_id=1, source_target_pairs={{0,4},{1,5},{2,6},{3,7},{4,0},{5,1},{6,2},{7,3},{8,12},{9,13},{10,... | collective-permute-start | bytes 196616 | tf_op jit(solution)/shard_map/ppermute | solution.py:31
  31.5 6.2 %collective-permute-start.6 = (bf16[256,128]{1,0:T(8,128)(2,1)S(1)}, bf16[256,128]{1,0:T(8,128)(2,1)S(1)}, u32[]{:S(2)}, u32[]{:S(2)}) collective-permute-start(bf16[256,128]{1,0:T(8,128)(2,1)S(1)} %get-tuple-element.54), channel_id=1, source_target_pairs={{0,6},{1,7},{2,4},{3,5},{4,2},{5,3},{6,0},{7,1},{8,14},{9,15},{10,... | collective-permute-start | bytes 196616 | tf_op jit(solution)/shard_map/ppermute | solution.py:31
  40.6 10.2 %collective-permute-start.11 = (bf16[256,512]{1,0:T(8,128)(2,1)S(1)}, bf16[256,512]{1,0:T(8,128)(2,1)S(1)}, u32[]{:S(2)}, u32[]{:S(2)}) collective-permute-start(bf16[256,512]{1,0:T(8,128)(2,1)S(1)} %constant_dynamic-update-slice_fusion.refs_0_), channel_id=1, source_target_pairs={{0,24},{8,16},{16,8},{24,0},{1,25},{9,17},{17,9},{25,1},{2,26},{10... | collective-permute-start | bytes 786440 | tf_op jit(solution)/shard_map/ppermute | solution.py:31
  41.0 13.3 %collective-permute-start.10 = (bf16[256,512]{1,0:T(8,128)(2,1)S(1)}, bf16[256,512]{1,0:T(8,128)(2,1)S(1)}, u32[]{:S(2)}, u32[]{:S(2)}) collective-permute-start(bf16[256,512]{1,0:T(8,128)(2,1)S(1)} %constant_dynamic-update-slice_fusion.refs_0_), channel_id=1, source_target_pairs={{0,16},{8,24},{16,0},{24,8},{1,17},{9,25},{17,1},{25,9},{2,18},{10... | collective-permute-start | bytes 786440 | tf_op jit(solution)/shard_map/ppermute | solution.py:31
  42.7 11.6 %collective-permute-start.9 = (bf16[256,512]{1,0:T(8,128)(2,1)S(1)}, bf16[256,512]{1,0:T(8,128)(2,1)S(1)}, u32[]{:S(2)}, u32[]{:S(2)}) collective-permute-start(bf16[256,512]{1,0:T(8,128)(2,1)S(1)} %constant_dynamic-update-slice_fusion.refs_0_), channel_id=1, source_target_pairs={{0,8},{8,0},{16,24},{24,16},{1,9},{9,1},{17,25},{25,17},{2,10},{10... | collective-permute-start | bytes 786440 | tf_op jit(solution)/shard_map/ppermute | solution.py:31
  45.4 9.0 %collective-permute-start.8 = (bf16[512,2048]{1,0:T(8,128)(2,1)S(1)}, bf16[512,2048]{1,0:T(8,128)(2,1)S(1)}, u32[]{:S(2)}, u32[]{:S(2)}) collective-permute-start(bf16[512,2048]{1,0:T(8,128)(2,1)S(1)} %lay.2.own_ref), channel_id=1, source_target_pairs={{0,1},{1,0},{2,3},{3,2},{4,5},{5,4},{6,7},{7,6},{8,9},{9,8},{10,11... | collective-permute-start | bytes 6291464 | tf_op jit(solution)/shard_map/ppermute | solution.py:31
  56.4 26.6 %collective-permute-start.12 = (bf16[1024,256]{1,0:T(8,128)(2,1)S(1)}, bf16[1024,256]{1,0:T(8,128)(2,1)S(1)}, u32[]{:S(2)}, u32[]{:S(2)}) collective-permute-start(bf16[1024,256]{1,0:T(8,128)(2,1)S(1)} %products.4), channel_id=1, source_target_pairs={{0,2},{1,3},{2,0},{3,1},{4,6},{5,7},{6,4},{7,5},{8,10},{9,11},{10,... | collective-permute-start | bytes 1572872 | tf_op jit(solution)/shard_map/ppermute | solution.py:31
  58.2 18.0 %collective-permute-start.13 = (bf16[1024,128]{1,0:T(8,128)(2,1)S(1)}, bf16[1024,128]{1,0:T(8,128)(2,1)S(1)}, u32[]{:S(2)}, u32[]{:S(2)}) collective-permute-start(bf16[1024,128]{1,0:T(8,128)(2,1)S(1)} %get-tuple-element.76), channel_id=1, source_target_pairs={{0,4},{1,5},{2,6},{3,7},{4,0},{5,1},{6,2},{7,3},{8,12},{9,13},{10,... | collective-permute-start | bytes 786440 | tf_op jit(solution)/shard_map/ppermute | solution.py:31
  60.8 22.3 %collective-permute-start.14 = (bf16[1024,128]{1,0:T(8,128)(2,1)S(1)}, bf16[1024,128]{1,0:T(8,128)(2,1)S(1)}, u32[]{:S(2)}, u32[]{:S(2)}) collective-permute-start(bf16[1024,128]{1,0:T(8,128)(2,1)S(1)} %get-tuple-element.77), channel_id=1, source_target_pairs={{0,6},{1,7},{2,4},{3,5},{4,2},{5,3},{6,0},{7,1},{8,14},{9,15},{10,... | collective-permute-start | bytes 786440 | tf_op jit(solution)/shard_map/ppermute | solution.py:31
  83.0 12.4 %copy-start.4 = (s32[2048,128]{1,0:T(8,128)S(1)}, s32[2048,128]{1,0:T(8,128)}, u32[]{:S(2)}) copy-start(s32[2048,128]{1,0:T(8,128)} %param.10) | copy-start | bytes 3145732
  83.1 11.9 %collective-permute-start.15 = (bf16[1024,128]{1,0:T(8,128)(2,1)S(1)}, bf16[1024,128]{1,0:T(8,128)(2,1)S(1)}, u32[]{:S(2)}, u32[]{:S(2)}) collective-permute-start(bf16[1024,128]{1,0:T(8,128)(2,1)S(1)} %add_convert_fusion), channel_id=1, source_target_pairs={{0,4},{1,5},{2,6},{3,7},{4,0},{5,1},{6,2},{7,3},{8,12},{9,13},{10,... | collective-permute-start | bytes 786440 | tf_op jit(solution)/shard_map/ppermute | solution.py:31
  84.8 10.5 %collective-permute-start.16 = (bf16[1024,128]{1,0:T(8,128)(2,1)S(1)}, bf16[1024,128]{1,0:T(8,128)(2,1)S(1)}, u32[]{:S(2)}, u32[]{:S(2)}) collective-permute-start(bf16[1024,128]{1,0:T(8,128)(2,1)S(1)} %get-tuple-element.83), channel_id=1, source_target_pairs={{0,2},{1,3},{2,0},{3,1},{4,6},{5,7},{6,4},{7,5},{8,10},{9,11},{10,... | collective-permute-start | bytes 786440 | tf_op jit(solution)/shard_map/ppermute | solution.py:31

commit v12 on v10

--- a/solution.py
+++ b/solution.py
@@ -229,25 +229,36 @@
     return [own, left, right, upper, lower], places
 
 
-def product_kernel(jobs, depth, own_ref, other_ref, own_grads_ref, other_grads_ref, *out_refs):
-    pairs = ((own_ref, own_grads_ref), (other_ref, other_grads_ref))
-    for (places, low, high, _), out_ref in zip(jobs, out_refs):
-        columns = slice(places[0] * depth, (places[-1] + 1) * depth)
-        total = sum(dot(ref[:, low:high], grads[:, columns], 0, 0) for ref, grads in pairs)
-        out_ref[...] = total.astype(out_ref.dtype)
-
-
-def products(pair, grads, depth, jobs, hint=TINY):
-    return pl.pallas_call(
-        functools.partial(product_kernel, jobs, depth),
+def product_kernel(jobs, depth, held, own_ref, other_ref, *refs):
+    grads, out_refs = refs[: 2 * len(held)], refs[2 * len(held) :]
+
+    def pick(steps, half):
+        parts = []
+        for step in steps:
+            group = [step in group for group in held].index(True)
+            place = held[group].index(step) * depth
+            parts.append(grads[2 * group + half][:, place : place + depth])
+        return jnp.concatenate(parts, 1)
+
+    for (steps, low, high, _), out_ref in zip(jobs, out_refs):
+        terms = [
+            dot(ref[:, low:high], pick(steps, half), 0, 0)
+            for half, ref in enumerate((own_ref, other_ref))
+        ]
+        out_ref[...] = (terms[0] + terms[1]).astype(out_ref.dtype)
+
+
+def products(pair, found, depth, jobs, hint=TINY):
+    return pl.pallas_call(
+        functools.partial(product_kernel, jobs, depth, [steps for steps, _ in found]),
         out_shape=[
-            jax.ShapeDtypeStruct((high - low, len(places) * depth), dtype)
-            for places, low, high, dtype in jobs
+            jax.ShapeDtypeStruct((high - low, len(steps) * depth), dtype)
+            for steps, low, high, dtype in jobs
         ],
         compiler_params=SMALL,
         cost_estimate=hint,
         name="products",
-    )(*pair, *grads)
+    )(*pair, *[array for _, arrays in found for array in arrays])
 
 
 def kv_kernel(rows, mine_ref, arrived_ref, mask_ref, *out_refs):
@@ -292,16 +303,18 @@
     blocks = [b if s == 0 else swap(b, "tensor", 2 * s) for s, b in enumerate(blocks)]
     parts, places = pass_rows(parts, block)
     blocks, parts = lax.optimization_barrier((blocks, parts))
-    order = sorted(range(chips), key=lambda s: [(s >> b) & 1 for b in range(8)])
-    evens, odds = order[: chips // 2], order[chips // 2 :]
-    stacked = jnp.concatenate([blocks[s] for s in order], 1)
-    found = [stacked if s == 0 else swap(stacked, "dp", s) for s in range(groups)]
-    whole = (groups * rows, chips * depth)
-    halves = [
-        (whole, [(s, slice(h * rows, (h + 1) * rows), slice(None), s * rows) for s in range(groups)])
-        for h in (0, 1)
-    ]
-    grads = lay(found, halves, LONG)
+
+    def gather(steps, hint):
+        value = jnp.concatenate([blocks[s] for s in steps], 1)
+        found = [value if s == 0 else swap(value, "dp", s) for s in range(groups)]
+        shape = (groups * rows, value.shape[1])
+        outputs = []
+        for half in range(2):
+            span = slice(half * rows, (half + 1) * rows)
+            outputs.append((shape, [(s, span, slice(None), s * rows) for s in range(groups)]))
+        return steps, lay(found, outputs, hint)
+
+    found = [gather(tuple(range(chips)), LONG)]
 
     entries, first = [], 0
     for source in places:
@@ -315,27 +328,29 @@
         return swap(value.astype(BF16), "tensor", 2 * step)
 
     wide, half = block // 2, chips // 2
-    far, near = (wide, block), (0, wide)
-    away = list(range(2, chips))
-    direct = products(pair, grads, depth, [((order.index(s),), *far, BF16) for s in away])
-    direct, grads = lax.optimization_barrier((direct, grads))
-    (first,) = products(pair, grads, depth, [(range(half, chips), *near, BF16)], LONG)
-    direct = [send(value, s) for value, s in zip(direct, away)]
-    sent = send(first, 1)
-    grads, _ = lax.optimization_barrier((grads, first))
-    jobs = [(range(half), *near, F32), ((0,), *far, F32), ((order.index(1),), *far, BF16)]
-    even, own, nearest = products(pair, grads, depth, jobs)
-    sent, direct = lax.optimization_barrier((sent, direct))
-    terms = [even, sent]
-    columns, bit = half * depth, 1
-    while columns > depth:
-        columns, bit = columns // 2, bit * 2
-        value = sum(t[:, columns : 2 * columns].astype(F32) for t in terms).astype(BF16)
-        terms.append(send(value, bit))
-    nearest, _ = lax.optimization_barrier((nearest, value))
-    direct.append(send(nearest, 1))
-    upper = sum(t[:, :depth].astype(F32) for t in terms)
-    lower = own + sum(t.astype(F32) for t in direct)
+    near, far = (0, wide), (wide, block)
+    order = sorted(range(chips), key=lambda s: [(s >> b) & 1 for b in range(8)])
+
+    def after(value):
+        arrays, _ = lax.optimization_barrier(([arrays for _, arrays in found], value))
+        return [(steps, array) for (steps, _), array in zip(found, arrays)]
+
+    (second,) = products(pair, found, depth, [(tuple(range(half, chips)), *far, BF16)])
+    (first,) = products(pair, after(second), depth, [(tuple(order[half:]), *near, BF16)], LONG)
+    jobs = [(tuple(order[:half]), *near, F32), (tuple(range(half)), *far, F32)]
+    even, low = products(pair, after(first), depth, jobs)
+
+    def reduce(kept, sent, bits):
+        terms, columns = [kept, send(sent, bits[0])], half * depth
+        for bit in bits[1:]:
+            columns //= 2
+            value = sum(t[:, columns : 2 * columns].astype(F32) for t in terms).astype(BF16)
+            terms.append(send(value, bit))
+        return sum(t[:, :depth].astype(F32) for t in terms)
+
+    bits = [2**b for b in range(chips.bit_length() - 1)]
+    lower = reduce(low, second, bits[::-1])
+    upper = reduce(even, first, bits)
     summed = jnp.concatenate([upper, lower], 0)
     weight_grad = jnp.where(weight_mask == 1, summed, 0.0)
     return (query_grad, weight_grad)

time: 92.8 us -> 92.3 us (level)
  waiting for transfers between devices: 42 us -> 46.6 us
  starting transfers between devices: 22 us -> 17.9 us
  Pallas kernels: 23.1 us -> 22.1 us
    ppermute x18 -> x17, waiting for transfers between devices: 42 us -> 46.6 us  [swap(): return lax.ppermute(value, axis, pairs)]
    ppermute x18 -> x17, starting transfers between devices: 22 us -> 17.9 us  [swap(): return lax.ppermute(value, axis, pairs)]
    pallas_call x3, Pallas kernels: 3.92 us -> 2.92 us  [products(): pl.pallas_call(functools.partial(product_kernel, jobs, depth, [steps for...]
  transfers between devices with their start and end apart: 18 -> 17, of which waited for: 9 -> 10; matrix products, arithmetic and copies ran while one was open for 0% -> 0% of each run, Pallas kernels for 23% -> 22%
where the time goes in v12:
time: 92.3 us; the launch traced here: 92.1 us
  waiting for transfers between devices  46.6 us (50%)
  Pallas kernels  22.1 us (24%)
  starting transfers between devices  17.9 us (19%)
  local copies, waits for them, and re-layouts  3.3 us (4%)
  other arithmetic  1.34 us (1%)
    ppermute x17, waiting for transfers between devices, swap(): return lax.ppermute(value, axis, pairs)  46.6 us
    ppermute x17, starting transfers between devices, swap(): return lax.ppermute(value, axis, pairs)  17.9 us
    pallas_call x1, Pallas kernels, attention(): pl.pallas_call(functools.partial(attention_kernel, height, heads), grid=(...  15.8 us
    unnamed x16, local copies, waits for them, and re-layouts  3.28 us
    pallas_call x3, Pallas kernels, products(): pl.pallas_call(functools.partial(product_kernel, jobs, depth, [steps for...  2.92 us
    pallas_call x3, Pallas kernels, lay(): pl.pallas_call(kernel, out_shape=[jax.ShapeDtypeStruct(shape, sources[0]....  2 us
  transfers between devices with their start and end apart: 17, of which 10 were waited for; matrix products, arithmetic and copies ran while one was open for 0% of the time, Pallas kernels for 22%

profile of v12, /device:TPU:0, one launch (start us, length us, event | category | flops | bytes accessed | tf_op | source)
XLA Modules:
  0.0 92.1 jit_solution(13398482929393178750)
XLA Ops:
  0.6 0.5 collective-permute-start
  1.1 1.6 %copy-done = bf16[128,8192]{1,0:T(8,128)(2,1)S(1)} copy-done((bf16[128,8192]{1,0:T(8,128)(2,1)S(1)}, bf16[128,8192]{1,0:T(8,128)(2,1)}, u32[]{:S(2)}) %copy-start) | copy-done | bytes 2097176
  2.7 0.1 spread.1
  2.9 2.6 %collective-permute-start.1 = (bf16[192,2048]{1,0:T(8,128)(2,1)S(1)}, bf16[192,2048]{1,0:T(8,128)(2,1)S(1)}, u32[]{:S(2)}, u32[]{:S(2)}) collective-permute-start(bf16[192,2048]{1,0:T(8,128)(2,1)S(1)} %get-tuple-element.38), channel_id=1, source_target_pairs={{0,8},{8,0},{16,24},{24,16},{1,9},{9,1},{17,25},{25,17},{2,10},{10... | collective-permute-start | bytes 2359304 | tf_op jit(solution)/shard_map/ppermute | solution.py:31
  5.4 1.5 %collective-permute-start.2 = (bf16[192,2048]{1,0:T(8,128)(2,1)S(1)}, bf16[192,2048]{1,0:T(8,128)(2,1)S(1)}, u32[]{:S(2)}, u32[]{:S(2)}) collective-permute-start(bf16[192,2048]{1,0:T(8,128)(2,1)S(1)} %get-tuple-element.39), channel_id=1, source_target_pairs={{0,16},{8,24},{16,0},{24,8},{1,17},{9,25},{17,1},{25,9},{2,18},{10... | collective-permute-start | bytes 2359304 | tf_op jit(solution)/shard_map/ppermute | solution.py:31
  7.0 0.0 collective-permute-done.other_ref
  7.0 0.0 copy-start.2
  7.0 1.4 %copy-done.2 = bf16[1024,768]{1,0:T(8,128)(2,1)S(1)} copy-done((bf16[1024,768]{1,0:T(8,128)(2,1)S(1)}, bf16[1024,768]{1,0:T(8,128)(2,1)}, u32[]{:S(2)}) %copy-start.2) | copy-done | bytes 1572888
  8.4 15.8 %attention.1 = (bf16[1024,768]{1,0:T(8,128)(2,1)}, f32[1024,128]{1,0:T(8,128)S(1)}, f32[1024,128]{1,0:T(8,128)}) custom-call(bf16[1024,128]{1,0:T(8,128)(2,1)S(1)} %copy-done.3, bf16[1024,128]{1,0:T(8,128)(2,1)S(1)} %collective-permute-done.other_ref, bf16[1024,768]{1,0:T(8,128)(2,1)S(1)} %copy-done.1, bf16[1024,768]{1,0:T(8,128)(2,1)S(1)} %copy-done.2), custom_call_target="tpu_custom_call" | custom-call | flops 16106127360 | bytes 9437184 | tf_op jit(solution)/shard_map/attention/pallas_call | solution.py:136
  24.2 0.9 collective-permute-done.2.refs_1_.refs_2_
  25.1 0.9 lay.3
  26.0 1.5 %collective-permute-start.7 = (bf16[64,2048]{1,0:T(8,128)(2,1)}, bf16[64,2048]{1,0:T(8,128)(2,1)S(1)}, u32[]{:S(2)}, u32[]{:S(2)}) collective-permute-start(bf16[64,2048]{1,0:T(8,128)(2,1)} %get-tuple-element.49), channel_id=1, source_target_pairs={{0,16},{8,24},{16,0},{24,8},{1,17},{9,25},{17,1},{25,9},{2,18},{10... | collective-permute-start | bytes 786440 | tf_op jit(solution)/shard_map/ppermute | solution.py:31
  27.5 0.5 collective-permute-start.8
  28.0 0.2 copy.8.mask_ref
  28.2 0.0 collective-permute-done.3.arrived_ref
  28.3 1.2 %kv_blocks.1 = (bf16[256,128]{1,0:T(8,128)(2,1)S(1)}, bf16[256,128]{1,0:T(8,128)(2,1)S(1)}, bf16[256,128]{1,0:T(8,128)(2,1)S(1)}, bf16[256,128]{1,0:T(8,128)(2,1)S(1)}) custom-call(f32[1024,128]{1,0:T(8,128)S(1)} %get-tuple-element.40.mine_ref, f32[1024,128]{1,0:T(8,128)} %collective-permute-done.3.arrived_ref, s32[1024,1]{1,0:T(8,128)S(1)} %copy.8.mask_ref), custom_call_target="tpu_custom_call" | custom-call | bytes 1024 | tf_op jit(solution)/shard_map/kv_blocks/pallas_call | solution.py:279
  29.5 1.6 %collective-permute-start.4 = (bf16[256,128]{1,0:T(8,128)(2,1)S(1)}, bf16[256,128]{1,0:T(8,128)(2,1)S(1)}, u32[]{:S(2)}, u32[]{:S(2)}) collective-permute-start(bf16[256,128]{1,0:T(8,128)(2,1)S(1)} %get-tuple-element.43), channel_id=1, source_target_pairs={{0,2},{1,3},{2,0},{3,1},{4,6},{5,7},{6,4},{7,5},{8,10},{9,11},{10,... | collective-permute-start | bytes 196616 | tf_op jit(solution)/shard_map/ppermute | solution.py:31
  31.1 2.6 %collective-permute-start.5 = (bf16[256,128]{1,0:T(8,128)(2,1)S(1)}, bf16[256,128]{1,0:T(8,128)(2,1)S(1)}, u32[]{:S(2)}, u32[]{:S(2)}) collective-permute-start(bf16[256,128]{1,0:T(8,128)(2,1)S(1)} %get-tuple-element.44), channel_id=1, source_target_pairs={{0,4},{1,5},{2,6},{3,7},{4,0},{5,1},{6,2},{7,3},{8,12},{9,13},{10,... | collective-permute-start | bytes 196616 | tf_op jit(solution)/shard_map/ppermute | solution.py:31
  33.7 0.2 collective-permute-start.6
  34.0 0.5 collective-permute-done.4
  34.5 3.2 %collective-permute-done.5 = bf16[256,128]{1,0:T(8,128)(2,1)S(1)} collective-permute-done((bf16[256,128]{1,0:T(8,128)(2,1)S(1)}, bf16[256,128]{1,0:T(8,128)(2,1)S(1)}, u32[]{:S(2)}, u32[]{:S(2)}) %collective-permute-start.5) | collective-permute-done | bytes 65568 | tf_op jit(solution)/shard_map/ppermute | solution.py:31
  37.7 2.1 %collective-permute-done.6 = bf16[256,128]{1,0:T(8,128)(2,1)S(1)} collective-permute-done((bf16[256,128]{1,0:T(8,128)(2,1)S(1)}, bf16[256,128]{1,0:T(8,128)(2,1)S(1)}, u32[]{:S(2)}, u32[]{:S(2)}) %collective-permute-start.6) | collective-permute-done | bytes 65568 | tf_op jit(solution)/shard_map/ppermute | solution.py:31
  39.8 0.0 collective-permute-done.7.refs_3_
  39.8 0.0 collective-permute-done.8.refs_4_
  39.9 1.5 %collective-permute-start.12 = (bf16[256,512]{1,0:T(8,128)(2,1)S(1)}, bf16[256,512]{1,0:T(8,128)(2,1)S(1)}, u32[]{:S(2)}, u32[]{:S(2)}) collective-permute-start(bf16[256,512]{1,0:T(8,128)(2,1)S(1)} %constant_dynamic-update-slice_fusion.refs_0_), channel_id=1, source_target_pairs={{0,24},{8,16},{16,8},{24,0},{1,25},{9,17},{17,9},{25,1},{2,26},{10... | collective-permute-start | bytes 786440 | tf_op jit(solution)/shard_map/ppermute | solution.py:31
  41.4 1.5 %collective-permute-start.11 = (bf16[256,512]{1,0:T(8,128)(2,1)S(1)}, bf16[256,512]{1,0:T(8,128)(2,1)S(1)}, u32[]{:S(2)}, u32[]{:S(2)}) collective-permute-start(bf16[256,512]{1,0:T(8,128)(2,1)S(1)} %constant_dynamic-update-slice_fusion.refs_0_), channel_id=1, source_target_pairs={{0,16},{8,24},{16,0},{24,8},{1,17},{9,25},{17,1},{25,9},{2,18},{10... | collective-permute-start | bytes 786440 | tf_op jit(solution)/shard_map/ppermute | solution.py:31
  42.9 0.5 collective-permute-start.10
  43.5 1.1 %lay.4.own_ref = bf16[512,2048]{1,0:T(8,128)(2,1)S(1)} custom-call(bf16[128,2048]{1,0:T(8,128)(2,1)S(1)} %get-tuple-element.51.refs_0_, bf16[192,2048]{1,0:T(8,128)(2,1)S(1)} %collective-permute-done.1.refs_0_.refs_1_, bf16[192,2048]{1,0:T(8,128)(2,1)S(1)} %collective-permute-done.2.refs_1_.refs_2_, bf16[64,2048]{1,0:T(8,128)(2,1)S(1)} %collective-permute-done.7.refs_3_, ...), custom_call_target="tpu_custom_call" | custom-call | bytes 1024 | tf_op jit(solution)/shard_map/lay/pallas_call | solution.py:188
  44.5 0.1 collective-permute-start.9
  44.6 4.8 %collective-permute-done.12.refs_3_ = bf16[256,512]{1,0:T(8,128)(2,1)S(1)} collective-permute-done((bf16[256,512]{1,0:T(8,128)(2,1)S(1)}, bf16[256,512]{1,0:T(8,128)(2,1)S(1)}, u32[]{:S(2)}, u32[]{:S(2)}) %collective-permute-start.12) | collective-permute-done | bytes 262176 | tf_op jit(solution)/shard_map/ppermute | solution.py:31
  49.4 2.7 %collective-permute-done.11.refs_2_ = bf16[256,512]{1,0:T(8,128)(2,1)S(1)} collective-permute-done((bf16[256,512]{1,0:T(8,128)(2,1)S(1)}, bf16[256,512]{1,0:T(8,128)(2,1)S(1)}, u32[]{:S(2)}, u32[]{:S(2)}) %collective-permute-start.11) | collective-permute-done | bytes 262176 | tf_op jit(solution)/shard_map/ppermute | solution.py:31
  52.1 0.1 lay.5
  52.2 0.8 products.3
  53.0 0.8 products.4
  53.8 0.1 collective-permute-start.13
  53.8 1.9 %collective-permute-start.15 = (bf16[1024,256]{1,0:T(8,128)(2,1)S(1)}, bf16[1024,256]{1,0:T(8,128)(2,1)S(1)}, u32[]{:S(2)}, u32[]{:S(2)}) collective-permute-start(bf16[1024,256]{1,0:T(8,128)(2,1)S(1)} %products.3), channel_id=1, source_target_pairs={{0,4},{1,5},{2,6},{3,7},{4,0},{5,1},{6,2},{7,3},{8,12},{9,13},{10,... | collective-permute-start | bytes 1572872 | tf_op jit(solution)/shard_map/ppermute | solution.py:31
  55.7 1.3 %products.5 = (f32[1024,256]{1,0:T(8,128)S(1)}, f32[1024,256]{1,0:T(8,128)S(1)}) custom-call(bf16[512,2048]{1,0:T(8,128)(2,1)S(1)} %lay.4.own_ref, bf16[512,2048]{1,0:T(8,128)(2,1)S(1)} %collective-permute-done.9.other_ref, bf16[512,512]{1,0:T(8,128)(2,1)S(1)} %get-tuple-element.64.refs_0_, bf16[512,512]{1,0:T(8,128)(2,1)S(1)} %get-tuple-element.65.refs_1_), custom_call_target="tpu_custom_call" | custom-call | bytes 1024 | tf_op jit(solution)/shard_map/products/pallas_call | solution.py:252
  57.0 19.8 %collective-permute-done.13 = bf16[1024,256]{1,0:T(8,128)(2,1)S(1)} collective-permute-done((bf16[1024,256]{1,0:T(8,128)(2,1)S(1)}, bf16[1024,256]{1,0:T(8,128)(2,1)S(1)}, u32[]{:S(2)}, u32[]{:S(2)}) %collective-permute-start.13) | collective-permute-done | bytes 524320 | tf_op jit(solution)/shard_map/ppermute | solution.py:31
  76.8 0.1 add_convert_fusion.1
  76.9 0.3 collective-permute-start.14
  77.2 1.7 %collective-permute-done.15 = bf16[1024,256]{1,0:T(8,128)(2,1)S(1)} collective-permute-done((bf16[1024,256]{1,0:T(8,128)(2,1)S(1)}, bf16[1024,256]{1,0:T(8,128)(2,1)S(1)}, u32[]{:S(2)}, u32[]{:S(2)}) %collective-permute-start.15) | collective-permute-done | bytes 524320 | tf_op jit(solution)/shard_map/ppermute | solution.py:31
  78.9 0.1 add_convert_fusion
  78.9 0.9 collective-permute-start.16
  79.8 10.5 %collective-permute-done.14 = bf16[1024,128]{1,0:T(8,128)(2,1)S(1)} collective-permute-done((bf16[1024,128]{1,0:T(8,128)(2,1)S(1)}, bf16[1024,128]{1,0:T(8,128)(2,1)S(1)}, u32[]{:S(2)}, u32[]{:S(2)}) %collective-permute-start.14) | collective-permute-done | bytes 262176 | tf_op jit(solution)/shard_map/ppermute | solution.py:31
  90.3 0.1 convert_add_fusion.1
  90.4 0.5 collective-permute-done.16
  90.9 0.1 convert_add_fusion
  91.0 1.1 %maximum_select_fusion = f32[2048,128]{1,0:T(8,128)} fusion(f32[1024,128]{1,0:T(8,128)S(1)} %convert_add_fusion, f32[1024,128]{1,0:T(8,128)S(1)} %convert_add_fusion.1, s32[2048,128]{1,0:T(8,128)S(1)} %copy-done.4), kind=kLoop, calls=%fused_computation | loop fusion | flops 786432 | bytes 3145728 | tf_op jit(solution)/shard_map/jit(_where)/select_n | solution.py:355
  (17 shorter events, 0.1 us)
Async XLA Ops:
  0.6 6.3 %collective-permute-start = (bf16[1024,128]{1,0:T(8,128)(2,1)}, bf16[1024,128]{1,0:T(8,128)(2,1)S(1)}, u32[]{:S(2)}, u32[]{:S(2)}) collective-permute-start(bf16[1024,128]{1,0:T(8,128)(2,1)} %own_ref.1), channel_id=1, source_target_pairs={{0,1},{1,0},{2,3},{3,2},{4,5},{5,4},{6,7},{7,6},{8,9},{9,8},{10,11... | collective-permute-start | bytes 786440 | tf_op jit(solution)/shard_map/ppermute | solution.py:31
  1.1 1.6 %copy-start = (bf16[128,8192]{1,0:T(8,128)(2,1)S(1)}, bf16[128,8192]{1,0:T(8,128)(2,1)}, u32[]{:S(2)}) copy-start(bf16[128,8192]{1,0:T(8,128)(2,1)} %source_ref.1) | copy-start | bytes 6291460
  2.7 4.2 %copy-start.1 = (bf16[1024,768]{1,0:T(8,128)(2,1)S(1)}, bf16[1024,768]{1,0:T(8,128)(2,1)}, u32[]{:S(2)}) copy-start(bf16[1024,768]{1,0:T(8,128)(2,1)} %q_ref.1) | copy-start | bytes 4718596
  2.7 4.2 %copy-start.3 = (bf16[1024,128]{1,0:T(8,128)(2,1)S(1)}, bf16[1024,128]{1,0:T(8,128)(2,1)}, u32[]{:S(2)}) copy-start(bf16[1024,128]{1,0:T(8,128)(2,1)} %own_ref.1) | copy-start | bytes 786436
  2.9 21.3 %collective-permute-start.1 = (bf16[192,2048]{1,0:T(8,128)(2,1)S(1)}, bf16[192,2048]{1,0:T(8,128)(2,1)S(1)}, u32[]{:S(2)}, u32[]{:S(2)}) collective-permute-start(bf16[192,2048]{1,0:T(8,128)(2,1)S(1)} %get-tuple-element.38), channel_id=1, source_target_pairs={{0,8},{8,0},{16,24},{24,16},{1,9},{9,1},{17,25},{25,17},{2,10},{10... | collective-permute-start | bytes 2359304 | tf_op jit(solution)/shard_map/ppermute | solution.py:31
  5.4 19.7 %collective-permute-start.2 = (bf16[192,2048]{1,0:T(8,128)(2,1)S(1)}, bf16[192,2048]{1,0:T(8,128)(2,1)S(1)}, u32[]{:S(2)}, u32[]{:S(2)}) collective-permute-start(bf16[192,2048]{1,0:T(8,128)(2,1)S(1)} %get-tuple-element.39), channel_id=1, source_target_pairs={{0,16},{8,24},{16,0},{24,8},{1,17},{9,25},{17,1},{25,9},{2,18},{10... | collective-permute-start | bytes 2359304 | tf_op jit(solution)/shard_map/ppermute | solution.py:31
  7.0 1.4 %copy-start.2 = (bf16[1024,768]{1,0:T(8,128)(2,1)S(1)}, bf16[1024,768]{1,0:T(8,128)(2,1)}, u32[]{:S(2)}) copy-start(bf16[1024,768]{1,0:T(8,128)(2,1)} %up_ref.1) | copy-start | bytes 4718596
  8.4 19.6 %copy-start.5 = (s32[1024,1]{0,1:T(1,128)S(1)}, s32[1024,1]{0,1:T(1,128)}, u32[]{:S(2)}) copy-start(s32[1024,1]{0,1:T(1,128)} %param.11) | copy-start | bytes 12292
  24.2 4.0 %collective-permute-start.3 = (f32[1024,128]{1,0:T(8,128)}, f32[1024,128]{1,0:T(8,128)}, u32[]{:S(2)}, u32[]{:S(2)}) collective-permute-start(f32[1024,128]{1,0:T(8,128)} %get-tuple-element.41), channel_id=1, source_target_pairs={{0,1},{1,0},{2,3},{3,2},{4,5},{5,4},{6,7},{7,6},{8,9},{9,8},{10,11... | collective-permute-start | bytes 1572872 | tf_op jit(solution)/shard_map/ppermute | solution.py:31
  26.0 13.8 %collective-permute-start.7 = (bf16[64,2048]{1,0:T(8,128)(2,1)}, bf16[64,2048]{1,0:T(8,128)(2,1)S(1)}, u32[]{:S(2)}, u32[]{:S(2)}) collective-permute-start(bf16[64,2048]{1,0:T(8,128)(2,1)} %get-tuple-element.49), channel_id=1, source_target_pairs={{0,16},{8,24},{16,0},{24,8},{1,17},{9,25},{17,1},{25,9},{2,18},{10... | collective-permute-start | bytes 786440 | tf_op jit(solution)/shard_map/ppermute | solution.py:31
  27.5 12.3 %collective-permute-start.8 = (bf16[64,2048]{1,0:T(8,128)(2,1)}, bf16[64,2048]{1,0:T(8,128)(2,1)}, u32[]{:S(2)}, u32[]{:S(2)}) collective-permute-start(bf16[64,2048]{1,0:T(8,128)(2,1)} %get-tuple-element.50), channel_id=1, source_target_pairs={{0,8},{8,0},{16,24},{24,16},{1,9},{9,1},{17,25},{25,17},{2,10},{10... | collective-permute-start | bytes 786440 | tf_op jit(solution)/shard_map/ppermute | solution.py:31
  29.5 5.0 %collective-permute-start.4 = (bf16[256,128]{1,0:T(8,128)(2,1)S(1)}, bf16[256,128]{1,0:T(8,128)(2,1)S(1)}, u32[]{:S(2)}, u32[]{:S(2)}) collective-permute-start(bf16[256,128]{1,0:T(8,128)(2,1)S(1)} %get-tuple-element.43), channel_id=1, source_target_pairs={{0,2},{1,3},{2,0},{3,1},{4,6},{5,7},{6,4},{7,5},{8,10},{9,11},{10,... | collective-permute-start | bytes 196616 | tf_op jit(solution)/shard_map/ppermute | solution.py:31
  31.1 6.6 %collective-permute-start.5 = (bf16[256,128]{1,0:T(8,128)(2,1)S(1)}, bf16[256,128]{1,0:T(8,128)(2,1)S(1)}, u32[]{:S(2)}, u32[]{:S(2)}) collective-permute-start(bf16[256,128]{1,0:T(8,128)(2,1)S(1)} %get-tuple-element.44), channel_id=1, source_target_pairs={{0,4},{1,5},{2,6},{3,7},{4,0},{5,1},{6,2},{7,3},{8,12},{9,13},{10,... | collective-permute-start | bytes 196616 | tf_op jit(solution)/shard_map/ppermute | solution.py:31
  33.7 6.1 %collective-permute-start.6 = (bf16[256,128]{1,0:T(8,128)(2,1)S(1)}, bf16[256,128]{1,0:T(8,128)(2,1)S(1)}, u32[]{:S(2)}, u32[]{:S(2)}) collective-permute-start(bf16[256,128]{1,0:T(8,128)(2,1)S(1)} %get-tuple-element.45), channel_id=1, source_target_pairs={{0,6},{1,7},{2,4},{3,5},{4,2},{5,3},{6,0},{7,1},{8,14},{9,15},{10,... | collective-permute-start | bytes 196616 | tf_op jit(solution)/shard_map/ppermute | solution.py:31
  39.9 9.5 %collective-permute-start.12 = (bf16[256,512]{1,0:T(8,128)(2,1)S(1)}, bf16[256,512]{1,0:T(8,128)(2,1)S(1)}, u32[]{:S(2)}, u32[]{:S(2)}) collective-permute-start(bf16[256,512]{1,0:T(8,128)(2,1)S(1)} %constant_dynamic-update-slice_fusion.refs_0_), channel_id=1, source_target_pairs={{0,24},{8,16},{16,8},{24,0},{1,25},{9,17},{17,9},{25,1},{2,26},{10... | collective-permute-start | bytes 786440 | tf_op jit(solution)/shard_map/ppermute | solution.py:31
  41.4 10.7 %collective-permute-start.11 = (bf16[256,512]{1,0:T(8,128)(2,1)S(1)}, bf16[256,512]{1,0:T(8,128)(2,1)S(1)}, u32[]{:S(2)}, u32[]{:S(2)}) collective-permute-start(bf16[256,512]{1,0:T(8,128)(2,1)S(1)} %constant_dynamic-update-slice_fusion.refs_0_), channel_id=1, source_target_pairs={{0,16},{8,24},{16,0},{24,8},{1,17},{9,25},{17,1},{25,9},{2,18},{10... | collective-permute-start | bytes 786440 | tf_op jit(solution)/shard_map/ppermute | solution.py:31
  42.9 9.2 %collective-permute-start.10 = (bf16[256,512]{1,0:T(8,128)(2,1)S(1)}, bf16[256,512]{1,0:T(8,128)(2,1)S(1)}, u32[]{:S(2)}, u32[]{:S(2)}) collective-permute-start(bf16[256,512]{1,0:T(8,128)(2,1)S(1)} %constant_dynamic-update-slice_fusion.refs_0_), channel_id=1, source_target_pairs={{0,8},{8,0},{16,24},{24,16},{1,9},{9,1},{17,25},{25,17},{2,10},{10... | collective-permute-start | bytes 786440 | tf_op jit(solution)/shard_map/ppermute | solution.py:31
  44.5 7.6 %collective-permute-start.9 = (bf16[512,2048]{1,0:T(8,128)(2,1)S(1)}, bf16[512,2048]{1,0:T(8,128)(2,1)S(1)}, u32[]{:S(2)}, u32[]{:S(2)}) collective-permute-start(bf16[512,2048]{1,0:T(8,128)(2,1)S(1)} %lay.4.own_ref), channel_id=1, source_target_pairs={{0,1},{1,0},{2,3},{3,2},{4,5},{5,4},{6,7},{7,6},{8,9},{9,8},{10,11... | collective-permute-start | bytes 6291464 | tf_op jit(solution)/shard_map/ppermute | solution.py:31
  53.8 23.1 %collective-permute-start.13 = (bf16[1024,256]{1,0:T(8,128)(2,1)S(1)}, bf16[1024,256]{1,0:T(8,128)(2,1)S(1)}, u32[]{:S(2)}, u32[]{:S(2)}) collective-permute-start(bf16[1024,256]{1,0:T(8,128)(2,1)S(1)} %products.4), channel_id=1, source_target_pairs={{0,2},{1,3},{2,0},{3,1},{4,6},{5,7},{6,4},{7,5},{8,10},{9,11},{10,... | collective-permute-start | bytes 1572872 | tf_op jit(solution)/shard_map/ppermute | solution.py:31
  53.8 25.0 %collective-permute-start.15 = (bf16[1024,256]{1,0:T(8,128)(2,1)S(1)}, bf16[1024,256]{1,0:T(8,128)(2,1)S(1)}, u32[]{:S(2)}, u32[]{:S(2)}) collective-permute-start(bf16[1024,256]{1,0:T(8,128)(2,1)S(1)} %products.3), channel_id=1, source_target_pairs={{0,4},{1,5},{2,6},{3,7},{4,0},{5,1},{6,2},{7,3},{8,12},{9,13},{10,... | collective-permute-start | bytes 1572872 | tf_op jit(solution)/shard_map/ppermute | solution.py:31
  76.9 13.4 %collective-permute-start.14 = (bf16[1024,128]{1,0:T(8,128)(2,1)S(1)}, bf16[1024,128]{1,0:T(8,128)(2,1)S(1)}, u32[]{:S(2)}, u32[]{:S(2)}) collective-permute-start(bf16[1024,128]{1,0:T(8,128)(2,1)S(1)} %add_convert_fusion.1), channel_id=1, source_target_pairs={{0,4},{1,5},{2,6},{3,7},{4,0},{5,1},{6,2},{7,3},{8,12},{9,13},{10,... | collective-permute-start | bytes 786440 | tf_op jit(solution)/shard_map/ppermute | solution.py:31
  78.9 12.1 %copy-start.4 = (s32[2048,128]{1,0:T(8,128)S(1)}, s32[2048,128]{1,0:T(8,128)}, u32[]{:S(2)}) copy-start(s32[2048,128]{1,0:T(8,128)} %param.10) | copy-start | bytes 3145732
  78.9 12.0 %collective-permute-start.16 = (bf16[1024,128]{1,0:T(8,128)(2,1)S(1)}, bf16[1024,128]{1,0:T(8,128)(2,1)S(1)}, u32[]{:S(2)}, u32[]{:S(2)}) collective-permute-start(bf16[1024,128]{1,0:T(8,128)(2,1)S(1)} %add_convert_fusion), channel_id=1, source_target_pairs={{0,2},{1,3},{2,0},{3,1},{4,6},{5,7},{6,4},{7,5},{8,10},{9,11},{10,... | collective-permute-start | bytes 786440 | tf_op jit(solution)/shard_map/ppermute | solution.py:31

commit v13 on v12

--- a/solution.py
+++ b/solution.py
@@ -306,12 +306,24 @@
 
     def gather(steps, hint):
         value = jnp.concatenate([blocks[s] for s in steps], 1)
-        found = [value if s == 0 else swap(value, "dp", s) for s in range(groups)]
         shape = (groups * rows, value.shape[1])
+        every = slice(None)
+        spans = [slice(half * rows, (half + 1) * rows) for half in range(2)]
+        if groups != 4:
+            found = [value if s == 0 else swap(value, "dp", s) for s in range(groups)]
+            outputs = [
+                (shape, [(s, span, every, s * rows) for s in range(groups)]) for span in spans
+            ]
+            return steps, lay(found, outputs, hint)
+        left, right = swap(value, "dp", 1), swap(value, "dp", 2)
+        piece = (rows, value.shape[1])
+        passed = [(piece, [(1, spans[0], every, 0)]), (piece, [(0, spans[1], every, 0)])]
+        upper, lower = lay([left, right], passed)
+        found = [value, left, right, swap(upper, "dp", 1), swap(lower, "dp", 2)]
         outputs = []
-        for half in range(2):
-            span = slice(half * rows, (half + 1) * rows)
-            outputs.append((shape, [(s, span, slice(None), s * rows) for s in range(groups)]))
+        for half, span in enumerate(spans):
+            entries = [(s, span, every, s * rows) for s in range(3)]
+            outputs.append((shape, entries + [(3 + half, spans[0], every, 3 * rows)]))
         return steps, lay(found, outputs, hint)
 
     found = [gather(tuple(range(chips)), LONG)]

time: 92.3 us -> 91.4 us (level)
  waiting for transfers between devices: 46.6 us -> 45.2 us
    ppermute x17 -> x18, waiting for transfers between devices: 46.6 us -> 45.2 us  [swap(): return lax.ppermute(value, axis, pairs)]
    ppermute x17 -> x18, starting transfers between devices: 17.9 us -> 18.4 us  [swap(): return lax.ppermute(value, axis, pairs)]
    pallas_call x3 -> x4, Pallas kernels: 2 us -> 2.01 us  [lay(): pl.pallas_call(kernel, out_shape=[jax.ShapeDtypeStruct(shape, sources[0]....]
  transfers between devices with their start and end apart: 17 -> 18, of which waited for: 10 -> 12; matrix products, arithmetic and copies ran while one was open for 0% -> 0% of each run, Pallas kernels for 22% -> 23%
where the time goes in v13:
time: 91.4 us; the launch traced here: 91.2 us
  waiting for transfers between devices  45.2 us (49%)
  Pallas kernels  22.1 us (24%)
  starting transfers between devices  18.4 us (20%)
  local copies, waits for them, and re-layouts  3.3 us (4%)
  other arithmetic  1.34 us (1%)
    ppermute x18, waiting for transfers between devices, swap(): return lax.ppermute(value, axis, pairs)  45.2 us
    ppermute x18, starting transfers between devices, swap(): return lax.ppermute(value, axis, pairs)  18.4 us
    pallas_call x1, Pallas kernels, attention(): pl.pallas_call(functools.partial(attention_kernel, height, heads), grid=(...  15.8 us
    unnamed x16, local copies, waits for them, and re-layouts  3.28 us
    pallas_call x3, Pallas kernels, products(): pl.pallas_call(functools.partial(product_kernel, jobs, depth, [steps for...  2.92 us
    pallas_call x4, Pallas kernels, lay(): pl.pallas_call(kernel, out_shape=[jax.ShapeDtypeStruct(shape, sources[0]....  2.01 us
  transfers between devices with their start and end apart: 18, of which 12 were waited for; matrix products, arithmetic and copies ran while one was open for 0% of the time, Pallas kernels for 23%

profile of v13, /device:TPU:0, one launch (start us, length us, event | category | flops | bytes accessed | tf_op | source)
XLA Modules:
  0.0 91.2 jit_solution(15454292167275385374)
XLA Ops:
  0.6 0.5 collective-permute-start
  1.1 1.6 %copy-done = bf16[128,8192]{1,0:T(8,128)(2,1)S(1)} copy-done((bf16[128,8192]{1,0:T(8,128)(2,1)S(1)}, bf16[128,8192]{1,0:T(8,128)(2,1)}, u32[]{:S(2)}) %copy-start) | copy-done | bytes 2097176
  2.7 0.1 spread.1
  2.9 2.6 %collective-permute-start.1 = (bf16[192,2048]{1,0:T(8,128)(2,1)S(1)}, bf16[192,2048]{1,0:T(8,128)(2,1)S(1)}, u32[]{:S(2)}, u32[]{:S(2)}) collective-permute-start(bf16[192,2048]{1,0:T(8,128)(2,1)S(1)} %get-tuple-element.40), channel_id=1, source_target_pairs={{0,8},{8,0},{16,24},{24,16},{1,9},{9,1},{17,25},{25,17},{2,10},{10... | collective-permute-start | bytes 2359304 | tf_op jit(solution)/shard_map/ppermute | solution.py:31
  5.4 1.5 %collective-permute-start.2 = (bf16[192,2048]{1,0:T(8,128)(2,1)S(1)}, bf16[192,2048]{1,0:T(8,128)(2,1)S(1)}, u32[]{:S(2)}, u32[]{:S(2)}) collective-permute-start(bf16[192,2048]{1,0:T(8,128)(2,1)S(1)} %get-tuple-element.41), channel_id=1, source_target_pairs={{0,16},{8,24},{16,0},{24,8},{1,17},{9,25},{17,1},{25,9},{2,18},{10... | collective-permute-start | bytes 2359304 | tf_op jit(solution)/shard_map/ppermute | solution.py:31
  7.0 0.0 collective-permute-done.other_ref
  7.0 0.0 copy-start.2
  7.0 1.4 %copy-done.2 = bf16[1024,768]{1,0:T(8,128)(2,1)S(1)} copy-done((bf16[1024,768]{1,0:T(8,128)(2,1)S(1)}, bf16[1024,768]{1,0:T(8,128)(2,1)}, u32[]{:S(2)}) %copy-start.2) | copy-done | bytes 1572888
  8.4 15.8 %attention.1 = (bf16[1024,768]{1,0:T(8,128)(2,1)}, f32[1024,128]{1,0:T(8,128)S(1)}, f32[1024,128]{1,0:T(8,128)}) custom-call(bf16[1024,128]{1,0:T(8,128)(2,1)S(1)} %copy-done.3, bf16[1024,128]{1,0:T(8,128)(2,1)S(1)} %collective-permute-done.other_ref, bf16[1024,768]{1,0:T(8,128)(2,1)S(1)} %copy-done.1, bf16[1024,768]{1,0:T(8,128)(2,1)S(1)} %copy-done.2), custom_call_target="tpu_custom_call" | custom-call | flops 16106127360 | bytes 9437184 | tf_op jit(solution)/shard_map/attention/pallas_call | solution.py:136
  24.2 0.9 collective-permute-done.2.refs_1_.refs_2_
  25.1 0.8 lay.4
  26.0 1.5 %collective-permute-start.7 = (bf16[64,2048]{1,0:T(8,128)(2,1)}, bf16[64,2048]{1,0:T(8,128)(2,1)S(1)}, u32[]{:S(2)}, u32[]{:S(2)}) collective-permute-start(bf16[64,2048]{1,0:T(8,128)(2,1)} %get-tuple-element.51), channel_id=1, source_target_pairs={{0,16},{8,24},{16,0},{24,8},{1,17},{9,25},{17,1},{25,9},{2,18},{10... | collective-permute-start | bytes 786440 | tf_op jit(solution)/shard_map/ppermute | solution.py:31
  27.5 0.5 collective-permute-start.8
  28.0 0.2 copy.8.mask_ref
  28.2 1.2 %kv_blocks.1 = (bf16[256,128]{1,0:T(8,128)(2,1)S(1)}, bf16[256,128]{1,0:T(8,128)(2,1)S(1)}, bf16[256,128]{1,0:T(8,128)(2,1)S(1)}, bf16[256,128]{1,0:T(8,128)(2,1)S(1)}) custom-call(f32[1024,128]{1,0:T(8,128)S(1)} %get-tuple-element.42.mine_ref, f32[1024,128]{1,0:T(8,128)} %collective-permute-done.3.arrived_ref, s32[1024,1]{1,0:T(8,128)S(1)} %copy.8.mask_ref), custom_call_target="tpu_custom_call" | custom-call | bytes 1024 | tf_op jit(solution)/shard_map/kv_blocks/pallas_call | solution.py:279
  29.5 1.6 %collective-permute-start.4 = (bf16[256,128]{1,0:T(8,128)(2,1)S(1)}, bf16[256,128]{1,0:T(8,128)(2,1)S(1)}, u32[]{:S(2)}, u32[]{:S(2)}) collective-permute-start(bf16[256,128]{1,0:T(8,128)(2,1)S(1)} %get-tuple-element.45), channel_id=1, source_target_pairs={{0,2},{1,3},{2,0},{3,1},{4,6},{5,7},{6,4},{7,5},{8,10},{9,11},{10,... | collective-permute-start | bytes 196616 | tf_op jit(solution)/shard_map/ppermute | solution.py:31
  31.1 2.6 %collective-permute-start.5 = (bf16[256,128]{1,0:T(8,128)(2,1)S(1)}, bf16[256,128]{1,0:T(8,128)(2,1)S(1)}, u32[]{:S(2)}, u32[]{:S(2)}) collective-permute-start(bf16[256,128]{1,0:T(8,128)(2,1)S(1)} %get-tuple-element.46), channel_id=1, source_target_pairs={{0,4},{1,5},{2,6},{3,7},{4,0},{5,1},{6,2},{7,3},{8,12},{9,13},{10,... | collective-permute-start | bytes 196616 | tf_op jit(solution)/shard_map/ppermute | solution.py:31
  33.7 0.2 collective-permute-start.6
  33.9 0.5 collective-permute-done.4
  34.5 3.2 %collective-permute-done.5 = bf16[256,128]{1,0:T(8,128)(2,1)S(1)} collective-permute-done((bf16[256,128]{1,0:T(8,128)(2,1)S(1)}, bf16[256,128]{1,0:T(8,128)(2,1)S(1)}, u32[]{:S(2)}, u32[]{:S(2)}) %collective-permute-start.5) | collective-permute-done | bytes 65568 | tf_op jit(solution)/shard_map/ppermute | solution.py:31
  37.7 2.1 %collective-permute-done.6 = bf16[256,128]{1,0:T(8,128)(2,1)S(1)} collective-permute-done((bf16[256,128]{1,0:T(8,128)(2,1)S(1)}, bf16[256,128]{1,0:T(8,128)(2,1)S(1)}, u32[]{:S(2)}, u32[]{:S(2)}) %collective-permute-start.6) | collective-permute-done | bytes 65568 | tf_op jit(solution)/shard_map/ppermute | solution.py:31
  39.9 0.6 collective-permute-start.11
  40.5 1.5 %collective-permute-start.10 = (bf16[256,512]{1,0:T(8,128)(2,1)S(1)}, bf16[256,512]{1,0:T(8,128)(2,1)S(1)}, u32[]{:S(2)}, u32[]{:S(2)}) collective-permute-start(bf16[256,512]{1,0:T(8,128)(2,1)S(1)} %constant_dynamic-update-slice_fusion.refs_0_), channel_id=1, source_target_pairs={{0,8},{8,0},{16,24},{24,16},{1,9},{9,1},{17,25},{25,17},{2,10},{10... | collective-permute-start | bytes 786440 | tf_op jit(solution)/shard_map/ppermute | solution.py:31
  42.0 1.1 %lay.5.own_ref = bf16[512,2048]{1,0:T(8,128)(2,1)S(1)} custom-call(bf16[128,2048]{1,0:T(8,128)(2,1)S(1)} %get-tuple-element.53.refs_0_, bf16[192,2048]{1,0:T(8,128)(2,1)S(1)} %collective-permute-done.1.refs_0_.refs_1_, bf16[192,2048]{1,0:T(8,128)(2,1)S(1)} %collective-permute-done.2.refs_1_.refs_2_, bf16[64,2048]{1,0:T(8,128)(2,1)S(1)} %collective-permute-done.7.refs_3_, ...), custom_call_target="tpu_custom_call" | custom-call | bytes 1024 | tf_op jit(solution)/shard_map/lay/pallas_call | solution.py:188
  43.0 0.1 collective-permute-start.9
  43.1 3.2 %collective-permute-done.11.refs_1_.refs_2_ = bf16[256,512]{1,0:T(8,128)(2,1)S(1)} collective-permute-done((bf16[256,512]{1,0:T(8,128)(2,1)S(1)}, bf16[256,512]{1,0:T(8,128)(2,1)S(1)}, u32[]{:S(2)}, u32[]{:S(2)}) %collective-permute-start.11) | collective-permute-done | bytes 262176 | tf_op jit(solution)/shard_map/ppermute | solution.py:31
  46.3 1.0 %collective-permute-done.10.refs_0_.refs_1_ = bf16[256,512]{1,0:T(8,128)(2,1)S(1)} collective-permute-done((bf16[256,512]{1,0:T(8,128)(2,1)S(1)}, bf16[256,512]{1,0:T(8,128)(2,1)S(1)}, u32[]{:S(2)}, u32[]{:S(2)}) %collective-permute-start.10) | collective-permute-done | bytes 262176 | tf_op jit(solution)/shard_map/ppermute | solution.py:31
  47.3 2.4 %collective-permute-start.12 = (bf16[128,512]{1,0:T(8,128)(2,1)S(1)}, bf16[128,512]{1,0:T(8,128)(2,1)S(1)}, u32[]{:S(2)}, u32[]{:S(2)}) collective-permute-start(bf16[128,512]{1,0:T(8,128)(2,1)S(1)} %get-tuple-element.62), channel_id=1, source_target_pairs={{0,8},{8,0},{16,24},{24,16},{1,9},{9,1},{17,25},{25,17},{2,10},{10... | collective-permute-start | bytes 393224 | tf_op jit(solution)/shard_map/ppermute | solution.py:31
  49.7 1.2 %collective-permute-start.13 = (bf16[128,512]{1,0:T(8,128)(2,1)S(1)}, bf16[128,512]{1,0:T(8,128)(2,1)S(1)}, u32[]{:S(2)}, u32[]{:S(2)}) collective-permute-start(bf16[128,512]{1,0:T(8,128)(2,1)S(1)} %get-tuple-element.63), channel_id=1, source_target_pairs={{0,16},{8,24},{16,0},{24,8},{1,17},{9,25},{17,1},{25,9},{2,18},{10... | collective-permute-start | bytes 393224 | tf_op jit(solution)/shard_map/ppermute | solution.py:31
  50.9 1.7 %collective-permute-done.12.refs_3_ = bf16[128,512]{1,0:T(8,128)(2,1)S(1)} collective-permute-done((bf16[128,512]{1,0:T(8,128)(2,1)S(1)}, bf16[128,512]{1,0:T(8,128)(2,1)S(1)}, u32[]{:S(2)}, u32[]{:S(2)}) %collective-permute-start.12) | collective-permute-done | bytes 131104 | tf_op jit(solution)/shard_map/ppermute | solution.py:31
  52.7 2.0 %collective-permute-done.13.refs_4_ = bf16[128,512]{1,0:T(8,128)(2,1)S(1)} collective-permute-done((bf16[128,512]{1,0:T(8,128)(2,1)S(1)}, bf16[128,512]{1,0:T(8,128)(2,1)S(1)}, u32[]{:S(2)}, u32[]{:S(2)}) %collective-permute-start.13) | collective-permute-done | bytes 131104 | tf_op jit(solution)/shard_map/ppermute | solution.py:31
  54.7 0.1 lay.7
  54.8 0.8 products.3
  55.6 0.8 products.4
  56.4 0.1 collective-permute-start.14
  56.4 1.3 %collective-permute-start.16 = (bf16[1024,256]{1,0:T(8,128)(2,1)S(1)}, bf16[1024,256]{1,0:T(8,128)(2,1)S(1)}, u32[]{:S(2)}, u32[]{:S(2)}) collective-permute-start(bf16[1024,256]{1,0:T(8,128)(2,1)S(1)} %products.3), channel_id=1, source_target_pairs={{0,4},{1,5},{2,6},{3,7},{4,0},{5,1},{6,2},{7,3},{8,12},{9,13},{10,... | collective-permute-start | bytes 1572872 | tf_op jit(solution)/shard_map/ppermute | solution.py:31
  57.7 1.3 %products.5 = (f32[1024,256]{1,0:T(8,128)S(1)}, f32[1024,256]{1,0:T(8,128)S(1)}) custom-call(bf16[512,2048]{1,0:T(8,128)(2,1)S(1)} %lay.5.own_ref, bf16[512,2048]{1,0:T(8,128)(2,1)S(1)} %collective-permute-done.9.other_ref, bf16[512,512]{1,0:T(8,128)(2,1)S(1)} %get-tuple-element.68.refs_0_, bf16[512,512]{1,0:T(8,128)(2,1)S(1)} %get-tuple-element.69.refs_1_), custom_call_target="tpu_custom_call" | custom-call | bytes 1024 | tf_op jit(solution)/shard_map/products/pallas_call | solution.py:252
  59.1 15.1 %collective-permute-done.14 = bf16[1024,256]{1,0:T(8,128)(2,1)S(1)} collective-permute-done((bf16[1024,256]{1,0:T(8,128)(2,1)S(1)}, bf16[1024,256]{1,0:T(8,128)(2,1)S(1)}, u32[]{:S(2)}, u32[]{:S(2)}) %collective-permute-start.14) | collective-permute-done | bytes 524320 | tf_op jit(solution)/shard_map/ppermute | solution.py:31
  74.2 0.1 add_convert_fusion.1
  74.3 0.1 collective-permute-start.15
  74.3 6.5 %collective-permute-done.16 = bf16[1024,256]{1,0:T(8,128)(2,1)S(1)} collective-permute-done((bf16[1024,256]{1,0:T(8,128)(2,1)S(1)}, bf16[1024,256]{1,0:T(8,128)(2,1)S(1)}, u32[]{:S(2)}, u32[]{:S(2)}) %collective-permute-start.16) | collective-permute-done | bytes 524320 | tf_op jit(solution)/shard_map/ppermute | solution.py:31
  80.9 0.1 add_convert_fusion
  80.9 0.1 collective-permute-start.17
  81.0 6.3 %collective-permute-done.15 = bf16[1024,128]{1,0:T(8,128)(2,1)S(1)} collective-permute-done((bf16[1024,128]{1,0:T(8,128)(2,1)S(1)}, bf16[1024,128]{1,0:T(8,128)(2,1)S(1)}, u32[]{:S(2)}, u32[]{:S(2)}) %collective-permute-start.15) | collective-permute-done | bytes 262176 | tf_op jit(solution)/shard_map/ppermute | solution.py:31
  87.3 0.1 convert_add_fusion.1
  87.4 2.6 %collective-permute-done.17 = bf16[1024,128]{1,0:T(8,128)(2,1)S(1)} collective-permute-done((bf16[1024,128]{1,0:T(8,128)(2,1)S(1)}, bf16[1024,128]{1,0:T(8,128)(2,1)S(1)}, u32[]{:S(2)}, u32[]{:S(2)}) %collective-permute-start.17) | collective-permute-done | bytes 262176 | tf_op jit(solution)/shard_map/ppermute | solution.py:31
  90.0 0.1 convert_add_fusion
  90.1 1.1 %maximum_select_fusion = f32[2048,128]{1,0:T(8,128)} fusion(f32[1024,128]{1,0:T(8,128)S(1)} %convert_add_fusion, f32[1024,128]{1,0:T(8,128)S(1)} %convert_add_fusion.1, s32[2048,128]{1,0:T(8,128)S(1)} %copy-done.4), kind=kLoop, calls=%fused_computation | loop fusion | flops 786432 | bytes 3145728 | tf_op jit(solution)/shard_map/jit(_where)/select_n | solution.py:367
  (20 shorter events, 0.1 us)
Async XLA Ops:
  0.6 6.3 %collective-permute-start = (bf16[1024,128]{1,0:T(8,128)(2,1)}, bf16[1024,128]{1,0:T(8,128)(2,1)S(1)}, u32[]{:S(2)}, u32[]{:S(2)}) collective-permute-start(bf16[1024,128]{1,0:T(8,128)(2,1)} %own_ref.1), channel_id=1, source_target_pairs={{0,1},{1,0},{2,3},{3,2},{4,5},{5,4},{6,7},{7,6},{8,9},{9,8},{10,11... | collective-permute-start | bytes 786440 | tf_op jit(solution)/shard_map/ppermute | solution.py:31
  1.1 1.6 %copy-start = (bf16[128,8192]{1,0:T(8,128)(2,1)S(1)}, bf16[128,8192]{1,0:T(8,128)(2,1)}, u32[]{:S(2)}) copy-start(bf16[128,8192]{1,0:T(8,128)(2,1)} %source_ref.1) | copy-start | bytes 6291460
  2.7 4.2 %copy-start.1 = (bf16[1024,768]{1,0:T(8,128)(2,1)S(1)}, bf16[1024,768]{1,0:T(8,128)(2,1)}, u32[]{:S(2)}) copy-start(bf16[1024,768]{1,0:T(8,128)(2,1)} %q_ref.1) | copy-start | bytes 4718596
  2.7 4.2 %copy-start.3 = (bf16[1024,128]{1,0:T(8,128)(2,1)S(1)}, bf16[1024,128]{1,0:T(8,128)(2,1)}, u32[]{:S(2)}) copy-start(bf16[1024,128]{1,0:T(8,128)(2,1)} %own_ref.1) | copy-start | bytes 786436
  2.9 21.3 %collective-permute-start.1 = (bf16[192,2048]{1,0:T(8,128)(2,1)S(1)}, bf16[192,2048]{1,0:T(8,128)(2,1)S(1)}, u32[]{:S(2)}, u32[]{:S(2)}) collective-permute-start(bf16[192,2048]{1,0:T(8,128)(2,1)S(1)} %get-tuple-element.40), channel_id=1, source_target_pairs={{0,8},{8,0},{16,24},{24,16},{1,9},{9,1},{17,25},{25,17},{2,10},{10... | collective-permute-start | bytes 2359304 | tf_op jit(solution)/shard_map/ppermute | solution.py:31
  5.4 19.7 %collective-permute-start.2 = (bf16[192,2048]{1,0:T(8,128)(2,1)S(1)}, bf16[192,2048]{1,0:T(8,128)(2,1)S(1)}, u32[]{:S(2)}, u32[]{:S(2)}) collective-permute-start(bf16[192,2048]{1,0:T(8,128)(2,1)S(1)} %get-tuple-element.41), channel_id=1, source_target_pairs={{0,16},{8,24},{16,0},{24,8},{1,17},{9,25},{17,1},{25,9},{2,18},{10... | collective-permute-start | bytes 2359304 | tf_op jit(solution)/shard_map/ppermute | solution.py:31
  7.0 1.4 %copy-start.2 = (bf16[1024,768]{1,0:T(8,128)(2,1)S(1)}, bf16[1024,768]{1,0:T(8,128)(2,1)}, u32[]{:S(2)}) copy-start(bf16[1024,768]{1,0:T(8,128)(2,1)} %up_ref.1) | copy-start | bytes 4718596
  8.4 19.6 %copy-start.5 = (s32[1024,1]{0,1:T(1,128)S(1)}, s32[1024,1]{0,1:T(1,128)}, u32[]{:S(2)}) copy-start(s32[1024,1]{0,1:T(1,128)} %param.11) | copy-start | bytes 12292
  24.2 4.0 %collective-permute-start.3 = (f32[1024,128]{1,0:T(8,128)}, f32[1024,128]{1,0:T(8,128)}, u32[]{:S(2)}, u32[]{:S(2)}) collective-permute-start(f32[1024,128]{1,0:T(8,128)} %get-tuple-element.43), channel_id=1, source_target_pairs={{0,1},{1,0},{2,3},{3,2},{4,5},{5,4},{6,7},{7,6},{8,9},{9,8},{10,11... | collective-permute-start | bytes 1572872 | tf_op jit(solution)/shard_map/ppermute | solution.py:31
  26.0 13.8 %collective-permute-start.7 = (bf16[64,2048]{1,0:T(8,128)(2,1)}, bf16[64,2048]{1,0:T(8,128)(2,1)S(1)}, u32[]{:S(2)}, u32[]{:S(2)}) collective-permute-start(bf16[64,2048]{1,0:T(8,128)(2,1)} %get-tuple-element.51), channel_id=1, source_target_pairs={{0,16},{8,24},{16,0},{24,8},{1,17},{9,25},{17,1},{25,9},{2,18},{10... | collective-permute-start | bytes 786440 | tf_op jit(solution)/shard_map/ppermute | solution.py:31
  27.5 12.3 %collective-permute-start.8 = (bf16[64,2048]{1,0:T(8,128)(2,1)}, bf16[64,2048]{1,0:T(8,128)(2,1)}, u32[]{:S(2)}, u32[]{:S(2)}) collective-permute-start(bf16[64,2048]{1,0:T(8,128)(2,1)} %get-tuple-element.52), channel_id=1, source_target_pairs={{0,8},{8,0},{16,24},{24,16},{1,9},{9,1},{17,25},{25,17},{2,10},{10... | collective-permute-start | bytes 786440 | tf_op jit(solution)/shard_map/ppermute | solution.py:31
  29.5 5.0 %collective-permute-start.4 = (bf16[256,128]{1,0:T(8,128)(2,1)S(1)}, bf16[256,128]{1,0:T(8,128)(2,1)S(1)}, u32[]{:S(2)}, u32[]{:S(2)}) collective-permute-start(bf16[256,128]{1,0:T(8,128)(2,1)S(1)} %get-tuple-element.45), channel_id=1, source_target_pairs={{0,2},{1,3},{2,0},{3,1},{4,6},{5,7},{6,4},{7,5},{8,10},{9,11},{10,... | collective-permute-start | bytes 196616 | tf_op jit(solution)/shard_map/ppermute | solution.py:31
  31.1 6.6 %collective-permute-start.5 = (bf16[256,128]{1,0:T(8,128)(2,1)S(1)}, bf16[256,128]{1,0:T(8,128)(2,1)S(1)}, u32[]{:S(2)}, u32[]{:S(2)}) collective-permute-start(bf16[256,128]{1,0:T(8,128)(2,1)S(1)} %get-tuple-element.46), channel_id=1, source_target_pairs={{0,4},{1,5},{2,6},{3,7},{4,0},{5,1},{6,2},{7,3},{8,12},{9,13},{10,... | collective-permute-start | bytes 196616 | tf_op jit(solution)/shard_map/ppermute | solution.py:31
  33.7 6.1 %collective-permute-start.6 = (bf16[256,128]{1,0:T(8,128)(2,1)S(1)}, bf16[256,128]{1,0:T(8,128)(2,1)S(1)}, u32[]{:S(2)}, u32[]{:S(2)}) collective-permute-start(bf16[256,128]{1,0:T(8,128)(2,1)S(1)} %get-tuple-element.47), channel_id=1, source_target_pairs={{0,6},{1,7},{2,4},{3,5},{4,2},{5,3},{6,0},{7,1},{8,14},{9,15},{10,... | collective-permute-start | bytes 196616 | tf_op jit(solution)/shard_map/ppermute | solution.py:31
  39.9 6.4 %collective-permute-start.11 = (bf16[256,512]{1,0:T(8,128)(2,1)S(1)}, bf16[256,512]{1,0:T(8,128)(2,1)S(1)}, u32[]{:S(2)}, u32[]{:S(2)}) collective-permute-start(bf16[256,512]{1,0:T(8,128)(2,1)S(1)} %constant_dynamic-update-slice_fusion.refs_0_), channel_id=1, source_target_pairs={{0,16},{8,24},{16,0},{24,8},{1,17},{9,25},{17,1},{25,9},{2,18},{10... | collective-permute-start | bytes 786440 | tf_op jit(solution)/shard_map/ppermute | solution.py:31
  40.5 6.8 %collective-permute-start.10 = (bf16[256,512]{1,0:T(8,128)(2,1)S(1)}, bf16[256,512]{1,0:T(8,128)(2,1)S(1)}, u32[]{:S(2)}, u32[]{:S(2)}) collective-permute-start(bf16[256,512]{1,0:T(8,128)(2,1)S(1)} %constant_dynamic-update-slice_fusion.refs_0_), channel_id=1, source_target_pairs={{0,8},{8,0},{16,24},{24,16},{1,9},{9,1},{17,25},{25,17},{2,10},{10... | collective-permute-start | bytes 786440 | tf_op jit(solution)/shard_map/ppermute | solution.py:31
  43.0 11.7 %collective-permute-start.9 = (bf16[512,2048]{1,0:T(8,128)(2,1)S(1)}, bf16[512,2048]{1,0:T(8,128)(2,1)S(1)}, u32[]{:S(2)}, u32[]{:S(2)}) collective-permute-start(bf16[512,2048]{1,0:T(8,128)(2,1)S(1)} %lay.5.own_ref), channel_id=1, source_target_pairs={{0,1},{1,0},{2,3},{3,2},{4,5},{5,4},{6,7},{7,6},{8,9},{9,8},{10,11... | collective-permute-start | bytes 6291464 | tf_op jit(solution)/shard_map/ppermute | solution.py:31
  47.3 5.3 %collective-permute-start.12 = (bf16[128,512]{1,0:T(8,128)(2,1)S(1)}, bf16[128,512]{1,0:T(8,128)(2,1)S(1)}, u32[]{:S(2)}, u32[]{:S(2)}) collective-permute-start(bf16[128,512]{1,0:T(8,128)(2,1)S(1)} %get-tuple-element.62), channel_id=1, source_target_pairs={{0,8},{8,0},{16,24},{24,16},{1,9},{9,1},{17,25},{25,17},{2,10},{10... | collective-permute-start | bytes 393224 | tf_op jit(solution)/shard_map/ppermute | solution.py:31
  49.7 5.0 %collective-permute-start.13 = (bf16[128,512]{1,0:T(8,128)(2,1)S(1)}, bf16[128,512]{1,0:T(8,128)(2,1)S(1)}, u32[]{:S(2)}, u32[]{:S(2)}) collective-permute-start(bf16[128,512]{1,0:T(8,128)(2,1)S(1)} %get-tuple-element.63), channel_id=1, source_target_pairs={{0,16},{8,24},{16,0},{24,8},{1,17},{9,25},{17,1},{25,9},{2,18},{10... | collective-permute-start | bytes 393224 | tf_op jit(solution)/shard_map/ppermute | solution.py:31
  56.4 17.8 %collective-permute-start.14 = (bf16[1024,256]{1,0:T(8,128)(2,1)S(1)}, bf16[1024,256]{1,0:T(8,128)(2,1)S(1)}, u32[]{:S(2)}, u32[]{:S(2)}) collective-permute-start(bf16[1024,256]{1,0:T(8,128)(2,1)S(1)} %products.4), channel_id=1, source_target_pairs={{0,2},{1,3},{2,0},{3,1},{4,6},{5,7},{6,4},{7,5},{8,10},{9,11},{10,... | collective-permute-start | bytes 1572872 | tf_op jit(solution)/shard_map/ppermute | solution.py:31
  56.4 24.4 %collective-permute-start.16 = (bf16[1024,256]{1,0:T(8,128)(2,1)S(1)}, bf16[1024,256]{1,0:T(8,128)(2,1)S(1)}, u32[]{:S(2)}, u32[]{:S(2)}) collective-permute-start(bf16[1024,256]{1,0:T(8,128)(2,1)S(1)} %products.3), channel_id=1, source_target_pairs={{0,4},{1,5},{2,6},{3,7},{4,0},{5,1},{6,2},{7,3},{8,12},{9,13},{10,... | collective-permute-start | bytes 1572872 | tf_op jit(solution)/shard_map/ppermute | solution.py:31
  74.3 13.0 %collective-permute-start.15 = (bf16[1024,128]{1,0:T(8,128)(2,1)S(1)}, bf16[1024,128]{1,0:T(8,128)(2,1)S(1)}, u32[]{:S(2)}, u32[]{:S(2)}) collective-permute-start(bf16[1024,128]{1,0:T(8,128)(2,1)S(1)} %add_convert_fusion.1), channel_id=1, source_target_pairs={{0,4},{1,5},{2,6},{3,7},{4,0},{5,1},{6,2},{7,3},{8,12},{9,13},{10,... | collective-permute-start | bytes 786440 | tf_op jit(solution)/shard_map/ppermute | solution.py:31
  80.9 9.2 %copy-start.4 = (s32[2048,128]{1,0:T(8,128)S(1)}, s32[2048,128]{1,0:T(8,128)}, u32[]{:S(2)}) copy-start(s32[2048,128]{1,0:T(8,128)} %param.10) | copy-start | bytes 3145732
  80.9 9.0 %collective-permute-start.17 = (bf16[1024,128]{1,0:T(8,128)(2,1)S(1)}, bf16[1024,128]{1,0:T(8,128)(2,1)S(1)}, u32[]{:S(2)}, u32[]{:S(2)}) collective-permute-start(bf16[1024,128]{1,0:T(8,128)(2,1)S(1)} %add_convert_fusion), channel_id=1, source_target_pairs={{0,2},{1,3},{2,0},{3,1},{4,6},{5,7},{6,4},{7,5},{8,10},{9,11},{10,... | collective-permute-start | bytes 786440 | tf_op jit(solution)/shard_map/ppermute | solution.py:31

commit v14 on v13

--- a/solution.py
+++ b/solution.py
@@ -122,7 +122,7 @@
     @pl.when(step == pl.num_programs(0) - 1)
     def _():
         mine_ref[...] = jnp.where(is_even, dk_ref[...], dv_ref[...])
-        theirs_ref[...] = jnp.where(is_even, dv_ref[...], dk_ref[...])
+        theirs_ref[...] = jnp.where(is_even, dv_ref[...], dk_ref[...]).astype(BF16)
 
 
 def attention(own, other, queries, out_grad):
@@ -138,7 +138,11 @@
         grid=(width // (heads * depth),),
         in_specs=[whole, whole, column, column],
         out_specs=[column, whole, whole],
-        out_shape=[jax.ShapeDtypeStruct((length, width), BF16), sums, sums],
+        out_shape=[
+            jax.ShapeDtypeStruct((length, width), BF16),
+            sums,
+            jax.ShapeDtypeStruct((length, depth), BF16),
+        ],
         scratch_shapes=[
             pltpu.VMEM((length, depth), BF16),
             pltpu.VMEM((length, depth), BF16),
@@ -268,7 +272,7 @@
         for half in range(2):
             start = ((chip ^ step) * 2 + (core ^ half)) * rows
             span = pl.ds(pl.multiple_of(start, rows), rows)
-            total = mine_ref[span, :] + arrived_ref[span, :].astype(F32)
+            total = mine_ref[span, :] + arrived_ref[span, :].astype(F32).astype(F32)
             keep = mask_ref[span, :].astype(F32)
             out_ref[half * rows : (half + 1) * rows, :] = (total * keep).astype(BF16)
 

time: 91.4 us -> 91.3 us (level)
  transfers between devices with their start and end apart: 18 -> 18, of which waited for: 12 -> 12; matrix products, arithmetic and copies ran while one was open for 0% -> 0% of each run, Pallas kernels for 23% -> 22%
where the time goes in v14:
time: 91.3 us; the launch traced here: 91.1 us
  waiting for transfers between devices  45.5 us (50%)
  Pallas kernels  22 us (24%)
  starting transfers between devices  18.2 us (20%)
  local copies, waits for them, and re-layouts  3.3 us (4%)
  other arithmetic  1.34 us (1%)
    ppermute x18, waiting for transfers between devices, swap(): return lax.ppermute(value, axis, pairs)  45.5 us
    ppermute x18, starting transfers between devices, swap(): return lax.ppermute(value, axis, pairs)  18.2 us
    pallas_call x1, Pallas kernels, attention(): pl.pallas_call(functools.partial(attention_kernel, height, heads), grid=(...  15.7 us
    unnamed x16, local copies, waits for them, and re-layouts  3.28 us
    pallas_call x3, Pallas kernels, products(): pl.pallas_call(functools.partial(product_kernel, jobs, depth, [steps for...  2.91 us
    pallas_call x4, Pallas kernels, lay(): pl.pallas_call(kernel, out_shape=[jax.ShapeDtypeStruct(shape, sources[0]....  2.03 us
  transfers between devices with their start and end apart: 18, of which 12 were waited for; matrix products, arithmetic and copies ran while one was open for 0% of the time, Pallas kernels for 22%

profile of v14, /device:TPU:0, one launch (start us, length us, event | category | flops | bytes accessed | tf_op | source)
XLA Modules:
  0.0 91.1 jit_solution(16279705622731496767)
XLA Ops:
  0.6 0.5 collective-permute-start
  1.1 1.6 %copy-done = bf16[128,8192]{1,0:T(8,128)(2,1)S(1)} copy-done((bf16[128,8192]{1,0:T(8,128)(2,1)S(1)}, bf16[128,8192]{1,0:T(8,128)(2,1)}, u32[]{:S(2)}) %copy-start) | copy-done | bytes 2097176
  2.7 0.1 spread.1
  2.9 2.6 %collective-permute-start.1 = (bf16[192,2048]{1,0:T(8,128)(2,1)S(1)}, bf16[192,2048]{1,0:T(8,128)(2,1)S(1)}, u32[]{:S(2)}, u32[]{:S(2)}) collective-permute-start(bf16[192,2048]{1,0:T(8,128)(2,1)S(1)} %get-tuple-element.40), channel_id=1, source_target_pairs={{0,8},{8,0},{16,24},{24,16},{1,9},{9,1},{17,25},{25,17},{2,10},{10... | collective-permute-start | bytes 2359304 | tf_op jit(solution)/shard_map/ppermute | solution.py:31
  5.4 1.5 %collective-permute-start.2 = (bf16[192,2048]{1,0:T(8,128)(2,1)S(1)}, bf16[192,2048]{1,0:T(8,128)(2,1)S(1)}, u32[]{:S(2)}, u32[]{:S(2)}) collective-permute-start(bf16[192,2048]{1,0:T(8,128)(2,1)S(1)} %get-tuple-element.41), channel_id=1, source_target_pairs={{0,16},{8,24},{16,0},{24,8},{1,17},{9,25},{17,1},{25,9},{2,18},{10... | collective-permute-start | bytes 2359304 | tf_op jit(solution)/shard_map/ppermute | solution.py:31
  7.0 0.0 copy-start.2
  7.0 1.4 %copy-done.2 = bf16[1024,768]{1,0:T(8,128)(2,1)S(1)} copy-done((bf16[1024,768]{1,0:T(8,128)(2,1)S(1)}, bf16[1024,768]{1,0:T(8,128)(2,1)}, u32[]{:S(2)}) %copy-start.2) | copy-done | bytes 1572888
  8.4 15.7 %attention.1 = (bf16[1024,768]{1,0:T(8,128)(2,1)}, f32[1024,128]{1,0:T(8,128)S(1)}, bf16[1024,128]{1,0:T(8,128)(2,1)}) custom-call(bf16[1024,128]{1,0:T(8,128)(2,1)S(1)} %copy-done.3, bf16[1024,128]{1,0:T(8,128)(2,1)S(1)} %collective-permute-done.other_ref, bf16[1024,768]{1,0:T(8,128)(2,1)S(1)} %copy-done.1, bf16[1024,768]{1,0:T(8,128)(2,1)S(1)} %copy-done.2), custom_call_target="tpu_custom_call" | custom-call | flops 16106127360 | bytes 9437184 | tf_op jit(solution)/shard_map/attention/pallas_call | solution.py:136
  24.1 1.0 %collective-permute-done.2.refs_1_.refs_2_ = bf16[192,2048]{1,0:T(8,128)(2,1)S(1)} collective-permute-done((bf16[192,2048]{1,0:T(8,128)(2,1)S(1)}, bf16[192,2048]{1,0:T(8,128)(2,1)S(1)}, u32[]{:S(2)}, u32[]{:S(2)}) %collective-permute-start.2) | collective-permute-done | bytes 786464 | tf_op jit(solution)/shard_map/ppermute | solution.py:31
  25.1 0.9 lay.4
  26.0 1.5 %collective-permute-start.7 = (bf16[64,2048]{1,0:T(8,128)(2,1)}, bf16[64,2048]{1,0:T(8,128)(2,1)S(1)}, u32[]{:S(2)}, u32[]{:S(2)}) collective-permute-start(bf16[64,2048]{1,0:T(8,128)(2,1)} %get-tuple-element.51), channel_id=1, source_target_pairs={{0,16},{8,24},{16,0},{24,8},{1,17},{9,25},{17,1},{25,9},{2,18},{10... | collective-permute-start | bytes 786440 | tf_op jit(solution)/shard_map/ppermute | solution.py:31
  27.5 0.5 collective-permute-start.8
  28.0 0.2 copy.8.mask_ref
  28.3 1.2 %kv_blocks.1 = (bf16[256,128]{1,0:T(8,128)(2,1)S(1)}, bf16[256,128]{1,0:T(8,128)(2,1)S(1)}, bf16[256,128]{1,0:T(8,128)(2,1)S(1)}, bf16[256,128]{1,0:T(8,128)(2,1)S(1)}) custom-call(f32[1024,128]{1,0:T(8,128)S(1)} %get-tuple-element.42.mine_ref, bf16[1024,128]{1,0:T(8,128)(2,1)} %collective-permute-done.3.arrived_ref, s32[1024,1]{1,0:T(8,128)S(1)} %copy.8.mask_ref), custom_call_target="tpu_custom_call" | custom-call | bytes 1024 | tf_op jit(solution)/shard_map/kv_blocks/pallas_call | solution.py:283
  29.4 1.6 %collective-permute-start.4 = (bf16[256,128]{1,0:T(8,128)(2,1)S(1)}, bf16[256,128]{1,0:T(8,128)(2,1)S(1)}, u32[]{:S(2)}, u32[]{:S(2)}) collective-permute-start(bf16[256,128]{1,0:T(8,128)(2,1)S(1)} %get-tuple-element.45), channel_id=1, source_target_pairs={{0,2},{1,3},{2,0},{3,1},{4,6},{5,7},{6,4},{7,5},{8,10},{9,11},{10,... | collective-permute-start | bytes 196616 | tf_op jit(solution)/shard_map/ppermute | solution.py:31
  31.1 2.6 %collective-permute-start.5 = (bf16[256,128]{1,0:T(8,128)(2,1)S(1)}, bf16[256,128]{1,0:T(8,128)(2,1)S(1)}, u32[]{:S(2)}, u32[]{:S(2)}) collective-permute-start(bf16[256,128]{1,0:T(8,128)(2,1)S(1)} %get-tuple-element.46), channel_id=1, source_target_pairs={{0,4},{1,5},{2,6},{3,7},{4,0},{5,1},{6,2},{7,3},{8,12},{9,13},{10,... | collective-permute-start | bytes 196616 | tf_op jit(solution)/shard_map/ppermute | solution.py:31
  33.7 0.2 collective-permute-start.6
  33.9 0.5 collective-permute-done.4
  34.4 3.2 %collective-permute-done.5 = bf16[256,128]{1,0:T(8,128)(2,1)S(1)} collective-permute-done((bf16[256,128]{1,0:T(8,128)(2,1)S(1)}, bf16[256,128]{1,0:T(8,128)(2,1)S(1)}, u32[]{:S(2)}, u32[]{:S(2)}) %collective-permute-start.5) | collective-permute-done | bytes 65568 | tf_op jit(solution)/shard_map/ppermute | solution.py:31
  37.6 2.1 %collective-permute-done.6 = bf16[256,128]{1,0:T(8,128)(2,1)S(1)} collective-permute-done((bf16[256,128]{1,0:T(8,128)(2,1)S(1)}, bf16[256,128]{1,0:T(8,128)(2,1)S(1)}, u32[]{:S(2)}, u32[]{:S(2)}) %collective-permute-start.6) | collective-permute-done | bytes 65568 | tf_op jit(solution)/shard_map/ppermute | solution.py:31
  39.8 0.6 collective-permute-start.11
  40.4 1.5 %collective-permute-start.10 = (bf16[256,512]{1,0:T(8,128)(2,1)S(1)}, bf16[256,512]{1,0:T(8,128)(2,1)S(1)}, u32[]{:S(2)}, u32[]{:S(2)}) collective-permute-start(bf16[256,512]{1,0:T(8,128)(2,1)S(1)} %constant_dynamic-update-slice_fusion.refs_0_), channel_id=1, source_target_pairs={{0,8},{8,0},{16,24},{24,16},{1,9},{9,1},{17,25},{25,17},{2,10},{10... | collective-permute-start | bytes 786440 | tf_op jit(solution)/shard_map/ppermute | solution.py:31
  41.9 1.1 %lay.5.own_ref = bf16[512,2048]{1,0:T(8,128)(2,1)S(1)} custom-call(bf16[128,2048]{1,0:T(8,128)(2,1)S(1)} %get-tuple-element.53.refs_0_, bf16[192,2048]{1,0:T(8,128)(2,1)S(1)} %collective-permute-done.1.refs_0_.refs_1_, bf16[192,2048]{1,0:T(8,128)(2,1)S(1)} %collective-permute-done.2.refs_1_.refs_2_, bf16[64,2048]{1,0:T(8,128)(2,1)S(1)} %collective-permute-done.7.refs_3_, ...), custom_call_target="tpu_custom_call" | custom-call | bytes 1024 | tf_op jit(solution)/shard_map/lay/pallas_call | solution.py:192
  43.0 0.1 collective-permute-start.9
  43.1 3.2 %collective-permute-done.11.refs_1_.refs_2_ = bf16[256,512]{1,0:T(8,128)(2,1)S(1)} collective-permute-done((bf16[256,512]{1,0:T(8,128)(2,1)S(1)}, bf16[256,512]{1,0:T(8,128)(2,1)S(1)}, u32[]{:S(2)}, u32[]{:S(2)}) %collective-permute-start.11) | collective-permute-done | bytes 262176 | tf_op jit(solution)/shard_map/ppermute | solution.py:31
  46.3 1.0 %collective-permute-done.10.refs_0_.refs_1_ = bf16[256,512]{1,0:T(8,128)(2,1)S(1)} collective-permute-done((bf16[256,512]{1,0:T(8,128)(2,1)S(1)}, bf16[256,512]{1,0:T(8,128)(2,1)S(1)}, u32[]{:S(2)}, u32[]{:S(2)}) %collective-permute-start.10) | collective-permute-done | bytes 262176 | tf_op jit(solution)/shard_map/ppermute | solution.py:31
  47.2 2.4 %collective-permute-start.12 = (bf16[128,512]{1,0:T(8,128)(2,1)S(1)}, bf16[128,512]{1,0:T(8,128)(2,1)S(1)}, u32[]{:S(2)}, u32[]{:S(2)}) collective-permute-start(bf16[128,512]{1,0:T(8,128)(2,1)S(1)} %get-tuple-element.62), channel_id=1, source_target_pairs={{0,8},{8,0},{16,24},{24,16},{1,9},{9,1},{17,25},{25,17},{2,10},{10... | collective-permute-start | bytes 393224 | tf_op jit(solution)/shard_map/ppermute | solution.py:31
  49.6 1.2 %collective-permute-start.13 = (bf16[128,512]{1,0:T(8,128)(2,1)S(1)}, bf16[128,512]{1,0:T(8,128)(2,1)S(1)}, u32[]{:S(2)}, u32[]{:S(2)}) collective-permute-start(bf16[128,512]{1,0:T(8,128)(2,1)S(1)} %get-tuple-element.63), channel_id=1, source_target_pairs={{0,16},{8,24},{16,0},{24,8},{1,17},{9,25},{17,1},{25,9},{2,18},{10... | collective-permute-start | bytes 393224 | tf_op jit(solution)/shard_map/ppermute | solution.py:31
  50.9 1.7 %collective-permute-done.12.refs_3_ = bf16[128,512]{1,0:T(8,128)(2,1)S(1)} collective-permute-done((bf16[128,512]{1,0:T(8,128)(2,1)S(1)}, bf16[128,512]{1,0:T(8,128)(2,1)S(1)}, u32[]{:S(2)}, u32[]{:S(2)}) %collective-permute-start.12) | collective-permute-done | bytes 131104 | tf_op jit(solution)/shard_map/ppermute | solution.py:31
  52.6 2.0 %collective-permute-done.13.refs_4_ = bf16[128,512]{1,0:T(8,128)(2,1)S(1)} collective-permute-done((bf16[128,512]{1,0:T(8,128)(2,1)S(1)}, bf16[128,512]{1,0:T(8,128)(2,1)S(1)}, u32[]{:S(2)}, u32[]{:S(2)}) %collective-permute-start.13) | collective-permute-done | bytes 131104 | tf_op jit(solution)/shard_map/ppermute | solution.py:31
  54.6 0.1 lay.7
  54.7 0.0 collective-permute-done.9.other_ref
  54.7 0.8 products.3
  55.5 0.8 products.4
  56.3 0.1 collective-permute-start.14
  56.4 1.1 %collective-permute-start.16 = (bf16[1024,256]{1,0:T(8,128)(2,1)S(1)}, bf16[1024,256]{1,0:T(8,128)(2,1)S(1)}, u32[]{:S(2)}, u32[]{:S(2)}) collective-permute-start(bf16[1024,256]{1,0:T(8,128)(2,1)S(1)} %products.3), channel_id=1, source_target_pairs={{0,4},{1,5},{2,6},{3,7},{4,0},{5,1},{6,2},{7,3},{8,12},{9,13},{10,... | collective-permute-start | bytes 1572872 | tf_op jit(solution)/shard_map/ppermute | solution.py:31
  57.5 1.3 %products.5 = (f32[1024,256]{1,0:T(8,128)S(1)}, f32[1024,256]{1,0:T(8,128)S(1)}) custom-call(bf16[512,2048]{1,0:T(8,128)(2,1)S(1)} %lay.5.own_ref, bf16[512,2048]{1,0:T(8,128)(2,1)S(1)} %collective-permute-done.9.other_ref, bf16[512,512]{1,0:T(8,128)(2,1)S(1)} %get-tuple-element.68.refs_0_, bf16[512,512]{1,0:T(8,128)(2,1)S(1)} %get-tuple-element.69.refs_1_), custom_call_target="tpu_custom_call" | custom-call | bytes 1024 | tf_op jit(solution)/shard_map/products/pallas_call | solution.py:256
  58.8 15.2 %collective-permute-done.14 = bf16[1024,256]{1,0:T(8,128)(2,1)S(1)} collective-permute-done((bf16[1024,256]{1,0:T(8,128)(2,1)S(1)}, bf16[1024,256]{1,0:T(8,128)(2,1)S(1)}, u32[]{:S(2)}, u32[]{:S(2)}) %collective-permute-start.14) | collective-permute-done | bytes 524320 | tf_op jit(solution)/shard_map/ppermute | solution.py:31
  74.0 0.1 add_convert_fusion.1
  74.1 0.1 collective-permute-start.15
  74.2 6.9 %collective-permute-done.16 = bf16[1024,256]{1,0:T(8,128)(2,1)S(1)} collective-permute-done((bf16[1024,256]{1,0:T(8,128)(2,1)S(1)}, bf16[1024,256]{1,0:T(8,128)(2,1)S(1)}, u32[]{:S(2)}, u32[]{:S(2)}) %collective-permute-start.16) | collective-permute-done | bytes 524320 | tf_op jit(solution)/shard_map/ppermute | solution.py:31
  81.1 0.1 add_convert_fusion
  81.1 0.1 collective-permute-start.17
  81.2 6.0 %collective-permute-done.15 = bf16[1024,128]{1,0:T(8,128)(2,1)S(1)} collective-permute-done((bf16[1024,128]{1,0:T(8,128)(2,1)S(1)}, bf16[1024,128]{1,0:T(8,128)(2,1)S(1)}, u32[]{:S(2)}, u32[]{:S(2)}) %collective-permute-start.15) | collective-permute-done | bytes 262176 | tf_op jit(solution)/shard_map/ppermute | solution.py:31
  87.2 0.1 convert_add_fusion.1
  87.3 2.6 %collective-permute-done.17 = bf16[1024,128]{1,0:T(8,128)(2,1)S(1)} collective-permute-done((bf16[1024,128]{1,0:T(8,128)(2,1)S(1)}, bf16[1024,128]{1,0:T(8,128)(2,1)S(1)}, u32[]{:S(2)}, u32[]{:S(2)}) %collective-permute-start.17) | collective-permute-done | bytes 262176 | tf_op jit(solution)/shard_map/ppermute | solution.py:31
  89.9 0.1 convert_add_fusion
  90.0 1.1 %maximum_select_fusion = f32[2048,128]{1,0:T(8,128)} fusion(f32[1024,128]{1,0:T(8,128)S(1)} %convert_add_fusion, f32[1024,128]{1,0:T(8,128)S(1)} %convert_add_fusion.1, s32[2048,128]{1,0:T(8,128)S(1)} %copy-done.4), kind=kLoop, calls=%fused_computation | loop fusion | flops 786432 | bytes 3145728 | tf_op jit(solution)/shard_map/jit(_where)/select_n | solution.py:371
  (20 shorter events, 0.1 us)
Async XLA Ops:
  0.6 6.3 %collective-permute-start = (bf16[1024,128]{1,0:T(8,128)(2,1)}, bf16[1024,128]{1,0:T(8,128)(2,1)S(1)}, u32[]{:S(2)}, u32[]{:S(2)}) collective-permute-start(bf16[1024,128]{1,0:T(8,128)(2,1)} %own_ref.1), channel_id=1, source_target_pairs={{0,1},{1,0},{2,3},{3,2},{4,5},{5,4},{6,7},{7,6},{8,9},{9,8},{10,11... | collective-permute-start | bytes 786440 | tf_op jit(solution)/shard_map/ppermute | solution.py:31
  1.1 1.6 %copy-start = (bf16[128,8192]{1,0:T(8,128)(2,1)S(1)}, bf16[128,8192]{1,0:T(8,128)(2,1)}, u32[]{:S(2)}) copy-start(bf16[128,8192]{1,0:T(8,128)(2,1)} %source_ref.1) | copy-start | bytes 6291460
  2.7 4.2 %copy-start.1 = (bf16[1024,768]{1,0:T(8,128)(2,1)S(1)}, bf16[1024,768]{1,0:T(8,128)(2,1)}, u32[]{:S(2)}) copy-start(bf16[1024,768]{1,0:T(8,128)(2,1)} %q_ref.1) | copy-start | bytes 4718596
  2.7 4.2 %copy-start.3 = (bf16[1024,128]{1,0:T(8,128)(2,1)S(1)}, bf16[1024,128]{1,0:T(8,128)(2,1)}, u32[]{:S(2)}) copy-start(bf16[1024,128]{1,0:T(8,128)(2,1)} %own_ref.1) | copy-start | bytes 786436
  2.9 21.2 %collective-permute-start.1 = (bf16[192,2048]{1,0:T(8,128)(2,1)S(1)}, bf16[192,2048]{1,0:T(8,128)(2,1)S(1)}, u32[]{:S(2)}, u32[]{:S(2)}) collective-permute-start(bf16[192,2048]{1,0:T(8,128)(2,1)S(1)} %get-tuple-element.40), channel_id=1, source_target_pairs={{0,8},{8,0},{16,24},{24,16},{1,9},{9,1},{17,25},{25,17},{2,10},{10... | collective-permute-start | bytes 2359304 | tf_op jit(solution)/shard_map/ppermute | solution.py:31
  5.4 19.7 %collective-permute-start.2 = (bf16[192,2048]{1,0:T(8,128)(2,1)S(1)}, bf16[192,2048]{1,0:T(8,128)(2,1)S(1)}, u32[]{:S(2)}, u32[]{:S(2)}) collective-permute-start(bf16[192,2048]{1,0:T(8,128)(2,1)S(1)} %get-tuple-element.41), channel_id=1, source_target_pairs={{0,16},{8,24},{16,0},{24,8},{1,17},{9,25},{17,1},{25,9},{2,18},{10... | collective-permute-start | bytes 2359304 | tf_op jit(solution)/shard_map/ppermute | solution.py:31
  7.0 1.4 %copy-start.2 = (bf16[1024,768]{1,0:T(8,128)(2,1)S(1)}, bf16[1024,768]{1,0:T(8,128)(2,1)}, u32[]{:S(2)}) copy-start(bf16[1024,768]{1,0:T(8,128)(2,1)} %up_ref.1) | copy-start | bytes 4718596
  8.4 19.6 %copy-start.5 = (s32[1024,1]{0,1:T(1,128)S(1)}, s32[1024,1]{0,1:T(1,128)}, u32[]{:S(2)}) copy-start(s32[1024,1]{0,1:T(1,128)} %param.11) | copy-start | bytes 12292
  24.1 4.1 %collective-permute-start.3 = (bf16[1024,128]{1,0:T(8,128)(2,1)}, bf16[1024,128]{1,0:T(8,128)(2,1)}, u32[]{:S(2)}, u32[]{:S(2)}) collective-permute-start(bf16[1024,128]{1,0:T(8,128)(2,1)} %get-tuple-element.43), channel_id=1, source_target_pairs={{0,1},{1,0},{2,3},{3,2},{4,5},{5,4},{6,7},{7,6},{8,9},{9,8},{10,11... | collective-permute-start | bytes 786440 | tf_op jit(solution)/shard_map/ppermute | solution.py:31
  26.0 13.8 %collective-permute-start.7 = (bf16[64,2048]{1,0:T(8,128)(2,1)}, bf16[64,2048]{1,0:T(8,128)(2,1)S(1)}, u32[]{:S(2)}, u32[]{:S(2)}) collective-permute-start(bf16[64,2048]{1,0:T(8,128)(2,1)} %get-tuple-element.51), channel_id=1, source_target_pairs={{0,16},{8,24},{16,0},{24,8},{1,17},{9,25},{17,1},{25,9},{2,18},{10... | collective-permute-start | bytes 786440 | tf_op jit(solution)/shard_map/ppermute | solution.py:31
  27.5 12.2 %collective-permute-start.8 = (bf16[64,2048]{1,0:T(8,128)(2,1)}, bf16[64,2048]{1,0:T(8,128)(2,1)}, u32[]{:S(2)}, u32[]{:S(2)}) collective-permute-start(bf16[64,2048]{1,0:T(8,128)(2,1)} %get-tuple-element.52), channel_id=1, source_target_pairs={{0,8},{8,0},{16,24},{24,16},{1,9},{9,1},{17,25},{25,17},{2,10},{10... | collective-permute-start | bytes 786440 | tf_op jit(solution)/shard_map/ppermute | solution.py:31
  29.4 5.0 %collective-permute-start.4 = (bf16[256,128]{1,0:T(8,128)(2,1)S(1)}, bf16[256,128]{1,0:T(8,128)(2,1)S(1)}, u32[]{:S(2)}, u32[]{:S(2)}) collective-permute-start(bf16[256,128]{1,0:T(8,128)(2,1)S(1)} %get-tuple-element.45), channel_id=1, source_target_pairs={{0,2},{1,3},{2,0},{3,1},{4,6},{5,7},{6,4},{7,5},{8,10},{9,11},{10,... | collective-permute-start | bytes 196616 | tf_op jit(solution)/shard_map/ppermute | solution.py:31
  31.1 6.6 %collective-permute-start.5 = (bf16[256,128]{1,0:T(8,128)(2,1)S(1)}, bf16[256,128]{1,0:T(8,128)(2,1)S(1)}, u32[]{:S(2)}, u32[]{:S(2)}) collective-permute-start(bf16[256,128]{1,0:T(8,128)(2,1)S(1)} %get-tuple-element.46), channel_id=1, source_target_pairs={{0,4},{1,5},{2,6},{3,7},{4,0},{5,1},{6,2},{7,3},{8,12},{9,13},{10,... | collective-permute-start | bytes 196616 | tf_op jit(solution)/shard_map/ppermute | solution.py:31
  33.7 6.1 %collective-permute-start.6 = (bf16[256,128]{1,0:T(8,128)(2,1)S(1)}, bf16[256,128]{1,0:T(8,128)(2,1)S(1)}, u32[]{:S(2)}, u32[]{:S(2)}) collective-permute-start(bf16[256,128]{1,0:T(8,128)(2,1)S(1)} %get-tuple-element.47), channel_id=1, source_target_pairs={{0,6},{1,7},{2,4},{3,5},{4,2},{5,3},{6,0},{7,1},{8,14},{9,15},{10,... | collective-permute-start | bytes 196616 | tf_op jit(solution)/shard_map/ppermute | solution.py:31
  39.8 6.4 %collective-permute-start.11 = (bf16[256,512]{1,0:T(8,128)(2,1)S(1)}, bf16[256,512]{1,0:T(8,128)(2,1)S(1)}, u32[]{:S(2)}, u32[]{:S(2)}) collective-permute-start(bf16[256,512]{1,0:T(8,128)(2,1)S(1)} %constant_dynamic-update-slice_fusion.refs_0_), channel_id=1, source_target_pairs={{0,16},{8,24},{16,0},{24,8},{1,17},{9,25},{17,1},{25,9},{2,18},{10... | collective-permute-start | bytes 786440 | tf_op jit(solution)/shard_map/ppermute | solution.py:31
  40.4 6.8 %collective-permute-start.10 = (bf16[256,512]{1,0:T(8,128)(2,1)S(1)}, bf16[256,512]{1,0:T(8,128)(2,1)S(1)}, u32[]{:S(2)}, u32[]{:S(2)}) collective-permute-start(bf16[256,512]{1,0:T(8,128)(2,1)S(1)} %constant_dynamic-update-slice_fusion.refs_0_), channel_id=1, source_target_pairs={{0,8},{8,0},{16,24},{24,16},{1,9},{9,1},{17,25},{25,17},{2,10},{10... | collective-permute-start | bytes 786440 | tf_op jit(solution)/shard_map/ppermute | solution.py:31
  43.0 11.7 %collective-permute-start.9 = (bf16[512,2048]{1,0:T(8,128)(2,1)S(1)}, bf16[512,2048]{1,0:T(8,128)(2,1)S(1)}, u32[]{:S(2)}, u32[]{:S(2)}) collective-permute-start(bf16[512,2048]{1,0:T(8,128)(2,1)S(1)} %lay.5.own_ref), channel_id=1, source_target_pairs={{0,1},{1,0},{2,3},{3,2},{4,5},{5,4},{6,7},{7,6},{8,9},{9,8},{10,11... | collective-permute-start | bytes 6291464 | tf_op jit(solution)/shard_map/ppermute | solution.py:31
  47.2 5.3 %collective-permute-start.12 = (bf16[128,512]{1,0:T(8,128)(2,1)S(1)}, bf16[128,512]{1,0:T(8,128)(2,1)S(1)}, u32[]{:S(2)}, u32[]{:S(2)}) collective-permute-start(bf16[128,512]{1,0:T(8,128)(2,1)S(1)} %get-tuple-element.62), channel_id=1, source_target_pairs={{0,8},{8,0},{16,24},{24,16},{1,9},{9,1},{17,25},{25,17},{2,10},{10... | collective-permute-start | bytes 393224 | tf_op jit(solution)/shard_map/ppermute | solution.py:31
  49.6 5.0 %collective-permute-start.13 = (bf16[128,512]{1,0:T(8,128)(2,1)S(1)}, bf16[128,512]{1,0:T(8,128)(2,1)S(1)}, u32[]{:S(2)}, u32[]{:S(2)}) collective-permute-start(bf16[128,512]{1,0:T(8,128)(2,1)S(1)} %get-tuple-element.63), channel_id=1, source_target_pairs={{0,16},{8,24},{16,0},{24,8},{1,17},{9,25},{17,1},{25,9},{2,18},{10... | collective-permute-start | bytes 393224 | tf_op jit(solution)/shard_map/ppermute | solution.py:31
  56.3 17.8 %collective-permute-start.14 = (bf16[1024,256]{1,0:T(8,128)(2,1)S(1)}, bf16[1024,256]{1,0:T(8,128)(2,1)S(1)}, u32[]{:S(2)}, u32[]{:S(2)}) collective-permute-start(bf16[1024,256]{1,0:T(8,128)(2,1)S(1)} %products.4), channel_id=1, source_target_pairs={{0,2},{1,3},{2,0},{3,1},{4,6},{5,7},{6,4},{7,5},{8,10},{9,11},{10,... | collective-permute-start | bytes 1572872 | tf_op jit(solution)/shard_map/ppermute | solution.py:31
  56.4 24.7 %collective-permute-start.16 = (bf16[1024,256]{1,0:T(8,128)(2,1)S(1)}, bf16[1024,256]{1,0:T(8,128)(2,1)S(1)}, u32[]{:S(2)}, u32[]{:S(2)}) collective-permute-start(bf16[1024,256]{1,0:T(8,128)(2,1)S(1)} %products.3), channel_id=1, source_target_pairs={{0,4},{1,5},{2,6},{3,7},{4,0},{5,1},{6,2},{7,3},{8,12},{9,13},{10,... | collective-permute-start | bytes 1572872 | tf_op jit(solution)/shard_map/ppermute | solution.py:31
  74.1 13.1 %collective-permute-start.15 = (bf16[1024,128]{1,0:T(8,128)(2,1)S(1)}, bf16[1024,128]{1,0:T(8,128)(2,1)S(1)}, u32[]{:S(2)}, u32[]{:S(2)}) collective-permute-start(bf16[1024,128]{1,0:T(8,128)(2,1)S(1)} %add_convert_fusion.1), channel_id=1, source_target_pairs={{0,4},{1,5},{2,6},{3,7},{4,0},{5,1},{6,2},{7,3},{8,12},{9,13},{10,... | collective-permute-start | bytes 786440 | tf_op jit(solution)/shard_map/ppermute | solution.py:31
  81.1 8.9 %copy-start.4 = (s32[2048,128]{1,0:T(8,128)S(1)}, s32[2048,128]{1,0:T(8,128)}, u32[]{:S(2)}) copy-start(s32[2048,128]{1,0:T(8,128)} %param.10) | copy-start | bytes 3145732
  81.1 8.8 %collective-permute-start.17 = (bf16[1024,128]{1,0:T(8,128)(2,1)S(1)}, bf16[1024,128]{1,0:T(8,128)(2,1)S(1)}, u32[]{:S(2)}, u32[]{:S(2)}) collective-permute-start(bf16[1024,128]{1,0:T(8,128)(2,1)S(1)} %add_convert_fusion), channel_id=1, source_target_pairs={{0,2},{1,3},{2,0},{3,1},{4,6},{5,7},{6,4},{7,5},{8,10},{9,11},{10,... | collective-permute-start | bytes 786440 | tf_op jit(solution)/shard_map/ppermute | solution.py:31
